TPU v7x, 32 devices: a whole 2x2x4 slice. The times are simulated.
32 devices in a mesh: seq: 8 (over z, y), wt: 4 (over x, core).
Axes of the slice: x: 2, y: 2, z: 4, core: 2. Of those that a mesh axis runs over, the one named last changes fastest.
Arguments:
- tokens: bfloat16 [4, 2048, 2048], P('wt', 'seq'), may hold values from -6 to 6
- in_proj: bfloat16 [3, 2048, 2048], P(None, None, 'wt'), may hold values from -0.125 to 0.125
- out_proj: bfloat16 [2048, 2048], P('wt'), may hold values from -0.125 to 0.125
- gate_up: bfloat16 [2, 2048, 5632], P(None, None, 'wt'), may hold values from -0.125 to 0.125
- down: bfloat16 [5632, 2048], P('wt'), may hold values from -0.078125 to 0.078125
- norm1_gain: float32 [2048], replicated, may hold values from 0.5 to 1.5
- mixer_gain: float32 [2048], replicated, may hold values from 0.5 to 1.5
- norm2_gain: float32 [2048], replicated, may hold values from 0.5 to 1.5
- lower_bound: float32 [2048], replicated, may hold values from 0.9 to 1
- cotangent: bfloat16 [4, 2048, 2048], P('wt', 'seq'), may hold values from -6 to 6
Outputs:
- block_out: bfloat16 [4, 2048, 2048], P('wt', 'seq')
- input_grad: float32 [4, 2048, 2048], P('wt', 'seq')
- in_proj_grad: float32 [3, 2048, 2048], P(None, 'seq', 'wt')
- out_proj_grad: float32 [2048, 2048], P('wt', 'seq')
- gate_up_grad: float32 [2, 2048, 5632], P(None, 'seq', 'wt')
- down_grad: float32 [5632, 2048], P('wt', 'seq')
- norm1_grad: float32 [2048], P('wt')
- mixer_grad: float32 [2048], P('wt')
- norm2_grad: float32 [2048], P('wt')
- bound_grad: float32 [2048], P('wt')
All inputs are finite; a program needn't handle non-finite values.
Results may differ from a plain program's by a relative error of at most 0.015.
Values may be sent and summed in bfloat16 or wider, within the bound.
No kernel may reach another device: no remote copies, remote signals or barrier semaphores. Data moves between devices by JAX's collectives and lax.ppermute only.
A program may use at most 320 MiB of HBM per device.

v0:
```python
import jax
import jax.numpy as jnp
from jax import lax
from jax.sharding import PartitionSpec as P

EPS = 1e-06


def rms_scale(values):
    return lax.rsqrt(jnp.mean(values * values, axis=-1, keepdims=True) + EPS)


def norm_back(grad_normed, values, scale, weight):
    weighted = grad_normed * weight
    return scale * weighted - values * (scale * scale * scale) * jnp.mean(
        weighted * values, axis=-1, keepdims=True
    )


def silu_slope(values):
    sigmoid_part = jax.nn.sigmoid(values)
    return sigmoid_part * (1.0 + values * (1.0 - sigmoid_part))


def left_product(left, right):
    return lax.dot_general(
        left, right, (((0,), (0,)), ((), ())), preferred_element_type=jnp.float32
    )


def right_product(left, right):
    return lax.dot_general(
        left, right, (((1,), (1,)), ((), ())), preferred_element_type=jnp.float32
    )


def shift_blocks(values, axis, reverse):
    edge = jnp.zeros_like(lax.slice_in_dim(values, 0, 1, axis=axis))
    extent = values.shape[axis]
    if reverse:
        return jnp.concatenate([lax.slice_in_dim(values, 1, extent, axis=axis), edge], axis=axis)
    return jnp.concatenate([edge, lax.slice_in_dim(values, 0, extent - 1, axis=axis)], axis=axis)


def chain_logs(logs, drive, last, reverse, first):
    axis = logs.ndim - 1
    length = logs.shape[axis]
    block = 32 if length > 32 and length % 32 == 0 else length
    count = length // block
    shape = logs.shape
    blocked = shape[:-1] + (count, block)
    form = "...cbs,ts->...cbt"
    logs_b = logs.reshape(blocked)
    drive_b = drive.reshape(blocked)
    later = lax.broadcasted_iota(jnp.int32, (block, block), 0)
    earlier = lax.broadcasted_iota(jnp.int32, (block, block), 1)
    keep = later <= earlier if reverse else later >= earlier
    tri = keep.astype(jnp.float32)
    cum = jnp.einsum(
        form, logs_b, tri, precision=lax.Precision.HIGHEST, preferred_element_type=jnp.float32
    )
    if first:
        local = jnp.exp(cum) * jnp.einsum(
            form,
            drive_b * jnp.exp(-cum),
            tri,
            precision=lax.Precision.HIGHEST,
            preferred_element_type=jnp.float32,
        )
    else:
        diff = cum[..., :, None] - cum[..., None, :]
        weight = jnp.exp(jnp.where(keep, diff, -1e30))
        local = jnp.sum(weight * drive_b[..., None, :], axis=-1)
    if count > 1:
        pick = 0 if reverse else block - 1
        inner_axis = len(blocked) - 1
        total_logs = lax.index_in_dim(cum, pick, axis=inner_axis, keepdims=False)
        total_state = lax.index_in_dim(local, pick, axis=inner_axis, keepdims=False)
        outer_logs, outer_state = chain_logs(total_logs, total_state, last, reverse, False)
        outer_axis = total_logs.ndim - 1
        prior_logs = jnp.expand_dims(shift_blocks(outer_logs, outer_axis, reverse), inner_axis)
        prior_state = jnp.expand_dims(shift_blocks(outer_state, outer_axis, reverse), inner_axis)
        local = local + jnp.exp(cum) * prior_state
        cum = cum + prior_logs
    return (cum.reshape(shape), local.reshape(shape))


def chain_scan(forget, drive, reverse):
    cum, state = chain_logs(jnp.log(forget), drive, True, reverse, True)
    return (jnp.exp(cum), state)


def on_device(
    tokens,
    in_proj,
    out_proj,
    gate_up,
    down,
    norm1_gain,
    mixer_gain,
    norm2_gain,
    lower_bound,
    cotangent,
):
    width = in_proj.shape[1]
    inputs = tokens[0].astype(jnp.float32)
    upstream = cotangent[0].astype(jnp.float32)
    grad_out = cotangent[0]
    positions = inputs.shape[0]
    scale_one = rms_scale(inputs)
    normed = (inputs * scale_one * norm1_gain).astype(jnp.bfloat16)
    in_use, out_use, gate_use, down_use = (in_proj, out_proj, gate_up, down)
    offset = lax.axis_index("wt") * in_proj.shape[2]
    lower_use = lax.dynamic_slice_in_dim(lower_bound, offset, in_proj.shape[2])
    mixer_use = lax.dynamic_slice_in_dim(mixer_gain, offset, in_proj.shape[2])
    normed_all, grad_out_all = (
        lax.all_gather(normed[None], "wt", axis=0, tiled=True),
        lax.all_gather(grad_out[None], "wt", axis=0, tiled=True),
    )
    groups = normed_all.shape[0]
    chans = in_use.shape[2]
    total_rows = groups * positions
    rows = normed_all.reshape(total_rows, width)
    grad_rows = grad_out_all.reshape(total_rows, width)

    def shaped(values):
        return values.reshape(groups, positions, values.shape[-1])

    project = jnp.einsum("rd,kdc->krc", rows, in_use, preferred_element_type=jnp.float32)
    pre_input, pre_forget, pre_gate = (project[0], project[1], project[2])
    forget_sig = jax.nn.sigmoid(pre_forget)
    forget = lower_use + (1.0 - lower_use) * forget_sig
    input_act = jax.nn.silu(pre_input)
    drive = input_act * (1.0 - forget)
    forget_turned = jnp.swapaxes(shaped(forget), 1, 2)
    drive_turned = jnp.swapaxes(shaped(drive), 1, 2)
    forget_chan, drive_chan = (
        lax.all_to_all(forget_turned, "seq", split_axis=1, concat_axis=2, tiled=True),
        lax.all_to_all(drive_turned, "seq", split_axis=1, concat_axis=2, tiled=True),
    )
    state_chan = chain_scan(forget_chan, drive_chan, False)[1]
    state_back_turned = lax.all_to_all(state_chan, "seq", split_axis=2, concat_axis=1, tiled=True)
    state = jnp.swapaxes(state_back_turned, 1, 2).reshape(total_rows, chans)
    squares = jnp.sum(state * state, axis=-1, keepdims=True)
    squares = lax.psum(squares, "wt")
    scale_two = lax.rsqrt(squares / width + EPS)
    unit_state = state * scale_two
    gate_act = jax.nn.silu(pre_gate)
    mixed = (unit_state * mixer_use * gate_act).astype(jnp.bfloat16)
    picked = mixed
    branch_own = lax.psum_scatter(
        jnp.dot(picked, out_use, preferred_element_type=jnp.float32).reshape(
            lax.axis_size("wt") * 1, positions, width
        ),
        "wt",
        scatter_dimension=0,
        tiled=True,
    )[0]
    middle = inputs + branch_own
    scale_three = rms_scale(middle)
    normed_two = (middle * scale_three * norm2_gain).astype(jnp.bfloat16)
    rows_two = lax.all_gather(normed_two[None], "wt", axis=0, tiled=True).reshape(total_rows, width)
    both = jnp.einsum("rd,kdf->krf", rows_two, gate_use, preferred_element_type=jnp.float32)
    gate_part = both[0]
    up_part = both[1]
    gate_sig = jax.nn.sigmoid(gate_part)
    hidden = (gate_part * gate_sig * up_part).astype(jnp.bfloat16)
    picked = hidden
    ffn_own = lax.psum_scatter(
        jnp.dot(picked, down_use, preferred_element_type=jnp.float32)
        .reshape(1 * lax.axis_size("wt"), positions, width)
        .astype(jnp.bfloat16),
        "wt",
        scatter_dimension=0,
        tiled=True,
    ).astype(jnp.float32)[0]
    result = middle + ffn_own
    grad_hidden = right_product(grad_rows, down_use)
    grad_gate = grad_hidden * up_part * gate_sig * (1.0 + gate_part * (1.0 - gate_sig))
    grad_up = grad_hidden * gate_part * gate_sig
    grad_both = jnp.stack([grad_gate, grad_up]).astype(jnp.bfloat16)
    picked = grad_both
    grad_normed_two = lax.psum_scatter(
        jnp.einsum("krf,kdf->rd", picked, gate_use, preferred_element_type=jnp.float32).reshape(
            lax.axis_size("wt") * 1, positions, width
        ),
        "wt",
        scatter_dimension=0,
        tiled=True,
    )[0]
    grad_middle = upstream + norm_back(grad_normed_two, middle, scale_three, norm2_gain)
    norm2_term = jnp.sum(grad_normed_two * middle * scale_three, axis=0)
    grad_branch = grad_middle.astype(jnp.bfloat16)
    branch_all = lax.all_gather(grad_branch[None], "wt", axis=0, tiled=True).reshape(
        total_rows, width
    )
    grad_mixed = right_product(branch_all, out_use)
    mixer_term = jnp.sum(grad_mixed * gate_act * unit_state, axis=0)
    grad_pre_gate = grad_mixed * mixer_use * unit_state * silu_slope(pre_gate)
    weighted = grad_mixed * gate_act * mixer_use
    inner = jnp.sum(weighted * state, axis=-1, keepdims=True)
    inner = lax.psum(inner, "wt")
    grad_state = scale_two * weighted - state * (scale_two * scale_two * scale_two) * (
        inner / width
    )
    grad_chan = lax.all_to_all(
        jnp.swapaxes(shaped(grad_state), 1, 2).astype(jnp.bfloat16),
        "seq",
        split_axis=1,
        concat_axis=2,
        tiled=True,
    ).astype(jnp.float32)
    next_forget = jnp.concatenate(
        [forget_chan[:, :, 1:], jnp.ones_like(forget_chan[:, :, :1])], axis=2
    )
    adjoint_chan = chain_scan(next_forget, grad_chan, True)[1]
    before_chan = jnp.concatenate(
        [jnp.zeros_like(state_chan[:, :, :1]), state_chan[:, :, :-1]], axis=2
    )
    grad_forget, grad_drive = (
        lax.all_to_all(
            (adjoint_chan * before_chan).astype(jnp.bfloat16),
            "seq",
            split_axis=2,
            concat_axis=1,
            tiled=True,
        ).astype(jnp.float32),
        lax.all_to_all(
            adjoint_chan.astype(jnp.bfloat16), "seq", split_axis=2, concat_axis=1, tiled=True
        ).astype(adjoint_chan.dtype),
    )
    grad_forget = jnp.swapaxes(grad_forget, 1, 2).reshape(total_rows, chans)
    grad_drive = jnp.swapaxes(grad_drive, 1, 2).reshape(total_rows, chans)
    grad_gate_total = grad_forget - grad_drive * input_act
    grad_pre_input = grad_drive * (1.0 - forget) * silu_slope(pre_input)
    grad_pre_forget = grad_gate_total * (1.0 - lower_use) * forget_sig * (1.0 - forget_sig)
    bound_term = jnp.sum(grad_gate_total * (1.0 - forget_sig), axis=0)
    grad_project = jnp.stack([grad_pre_input, grad_pre_forget, grad_pre_gate]).astype(jnp.bfloat16)
    picked = grad_project
    grad_normed = lax.psum_scatter(
        jnp.einsum("krc,kdc->rd", picked, in_use, preferred_element_type=jnp.float32)
        .reshape(1 * lax.axis_size("wt"), positions, width)
        .astype(jnp.bfloat16),
        "wt",
        scatter_dimension=0,
        tiled=True,
    ).astype(jnp.float32)[0]
    norm1_term = jnp.sum(grad_normed * inputs * scale_one, axis=0)
    grad_inputs = grad_middle + norm_back(grad_normed, inputs, scale_one, norm1_gain)
    in_term = jnp.einsum("rd,krc->kdc", rows, grad_project, preferred_element_type=jnp.float32)
    out_term = left_product(mixed, branch_all)
    gate_term = jnp.einsum("rd,krf->kdf", rows_two, grad_both, preferred_element_type=jnp.float32)
    down_term = left_product(hidden, grad_rows)
    in_proj_grad, out_proj_grad, gate_up_grad, down_grad = (
        lax.psum_scatter(
            in_term.astype(jnp.bfloat16), "seq", scatter_dimension=1, tiled=True
        ).astype(jnp.float32),
        lax.psum_scatter(
            out_term.astype(jnp.bfloat16), "seq", scatter_dimension=1, tiled=True
        ).astype(jnp.float32),
        lax.psum_scatter(
            gate_term.astype(jnp.bfloat16), "seq", scatter_dimension=1, tiled=True
        ).astype(jnp.float32),
        lax.psum_scatter(
            down_term.astype(jnp.bfloat16), "seq", scatter_dimension=1, tiled=True
        ).astype(jnp.float32),
    )
    mixer_full = lax.dynamic_update_slice_in_dim(
        jnp.zeros((width,), jnp.float32), mixer_term, offset, 0
    )
    bound_full = lax.dynamic_update_slice_in_dim(
        jnp.zeros((width,), jnp.float32), bound_term, offset, 0
    )
    gain_total = lax.psum(
        jnp.stack([norm1_term, mixer_full, norm2_term, bound_full]), ("seq", "wt")
    )
    block = width // lax.axis_size("wt")
    gain_own = lax.dynamic_slice_in_dim(gain_total, lax.axis_index("wt") * block, block, 1)
    return (
        result.astype(jnp.bfloat16)[None],
        grad_inputs[None],
        in_proj_grad,
        out_proj_grad,
        gate_up_grad,
        down_grad,
        gain_own[0],
        gain_own[1],
        gain_own[2],
        gain_own[3],
    )


def solution(mesh):
    placed = (
        P("wt", "seq", None),
        P(None, None, "wt"),
        P("wt", None),
        P(None, None, "wt"),
        P("wt", None),
        P(),
        P(),
        P(),
        P(),
        P("wt", "seq", None),
    )
    return jax.shard_map(
        on_device,
        mesh=mesh,
        in_specs=placed,
        out_specs=(
            P("wt", "seq", None),
            P("wt", "seq", None),
            P(None, "seq", "wt"),
            P("wt", "seq"),
            P(None, "seq", "wt"),
            P("wt", "seq"),
            P("wt"),
            P("wt"),
            P("wt"),
            P("wt"),
        ),
        check_vma=False,
    )
```

profile of v0, /device:TPU:0, one launch (start us, length us, event | category | flops | bytes accessed | tf_op | source)
XLA Modules:
  0.0 1302.5 jit_solution(14505970257106388783)
XLA Ops:
  12.8 36.5 %all-gather.5.cloned.1.call-done = bf16[4,256,2048]{2,1,0:T(8,128)(2,1)} async-done(((bf16[1,256,2048]{2,1,0:T(8,128)(2,1)}), bf16[4,256,2048]{2,1,0:T(8,128)(2,1)}) %all-gather.5.cloned.1.call-update) | async-done | bytes 4194320 | tf_op jit(solution)/shard_map/all_gather | solution.py:117
  49.4 10.2 convolution_bitcast_fusion.1
  86.6 44.5 %all-to-all-done.1 = f32[4,512,256]{2,0,1:T(4,128)} async-done(((f32[4,512,256]{2,0,1:T(4,128)}), f32[4,512,256]{2,0,1:T(4,128)}, u32[]{:S(2)}, u32[]{:S(2)}) %all-to-all-start.1) | async-done | bytes 2097184 | tf_op jit(solution)/shard_map/all_to_all | solution.py:139
  142.8 6.8 copy.265
  149.7 33.9 %all-to-all-done = f32[4,512,256]{2,0,1:T(4,128)} async-done(((f32[4,512,256]{2,0,1:T(4,128)}), f32[4,512,256]{2,0,1:T(4,128)}, u32[]{:S(2)}, u32[]{:S(2)}) %all-to-all-start) | async-done | bytes 2097184 | tf_op jit(solution)/shard_map/all_to_all | solution.py:138
  192.2 6.8 copy.259
  211.6 6.7 multiply_add_fusion.1
  218.4 6.8 copy.273
  225.1 7.4 copy.327
  232.5 17.1 %reshape.438 = f32[8,1,65536]{2,1,0:T(1,128)} reshape(f32[2048,4,64]{2,1,0:T(4,128)} %bitcast.368) | data formatting | bytes 4194304
  257.6 44.1 %all-to-all-done.2 = f32[8,1,65536]{2,1,0:T(1,128)} async-done(((f32[8,1,65536]{2,1,0:T(1,128)}), f32[8,1,65536]{2,1,0:T(1,128)}, u32[]{:S(2)}, u32[]{:S(2)}) %all-to-all-start.2) | async-done | bytes 2097184 | tf_op jit(solution)/shard_map/all_to_all | solution.py:142
  302.2 8.5 reduce.8
  310.8 6.5 reshape.439
  323.8 5.9 psum.21
  340.2 70.8 %reduce-scatter.9.cloned.1.call-done = f32[1,256,2048]{2,1,0:T(8,128)} async-done(((f32[4,256,2048]{2,1,0:T(8,128)}), f32[1,256,2048]{2,1,0:T(8,128)}) %reduce-scatter.9.cloned.1.call-update) | async-done | bytes 2097168 | tf_op jit(solution)/shard_map/reduce_scatter | solution.py:151
  415.4 33.8 %all-gather.7.cloned.1.call-done = bf16[4,256,2048]{2,1,0:T(8,128)(2,1)} async-done(((bf16[1,256,2048]{2,1,0:T(8,128)(2,1)}), bf16[4,256,2048]{2,1,0:T(8,128)(2,1)}) %all-gather.7.cloned.1.call-update) | async-done | bytes 4194320 | tf_op jit(solution)/shard_map/all_gather | solution.py:162
  449.2 18.7 %convolution_bitcast_fusion = f32[2,1024,1408]{2,1,0:T(8,128)} fusion(bf16[1024,2048,1]{1,0,2:T(8,128)(2,1)} %bitcast.423, bf16[2,2048,1408]{2,1,0:T(8,128)(2,1)} %param.13), kind=kOutput, calls=%fused_computation.3 | convolution fusion | flops 11811160064 | bytes 27262976 | tf_op jit(solution)/shard_map/rd,kdf->krf/dot_general | solution.py:163
  468.0 17.3 %all-gather.9.cloned.1.call-done = bf16[4,256,2048]{2,1,0:T(8,128)(2,1)} async-done(((bf16[1,256,2048]{2,1,0:T(8,128)(2,1)}), bf16[4,256,2048]{2,1,0:T(8,128)(2,1)}) %all-gather.9.cloned.1.call-update) | async-done | bytes 4194320 | tf_op jit(solution)/shard_map/all_gather | solution.py:118
  485.3 14.1 %fusion.31 = (bf16[1,1024,1408]{2,1,0:T(8,128)(2,1)S(1)}, bf16[1,1024,1408]{2,1,0:T(8,128)(2,1)S(1)}) fusion(f32[2,1024,1408]{2,1,0:T(8,128)} %convolution_bitcast_fusion, bf16[1024,2048]{1,0:T(8,128)(2,1)} %bitcast.425, bf16[1408,2048]{1,0:T(8,128)(2,1)} %param.14), kind=kOutput, calls=%fused_computation.55 | convolution fusion | flops 5924323328 | bytes 27262976 | tf_op jit(solution)/shard_map/dot_general | solution.py:32
  499.4 19.0 %fusion.23 = f32[1024,2048,1]{1,0,2:T(8,128)} fusion(bf16[2,2048,1408]{2,1,0:T(8,128)(2,1)} %param.13, bf16[1,1024,1408]{2,1,0:T(8,128)(2,1)S(1)} %get-tuple-element.83, bf16[1,1024,1408]{2,1,0:T(8,128)(2,1)S(1)} %get-tuple-element.82), kind=kOutput, calls=%fused_computation.42 | convolution fusion | flops 11814043648 | bytes 25690112 | tf_op jit(solution)/shard_map/krf,kdf->rd/dot_general | solution.py:184
  518.8 7.6 fusion.98
  526.5 13.8 %fusion.20 = bf16[4,256,2048]{2,1,0:T(8,128)(2,1)} fusion(bf16[1408,2048]{1,0:T(8,128)(2,1)} %param.14, f32[4,256,1408]{2,1,0:T(8,128)} %bitcast.384, f32[4,256,1408]{2,1,0:T(8,128)S(1)} %bitcast.383), kind=kOutput, calls=%fused_computation.41 | convolution fusion | flops 5916327936 | bytes 21495808 | tf_op jit(solution)/shard_map/dot_general | solution.py:170
  540.4 49.9 %reduce-scatter.13.cloned.1.call-done = f32[1,256,2048]{2,1,0:T(8,128)} async-done(((f32[4,256,2048]{2,1,0:T(8,128)}), f32[1,256,2048]{2,1,0:T(8,128)}) %reduce-scatter.13.cloned.1.call-update) | async-done | bytes 2097168 | tf_op jit(solution)/shard_map/reduce_scatter | solution.py:183
  593.1 44.1 %reduce-scatter.11.cloned.1.call-done = bf16[1,256,2048]{2,1,0:T(8,128)(2,1)} async-done(((bf16[4,256,2048]{2,1,0:T(8,128)(2,1)}), bf16[1,256,2048]{2,1,0:T(8,128)(2,1)}) %reduce-scatter.11.cloned.1.call-update) | async-done | bytes 1048592 | tf_op jit(solution)/shard_map/reduce_scatter | solution.py:169
  637.2 5.7 fusion.97
  643.0 13.3 %convolution_convert_fusion = bf16[1408,2048]{1,0:T(8,128)(2,1)} fusion(bf16[1024,2048]{1,0:T(8,128)(2,1)} %bitcast.426, f32[2,1024,1408]{2,1,0:T(8,128)} %convolution_bitcast_fusion), kind=kOutput, calls=%fused_computation.2 | convolution fusion | flops 5917114368 | bytes 21495808 | tf_op jit(solution)/shard_map/dot_general | solution.py:26
  656.5 18.4 %convert_bitcast_fusion = bf16[2,2048,1408]{1,2,0:T(8,128)(2,1)} fusion(bf16[1024,2048,1]{1,0,2:T(8,128)(2,1)} %bitcast.424, bf16[1,1024,1408]{2,1,0:T(8,128)(2,1)} %copy-done.28, bf16[1,1024,1408]{2,1,0:T(8,128)(2,1)} %copy-done.27), kind=kOutput, calls=%fused_computation | convolution fusion | flops 11819810816 | bytes 21495808 | tf_op jit(solution)/shard_map/rd,krf->kdf/dot_general | solution.py:252
  677.8 8.3 multiply_reduce_fusion.3
  686.1 5.7 psum.22
  698.7 6.2 all-to-all-start.3
  713.3 6.8 copy.282
  727.0 29.7 %all-to-all-done.3 = bf16[4,512,256]{2,0,1:T(4,128)(2,1)} async-done(((bf16[4,512,256]{2,0,1:T(4,128)(2,1)}), bf16[4,512,256]{2,0,1:T(4,128)(2,1)}, u32[]{:S(2)}, u32[]{:S(2)}) %all-to-all-start.3) | async-done | bytes 1048608 | tf_op jit(solution)/shard_map/all_to_all | solution.py:206
  763.6 6.7 copy.287
  770.3 8.1 exponential_multiply_fusion
  783.2 6.7 multiply_add_fusion
  790.0 6.7 copy.295
  799.2 10.9 copy.329
  822.8 10.7 copy.328
  837.9 27.6 %all-to-all-done.4 = bf16[8,2,32768]{2,1,0:T(2,128)(2,1)} async-done(((bf16[8,2,32768]{2,1,0:T(2,128)(2,1)}), bf16[8,2,32768]{2,1,0:T(2,128)(2,1)}, u32[]{:S(2)}, u32[]{:S(2)}) %all-to-all-start.4) | async-done | bytes 1048608 | tf_op jit(solution)/shard_map/all_to_all | solution.py:228
  871.2 6.3 bitcast_convert_fusion.1
  889.5 35.1 %all-to-all-done.5 = bf16[8,2,32768]{2,1,0:T(2,128)(2,1)} async-done(((bf16[8,2,32768]{2,1,0:T(2,128)(2,1)}), bf16[8,2,32768]{2,1,0:T(2,128)(2,1)}, u32[]{:S(2)}, u32[]{:S(2)}) %all-to-all-start.5) | async-done | bytes 1048608 | tf_op jit(solution)/shard_map/all_to_all | solution.py:221
  946.9 12.0 bitcast_convert_fusion
  959.2 11.8 convert_bitcast_fusion.1
  973.3 79.2 %reduce-scatter.21.cloned.1.call-done = bf16[2,256,1408]{1,2,0:T(8,128)(2,1)} async-done(((bf16[2,2048,1408]{1,2,0:T(8,128)(2,1)}), bf16[2,256,1408]{1,2,0:T(8,128)(2,1)}) %reduce-scatter.21.cloned.1.call-update) | async-done | bytes 1441808 | tf_op jit(solution)/shard_map/reduce_scatter | solution.py:261
  1059.8 63.6 %reduce-scatter.19.cloned.1.call-done = bf16[512,256]{1,0:T(8,128)(2,1)} async-done(((bf16[512,2048]{1,0:T(8,128)(2,1)}), bf16[512,256]{1,0:T(8,128)(2,1)}) %reduce-scatter.19.cloned.1.call-update) | async-done | bytes 262160 | tf_op jit(solution)/shard_map/reduce_scatter | solution.py:258
  1125.3 44.4 %reduce-scatter.15.cloned.1.call-done = bf16[1,256,2048]{2,1,0:T(8,128)(2,1)} async-done(((bf16[4,256,2048]{2,1,0:T(8,128)(2,1)}), bf16[1,256,2048]{2,1,0:T(8,128)(2,1)}) %reduce-scatter.15.cloned.1.call-update) | async-done | bytes 1048592 | tf_op jit(solution)/shard_map/reduce_scatter | solution.py:240
  1171.6 42.8 %psum.23 = f32[4,2048]{1,0:T(4,128)S(1)} all-reduce(f32[4,2048]{1,0:T(4,128)S(1)} %pad_maximum_fusion.6), channel_id=1, replica_groups=mesh['seq'=8,'wt'=4] {'seq','wt'}, use_global_device_ids=true, to_apply=%region_24.25 | all-reduce | flops 8192 | bytes 65536 | tf_op jit(solution)/shard_map/psum | solution.py:274
  1218.9 73.7 %reduce-scatter.17.cloned.1.call-done = bf16[3,256,512]{1,2,0:T(8,128)(2,1)} async-done(((bf16[3,2048,512]{1,2,0:T(8,128)(2,1)}), bf16[3,256,512]{1,2,0:T(8,128)(2,1)}) %reduce-scatter.17.cloned.1.call-update) | async-done | bytes 786448 | tf_op jit(solution)/shard_map/reduce_scatter | solution.py:255
  (205 shorter events, 215.7 us)
Async XLA Ops:
  7.2 327.3 %copy-start = (bf16[512,2048]{1,0:T(8,128)(2,1)S(1)}, bf16[512,2048]{1,0:T(8,128)(2,1)}, u32[]{:S(2)}) copy-start(bf16[512,2048]{1,0:T(8,128)(2,1)} %param.12) | copy-start | bytes 6291460
  7.2 42.2 %all-gather.5.cloned.1.call-start = ((), (), s32[]{:S(2)}) async-start(), calls=%async_computation.14 | async-start | bytes 5242880 | tf_op jit(solution)/shard_map/all_gather | solution.py:117
  9.5 2.5 copy-start.23
  12.8 57.1 %copy-start.18 = (f32[512]{0:T(512)}, f32[512]{0:T(512)S(1)}, u32[]{:S(2)}) copy-start(f32[512]{0:T(512)S(1)} %get-tuple-element.80) | copy-start | bytes 6148
  12.8 57.1 %copy-start.20 = (f32[512]{0:T(512)}, f32[512]{0:T(512)S(1)}, u32[]{:S(2)}) copy-start(f32[512]{0:T(512)S(1)} %get-tuple-element.81) | copy-start | bytes 6148
  59.5 4.6 copy-start.5
  76.8 54.3 %all-to-all-start.1 = ((f32[4,512,256]{2,0,1:T(4,128)}), f32[4,512,256]{2,0,1:T(4,128)}, u32[]{:S(2)}, u32[]{:S(2)}) async-start(f32[4,512,256]{2,0,1:T(4,128)} %copy.262), calls=%async_computation.1 | async-start | bytes 4194304 | tf_op jit(solution)/shard_map/all_to_all | solution.py:139
  131.1 52.4 %all-to-all-start = ((f32[4,512,256]{2,0,1:T(4,128)}), f32[4,512,256]{2,0,1:T(4,128)}, u32[]{:S(2)}, u32[]{:S(2)}) async-start(f32[4,512,256]{2,0,1:T(4,128)} %copy.256), calls=%async_computation | async-start | bytes 4194304 | tf_op jit(solution)/shard_map/all_to_all | solution.py:138
  185.5 1.3 copy-start.6
  199.0 4.7 copy-start.9
  203.6 3.6 copy-start.3
  207.2 2.0 copy-start.7
  249.6 52.2 %all-to-all-start.2 = ((f32[8,1,65536]{2,1,0:T(1,128)}), f32[8,1,65536]{2,1,0:T(1,128)}, u32[]{:S(2)}, u32[]{:S(2)}) async-start(f32[8,1,65536]{2,1,0:T(1,128)} %reshape.438), calls=%async_computation.2 | async-start | bytes 4194304 | tf_op jit(solution)/shard_map/all_to_all | solution.py:142
  253.9 157.1 %reduce-scatter.9.cloned.1.call-start = ((), (), s32[]{:S(2)}) async-start(), calls=%async_computation.15 | async-start | bytes 10485760 | tf_op jit(solution)/shard_map/reduce_scatter | solution.py:151
  330.4 1.2 copy-start.16
  334.5 5.6 copy-start.13
  340.1 70.9 %copy-start.1 = (bf16[1,256,2048]{2,1,0:T(8,128)(2,1)S(1)}, bf16[1,256,2048]{2,1,0:T(8,128)(2,1)}, u32[]{:S(2)}) copy-start(bf16[1,256,2048]{2,1,0:T(8,128)(2,1)} %param.10) | copy-start | bytes 3145732
  340.1 73.0 %copy-start.15 = (f32[2048]{0:T(1024)S(1)}, f32[2048]{0:T(1024)}, u32[]{:S(2)}) copy-start(f32[2048]{0:T(1024)} %param.17) | copy-start | bytes 24580
  340.1 109.1 %all-gather.7.cloned.1.call-start = ((), (), s32[]{:S(2)}) async-start(), calls=%async_computation.16 | async-start | bytes 5242880 | tf_op jit(solution)/shard_map/all_gather | solution.py:162
  411.0 2.2 copy-start.4
  414.6 70.7 %all-gather.9.cloned.1.call-start = ((), (), s32[]{:S(2)}) async-start(), calls=%async_computation.18 | async-start | bytes 5242880 | tf_op jit(solution)/shard_map/all_gather | solution.py:118
  415.2 175.1 %reduce-scatter.13.cloned.1.call-start = ((), (), s32[]{:S(2)}) async-start(), calls=%async_computation.19 | async-start | bytes 10485760 | tf_op jit(solution)/shard_map/reduce_scatter | solution.py:183
  499.3 19.0 %copy-start.27 = (bf16[1,1024,1408]{2,1,0:T(8,128)(2,1)}, bf16[1,1024,1408]{2,1,0:T(8,128)(2,1)S(1)}, u32[]{:S(2)}) copy-start(bf16[1,1024,1408]{2,1,0:T(8,128)(2,1)S(1)} %get-tuple-element.82) | copy-start | bytes 8650756
  499.4 19.0 %copy-start.28 = (bf16[1,1024,1408]{2,1,0:T(8,128)(2,1)}, bf16[1,1024,1408]{2,1,0:T(8,128)(2,1)S(1)}, u32[]{:S(2)}) copy-start(bf16[1,1024,1408]{2,1,0:T(8,128)(2,1)S(1)} %get-tuple-element.83) | copy-start | bytes 8650756
  518.4 118.8 %reduce-scatter.11.cloned.1.call-start = ((), (), s32[]{:S(2)}) async-start(), calls=%async_computation.17 | async-start | bytes 5242880 | tf_op jit(solution)/shard_map/reduce_scatter | solution.py:169
  540.3 137.5 %all-gather.11.cloned.1.call-start = ((), (), s32[]{:S(2)}) async-start(), calls=%async_computation.20 | async-start | bytes 5242880 | tf_op jit(solution)/shard_map/all_gather | solution.py:194
  642.9 328.0 %reduce-scatter.23.cloned.1.call-start = ((), (), s32[]{:S(2)}) async-start(), calls=%async_computation.25 | async-start | bytes 6488064 | tf_op jit(solution)/shard_map/reduce_scatter | solution.py:264
  656.3 396.2 %reduce-scatter.21.cloned.1.call-start = ((), (), s32[]{:S(2)}) async-start(), calls=%async_computation.24 | async-start | bytes 12976128 | tf_op jit(solution)/shard_map/reduce_scatter | solution.py:261
  674.9 2.9 copy-start.17
  677.8 14.0 %copy-start.22 = (f32[1024,1]{0,1:T(1,128)S(1)}, f32[1024,1]{0,1:T(1,128)}, u32[]{:S(2)}) copy-start(f32[1024,1]{0,1:T(1,128)} %get-tuple-element.76) | copy-start | bytes 12292
  698.7 58.1 %all-to-all-start.3 = ((bf16[4,512,256]{2,0,1:T(4,128)(2,1)}), bf16[4,512,256]{2,0,1:T(4,128)(2,1)}, u32[]{:S(2)}, u32[]{:S(2)}) async-start(bf16[4,512,256]{2,0,1:T(4,128)(2,1)} %bitcast.390), calls=%async_computation.6 | async-start | bytes 2097152 | tf_op jit(solution)/shard_map/all_to_all | solution.py:206
  724.5 1.9 copy-start.2
  778.5 2.1 copy-start.8
  814.4 51.1 %all-to-all-start.4 = ((bf16[8,2,32768]{2,1,0:T(2,128)(2,1)}), bf16[8,2,32768]{2,1,0:T(2,128)(2,1)}, u32[]{:S(2)}, u32[]{:S(2)}) async-start(bf16[8,2,32768]{2,1,0:T(2,128)(2,1)} %reshape.442), calls=%async_computation.7 | async-start | bytes 2097152 | tf_op jit(solution)/shard_map/all_to_all | solution.py:228
  865.5 59.0 %all-to-all-start.5 = ((bf16[8,2,32768]{2,1,0:T(2,128)(2,1)}), bf16[8,2,32768]{2,1,0:T(2,128)(2,1)}, u32[]{:S(2)}, u32[]{:S(2)}) async-start(bf16[8,2,32768]{2,1,0:T(2,128)(2,1)} %reshape.440), calls=%async_computation.8 | async-start | bytes 2097152 | tf_op jit(solution)/shard_map/all_to_all | solution.py:221
  871.2 252.3 %reduce-scatter.19.cloned.1.call-start = ((), (), s32[]{:S(2)}) async-start(), calls=%async_computation.23 | async-start | bytes 2359296 | tf_op jit(solution)/shard_map/reduce_scatter | solution.py:258
  877.5 292.2 %reduce-scatter.15.cloned.1.call-start = ((), (), s32[]{:S(2)}) async-start(), calls=%async_computation.21 | async-start | bytes 5242880 | tf_op jit(solution)/shard_map/reduce_scatter | solution.py:240
  939.5 2.9 copy-start.19
  939.5 2.9 copy-start.21
  942.4 4.4 copy-start.10
  946.8 12.0 copy-start.11
  946.8 12.0 copy-start.12
  958.9 333.8 %reduce-scatter.17.cloned.1.call-start = ((), (), s32[]{:S(2)}) async-start(), calls=%async_computation.22 | async-start | bytes 7077888 | tf_op jit(solution)/shard_map/reduce_scatter | solution.py:255
  973.3 82.2 %copy-start.26 = (f32[512]{0:T(512)S(1)}, f32[512]{0:T(512)}, u32[]{:S(2)}) copy-start(f32[512]{0:T(512)} %get-tuple-element.70) | copy-start | bytes 6148
  1055.5 114.2 %copy-start.14 = (f32[2048]{0:T(1024)S(1)}, f32[2048]{0:T(1024)}, u32[]{:S(2)}) copy-start(f32[2048]{0:T(1024)} %param.15) | copy-start | bytes 24580
  1055.5 114.2 %copy-start.24 = (f32[256]{0:T(256)S(1)}, f32[256]{0:T(256)}, u32[]{:S(2)}) copy-start(f32[256]{0:T(256)} %copy-done.23) | copy-start | bytes 3076
  1059.8 155.3 %copy-start.25 = (f32[256]{0:T(256)S(1)}, f32[256]{0:T(256)}, u32[]{:S(2)}) copy-start(f32[256]{0:T(256)} %get-tuple-element.100) | copy-start | bytes 3076
Sparse Core Ops, SparseCore 0:
  12.1 37.1 all-gather.4
  340.2 70.7 reduce-scatter.8
  414.7 34.4 all-gather.6
  450.7 34.4 all-gather.8
  518.5 71.7 reduce-scatter.12
  592.7 44.4 reduce-scatter.10
  643.0 34.4 all-gather.10
  681.7 133.8 reduce-scatter.22
  819.6 232.8 reduce-scatter.20
  1056.3 67.1 reduce-scatter.18
  1126.2 43.4 reduce-scatter.14
  1173.2 119.4 reduce-scatter.16
where the time goes:
time: 1310 us; the launch traced here: 1300 us
  waiting for transfers between devices  729 us (56%)
  local copies, waits for them, and re-layouts  211 us (16%)
  matrix products  172 us (13%)
  other arithmetic  88.3 us (7%)
  blocking collectives  54.5 us (4%)
  starting transfers between devices  32.1 us (2%)
  between operations  15.3 us (1%)
    reduce_scatter x1, waiting for transfers between devices, on_device(): lax.psum_scatter(gate_term.astype(jnp.bfloat16), 'seq', scatter_dimension...  79.2 us
    reduce_scatter x1, waiting for transfers between devices, on_device(): lax.psum_scatter(in_term.astype(jnp.bfloat16), 'seq', scatter_dimension=1...  73.7 us
    reduce_scatter x1, waiting for transfers between devices, on_device(): lax.psum_scatter(jnp.dot(picked, out_use, preferred_element_type=jnp.floa...  70.8 us
    reduce_scatter x1, waiting for transfers between devices, on_device(): lax.psum_scatter(out_term.astype(jnp.bfloat16), 'seq', scatter_dimension=...  63.6 us
    unnamed x71, local copies, waits for them, and re-layouts  58.4 us
    reduce_scatter x1, waiting for transfers between devices, on_device(): lax.psum_scatter(jnp.einsum('krf,kdf->rd', picked, gate_use, preferred_el...  49.9 us
    all_to_all x1, waiting for transfers between devices, on_device(): lax.all_to_all(drive_turned, 'seq', split_axis=1, concat_axis=2, tiled=True)  44.5 us
    reduce_scatter x1, waiting for transfers between devices, on_device(): lax.psum_scatter(jnp.einsum('krc,kdc->rd', picked, in_use, preferred_elem...  44.4 us
  transfers between devices with their start and end apart: 18, of which 16 were waited for; matrix products, arithmetic and copies ran while one was open for 22% of the time, Pallas kernels for 0%

commit v1 on v0

v1 whole, which is shorter than its diff:
```python
import functools

import jax
import jax.numpy as jnp
from jax import lax
from jax.experimental import pallas as pl
from jax.experimental.pallas import tpu as pltpu
from jax.sharding import PartitionSpec as P

EPS = 1e-06
BF = jnp.bfloat16
F32 = jnp.float32
CHUNKS = 8


def swap(values, axis, bit):
    size = lax.axis_size(axis)
    return lax.ppermute(values, axis, [(i, i ^ bit) for i in range(size)])


def shift(values, axis, step):
    size = lax.axis_size(axis)
    pairs = [(i, i + step) for i in range(size) if 0 <= i + step < size]
    return lax.ppermute(values, axis, pairs)


def rms_scale(values):
    return lax.rsqrt(jnp.mean(values * values, axis=-1, keepdims=True) + EPS)


def norm_back(grad_normed, values, scale, weight):
    weighted = grad_normed * weight
    return scale * weighted - values * (scale * scale * scale) * jnp.mean(
        weighted * values, axis=-1, keepdims=True
    )


def sigmoid(v):
    return 1.0 / (1.0 + jnp.exp(-v))


def scan_local_kernel(pi_ref, pf_ref, lb_ref, loc_ref, cum_ref, tot_ref):
    rows = loc_ref.shape[1]
    steps = rows // CHUNKS
    lb = lb_ref[...]
    s = jnp.zeros((CHUNKS, loc_ref.shape[2]), F32)
    p = jnp.ones_like(s)
    for t in range(steps):
        at = pl.ds(t, CHUNKS, stride=steps)
        pi = pi_ref[0, 0, at, :]
        sig = sigmoid(pf_ref[0, 0, at, :])
        f = lb + (1.0 - lb) * sig
        d = pi * sigmoid(pi) * ((1.0 - lb) * (1.0 - sig))
        s = f * s + d
        p = p * f
        loc_ref[0, at, :] = s
        cum_ref[0, at, :] = p
    a = p[0:1]
    b = s[0:1]
    for c in range(1, CHUNKS):
        b = p[c : c + 1] * b + s[c : c + 1]
        a = a * p[c : c + 1]
    tot_ref[0, 0:1, :] = a
    tot_ref[0, 1:2, :] = b


def scan_mix_kernel(loc_ref, cum_ref, pg_ref, carry_ref, gain_ref, state_ref, mix_ref, sq_ref):
    rows = loc_ref.shape[1]
    steps = rows // CHUNKS
    first = pl.program_id(1) == 0
    gain = gain_ref[...]
    cin = carry_ref[0]
    for c in range(CHUNKS):
        at = pl.ds(c * steps, steps)
        st = loc_ref[0, at, :] + cum_ref[0, at, :] * cin
        cin = st[steps - 1 : steps]
        pg = pg_ref[0, 0, at, :]
        state_ref[0, at, :] = st
        mix_ref[0, at, :] = (st * gain * (pg * sigmoid(pg))).astype(BF)
        part = jnp.sum(st * st, axis=-1, keepdims=True)

        @pl.when(first)
        def _():
            sq_ref[0, at, :] = part

        @pl.when(jnp.logical_not(first))
        def _():
            sq_ref[0, at, :] += part


def back_local_kernel(
    width,
    gm_ref,
    pg_ref,
    pf_ref,
    state_ref,
    scale_ref,
    inner_ref,
    gain_ref,
    lb_ref,
    mixed_ref,
    gpg_ref,
    loc_ref,
    cum_ref,
    tot_ref,
    term_ref,
):
    rows = loc_ref.shape[1]
    steps = rows // CHUNKS
    gain = gain_ref[...]
    lb = lb_ref[...]
    term = jnp.zeros((1, loc_ref.shape[2]), F32)
    for c in range(CHUNKS):
        at = pl.ds(c * steps, steps)
        scale = scale_ref[0, at, :]
        coef = scale * scale * scale * inner_ref[0, at, :] * (1.0 / width)
        pg = pg_ref[0, 0, at, :]
        gm = gm_ref[0, at, :]
        st = state_ref[0, at, :]
        sig = sigmoid(pg)
        act = pg * sig
        unit = st * scale
        gact = gm * act
        mixed_ref[0, at, :] = (unit * gain * act).astype(BF)
        gpg_ref[0, at, :] = (gm * gain * unit * (sig * (1.0 + pg * (1.0 - sig)))).astype(BF)
        term = term + jnp.sum(gact * unit, axis=0, keepdims=True)
        loc_ref[0, at, :] = scale * (gact * gain) - st * coef
    term_ref[0] = term
    s = jnp.zeros((CHUNKS, loc_ref.shape[2]), F32)
    q = jnp.ones_like(s)
    for t in range(steps - 1, -1, -1):
        at = pl.ds(t, CHUNKS, stride=steps)
        f = lb + (1.0 - lb) * sigmoid(pf_ref[0, 0, at, :])
        adj = loc_ref[0, at, :] + s
        loc_ref[0, at, :] = adj
        cum_ref[0, at, :] = q
        s = f * adj
        q = q * f
    last = CHUNKS - 1
    a = q[last : last + 1]
    b = s[last : last + 1]
    for c in range(CHUNKS - 2, -1, -1):
        b = q[c : c + 1] * b + s[c : c + 1]
        a = a * q[c : c + 1]
    tot_ref[0, 0:1, :] = a
    tot_ref[0, 1:2, :] = b


def back_mix_kernel(
    loc_ref, cum_ref, state_ref, pi_ref, pf_ref, carry_ref, prior_ref, lb_ref, gpi_ref, gpf_ref, term_ref
):
    rows = loc_ref.shape[1]
    steps = rows // CHUNKS
    lb = lb_ref[...]
    rest = 1.0 - lb
    cin = carry_ref[0]
    term = jnp.zeros((1, loc_ref.shape[2]), F32)
    top = lax.broadcasted_iota(jnp.int32, (steps, loc_ref.shape[2]), 0) == 0
    for c in range(CHUNKS - 1, -1, -1):
        at = pl.ds(c * steps, steps)
        adj = loc_ref[0, at, :] + cum_ref[0, at, :] * cin
        pi = pi_ref[0, 0, at, :]
        sig = sigmoid(pf_ref[0, 0, at, :])
        cin = (lb + rest * sig[0:1]) * adj[0:1]
        st = state_ref[0, at, :]
        before = prior_ref[0] if c == 0 else state_ref[0, pl.ds(c * steps - 1, 1), :]
        prev = jnp.where(top, before, pltpu.roll(st, 1, 0))
        sig_in = sigmoid(pi)
        total = adj * (prev - pi * sig_in)
        left = 1.0 - sig
        gpi_ref[0, at, :] = (adj * (rest * left) * (sig_in * (1.0 + pi * (1.0 - sig_in)))).astype(BF)
        gpf_ref[0, at, :] = (total * rest * sig * left).astype(BF)
        term = term + jnp.sum(total * left, axis=0, keepdims=True)
    term_ref[0] = term


def tile_of(chans):
    return 128 if chans % 128 == 0 else chans


def sds(shape, dtype=F32):
    return jax.ShapeDtypeStruct(shape, dtype)


def piece_specs(rows, tile):
    full = pl.BlockSpec((1, rows, tile), lambda g, c: (g, 0, c))
    row = pl.BlockSpec((1, tile), lambda g, c: (0, c))
    per = pl.BlockSpec((1, 1, tile), lambda g, c: (g, 0, c))
    tot = pl.BlockSpec((1, 2, tile), lambda g, c: (g, 0, c))
    col = pl.BlockSpec((1, rows, 1), lambda g, c: (g, 0, 0))

    def pick(k):
        return pl.BlockSpec((1, 1, rows, tile), lambda g, c: (k, g, 0, c))

    return full, row, per, tot, col, pick


def cost(elements, arrays):
    return pl.CostEstimate(
        flops=20 * elements, bytes_accessed=4 * arrays * elements, transcendentals=2 * elements
    )


def scan_local(project, lower):
    _, groups, rows, chans = project.shape
    tile = tile_of(chans)
    full, row, per, tot, col, pick = piece_specs(rows, tile)
    return pl.pallas_call(
        scan_local_kernel,
        grid=(groups, chans // tile),
        in_specs=[pick(0), pick(1), row],
        out_specs=[full, full, tot],
        out_shape=[sds((groups, rows, chans)), sds((groups, rows, chans)), sds((groups, 2, chans))],
        cost_estimate=cost(groups * rows * chans, 4),
        name="scan_local",
    )(project, project, lower)


def scan_mix(loc, cum, project, carry, gain):
    groups, rows, chans = loc.shape
    tile = tile_of(chans)
    full, row, per, tot, col, pick = piece_specs(rows, tile)
    return pl.pallas_call(
        scan_mix_kernel,
        grid=(groups, chans // tile),
        in_specs=[full, full, pick(2), per, row],
        out_specs=[full, full, col],
        out_shape=[
            sds((groups, rows, chans)),
            sds((groups, rows, chans), BF),
            sds((groups, rows, 1)),
        ],
        cost_estimate=cost(groups * rows * chans, 5),
        name="scan_mix",
    )(loc, cum, project, carry, gain)


def back_local(width, grad_mixed, project, state, scale, inner, gain, lower):
    groups, rows, chans = state.shape
    tile = tile_of(chans)
    full, row, per, tot, col, pick = piece_specs(rows, tile)
    shape = (groups, rows, chans)
    return pl.pallas_call(
        functools.partial(back_local_kernel, width),
        grid=(groups, chans // tile),
        in_specs=[full, pick(2), pick(1), full, col, col, row, row],
        out_specs=[full, full, full, full, tot, per],
        out_shape=[
            sds(shape, BF),
            sds(shape, BF),
            sds(shape),
            sds(shape),
            sds((groups, 2, chans)),
            sds((groups, 1, chans)),
        ],
        cost_estimate=cost(groups * rows * chans, 7),
        name="back_local",
    )(grad_mixed, project, project, state, scale, inner, gain, lower)


def back_mix(loc, cum, state, project, carry, prior, lower):
    groups, rows, chans = state.shape
    tile = tile_of(chans)
    full, row, per, tot, col, pick = piece_specs(rows, tile)
    shape = (groups, rows, chans)
    return pl.pallas_call(
        back_mix_kernel,
        grid=(groups, chans // tile),
        in_specs=[full, full, full, pick(0), pick(1), per, per, row],
        out_specs=[full, full, per],
        out_shape=[sds(shape, BF), sds(shape, BF), sds((groups, 1, chans))],
        cost_estimate=cost(groups * rows * chans, 6),
        name="back_mix",
    )(loc, cum, state, project, project, carry, prior, lower)


def chain_carry(total, reverse):
    size = lax.axis_size("seq")
    odd = (lax.axis_index("seq") % 2) == 1
    other = swap(total, "seq", 1)
    low_a, low_b = jnp.where(odd, other[:, 0], total[:, 0]), jnp.where(odd, other[:, 1], total[:, 1])
    high_a, high_b = jnp.where(odd, total[:, 0], other[:, 0]), jnp.where(odd, total[:, 1], other[:, 1])
    if reverse:
        pair = jnp.stack([low_a * high_a, low_a * high_b + low_b], axis=1)
    else:
        pair = jnp.stack([low_a * high_a, high_a * low_b + high_b], axis=1)
    sign = -1 if reverse else 1
    reached = [shift(pair, "seq", 2 * sign * d) for d in range(1, size // 2)]
    enter = jnp.zeros_like(total[:, 0])
    for got in reversed(reached):
        enter = got[:, 0] * enter + got[:, 1]
    if reverse:
        enter = jnp.where(odd, enter, high_a * enter + high_b)
    else:
        enter = jnp.where(odd, low_a * enter + low_b, enter)
    return enter[:, None]


def far_of(own):
    step = swap(own, "wt", 2)
    return step, swap(step, "wt", 1)


def sum_to_owner(near, far):
    across = far[0].astype(F32) + swap(far[1], "wt", 1).astype(F32)
    moved = swap(across.astype(near.dtype), "wt", 2)
    own = near[0].astype(F32) + swap(near[1], "wt", 1).astype(F32)
    return own + moved.astype(F32)


def block_order(bits, count):
    order = [0]
    for bit in reversed(bits):
        order = order + [j ^ bit for j in order]
    return order


def reordered(values, axis, order, count):
    me = lax.axis_index("seq")
    size = values.shape[axis] // count
    return [lax.dynamic_slice_in_dim(values, (me ^ j) * size, size, axis) for j in order]


def halving(send, keep, bits, axis):
    for n, bit in enumerate(bits):
        got = swap(send, "seq", bit)
        total = keep.astype(F32) + got.astype(F32)
        if n == len(bits) - 1:
            return total
        total = total.astype(BF)
        half = total.shape[axis] // 2
        keep = lax.slice_in_dim(total, 0, half, axis=axis)
        send = lax.slice_in_dim(total, half, 2 * half, axis=axis)


def seq_bits():
    size = lax.axis_size("seq")
    bits = []
    bit = 1
    while bit < size:
        bits.append(bit)
        bit *= 2
    return bits


def left_product(left, right):
    return lax.dot_general(left, right, (((0,), (0,)), ((), ())), preferred_element_type=F32)


def right_product(left, right):
    return lax.dot_general(left, right, (((1,), (1,)), ((), ())), preferred_element_type=F32)


def reduced_left(left, right, bits):
    count = lax.axis_size("seq")
    blocks = reordered(left, 1, block_order(bits, count), count)
    half = count // 2
    send = left_product(jnp.concatenate(blocks[half:], axis=1), right).astype(BF)
    keep = left_product(jnp.concatenate(blocks[:half], axis=1), right).astype(BF)
    return halving(send, keep, bits, 0)


def reduced_right(left, right, bits):
    count = lax.axis_size("seq")
    blocks = reordered(right, 1, block_order(bits, count), count)
    half = count // 2
    send = left_product(left, jnp.concatenate(blocks[half:], axis=1)).astype(BF)
    keep = left_product(left, jnp.concatenate(blocks[:half], axis=1)).astype(BF)
    return halving(send, keep, bits, 1)


def on_device(
    tokens,
    in_proj,
    out_proj,
    gate_up,
    down,
    norm1_gain,
    mixer_gain,
    norm2_gain,
    lower_bound,
    cotangent,
):
    width = in_proj.shape[1]
    chans = in_proj.shape[2]
    inputs = tokens[0].astype(F32)
    grad_out = cotangent[0]
    upstream = grad_out.astype(F32)
    rows = inputs.shape[0]
    bits = seq_bits()
    y_first = bits
    z_first = bits[1:] + bits[:1]

    offset = lax.axis_index("wt") * chans
    lower_use = lax.dynamic_slice_in_dim(lower_bound, offset, chans)[None]
    mixer_use = lax.dynamic_slice_in_dim(mixer_gain, offset, chans)[None]

    def pair(one, two):
        return jnp.concatenate([one, two], axis=0)

    def grouped(values):
        return values.reshape(2, rows, values.shape[-1])

    scale_one = rms_scale(inputs)
    normed = (inputs * scale_one * norm1_gain).astype(BF)
    normed_near = pair(normed, swap(normed, "wt", 1))
    normed_far = pair(*far_of(normed))
    grad_near = pair(grad_out, swap(grad_out, "wt", 1))
    grad_far = pair(*far_of(grad_out))

    def project(piece):
        return jnp.einsum("rd,kdc->krc", piece, in_proj, preferred_element_type=F32).reshape(
            3, 2, rows, chans
        )

    def forward(piece):
        pre = project(piece)
        loc, cum, total = scan_local(pre, lower_use)
        enter = chain_carry(total, False)
        state, mix, squares = scan_mix(loc, cum, pre, enter, mixer_use)
        branch = jnp.dot(mix.reshape(2 * rows, chans), out_proj, preferred_element_type=F32)
        return pre, enter, state, squares, grouped(branch.astype(BF))

    pre_n, enter_n, state_n, squares_n, branch_n = forward(normed_near)
    pre_f, enter_f, state_f, squares_f, branch_f = forward(normed_far)
    branch_raw = sum_to_owner(branch_n, branch_f)
    squares = sum_to_owner(squares_n.reshape(2, 1, rows), squares_f.reshape(2, 1, rows))
    scale_two = lax.rsqrt(squares / width + EPS)
    middle = inputs + branch_raw * scale_two.reshape(rows, 1)

    scale_three = rms_scale(middle)
    normed_two = (middle * scale_three * norm2_gain).astype(BF)
    two_near = pair(normed_two, swap(normed_two, "wt", 1))
    two_far = pair(*far_of(normed_two))

    def feed(piece, grad_rows):
        grad_hidden = right_product(grad_rows, down)
        gate_part = jnp.dot(piece, gate_up[0], preferred_element_type=F32)
        up_part = jnp.dot(piece, gate_up[1], preferred_element_type=F32)
        sig = sigmoid(gate_part)
        act = gate_part * sig
        hidden = (act * up_part).astype(BF)
        grad_gate = (grad_hidden * up_part * sig * (1.0 + gate_part * (1.0 - sig))).astype(BF)
        grad_up = (grad_hidden * act).astype(BF)
        back = right_product(grad_gate, gate_up[0]) + right_product(grad_up, gate_up[1])
        return hidden, grad_gate, grad_up, grouped(back.astype(BF))

    hidden_n, gg_n, gu_n, back_n = feed(two_near, grad_near)
    hidden_f, gg_f, gu_f, back_f = feed(two_far, grad_far)
    grad_normed_two = sum_to_owner(back_n, back_f)

    grad_middle = upstream + norm_back(grad_normed_two, middle, scale_three, norm2_gain)
    norm2_term = jnp.sum(grad_normed_two * middle * scale_three, axis=0)

    grad_branch = grad_middle.astype(BF)
    inner = jnp.sum(grad_branch.astype(F32) * branch_raw, axis=-1)
    small = jnp.stack([scale_two.reshape(rows), inner])[None]
    small_near = pair(small, swap(small, "wt", 1))
    small_far = pair(*far_of(small))
    gb_near = pair(grad_branch, swap(grad_branch, "wt", 1))
    gb_far = pair(*far_of(grad_branch))

    def backward(gb, small_piece, pre, state, enter):
        grad_mixed = grouped(right_product(gb, out_proj))
        scale = small_piece[:, 0, :, None]
        inner_piece = small_piece[:, 1, :, None]
        mixed, gpg, loc, cum, total, mixer_term = back_local(
            width, grad_mixed, pre, state, scale, inner_piece, mixer_use, lower_use
        )
        carry = chain_carry(total, True)
        gpi, gpf, bound_term = back_mix(loc, cum, state, pre, carry, enter, lower_use)
        flat = [v.reshape(2 * rows, chans) for v in (gpi, gpf, gpg)]
        back = (
            right_product(flat[0], in_proj[0])
            + right_product(flat[1], in_proj[1])
            + right_product(flat[2], in_proj[2])
        )
        return (
            mixed.reshape(2 * rows, chans),
            flat,
            jnp.sum(mixer_term, axis=(0, 1)),
            jnp.sum(bound_term, axis=(0, 1)),
            grouped(back.astype(BF)),
        )

    mixed_n, flat_n, mixer_n, bound_n, down_n = backward(gb_near, small_near, pre_n, state_n, enter_n)
    mixed_f, flat_f, mixer_f, bound_f, down_f = backward(gb_far, small_far, pre_f, state_f, enter_f)
    grad_normed = sum_to_owner(down_n, down_f)
    norm1_term = jnp.sum(grad_normed * inputs * scale_one, axis=0)
    grad_inputs = grad_middle + norm_back(grad_normed, inputs, scale_one, norm1_gain)

    ffn_n = grouped(jnp.dot(hidden_n, down, preferred_element_type=F32).astype(BF))
    ffn_f = grouped(jnp.dot(hidden_f, down, preferred_element_type=F32).astype(BF))
    result = middle + sum_to_owner(ffn_n, ffn_f)

    two_rows = pair(two_near, two_far)
    gate_grad = reduced_left(two_rows, pair(gg_n, gg_f), y_first)
    up_grad = reduced_left(two_rows, pair(gu_n, gu_f), y_first)
    down_grad = reduced_right(pair(hidden_n, hidden_f), pair(grad_near, grad_far), y_first)
    out_grad = reduced_right(pair(mixed_n, mixed_f), pair(gb_near, gb_far), z_first)
    normed_rows = pair(normed_near, normed_far)
    in_grads = [
        reduced_left(normed_rows, pair(flat_n[k], flat_f[k]), z_first if k == 2 else y_first)
        for k in range(3)
    ]

    me = lax.axis_index("wt")

    def block(values, j):
        return lax.dynamic_slice_in_dim(values, (me ^ j) * chans, chans, values.ndim - 1)

    norm_terms = jnp.stack([norm1_term, norm2_term])
    low = jnp.stack([block(norm_terms, 0), block(norm_terms, 1)])
    high = jnp.stack([block(norm_terms, 2), block(norm_terms, 3)])
    norms = sum_to_owner(low, high)
    gains = jnp.stack([norms[0], mixer_n + mixer_f, norms[1], bound_n + bound_f])
    for bit in bits:
        gains = gains + swap(gains, "seq", bit)

    return (
        result.astype(BF)[None],
        grad_inputs[None],
        jnp.stack(in_grads),
        out_grad,
        jnp.stack([gate_grad, up_grad]),
        down_grad,
        gains[0],
        gains[1],
        gains[2],
        gains[3],
    )


def solution(mesh):
    placed = (
        P("wt", "seq", None),
        P(None, None, "wt"),
        P("wt", None),
        P(None, None, "wt"),
        P("wt", None),
        P(),
        P(),
        P(),
        P(),
        P("wt", "seq", None),
    )
    return jax.shard_map(
        on_device,
        mesh=mesh,
        in_specs=placed,
        out_specs=(
            P("wt", "seq", None),
            P("wt", "seq", None),
            P(None, "seq", "wt"),
            P("wt", "seq"),
            P(None, "seq", "wt"),
            P("wt", "seq"),
            P("wt"),
            P("wt"),
            P("wt"),
            P("wt"),
        ),
        check_vma=False,
    )
```

time: 1310 us -> 782 us (0.60)
  waiting for transfers between devices: 729 us -> 364 us
  local copies, waits for them, and re-layouts: 211 us -> 29.7 us
  Pallas kernels: 0 us -> 60.6 us
  blocking collectives: 54.5 us -> 0 us
  starting transfers between devices: 32.1 us -> 77.8 us
  other arithmetic: 88.3 us -> 59 us
    reduce_scatter x8 -> x0, waiting for transfers between devices: 426 us -> none  [the longest x1 79.2 us: on_device(): lax.psum_scatter(gate_term.astype(jnp.bfloat16), 'seq', scatter_dimension...]
    ppermute x0 -> x73, waiting for transfers between devices: none -> 364 us  [the longest x61 359 us: swap(): return lax.ppermute(values, axis, [(i, i ^ bit) for i in range(size)])]
    all_to_all x6 -> x0, waiting for transfers between devices: 215 us -> none  [the longest x1 44.5 us: on_device(): lax.all_to_all(drive_turned, 'seq', split_axis=1, concat_axis=2, tiled=True)]
    all_gather x4 -> x0, waiting for transfers between devices: 87.7 us -> none  [the longest x1 36.5 us: on_device(): lax.all_gather(normed[None], 'wt', axis=0, tiled=True)]
    ppermute x0 -> x73, starting transfers between devices: none -> 77.8 us  [the longest x61 54.3 us: swap(): return lax.ppermute(values, axis, [(i, i ^ bit) for i in range(size)])]
    dot_general x16 -> x10, matrix products: 131 us -> 64.8 us  [the longest x2 17.5 us: feed(): gate_part = jnp.dot(piece, gate_up[0], preferred_element_type=F32)]
    pallas_call x0 -> x8, Pallas kernels: none -> 60.6 us  [the longest x2 17.2 us: scan_mix(): pl.pallas_call(scan_mix_kernel, grid=(groups, chans // tile), in_specs=[f...]
    psum x3 -> x0, blocking collectives: 54.5 us -> none  [the longest x1 42.8 us: on_device(): lax.psum(jnp.stack([norm1_term, mixer_full, norm2_term, bound_full]), ('s...]
  transfers between devices with their start and end apart: 18 -> 73, of which waited for: 16 -> 25; matrix products, arithmetic and copies ran while one was open for 22% -> 33% of each run, Pallas kernels for 0% -> 8%
where the time goes in v1:
time: 782 us; the launch traced here: 774 us
  waiting for transfers between devices  364 us (47%)
  matrix products  179 us (23%)
  starting transfers between devices  77.8 us (10%)
  Pallas kernels  60.6 us (8%)
  other arithmetic  59 us (8%)
  local copies, waits for them, and re-layouts  29.7 us (4%)
    ppermute x61, waiting for transfers between devices, swap(): return lax.ppermute(values, axis, [(i, i ^ bit) for i in range(size)])  359 us
    dot_general x14, matrix products, right_product(): lax.dot_general(left, right, (((1,), (1,)), ((), ())), preferred_element_...  65.9 us
    ppermute x61, starting transfers between devices, swap(): return lax.ppermute(values, axis, [(i, i ^ bit) for i in range(size)])  54.3 us
    dot_general x14, matrix products, left_product(): lax.dot_general(left, right, (((0,), (0,)), ((), ())), preferred_element_...  48.7 us
    ppermute x12, starting transfers between devices, shift(): return lax.ppermute(values, axis, pairs)  23.5 us
    dot_general x2, matrix products, feed(): gate_part = jnp.dot(piece, gate_up[0], preferred_element_type=F32)  17.5 us
    pallas_call x2, Pallas kernels, scan_mix(): pl.pallas_call(scan_mix_kernel, grid=(groups, chans // tile), in_specs=[f...  17.2 us
    dot_general x2, matrix products, project(): jnp.einsum('rd,kdc->krc', piece, in_proj, preferred_element_type=F32)  16.8 us
  transfers between devices with their start and end apart: 73, of which 25 were waited for; matrix products, arithmetic and copies ran while one was open for 33% of the time, Pallas kernels for 8%

profile of v1, /device:TPU:0, one launch (start us, length us, event | category | flops | bytes accessed | tf_op | source)
XLA Modules:
  0.0 773.7 jit_solution(10799412201589448274)
XLA Ops:
  8.4 23.4 %collective-permute-done.6 = bf16[256,2048]{1,0:T(8,128)(2,1)S(1)} collective-permute-done((bf16[256,2048]{1,0:T(8,128)(2,1)}, bf16[256,2048]{1,0:T(8,128)(2,1)S(1)}, u32[]{:S(2)}, u32[]{:S(2)}) %collective-permute-start.6) | collective-permute-done | bytes 1048608 | tf_op jit(solution)/shard_map/ppermute | solution.py:18
  35.3 8.2 %fusion.50 = f32[512,3,512]{2,0,1:T(8,128)} fusion(bf16[3,2048,512]{2,1,0:T(8,128)(2,1)} %param.11, bf16[256,2048]{1,0:T(8,128)(2,1)} %collective-permute-done.7, bf16[256,2048]{1,0:T(8,128)(2,1)S(1)} %collective-permute-done.6), kind=kOutput, calls=%fused_computation.93 | convolution fusion | flops 3225419776 | bytes 11534336 | tf_op jit(solution)/shard_map/rd,kdc->krc/dot_general | solution.py:412
  43.5 6.9 scan_local.3
  55.1 4.7 collective-permute-start.10
  68.3 8.6 %scan_mix.3 = (f32[2,256,512]{2,1,0:T(8,128)}, bf16[2,256,512]{2,1,0:T(8,128)(2,1)}, f32[2,256,1]{2,1,0:T(8,128)}) custom-call(f32[2,256,512]{2,1,0:T(8,128)} %get-tuple-element.44.loc_ref, f32[2,256,512]{2,1,0:T(8,128)} %get-tuple-element.45.cum_ref, f32[3,2,256,512]{3,2,1,0:T(8,128)} %bitcast.137, ...), custom_call_target="tpu_custom_call" | custom-call | flops 5242880 | bytes 5242880 | tf_op jit(solution)/shard_map/scan_mix/pallas_call | solution.py:223
  81.6 8.6 %fusion.47 = f32[512,3,512]{2,0,1:T(8,128)} fusion(bf16[3,2048,512]{2,1,0:T(8,128)(2,1)} %param.11, bf16[256,2048]{1,0:T(8,128)(2,1)} %collective-permute-done, bf16[256,2048]{1,0:T(8,128)(2,1)} %fusion.39), kind=kOutput, calls=%fused_computation.89 | convolution fusion | flops 3225419776 | bytes 11534336 | tf_op jit(solution)/shard_map/rd,kdc->krc/dot_general | solution.py:412
  90.2 6.8 scan_local.2
  110.8 8.6 %scan_mix.2 = (f32[2,256,512]{2,1,0:T(8,128)}, bf16[2,256,512]{2,1,0:T(8,128)(2,1)}, f32[2,256,1]{2,1,0:T(8,128)}) custom-call(f32[2,256,512]{2,1,0:T(8,128)} %get-tuple-element.40.loc_ref, f32[2,256,512]{2,1,0:T(8,128)} %get-tuple-element.41.cum_ref, f32[3,2,256,512]{3,2,1,0:T(8,128)} %bitcast.144, ...), custom_call_target="tpu_custom_call" | custom-call | flops 5242880 | bytes 5242880 | tf_op jit(solution)/shard_map/scan_mix/pallas_call | solution.py:223
  127.4 8.0 %fusion.53 = f32[512,1408]{1,0:T(8,128)} fusion(bf16[1408,2048]{1,0:T(8,128)(2,1)} %param.14, bf16[256,2048]{1,0:T(8,128)(2,1)} %collective-permute-done.23, bf16[256,2048]{1,0:T(8,128)(2,1)S(1)} %bitcast.151), kind=kOutput, calls=%fused_computation.97 | convolution fusion | flops 2956984320 | bytes 10747904 | tf_op jit(solution)/shard_map/dot_general | solution.py:351
  135.4 14.7 %collective-permute-done.16 = f32[1,256]{1,0:T(1,128)S(1)} collective-permute-done((f32[1,256]{1,0:T(1,128)S(1)}, f32[1,256]{1,0:T(1,128)S(1)}, u32[]{:S(2)}, u32[]{:S(2)}) %collective-permute-start.16) | collective-permute-done | bytes 1056 | tf_op jit(solution)/shard_map/ppermute | solution.py:18
  155.5 6.6 fusion.57
  163.5 6.3 fusion.6
  169.8 8.7 %multiply_convert_fusion.3 = (bf16[512,1408]{1,0:T(8,128)(2,1)S(1)}, bf16[512,1408]{1,0:T(8,128)(2,1)}, bf16[512,1408]{1,0:T(8,128)(2,1)}) fusion(f32[512,1408]{1,0:T(8,128)S(1)} %copy-done.81, f32[512,1408]{1,0:T(8,128)S(1)} %fusion.6, bf16[2,2048,1408]{2,1,0:T(8,128)(2,1)} %param.13, bf16[256,2048]{1,0:T(8,128)(2,1)S(1)} %collective-permute-done.17, ...), kind=kOutput, calls=%fused_computation.61 | convolution fusion | flops 2967797760 | bytes 17956864 | tf_op jit(solution)/shard_map/dot_general | solution.py:438
  178.5 6.4 fusion.2
  185.0 6.3 add_convert_fusion.6
  193.0 6.8 convolution_convert_fusion.9
  201.4 5.0 fusion.4
  206.4 8.8 %multiply_convert_fusion.1 = (bf16[512,1408]{1,0:T(8,128)(2,1)S(1)}, bf16[512,1408]{1,0:T(8,128)(2,1)S(1)}, bf16[512,1408]{1,0:T(8,128)(2,1)S(1)}) fusion(f32[512,1408]{1,0:T(8,128)} %fusion.57, f32[512,1408]{1,0:T(8,128)} %fusion.4, bf16[512,2048]{1,0:T(8,128)(2,1)S(1)} %constant_dynamic-update-slice_fusion, bf16[2,2048,1408]{2,1,0:T(8,128)(2,1)} %param.13), kind=kOutput, calls=%fused_computation.59 | convolution fusion | flops 2963603456 | bytes 17956864 | tf_op jit(solution)/shard_map/dot_general | solution.py:438
  215.2 7.8 %convolution_convert_fusion.8 = bf16[512,2048]{1,0:T(8,128)(2,1)S(1)} fusion(bf16[512,1408]{1,0:T(8,128)(2,1)S(1)} %get-tuple-element.92, bf16[1408,2048]{1,0:T(8,128)(2,1)} %param.14), kind=kOutput, calls=%fused_computation.49 | convolution fusion | flops 2953838592 | bytes 9306112 | tf_op jit(solution)/shard_map/dot_general | solution.py:493
  224.4 7.7 fusion
  232.1 7.0 add_convert_fusion.5
  240.5 6.2 convolution_convert_fusion
  259.1 4.9 convolution_convert_fusion.2
  264.6 16.9 %collective-permute-done.28 = bf16[256,2048]{1,0:T(8,128)(2,1)S(1)} collective-permute-done((bf16[256,2048]{1,0:T(8,128)(2,1)S(1)}, bf16[256,2048]{1,0:T(8,128)(2,1)S(1)}, u32[]{:S(2)}, u32[]{:S(2)}) %collective-permute-start.28) | collective-permute-done | bytes 1048608 | tf_op jit(solution)/shard_map/ppermute | solution.py:18
  282.9 19.9 %collective-permute-done.22 = bf16[256,2048]{1,0:T(8,128)(2,1)S(1)} collective-permute-done((bf16[256,2048]{1,0:T(8,128)(2,1)S(1)}, bf16[256,2048]{1,0:T(8,128)(2,1)S(1)}, u32[]{:S(2)}, u32[]{:S(2)}) %collective-permute-start.22) | collective-permute-done | bytes 1048608 | tf_op jit(solution)/shard_map/ppermute | solution.py:18
  302.9 4.4 multiply_reduce_fusion.1
  308.1 4.5 pad_maximum_fusion
  318.1 5.2 add_convert_fusion
  324.6 49.5 %collective-permute-done.58 = bf16[1024,1408]{1,0:T(8,128)(2,1)} collective-permute-done((bf16[1024,1408]{1,0:T(8,128)(2,1)S(1)}, bf16[1024,1408]{1,0:T(8,128)(2,1)}, u32[]{:S(2)}, u32[]{:S(2)}) %collective-permute-start.58) | collective-permute-done | bytes 2883616 | tf_op jit(solution)/shard_map/ppermute | solution.py:18
  374.1 5.3 add_convert_fusion.2
  380.7 54.4 %collective-permute-done.61 = bf16[1024,1408]{1,0:T(8,128)(2,1)} collective-permute-done((bf16[1024,1408]{1,0:T(8,128)(2,1)S(1)}, bf16[1024,1408]{1,0:T(8,128)(2,1)}, u32[]{:S(2)}, u32[]{:S(2)}) %collective-permute-start.61) | collective-permute-done | bytes 2883616 | tf_op jit(solution)/shard_map/ppermute | solution.py:18
  435.2 5.3 add_convert_fusion.1
  444.2 8.1 %back_local.2 = (bf16[2,256,512]{2,1,0:T(8,128)(2,1)}, bf16[2,256,512]{2,1,0:T(8,128)(2,1)}, f32[2,256,512]{2,1,0:T(8,128)}, f32[2,256,512]{2,1,0:T(8,128)}, f32[2,2,512]{2,1,0:T(2,128)}, /*index=5*/f32[2,1,512]{2,1,0:T(1,128)}) custom-call(f32[2,256,512]{2,1,0:T(8,128)} %bitcast.166, f32[3,2,256,512]{3,2,1,0:T(8,128)} %bitcast.145, ...), custom_call_target="tpu_custom_call" | custom-call | flops 5242880 | bytes 7340032 | tf_op jit(solution)/shard_map/back_local/pallas_call | solution.py:243
  458.6 8.0 %back_local.3 = (bf16[2,256,512]{2,1,0:T(8,128)(2,1)}, bf16[2,256,512]{2,1,0:T(8,128)(2,1)}, f32[2,256,512]{2,1,0:T(8,128)}, f32[2,256,512]{2,1,0:T(8,128)}, f32[2,2,512]{2,1,0:T(2,128)}, /*index=5*/f32[2,1,512]{2,1,0:T(1,128)}) custom-call(f32[2,256,512]{2,1,0:T(8,128)} %bitcast.165, f32[3,2,256,512]{3,2,1,0:T(8,128)} %bitcast.138, ...), custom_call_target="tpu_custom_call" | custom-call | flops 5242880 | bytes 7340032 | tf_op jit(solution)/shard_map/back_local/pallas_call | solution.py:243
  497.4 6.6 back_mix.3
  516.7 4.7 collective-permute-done.32
  521.4 4.5 collective-permute-start.55
  527.4 7.0 back_mix.2
  564.4 49.6 %collective-permute-done.66 = bf16[1408,256]{1,0:T(8,128)(2,1)S(1)} collective-permute-done((bf16[1408,256]{1,0:T(8,128)(2,1)S(1)}, bf16[1408,256]{1,0:T(8,128)(2,1)S(1)}, u32[]{:S(2)}, u32[]{:S(2)}) %collective-permute-start.66) | collective-permute-done | bytes 720928 | tf_op jit(solution)/shard_map/ppermute | solution.py:18
  618.8 10.8 %collective-permute-done.60 = bf16[256,1408]{1,0:T(8,128)(2,1)S(1)} collective-permute-done((bf16[256,1408]{1,0:T(8,128)(2,1)S(1)}, bf16[256,1408]{1,0:T(8,128)(2,1)S(1)}, u32[]{:S(2)}, u32[]{:S(2)}) %collective-permute-start.60) | collective-permute-done | bytes 720928 | tf_op jit(solution)/shard_map/ppermute | solution.py:18
  629.7 33.4 %collective-permute-done.63 = bf16[256,1408]{1,0:T(8,128)(2,1)S(1)} collective-permute-done((bf16[256,1408]{1,0:T(8,128)(2,1)S(1)}, bf16[256,1408]{1,0:T(8,128)(2,1)S(1)}, u32[]{:S(2)}, u32[]{:S(2)}) %collective-permute-start.63) | collective-permute-done | bytes 720928 | tf_op jit(solution)/shard_map/ppermute | solution.py:18
  673.8 15.3 %collective-permute-done.46 = bf16[1024,512]{1,0:T(8,128)(2,1)S(1)} collective-permute-done((bf16[1024,512]{1,0:T(8,128)(2,1)S(1)}, bf16[1024,512]{1,0:T(8,128)(2,1)S(1)}, u32[]{:S(2)}, u32[]{:S(2)}) %collective-permute-start.46) | collective-permute-done | bytes 1048608 | tf_op jit(solution)/shard_map/ppermute | solution.py:18
  689.8 20.9 %collective-permute-done.49 = bf16[1024,512]{1,0:T(8,128)(2,1)S(1)} collective-permute-done((bf16[1024,512]{1,0:T(8,128)(2,1)S(1)}, bf16[1024,512]{1,0:T(8,128)(2,1)S(1)}, u32[]{:S(2)}, u32[]{:S(2)}) %collective-permute-start.49) | collective-permute-done | bytes 1048608 | tf_op jit(solution)/shard_map/ppermute | solution.py:18
  715.1 10.5 %collective-permute-done.47 = bf16[512,512]{1,0:T(8,128)(2,1)S(1)} collective-permute-done((bf16[512,512]{1,0:T(8,128)(2,1)S(1)}, bf16[512,512]{1,0:T(8,128)(2,1)S(1)}, u32[]{:S(2)}, u32[]{:S(2)}) %collective-permute-start.47) | collective-permute-done | bytes 524320 | tf_op jit(solution)/shard_map/ppermute | solution.py:18
  727.4 8.2 %collective-permute-done.50 = bf16[512,512]{1,0:T(8,128)(2,1)S(1)} collective-permute-done((bf16[512,512]{1,0:T(8,128)(2,1)S(1)}, bf16[512,512]{1,0:T(8,128)(2,1)S(1)}, u32[]{:S(2)}, u32[]{:S(2)}) %collective-permute-start.50) | collective-permute-done | bytes 524320 | tf_op jit(solution)/shard_map/ppermute | solution.py:18
  741.4 14.7 %collective-permute-done.48 = bf16[256,512]{1,0:T(8,128)(2,1)S(1)} collective-permute-done((bf16[256,512]{1,0:T(8,128)(2,1)S(1)}, bf16[256,512]{1,0:T(8,128)(2,1)S(1)}, u32[]{:S(2)}, u32[]{:S(2)}) %collective-permute-start.48) | collective-permute-done | bytes 262176 | tf_op jit(solution)/shard_map/ppermute | solution.py:18
  756.9 3.6 collective-permute-done.51
  764.6 3.6 collective-permute-done.71
  (458 shorter events, 209.0 us)
Async XLA Ops:
  5.4 26.3 %collective-permute-start.6 = (bf16[256,2048]{1,0:T(8,128)(2,1)}, bf16[256,2048]{1,0:T(8,128)(2,1)S(1)}, u32[]{:S(2)}, u32[]{:S(2)}) collective-permute-start(bf16[256,2048]{1,0:T(8,128)(2,1)} %fusion.39), channel_id=1, source_target_pairs={{0,2},{1,3},{2,0},{3,1},{4,6},{5,7},{6,4},{7,5},{8,10},{9,11},{10,... | collective-permute-start | bytes 3145736 | tf_op jit(solution)/shard_map/ppermute | solution.py:18
  31.7 49.9 %collective-permute-start = (bf16[256,2048]{1,0:T(8,128)(2,1)}, bf16[256,2048]{1,0:T(8,128)(2,1)}, u32[]{:S(2)}, u32[]{:S(2)}) collective-permute-start(bf16[256,2048]{1,0:T(8,128)(2,1)} %fusion.39), channel_id=1, source_target_pairs={{0,1},{1,0},{2,3},{3,2},{4,5},{5,4},{6,7},{7,6},{8,9},{9,8},{10,11... | collective-permute-start | bytes 3145736 | tf_op jit(solution)/shard_map/ppermute | solution.py:18
  64.0 44.6 %collective-permute-start.25 = (bf16[256,2048]{1,0:T(8,128)(2,1)S(1)}, bf16[256,2048]{1,0:T(8,128)(2,1)}, u32[]{:S(2)}, u32[]{:S(2)}) collective-permute-start(bf16[256,2048]{1,0:T(8,128)(2,1)S(1)} %bitcast.149), channel_id=1, source_target_pairs={{0,2},{1,3},{2,0},{3,1},{4,6},{5,7},{6,4},{7,5},{8,10},{9,11},{10,... | collective-permute-start | bytes 3145736 | tf_op jit(solution)/shard_map/ppermute | solution.py:18
  81.6 41.0 %collective-permute-start.12 = (bf16[256,2048]{1,0:T(8,128)(2,1)}, bf16[256,2048]{1,0:T(8,128)(2,1)}, u32[]{:S(2)}, u32[]{:S(2)}) collective-permute-start(bf16[256,2048]{1,0:T(8,128)(2,1)} %slice.476), channel_id=1, source_target_pairs={{0,1},{1,0},{2,3},{3,2},{4,5},{5,4},{6,7},{7,6},{8,9},{9,8},{10,11... | collective-permute-start | bytes 3145736 | tf_op jit(solution)/shard_map/ppermute | solution.py:18
  108.6 18.1 %collective-permute-start.23 = (bf16[256,2048]{1,0:T(8,128)(2,1)S(1)}, bf16[256,2048]{1,0:T(8,128)(2,1)}, u32[]{:S(2)}, u32[]{:S(2)}) collective-permute-start(bf16[256,2048]{1,0:T(8,128)(2,1)S(1)} %bitcast.150), channel_id=1, source_target_pairs={{0,1},{1,0},{2,3},{3,2},{4,5},{5,4},{6,7},{7,6},{8,9},{9,8},{10,11... | collective-permute-start | bytes 3145736 | tf_op jit(solution)/shard_map/ppermute | solution.py:18
  108.7 42.5 %collective-permute-start.26 = (bf16[256,2048]{1,0:T(8,128)(2,1)}, bf16[256,2048]{1,0:T(8,128)(2,1)}, u32[]{:S(2)}, u32[]{:S(2)}) collective-permute-start(bf16[256,2048]{1,0:T(8,128)(2,1)} %collective-permute-done.25), channel_id=1, source_target_pairs={{0,1},{1,0},{2,3},{3,2},{4,5},{5,4},{6,7},{7,6},{8,9},{9,8},{10,11... | collective-permute-start | bytes 3145736 | tf_op jit(solution)/shard_map/ppermute | solution.py:18
  121.8 28.2 %collective-permute-start.5 = (bf16[256,2048]{1,0:T(8,128)(2,1)S(1)}, bf16[256,2048]{1,0:T(8,128)(2,1)S(1)}, u32[]{:S(2)}, u32[]{:S(2)}) collective-permute-start(bf16[256,2048]{1,0:T(8,128)(2,1)S(1)} %slice.466), channel_id=1, source_target_pairs={{0,1},{1,0},{2,3},{3,2},{4,5},{5,4},{6,7},{7,6},{8,9},{9,8},{10,11... | collective-permute-start | bytes 3145736 | tf_op jit(solution)/shard_map/ppermute | solution.py:18
  124.9 25.1 %collective-permute-start.13 = (bf16[256,2048]{1,0:T(8,128)(2,1)S(1)}, bf16[256,2048]{1,0:T(8,128)(2,1)S(1)}, u32[]{:S(2)}, u32[]{:S(2)}) collective-permute-start(bf16[256,2048]{1,0:T(8,128)(2,1)S(1)} %add_convert_fusion.18), channel_id=1, source_target_pairs={{0,2},{1,3},{2,0},{3,1},{4,6},{5,7},{6,4},{7,5},{8,10},{9,11},{10,... | collective-permute-start | bytes 3145736 | tf_op jit(solution)/shard_map/ppermute | solution.py:18
  126.8 23.3 %collective-permute-start.16 = (f32[1,256]{1,0:T(1,128)S(1)}, f32[1,256]{1,0:T(1,128)S(1)}, u32[]{:S(2)}, u32[]{:S(2)}) collective-permute-start(f32[1,256]{1,0:T(1,128)S(1)} %add.412), channel_id=1, source_target_pairs={{0,2},{1,3},{2,0},{3,1},{4,6},{5,7},{6,4},{7,5},{8,10},{9,11},{10,... | collective-permute-start | bytes 3080 | tf_op jit(solution)/shard_map/ppermute | solution.py:18
  162.0 29.3 %collective-permute-start.19 = (bf16[256,2048]{1,0:T(8,128)(2,1)S(1)}, bf16[256,2048]{1,0:T(8,128)(2,1)S(1)}, u32[]{:S(2)}, u32[]{:S(2)}) collective-permute-start(bf16[256,2048]{1,0:T(8,128)(2,1)S(1)} %multiply_convert_fusion.6), channel_id=1, source_target_pairs={{0,2},{1,3},{2,0},{3,1},{4,6},{5,7},{6,4},{7,5},{8,10},{9,11},{10,... | collective-permute-start | bytes 3145736 | tf_op jit(solution)/shard_map/ppermute | solution.py:18
  192.7 71.3 %collective-permute-start.24 = (bf16[256,2048]{1,0:T(8,128)(2,1)}, bf16[256,2048]{1,0:T(8,128)(2,1)S(1)}, u32[]{:S(2)}, u32[]{:S(2)}) collective-permute-start(bf16[256,2048]{1,0:T(8,128)(2,1)} %slice.482), channel_id=1, source_target_pairs={{0,1},{1,0},{2,3},{3,2},{4,5},{5,4},{6,7},{7,6},{8,9},{9,8},{10,11... | collective-permute-start | bytes 3145736 | tf_op jit(solution)/shard_map/ppermute | solution.py:18
  200.9 82.0 %collective-permute-start.18 = (bf16[256,2048]{1,0:T(8,128)(2,1)}, bf16[256,2048]{1,0:T(8,128)(2,1)}, u32[]{:S(2)}, u32[]{:S(2)}) collective-permute-start(bf16[256,2048]{1,0:T(8,128)(2,1)} %slice.478), channel_id=1, source_target_pairs={{0,1},{1,0},{2,3},{3,2},{4,5},{5,4},{6,7},{7,6},{8,9},{9,8},{10,11... | collective-permute-start | bytes 3145736 | tf_op jit(solution)/shard_map/ppermute | solution.py:18
  224.1 32.1 %collective-permute-start.21 = (bf16[256,2048]{1,0:T(8,128)(2,1)}, bf16[256,2048]{1,0:T(8,128)(2,1)}, u32[]{:S(2)}, u32[]{:S(2)}) collective-permute-start(bf16[256,2048]{1,0:T(8,128)(2,1)} %slice.480), channel_id=1, source_target_pairs={{0,1},{1,0},{2,3},{3,2},{4,5},{5,4},{6,7},{7,6},{8,9},{9,8},{10,11... | collective-permute-start | bytes 3145736 | tf_op jit(solution)/shard_map/ppermute | solution.py:18
  239.2 15.7 %collective-permute-start.27 = (bf16[256,2048]{1,0:T(8,128)(2,1)S(1)}, bf16[256,2048]{1,0:T(8,128)(2,1)S(1)}, u32[]{:S(2)}, u32[]{:S(2)}) collective-permute-start(bf16[256,2048]{1,0:T(8,128)(2,1)S(1)} %slice.484), channel_id=1, source_target_pairs={{0,1},{1,0},{2,3},{3,2},{4,5},{5,4},{6,7},{7,6},{8,9},{9,8},{10,11... | collective-permute-start | bytes 3145736 | tf_op jit(solution)/shard_map/ppermute | solution.py:18
  246.7 71.4 %collective-permute-start.64 = (bf16[1408,1024]{1,0:T(8,128)(2,1)}, bf16[1408,1024]{1,0:T(8,128)(2,1)}, u32[]{:S(2)}, u32[]{:S(2)}) collective-permute-start(bf16[1408,1024]{1,0:T(8,128)(2,1)} %convolution_convert_fusion), channel_id=1, source_target_pairs={{0,4},{4,0},{8,12},{12,8},{16,20},{20,16},{24,28},{28,24},{1,5},{5... | collective-permute-start | bytes 8650760 | tf_op jit(solution)/shard_map/ppermute | solution.py:18
  255.3 26.1 %collective-permute-start.28 = (bf16[256,2048]{1,0:T(8,128)(2,1)S(1)}, bf16[256,2048]{1,0:T(8,128)(2,1)S(1)}, u32[]{:S(2)}, u32[]{:S(2)}) collective-permute-start(bf16[256,2048]{1,0:T(8,128)(2,1)S(1)} %add_convert_fusion.15), channel_id=1, source_target_pairs={{0,2},{1,3},{2,0},{3,1},{4,6},{5,7},{6,4},{7,5},{8,10},{9,11},{10,... | collective-permute-start | bytes 3145736 | tf_op jit(solution)/shard_map/ppermute | solution.py:18
  257.9 45.0 %collective-permute-start.22 = (bf16[256,2048]{1,0:T(8,128)(2,1)S(1)}, bf16[256,2048]{1,0:T(8,128)(2,1)S(1)}, u32[]{:S(2)}, u32[]{:S(2)}) collective-permute-start(bf16[256,2048]{1,0:T(8,128)(2,1)S(1)} %add_convert_fusion.17), channel_id=1, source_target_pairs={{0,2},{1,3},{2,0},{3,1},{4,6},{5,7},{6,4},{7,5},{8,10},{9,11},{10,... | collective-permute-start | bytes 3145736 | tf_op jit(solution)/shard_map/ppermute | solution.py:18
  264.0 110.1 %collective-permute-start.58 = (bf16[1024,1408]{1,0:T(8,128)(2,1)S(1)}, bf16[1024,1408]{1,0:T(8,128)(2,1)}, u32[]{:S(2)}, u32[]{:S(2)}) collective-permute-start(bf16[1024,1408]{1,0:T(8,128)(2,1)S(1)} %convolution_convert_fusion.4), channel_id=1, source_target_pairs={{0,4},{4,0},{8,12},{12,8},{16,20},{20,16},{24,28},{28,24},{1,5},{5... | collective-permute-start | bytes 8650760 | tf_op jit(solution)/shard_map/ppermute | solution.py:18
  281.5 153.7 %collective-permute-start.61 = (bf16[1024,1408]{1,0:T(8,128)(2,1)S(1)}, bf16[1024,1408]{1,0:T(8,128)(2,1)}, u32[]{:S(2)}, u32[]{:S(2)}) collective-permute-start(bf16[1024,1408]{1,0:T(8,128)(2,1)S(1)} %convolution_convert_fusion.2), channel_id=1, source_target_pairs={{0,4},{4,0},{8,12},{12,8},{16,20},{20,16},{24,28},{28,24},{1,5},{5... | collective-permute-start | bytes 8650760 | tf_op jit(solution)/shard_map/ppermute | solution.py:18
  313.8 66.9 %collective-permute-start.36 = (bf16[256,2048]{1,0:T(8,128)(2,1)S(1)}, bf16[256,2048]{1,0:T(8,128)(2,1)S(1)}, u32[]{:S(2)}, u32[]{:S(2)}) collective-permute-start(bf16[256,2048]{1,0:T(8,128)(2,1)S(1)} %get-tuple-element.83), channel_id=1, source_target_pairs={{0,2},{1,3},{2,0},{3,1},{4,6},{5,7},{6,4},{7,5},{8,10},{9,11},{10,... | collective-permute-start | bytes 3145736 | tf_op jit(solution)/shard_map/ppermute | solution.py:18
  316.4 125.4 %collective-permute-start.29 = (bf16[256,2048]{1,0:T(8,128)(2,1)S(1)}, bf16[256,2048]{1,0:T(8,128)(2,1)S(1)}, u32[]{:S(2)}, u32[]{:S(2)}) collective-permute-start(bf16[256,2048]{1,0:T(8,128)(2,1)S(1)} %get-tuple-element.83), channel_id=1, source_target_pairs={{0,1},{1,0},{2,3},{3,2},{4,5},{5,4},{6,7},{7,6},{8,9},{9,8},{10,11... | collective-permute-start | bytes 3145736 | tf_op jit(solution)/shard_map/ppermute | solution.py:18
  324.6 230.3 %collective-permute-start.65 = (bf16[1408,512]{1,0:T(8,128)(2,1)}, bf16[1408,512]{1,0:T(8,128)(2,1)}, u32[]{:S(2)}, u32[]{:S(2)}) collective-permute-start(bf16[1408,512]{1,0:T(8,128)(2,1)} %slice.534), channel_id=1, source_target_pairs={{0,8},{4,12},{8,0},{12,4},{16,24},{20,28},{24,16},{28,20},{1,9},{5... | collective-permute-start | bytes 4325384 | tf_op jit(solution)/shard_map/ppermute | solution.py:18
  380.7 74.4 %collective-permute-start.37 = (bf16[256,2048]{1,0:T(8,128)(2,1)S(1)}, bf16[256,2048]{1,0:T(8,128)(2,1)}, u32[]{:S(2)}, u32[]{:S(2)}) collective-permute-start(bf16[256,2048]{1,0:T(8,128)(2,1)S(1)} %collective-permute-done.36), channel_id=1, source_target_pairs={{0,1},{1,0},{2,3},{3,2},{4,5},{5,4},{6,7},{7,6},{8,9},{9,8},{10,11... | collective-permute-start | bytes 3145736 | tf_op jit(solution)/shard_map/ppermute | solution.py:18
  452.3 35.7 %collective-permute-start.31 = (f32[2,2,512]{2,1,0:T(2,128)}, f32[2,2,512]{2,1,0:T(2,128)}, u32[]{:S(2)}, u32[]{:S(2)}) collective-permute-start(f32[2,2,512]{2,1,0:T(2,128)} %get-tuple-element.53), channel_id=1, source_target_pairs={{0,4},{4,0},{8,12},{12,8},{16,20},{20,16},{24,28},{28,24},{1,5},{5... | collective-permute-start | bytes 24584 | tf_op jit(solution)/shard_map/ppermute | solution.py:18
  488.0 69.8 %collective-permute-start.59 = (bf16[512,1408]{1,0:T(8,128)(2,1)S(1)}, bf16[512,1408]{1,0:T(8,128)(2,1)}, u32[]{:S(2)}, u32[]{:S(2)}) collective-permute-start(bf16[512,1408]{1,0:T(8,128)(2,1)S(1)} %copy-done.20), channel_id=1, source_target_pairs={{0,8},{4,12},{8,0},{12,4},{16,24},{20,28},{24,16},{28,20},{1,9},{5... | collective-permute-start | bytes 4325384 | tf_op jit(solution)/shard_map/ppermute | solution.py:18
  493.5 27.9 %collective-permute-start.32 = (f32[2,2,512]{2,1,0:T(2,128)}, f32[2,2,512]{2,1,0:T(2,128)}, u32[]{:S(2)}, u32[]{:S(2)}) collective-permute-start(f32[2,2,512]{2,1,0:T(2,128)} %pad_maximum_fusion.47), channel_id=1, source_target_pairs={{8,0},{12,4},{16,8},{20,12},{24,16},{28,20},{9,1},{13,5},{17,9},{2... | collective-permute-start | bytes 24584 | tf_op jit(solution)/shard_map/ppermute | solution.py:24
  494.8 26.6 %collective-permute-start.33 = (f32[2,2,512]{2,1,0:T(2,128)}, f32[2,2,512]{2,1,0:T(2,128)}, u32[]{:S(2)}, u32[]{:S(2)}) collective-permute-start(f32[2,2,512]{2,1,0:T(2,128)} %pad_maximum_fusion.47), channel_id=1, source_target_pairs={{16,0},{20,4},{24,8},{28,12},{17,1},{21,5},{25,9},{29,13},{18,2},{... | collective-permute-start | bytes 24584 | tf_op jit(solution)/shard_map/ppermute | solution.py:24
  496.1 29.8 %collective-permute-start.34 = (f32[2,2,512]{2,1,0:T(2,128)}, f32[2,2,512]{2,1,0:T(2,128)}, u32[]{:S(2)}, u32[]{:S(2)}) collective-permute-start(f32[2,2,512]{2,1,0:T(2,128)} %pad_maximum_fusion.47), channel_id=1, source_target_pairs={{24,0},{28,4},{25,1},{29,5},{26,2},{30,6},{27,3},{31,7}} | collective-permute-start | bytes 24584 | tf_op jit(solution)/shard_map/ppermute | solution.py:24
  521.4 40.2 %collective-permute-start.62 = (bf16[512,1408]{1,0:T(8,128)(2,1)}, bf16[512,1408]{1,0:T(8,128)(2,1)}, u32[]{:S(2)}, u32[]{:S(2)}) collective-permute-start(bf16[512,1408]{1,0:T(8,128)(2,1)} %slice.530), channel_id=1, source_target_pairs={{0,8},{4,12},{8,0},{12,4},{16,24},{20,28},{24,16},{28,20},{1,9},{5... | collective-permute-start | bytes 4325384 | tf_op jit(solution)/shard_map/ppermute | solution.py:18
  521.4 145.2 %collective-permute-start.55 = (bf16[512,1024]{1,0:T(8,128)(2,1)}, bf16[512,1024]{1,0:T(8,128)(2,1)}, u32[]{:S(2)}, u32[]{:S(2)}) collective-permute-start(bf16[512,1024]{1,0:T(8,128)(2,1)} %fusion.123), channel_id=1, source_target_pairs={{0,8},{4,12},{8,0},{12,4},{16,24},{20,28},{24,16},{28,20},{1,9},{5... | collective-permute-start | bytes 3145736 | tf_op jit(solution)/shard_map/ppermute | solution.py:18
  525.9 142.9 %collective-permute-start.52 = (bf16[1024,512]{1,0:T(8,128)(2,1)}, bf16[1024,512]{1,0:T(8,128)(2,1)}, u32[]{:S(2)}, u32[]{:S(2)}) collective-permute-start(bf16[1024,512]{1,0:T(8,128)(2,1)} %fusion.132), channel_id=1, source_target_pairs={{0,8},{4,12},{8,0},{12,4},{16,24},{20,28},{24,16},{28,20},{1,9},{5... | collective-permute-start | bytes 3145736 | tf_op jit(solution)/shard_map/ppermute | solution.py:18
  555.0 115.6 %collective-permute-start.44 = (bf16[256,2048]{1,0:T(8,128)(2,1)S(1)}, bf16[256,2048]{1,0:T(8,128)(2,1)S(1)}, u32[]{:S(2)}, u32[]{:S(2)}) collective-permute-start(bf16[256,2048]{1,0:T(8,128)(2,1)S(1)} %copy-done.30), channel_id=1, source_target_pairs={{0,1},{1,0},{2,3},{3,2},{4,5},{5,4},{6,7},{7,6},{8,9},{9,8},{10,11... | collective-permute-start | bytes 3145736 | tf_op jit(solution)/shard_map/ppermute | solution.py:18
  557.8 56.3 %collective-permute-start.66 = (bf16[1408,256]{1,0:T(8,128)(2,1)S(1)}, bf16[1408,256]{1,0:T(8,128)(2,1)S(1)}, u32[]{:S(2)}, u32[]{:S(2)}) collective-permute-start(bf16[1408,256]{1,0:T(8,128)(2,1)S(1)} %slice.536), channel_id=1, source_target_pairs={{0,16},{4,20},{8,24},{12,28},{16,0},{20,4},{24,8},{28,12},{1,17},{... | collective-permute-start | bytes 2162696 | tf_op jit(solution)/shard_map/ppermute | solution.py:18
  561.6 67.9 %collective-permute-start.60 = (bf16[256,1408]{1,0:T(8,128)(2,1)S(1)}, bf16[256,1408]{1,0:T(8,128)(2,1)S(1)}, u32[]{:S(2)}, u32[]{:S(2)}) collective-permute-start(bf16[256,1408]{1,0:T(8,128)(2,1)S(1)} %slice.528), channel_id=1, source_target_pairs={{0,16},{4,20},{8,24},{12,28},{16,0},{20,4},{24,8},{28,12},{1,17},{... | collective-permute-start | bytes 2162696 | tf_op jit(solution)/shard_map/ppermute | solution.py:18
  614.1 49.0 %collective-permute-start.63 = (bf16[256,1408]{1,0:T(8,128)(2,1)S(1)}, bf16[256,1408]{1,0:T(8,128)(2,1)S(1)}, u32[]{:S(2)}, u32[]{:S(2)}) collective-permute-start(bf16[256,1408]{1,0:T(8,128)(2,1)S(1)} %slice.532), channel_id=1, source_target_pairs={{0,16},{4,20},{8,24},{12,28},{16,0},{20,4},{24,8},{28,12},{1,17},{... | collective-permute-start | bytes 2162696 | tf_op jit(solution)/shard_map/ppermute | solution.py:18
  629.6 110.2 %collective-permute-start.35 = (bf16[256,2048]{1,0:T(8,128)(2,1)S(1)}, bf16[256,2048]{1,0:T(8,128)(2,1)S(1)}, u32[]{:S(2)}, u32[]{:S(2)}) collective-permute-start(bf16[256,2048]{1,0:T(8,128)(2,1)S(1)} %copy-done.29), channel_id=1, source_target_pairs={{0,1},{1,0},{2,3},{3,2},{4,5},{5,4},{6,7},{7,6},{8,9},{9,8},{10,11... | collective-permute-start | bytes 3145736 | tf_op jit(solution)/shard_map/ppermute | solution.py:18
  663.1 26.0 %collective-permute-start.46 = (bf16[1024,512]{1,0:T(8,128)(2,1)S(1)}, bf16[1024,512]{1,0:T(8,128)(2,1)S(1)}, u32[]{:S(2)}, u32[]{:S(2)}) collective-permute-start(bf16[1024,512]{1,0:T(8,128)(2,1)S(1)} %copy-done.78), channel_id=1, source_target_pairs={{0,4},{4,0},{8,12},{12,8},{16,20},{20,16},{24,28},{28,24},{1,5},{5... | collective-permute-start | bytes 3145736 | tf_op jit(solution)/shard_map/ppermute | solution.py:18
  666.6 44.0 %collective-permute-start.49 = (bf16[1024,512]{1,0:T(8,128)(2,1)S(1)}, bf16[1024,512]{1,0:T(8,128)(2,1)S(1)}, u32[]{:S(2)}, u32[]{:S(2)}) collective-permute-start(bf16[1024,512]{1,0:T(8,128)(2,1)S(1)} %convolution_convert_fusion.10), channel_id=1, source_target_pairs={{0,4},{4,0},{8,12},{12,8},{16,20},{20,16},{24,28},{28,24},{1,5},{5... | collective-permute-start | bytes 3145736 | tf_op jit(solution)/shard_map/ppermute | solution.py:18
  668.8 42.2 %collective-permute-start.56 = (bf16[512,512]{1,0:T(8,128)(2,1)S(1)}, bf16[512,512]{1,0:T(8,128)(2,1)S(1)}, u32[]{:S(2)}, u32[]{:S(2)}) collective-permute-start(bf16[512,512]{1,0:T(8,128)(2,1)S(1)} %slice.522), channel_id=1, source_target_pairs={{0,16},{4,20},{8,24},{12,28},{16,0},{20,4},{24,8},{28,12},{1,17},{... | collective-permute-start | bytes 1572872 | tf_op jit(solution)/shard_map/ppermute | solution.py:18
  670.6 42.7 %collective-permute-start.53 = (bf16[512,512]{1,0:T(8,128)(2,1)S(1)}, bf16[512,512]{1,0:T(8,128)(2,1)S(1)}, u32[]{:S(2)}, u32[]{:S(2)}) collective-permute-start(bf16[512,512]{1,0:T(8,128)(2,1)S(1)} %slice.518), channel_id=1, source_target_pairs={{0,16},{4,20},{8,24},{12,28},{16,0},{20,4},{24,8},{28,12},{1,17},{... | collective-permute-start | bytes 1572872 | tf_op jit(solution)/shard_map/ppermute | solution.py:18
  689.1 50.6 %collective-permute-start.45 = (bf16[256,2048]{1,0:T(8,128)(2,1)S(1)}, bf16[256,2048]{1,0:T(8,128)(2,1)S(1)}, u32[]{:S(2)}, u32[]{:S(2)}) collective-permute-start(bf16[256,2048]{1,0:T(8,128)(2,1)S(1)} %add_convert_fusion.14), channel_id=1, source_target_pairs={{0,2},{1,3},{2,0},{3,1},{4,6},{5,7},{6,4},{7,5},{8,10},{9,11},{10,... | collective-permute-start | bytes 3145736 | tf_op jit(solution)/shard_map/ppermute | solution.py:18
  710.6 14.9 %collective-permute-start.47 = (bf16[512,512]{1,0:T(8,128)(2,1)S(1)}, bf16[512,512]{1,0:T(8,128)(2,1)S(1)}, u32[]{:S(2)}, u32[]{:S(2)}) collective-permute-start(bf16[512,512]{1,0:T(8,128)(2,1)S(1)} %slice.510), channel_id=1, source_target_pairs={{0,8},{4,12},{8,0},{12,4},{16,24},{20,28},{24,16},{28,20},{1,9},{5... | collective-permute-start | bytes 1572872 | tf_op jit(solution)/shard_map/ppermute | solution.py:18
  711.0 24.6 %collective-permute-start.50 = (bf16[512,512]{1,0:T(8,128)(2,1)S(1)}, bf16[512,512]{1,0:T(8,128)(2,1)S(1)}, u32[]{:S(2)}, u32[]{:S(2)}) collective-permute-start(bf16[512,512]{1,0:T(8,128)(2,1)S(1)} %slice.514), channel_id=1, source_target_pairs={{0,8},{4,12},{8,0},{12,4},{16,24},{20,28},{24,16},{28,20},{1,9},{5... | collective-permute-start | bytes 1572872 | tf_op jit(solution)/shard_map/ppermute | solution.py:18
  713.3 23.2 %collective-permute-start.57 = (bf16[512,256]{1,0:T(8,128)(2,1)S(1)}, bf16[512,256]{1,0:T(8,128)(2,1)S(1)}, u32[]{:S(2)}, u32[]{:S(2)}) collective-permute-start(bf16[512,256]{1,0:T(8,128)(2,1)S(1)} %slice.524), channel_id=1, source_target_pairs={{0,4},{4,0},{8,12},{12,8},{16,20},{20,16},{24,28},{28,24},{1,5},{5... | collective-permute-start | bytes 786440 | tf_op jit(solution)/shard_map/ppermute | solution.py:18
  725.5 14.1 %collective-permute-start.54 = (bf16[256,512]{1,0:T(8,128)(2,1)S(1)}, bf16[256,512]{1,0:T(8,128)(2,1)S(1)}, u32[]{:S(2)}, u32[]{:S(2)}) collective-permute-start(bf16[256,512]{1,0:T(8,128)(2,1)S(1)} %slice.520), channel_id=1, source_target_pairs={{0,4},{4,0},{8,12},{12,8},{16,20},{20,16},{24,28},{28,24},{1,5},{5... | collective-permute-start | bytes 786440 | tf_op jit(solution)/shard_map/ppermute | solution.py:18
  735.6 20.5 %collective-permute-start.48 = (bf16[256,512]{1,0:T(8,128)(2,1)S(1)}, bf16[256,512]{1,0:T(8,128)(2,1)S(1)}, u32[]{:S(2)}, u32[]{:S(2)}) collective-permute-start(bf16[256,512]{1,0:T(8,128)(2,1)S(1)} %slice.512), channel_id=1, source_target_pairs={{0,16},{4,20},{8,24},{12,28},{16,0},{20,4},{24,8},{28,12},{1,17},{... | collective-permute-start | bytes 786440 | tf_op jit(solution)/shard_map/ppermute | solution.py:18
  736.5 24.1 %collective-permute-start.51 = (bf16[256,512]{1,0:T(8,128)(2,1)S(1)}, bf16[256,512]{1,0:T(8,128)(2,1)S(1)}, u32[]{:S(2)}, u32[]{:S(2)}) collective-permute-start(bf16[256,512]{1,0:T(8,128)(2,1)S(1)} %slice.516), channel_id=1, source_target_pairs={{0,16},{4,20},{8,24},{12,28},{16,0},{20,4},{24,8},{28,12},{1,17},{... | collective-permute-start | bytes 786440 | tf_op jit(solution)/shard_map/ppermute | solution.py:18
  741.4 14.8 %collective-permute-start.68 = (f32[2,512]{1,0:T(2,128)S(1)}, f32[2,512]{1,0:T(2,128)S(1)}, u32[]{:S(2)}, u32[]{:S(2)}) collective-permute-start(f32[2,512]{1,0:T(2,128)S(1)} %fusion.136), channel_id=1, source_target_pairs={{0,1},{1,0},{2,3},{3,2},{4,5},{5,4},{6,7},{7,6},{8,9},{9,8},{10,11... | collective-permute-start | bytes 12296 | tf_op jit(solution)/shard_map/ppermute | solution.py:18
  (127 other events, 1517.9 us)

commit v2 on v0

v2 whole, which is shorter than its diff:
```python
import functools

import jax
import jax.numpy as jnp
from jax import lax
from jax.experimental import pallas as pl
from jax.experimental.pallas import tpu as pltpu
from jax.sharding import PartitionSpec as P

EPS = 1e-06
BF = jnp.bfloat16
F32 = jnp.float32
CHUNKS = 8


def swap(values, axis, bit):
    size = lax.axis_size(axis)
    return lax.ppermute(values, axis, [(i, i ^ bit) for i in range(size)])


def shift(values, axis, step):
    size = lax.axis_size(axis)
    pairs = [(i, i + step) for i in range(size) if 0 <= i + step < size]
    return lax.ppermute(values, axis, pairs)


def rms_scale(values):
    return lax.rsqrt(jnp.mean(values * values, axis=-1, keepdims=True) + EPS)


def norm_back(grad_normed, values, scale, weight):
    weighted = grad_normed * weight
    return scale * weighted - values * (scale * scale * scale) * jnp.mean(
        weighted * values, axis=-1, keepdims=True
    )


def sigmoid(v):
    return 0.5 * jnp.tanh(0.5 * v) + 0.5


ANYWHERE = pl.BlockSpec(memory_space=pl.ANY)
EXTRA = 16
VMEM_LIMIT = 60 * 1024 * 1024


def sds(shape, dtype=F32):
    return jax.ShapeDtypeStruct(shape, dtype)


def call(kernel, name, grid, inputs, outputs, flops=0, after=(), scratch=(), blocks=None):
    in_specs = [pl.BlockSpec(block, index) for _, block, index in inputs]
    in_specs += [ANYWHERE] * len(after)
    out_specs = [pl.BlockSpec(block, index) for _, _, block, index in outputs]
    count = len(inputs)
    skip = len(after)
    lead = 0 if blocks is None else 1

    def body(*refs):
        kernel(*refs[: lead + count], *refs[lead + count + skip :])

    settings = dict(
        out_shape=[sds(shape, dtype) for shape, dtype, _, _ in outputs],
        compiler_params=pltpu.CompilerParams(vmem_limit_bytes=VMEM_LIMIT),
        cost_estimate=pl.CostEstimate(flops=0, bytes_accessed=0, transcendentals=0),
        name=name,
    )
    operands = [a for a, _, _ in inputs] + list(after)
    if blocks is None:
        got = pl.pallas_call(
            body, grid=grid, in_specs=in_specs, out_specs=out_specs, scratch_shapes=list(scratch), **settings
        )(*operands)
    else:
        spec = pltpu.PrefetchScalarGridSpec(
            num_scalar_prefetch=1,
            grid=grid,
            in_specs=in_specs,
            out_specs=out_specs,
            scratch_shapes=list(scratch),
        )
        got = pl.pallas_call(body, grid_spec=spec, **settings)(blocks, *operands)
    return got[0] if len(outputs) == 1 else got


def fixed(array):
    zeros = (0,) * array.ndim
    return (array, array.shape, lambda *_: zeros)


def hold_kernel(*refs):
    pass


def after(value, *earlier):
    return pl.pallas_call(
        hold_kernel,
        in_specs=[ANYWHERE] * (1 + len(earlier)),
        out_specs=ANYWHERE,
        out_shape=jax.ShapeDtypeStruct(value.shape, value.dtype),
        input_output_aliases={0: 0},
        cost_estimate=pl.CostEstimate(flops=0, bytes_accessed=0, transcendentals=0),
        name="hold",
    )(value, *earlier)


def dot(left, right):
    return jnp.dot(left, right, preferred_element_type=F32)


def dot_last(left, right):
    return lax.dot_general(left, right, (((1,), (1,)), ((), ())), preferred_element_type=F32)


def dot_first(left, right):
    return lax.dot_general(left, right, (((0,), (0,)), ((), ())), preferred_element_type=F32)


def wide(column):
    return jnp.broadcast_to(column, (column.shape[0], 128))


def upright(row):
    return jnp.broadcast_to(row, (128, row.shape[1])).T


def stack(*refs):
    return jnp.concatenate([r[...] for r in refs], axis=0)


def tile_of(size, most):
    best = size
    for tile in range(128, most + 1, 128):
        if size % tile == 0:
            best = tile
    return best


def project_kernel(x0, x1, w, lb_ref, *refs):
    pi_ref, pf_ref, pg_ref, loc_ref, cum_ref, tot_ref = refs[-6:]
    groups, rows, tile = loc_ref.shape
    steps = rows // CHUNKS
    y = dot(stack(x0, x1), jnp.concatenate([w[0], w[1], w[2]], axis=1))
    lb = lb_ref[...]
    for g in range(groups):
        part = y[g * rows : (g + 1) * rows]
        pi_ref[g] = part[:, :tile]
        pf_ref[g] = part[:, tile : 2 * tile]
        pg_ref[g] = part[:, 2 * tile :]
    for g in range(groups):
        s = jnp.zeros((CHUNKS, tile), F32)
        p = jnp.ones_like(s)
        for t in range(steps):
            at = pl.ds(t, CHUNKS, stride=steps)
            pi = pi_ref[g, at, :]
            sig = sigmoid(pf_ref[g, at, :])
            f = lb + (1.0 - lb) * sig
            s = f * s + pi * sigmoid(pi) * ((1.0 - lb) * (1.0 - sig))
            p = p * f
            loc_ref[g, at, :] = s
            cum_ref[g, at, :] = p
        a = p[0:1]
        b = s[0:1]
        for c in range(1, CHUNKS):
            b = p[c : c + 1] * b + s[c : c + 1]
            a = a * p[c : c + 1]
        put_total(tot_ref, g, a, b, refs[:-6])


def put_total(tot_ref, g, a, b, prior):
    at = g
    if prior:
        at = g + prior[0].shape[1]
        if g == 0:
            tot_ref[:, : prior[0].shape[1], :] = prior[0][...]
    tot_ref[0, at : at + 1, :] = a
    tot_ref[1, at : at + 1, :] = b


def total_blocks(prior, chans, tile):
    count = 2 + sum(p.shape[1] for p in prior)
    inputs = [(p, (2, p.shape[1], tile), lambda c: (0, 0, c)) for p in prior]
    return inputs, ((2, count, chans), F32, (2, count, tile), lambda c: (0, 0, c))


def project(x0, x1, in_proj, lower, prior=(), after=()):
    rows, width = x0.shape
    chans = in_proj.shape[2]
    tile = tile_of(chans, 128)
    full = ((2, rows, chans), F32, (2, rows, tile), lambda c: (0, 0, c))
    before, total = total_blocks(prior, chans, tile)
    return call(
        project_kernel,
        "project",
        (chans // tile,),
        [
            fixed(x0),
            fixed(x1),
            (in_proj, (3, width, tile), lambda c: (0, 0, c)),
            (lower, (1, tile), lambda c: (0, c)),
            *before,
        ],
        [full] * 5 + [total],
        flops=12 * rows * width * chans,
        after=after,
    )


def mix_kernel(loc_ref, cum_ref, pg_ref, carry_ref, gain_ref, w_ref, state_ref, b0, b1, q0, q1, mix_ref, sq_ref):
    rows = loc_ref.shape[1]
    steps = rows // CHUNKS
    gain = gain_ref[...]
    cin = carry_ref[0]
    for c in range(CHUNKS):
        at = pl.ds(c * steps, steps)
        st = loc_ref[0, at, :] + cum_ref[0, at, :] * cin
        cin = st[steps - 1 : steps]
        pg = pg_ref[0, at, :]
        state_ref[0, at, :] = st
        mix_ref[at, :] = (st * gain * (pg * sigmoid(pg))).astype(BF)
        sq_ref[at, :] = wide(jnp.sum(st * st, axis=-1, keepdims=True))
    out = dot(mix_ref[...], w_ref[...]).astype(BF)
    first = pl.program_id(0) == 0

    @pl.when(first)
    def _():
        b0[...] = out
        q0[...] = sq_ref[...]

    @pl.when(jnp.logical_not(first))
    def _():
        b1[...] = out
        q1[...] = sq_ref[...]


def mix(loc, cum, pg, carry, shift, gain, out_proj, after=()):
    _, rows, chans = loc.shape
    width = out_proj.shape[1]
    piece = ((1, rows, chans), lambda g: (g, 0, 0))
    whole = ((rows, width), BF, (rows, width), lambda g: (0, 0))
    return call(
        mix_kernel,
        "mix",
        (2,),
        [
            (loc, *piece),
            (cum, *piece),
            (pg, *piece),
            (carry, (1, 1, chans), lambda g: (g + shift, 0, 0)),
            fixed(gain),
            fixed(out_proj),
        ],
        [
            (loc.shape, F32, *piece),
            whole,
            whole,
            ((rows, 128), F32, (rows, 128), lambda g: (0, 0)),
            ((rows, 128), F32, (rows, 128), lambda g: (0, 0)),
        ],
        flops=4 * rows * chans * width,
        after=after,
        scratch=[pltpu.VMEM((rows, chans), BF), pltpu.VMEM((rows, 128), F32)],
    )


def hidden_grad_kernel(g0, g1, w, out):
    out[...] = dot_last(stack(g0, g1), w[...])


def hidden_grad(g0, g1, down, after=()):
    rows, width = g0.shape
    units = down.shape[0]
    tile = min(256, units)
    return call(
        hidden_grad_kernel,
        "hidden_grad",
        (pl.cdiv(units, tile),),
        [fixed(g0), fixed(g1), (down, (tile, width), lambda n: (n, 0))],
        [((2 * rows, units), F32, (2 * rows, tile), lambda n: (0, n))],
        flops=4 * rows * width * units,
        after=after,
    )


def feed_kernel(x0, x1, w, gh_ref, hidden, gg, gu):
    x = stack(x0, x1)
    gate = dot(x, w[0])
    up = dot(x, w[1])
    gh = gh_ref[...]
    sig = sigmoid(gate)
    act = gate * sig
    hidden[...] = (act * up).astype(BF)
    gg[...] = (gh * up * (sig * (1.0 + gate * (1.0 - sig)))).astype(BF)
    gu[...] = (gh * act).astype(BF)


def feed(x0, x1, gate_up, gh, after=()):
    rows, width = x0.shape
    units = gate_up.shape[2]
    tile = min(256, units)
    col = ((2 * rows, tile), lambda n: (0, n))
    return call(
        feed_kernel,
        "feed",
        (pl.cdiv(units, tile),),
        [
            fixed(x0),
            fixed(x1),
            (gate_up, (2, width, tile), lambda n: (0, 0, n)),
            (gh, *col),
        ],
        [((2 * rows, units), BF, *col)] * 3,
        flops=8 * rows * width * units,
        after=after,
    )


def feed_back_kernel(gg, gu, w, b0, b1):
    rows = b0.shape[0]
    out = (dot_last(gg[...], w[0]) + dot_last(gu[...], w[1])).astype(BF)
    b0[...] = out[:rows]
    b1[...] = out[rows:]


def feed_back(gg, gu, gate_up, after=()):
    rows = gg.shape[0] // 2
    _, width, units = gate_up.shape
    tile = tile_of(width, 512)
    part = ((rows, width), BF, (rows, tile), lambda d: (0, d))
    return call(
        feed_back_kernel,
        "feed_back",
        (width // tile,),
        [fixed(gg), fixed(gu), (gate_up, (2, tile, units), lambda d: (0, d, 0))],
        [part, part],
        flops=8 * rows * width * units,
        after=after,
    )


def feed_out_kernel(h, w, b0, b1):
    rows = b0.shape[0]
    out = dot(h[...], w[...]).astype(BF)
    b0[...] = out[:rows]
    b1[...] = out[rows:]


def feed_out(hidden, down, after=()):
    rows = hidden.shape[0] // 2
    units, width = down.shape
    tile = tile_of(width, 512)
    part = ((rows, width), BF, (rows, tile), lambda d: (0, d))
    return call(
        feed_out_kernel,
        "feed_out",
        (width // tile,),
        [fixed(hidden), (down, (units, tile), lambda d: (0, d))],
        [part, part],
        flops=4 * rows * width * units,
        after=after,
    )


def back_local_kernel(
    width, g0, g1, w, pg_ref, pf_ref, state_ref, gain_ref, lb_ref, *refs
):
    mixed_ref, gpg_ref, loc_ref, cum_ref, tot_ref, term_ref = refs[-6:]
    groups, rows, tile = loc_ref.shape
    steps = rows // CHUNKS
    gain = gain_ref[...]
    lb = lb_ref[...]
    grads = dot_last(jnp.concatenate([g0[:rows], g1[:rows]], axis=0), w[...])
    term = jnp.zeros((1, tile), F32)
    for g in range(groups):
        extra = (g1 if g else g0)[rows:, :rows].astype(F32)
        scales = upright(extra[0:1] + extra[1:2])
        inners = upright(extra[2:3] + extra[3:4])
        for c in range(CHUNKS):
            at = pl.ds(c * steps, steps)
            part = slice(c * steps, (c + 1) * steps)
            scale = scales[part, :1]
            coef = scale * scale * scale * inners[part, :1] * (1.0 / width)
            pg = pg_ref[g, at, :]
            gm = grads[g * rows + c * steps : g * rows + (c + 1) * steps]
            st = state_ref[g, at, :]
            sig = sigmoid(pg)
            act = pg * sig
            unit = st * scale
            gact = gm * act
            mixed_ref[g, at, :] = (unit * gain * act).astype(BF)
            gpg_ref[g, at, :] = (gm * gain * unit * (sig * (1.0 + pg * (1.0 - sig)))).astype(BF)
            term = term + jnp.sum(gact * unit, axis=0, keepdims=True)
            loc_ref[g, at, :] = scale * (gact * gain) - st * coef
    term_ref[...] = term
    for g in range(groups):
        s = jnp.zeros((CHUNKS, tile), F32)
        q = jnp.ones_like(s)
        for t in range(steps - 1, -1, -1):
            at = pl.ds(t, CHUNKS, stride=steps)
            f = lb + (1.0 - lb) * sigmoid(pf_ref[g, at, :])
            adj = loc_ref[g, at, :] + s
            loc_ref[g, at, :] = adj
            cum_ref[g, at, :] = q
            s = f * adj
            q = q * f
        last = CHUNKS - 1
        a = q[last : last + 1]
        b = s[last : last + 1]
        for c in range(CHUNKS - 2, -1, -1):
            b = q[c : c + 1] * b + s[c : c + 1]
            a = a * q[c : c + 1]
        put_total(tot_ref, g, a, b, refs[:-6])


def back_local(g0, g1, out_proj, pg, pf, state, gain, lower, prior=(), after=()):
    rows, width = pg.shape[1], g0.shape[1]
    chans = out_proj.shape[0]
    tile = tile_of(chans, 128)
    piece = ((2, rows, tile), lambda c: (0, 0, c))
    row = ((1, tile), lambda c: (0, c))
    shape = (2, rows, chans)
    before, total = total_blocks(prior, chans, tile)
    return call(
        functools.partial(back_local_kernel, width),
        "back_local",
        (chans // tile,),
        [
            fixed(g0),
            fixed(g1),
            (out_proj, (tile, width), lambda c: (c, 0)),
            (pg, *piece),
            (pf, *piece),
            (state, *piece),
            (gain, *row),
            (lower, *row),
            *before,
        ],
        [
            (shape, BF, *piece),
            (shape, BF, *piece),
            (shape, F32, *piece),
            (shape, F32, *piece),
            total,
            ((1, chans), F32, *row),
        ],
        flops=4 * rows * width * chans,
        after=after,
    )


def back_mix_kernel(
    loc_ref, cum_ref, state_ref, pi_ref, pf_ref, gpg_ref, carry_ref, prior_ref, lb_ref, w,
    gpi_ref, gpf_ref, b0, b1, term_ref,
):
    rows = loc_ref.shape[1]
    steps = rows // CHUNKS
    lb = lb_ref[...]
    rest = 1.0 - lb
    cin = carry_ref[0]
    term = jnp.zeros((1, loc_ref.shape[2]), F32)
    top = lax.broadcasted_iota(jnp.int32, (steps, loc_ref.shape[2]), 0) == 0
    for c in range(CHUNKS - 1, -1, -1):
        at = pl.ds(c * steps, steps)
        adj = loc_ref[0, at, :] + cum_ref[0, at, :] * cin
        pi = pi_ref[0, at, :]
        sig = sigmoid(pf_ref[0, at, :])
        cin = (lb + rest * sig[0:1]) * adj[0:1]
        st = state_ref[0, at, :]
        before = prior_ref[0] if c == 0 else state_ref[0, pl.ds(c * steps - 1, 1), :]
        prev = jnp.where(top, before, pltpu.roll(st, 1, 0))
        sig_in = sigmoid(pi)
        total = adj * (prev - pi * sig_in)
        left = 1.0 - sig
        gpi_ref[0, at, :] = (adj * (rest * left) * (sig_in * (1.0 + pi * (1.0 - sig_in)))).astype(BF)
        gpf_ref[0, at, :] = (total * rest * sig * left).astype(BF)
        term = term + jnp.sum(total * left, axis=0, keepdims=True)
    term_ref[0] = term
    out = (
        dot_last(gpi_ref[0], w[0]) + dot_last(gpf_ref[0], w[1]) + dot_last(gpg_ref[0], w[2])
    ).astype(BF)
    first = pl.program_id(0) == 0

    @pl.when(first)
    def _():
        b0[...] = out

    @pl.when(jnp.logical_not(first))
    def _():
        b1[...] = out


def back_mix(loc, cum, state, pi, pf, gpg, carry, prior, shift, lower, in_proj, after=()):
    _, rows, chans = state.shape
    width = in_proj.shape[1]
    piece = ((1, rows, chans), lambda g: (g, 0, 0))
    per = ((1, 1, chans), lambda g: (g, 0, 0))
    moved = ((1, 1, chans), lambda g: (g + shift, 0, 0))
    whole = ((rows, width), BF, (rows, width), lambda g: (0, 0))
    return call(
        back_mix_kernel,
        "back_mix",
        (2,),
        [(v, *piece) for v in (loc, cum, state, pi, pf, gpg)]
        + [(carry, *moved), (prior, *moved), fixed(lower), fixed(in_proj)],
        [
            (state.shape, BF, *piece),
            (state.shape, BF, *piece),
            whole,
            whole,
            ((2, 1, chans), F32, *per),
        ],
        flops=12 * rows * width * chans,
        after=after,
    )


def product_kernel(me, x0, x1, x2, x3, near, far, out):
    out[...] = (dot_first(stack(x0, x1), near[...]) + dot_first(stack(x2, x3), far[...])).astype(BF)


def product_add_kernel(half, me, x0, x1, x2, x3, near, far, got, send, keep):
    total = dot_first(stack(x0, x1), near[...]) + dot_first(stack(x2, x3), far[...])
    total = (total + got[...].astype(F32)).astype(BF)
    early = pl.program_id(0) < half

    @pl.when(early)
    def _():
        send[...] = total

    @pl.when(jnp.logical_not(early))
    def _():
        keep[...] = total


def product(me, lefts, near, far, bits, size, got=None, after=()):
    levels = len(bits)
    count = 1 << (levels - 1)
    base = 0 if got is None else count
    top = 2 * count - 1 - base
    rows = near.shape[0] // 2
    units = near.shape[1]

    def place(j, me):
        turned = top - j
        block = me[0]
        for n, bit in enumerate(bits):
            block = block ^ (((turned >> (levels - 1 - n)) & 1) * bit)
        return (0, block)

    if size % 128:
        def ordered(x):
            parts = [
                lax.dynamic_slice_in_dim(x[:rows], place(j, me)[1] * size, size, 1)
                for j in range(count)
            ]
            return jnp.concatenate(parts, axis=1)

        lefts = [ordered(x) for x in lefts]
        count, size = count * size // 128, 128
        position = lambda j, me: (0, j)
    else:
        position = place
    inputs = [(x, (rows, size), position) for x in lefts]
    inputs += [fixed(near), fixed(far)]
    flops = 8 * rows * units * size * count
    if got is None:
        out = ((count * size, units), BF, (size, units), lambda j, me: (j, 0))
        return call(product_kernel, "product", (count,), inputs, [out], flops, after, blocks=me)
    half = count // 2
    inputs.append((got, (size, units), lambda j, me: (j, 0)))
    shape = (half * size, units)
    send = (shape, BF, (size, units), lambda j, me: (jnp.minimum(j, half - 1), 0))
    keep = (shape, BF, (size, units), lambda j, me: (jnp.maximum(j - half, 0), 0))
    return call(
        functools.partial(product_add_kernel, half),
        "product_add",
        (count,),
        inputs,
        [send, keep],
        flops,
        after,
        blocks=me,
    )


def halve_kernel(half, one, two, send, keep):
    total = (one[...].astype(F32) + two[...].astype(F32)).astype(BF)
    early = pl.program_id(0) < half

    @pl.when(early)
    def _():
        send[...] = total

    @pl.when(jnp.logical_not(early))
    def _():
        keep[...] = total


def halve(one, two, size, after=()):
    count = one.shape[0] // size
    half = count // 2
    units = one.shape[1]
    block = ((size, units), lambda j: (j, 0))
    shape = (half * size, units)
    return call(
        functools.partial(halve_kernel, half),
        "halve",
        (count,),
        [(one, *block), (two, *block)],
        [
            (shape, BF, (size, units), lambda j: (jnp.minimum(j, half - 1), 0)),
            (shape, BF, (size, units), lambda j: (jnp.maximum(j - half, 0), 0)),
        ],
        after=after,
    )


def finish_kernel(turned, *refs):
    out = refs[-1]
    for k in range(len(refs) // 2):
        total = refs[2 * k][...].astype(F32) + refs[2 * k + 1][...].astype(F32)
        if turned:
            out[...] = total.T
        else:
            out[k] = total


def finish(pairs, turned=False, after=()):
    rows, units = pairs[0][0].shape
    flat = [v for one in pairs for v in one]
    if turned:
        tile = 128 if rows % 128 == 0 else rows
        out = ((units, rows), F32, (units, tile), lambda n: (0, n))
    else:
        tile = 64 if rows % 64 == 0 else rows
        count = len(pairs)
        out = ((count, rows, units), F32, (count, tile, units), lambda n: (0, n, 0))
    return call(
        functools.partial(finish_kernel, turned),
        "finish",
        (rows // tile,),
        [(v, (tile, units), lambda n: (n, 0)) for v in flat],
        [out],
        after=after,
    )


def row_call(kernel, name, arrays, gains, outputs, sums=0, after=(), most=64, more=()):
    rows, width = arrays[0].shape[-2:]
    tile = most if rows % most == 0 else rows

    def block(shape):
        lead = len(shape) - 2
        return (*shape[:-2], tile, shape[-1]), lambda r: (*(0,) * lead, r, 0)

    inputs = [(a, *block(a.shape)) for a in arrays] + [fixed(g) for g in gains]
    results = [(shape, dtype, *block(shape)) for shape, dtype in outputs]
    results += [((1, width), F32, (1, width), lambda r: (0, 0))] * sums + list(more)
    return call(kernel, name, (rows // tile,), inputs, results, after=after)


def add_to(ref, term):
    first = pl.program_id(0) == 0

    @pl.when(first)
    def _():
        ref[...] = term

    @pl.when(jnp.logical_not(first))
    def _():
        ref[...] += term


def first_norm_kernel(x_ref, gain_ref, out):
    x = x_ref[...].astype(F32)
    out[...] = (x * rms_scale(x) * gain_ref[...]).astype(BF)


def plus_kernel(one, two, out):
    out[...] = (one[...].astype(F32) + two[...].astype(F32)).astype(BF)


def plus(one, two, after=()):
    return row_call(plus_kernel, "plus", [one, two], [], [(one.shape, BF)], after=after)


def middle_kernel(x, own, core, hop, q0, q1, q2, q3, gain, branch_ref, middle_ref, out, scale_ref):
    width = x.shape[1]
    branch = own[...].astype(F32) + core[...].astype(F32) + hop[...].astype(F32)
    scale = lax.rsqrt((q0[...] + q1[...] + q2[...] + q3[...]) / width + EPS)
    middle = x[...].astype(F32) + branch * scale[:, :1]
    branch_ref[...] = branch
    scale_ref[...] = scale
    middle_ref[...] = middle
    out[...] = (middle * rms_scale(middle) * gain[...]).astype(BF)


def turn_kernel(up, own, core, hop, middle_ref, branch, scale_ref, gain, grad_ref, term, out):
    tile = up.shape[0]
    step = pl.program_id(0)
    rows = out.shape[0] - EXTRA
    grad = own[...].astype(F32) + core[...].astype(F32) + hop[...].astype(F32)
    middle = middle_ref[...]
    scale = rms_scale(middle)
    total = up[...].astype(F32) + norm_back(grad, middle, scale, gain[...])
    low = total.astype(BF)
    grad_ref[...] = total
    out[pl.ds(pl.multiple_of(step * tile, tile), tile), :] = low
    inner = wide(jnp.sum(low.astype(F32) * branch[...], axis=-1, keepdims=True)).T[:EXTRA]
    outer = scale_ref[...].T[:EXTRA]
    high_outer = outer.astype(BF).astype(F32)
    high_inner = inner.astype(BF).astype(F32)
    which = lax.broadcasted_iota(jnp.int32, inner.shape, 0)
    both = jnp.where(which < 2, outer, inner)
    high = jnp.where(which < 2, high_outer, high_inner)
    extra = jnp.where(which % 2 == 0, high, both - high)

    @pl.when(step == 0)
    def _():
        out[rows:, :] = jnp.zeros((EXTRA, out.shape[1]), BF)

    out[rows:, pl.ds(pl.multiple_of(step * tile, tile), tile)] = extra.astype(BF)
    add_to(term, jnp.sum(grad * middle * scale, axis=0, keepdims=True))


def turn(up, own, core, hop, middle, branch, scale, gain, after=()):
    rows, width = up.shape
    shape = (rows + EXTRA, width)
    return row_call(
        turn_kernel, "turn", [up, own, core, hop, middle, branch, scale], [gain],
        [(up.shape, F32)], sums=1, after=after, most=128,
        more=[(shape, BF, shape, lambda r: (0, 0))],
    )


def last_kernel(x_ref, own, core, hop, grad_middle, gain, out, term):
    grad = own[...].astype(F32) + core[...].astype(F32) + hop[...].astype(F32)
    x = x_ref[...].astype(F32)
    scale = rms_scale(x)
    out[...] = grad_middle[...] + norm_back(grad, x, scale, gain[...])
    add_to(term, jnp.sum(grad * x * scale, axis=0, keepdims=True))


def result_kernel(middle, own, core, hop, out):
    out[...] = (
        middle[...] + (own[...].astype(F32) + core[...].astype(F32) + hop[...].astype(F32))
    ).astype(BF)


def in_order(me, total, other):
    odd = (me[0] % 2) == 1
    return (
        odd,
        jnp.where(odd, other[0], total[0]),
        jnp.where(odd, other[1], total[1]),
        jnp.where(odd, total[0], other[0]),
        jnp.where(odd, total[1], other[1]),
    )


def pair_kernel(reverse, me, total, other, pair):
    odd, low_a, low_b, high_a, high_b = in_order(me, total, other)
    pair[0] = low_a * high_a
    pair[1] = low_a * high_b + low_b if reverse else high_a * low_b + high_b


def enter_kernel(reverse, me, total, other, *refs):
    odd, low_a, low_b, high_a, high_b = in_order(me, total, other)
    enter = jnp.zeros_like(low_a)
    for got in reversed(refs[:-1]):
        enter = got[0] * enter + got[1]
    if reverse:
        enter = jnp.where(odd, enter, high_a * enter + high_b)
    else:
        enter = jnp.where(odd, low_a * enter + low_b, enter)
    for g in range(enter.shape[0]):
        refs[-1][g] = enter[g : g + 1]


def chain(me, total, reverse, between=None, beside=None):
    size = lax.axis_size("seq")
    _, groups, chans = total.shape
    other = swap(total, "seq", 1)
    got = between() if between else ()
    whole = (total.shape, F32, total.shape, lambda i, me: (0, 0, 0))
    pair = call(
        functools.partial(pair_kernel, reverse), "pair", (1,), [fixed(total), fixed(other)], [whole],
        after=got, blocks=me,
    )
    sign = -1 if reverse else 1
    reached = [shift(pair, "seq", 2 * sign * d) for d in range(1, size // 2)]
    shape = (groups, 1, chans)
    got = beside(pair) if beside else ()
    return call(
        functools.partial(enter_kernel, reverse), "enter", (1,),
        [fixed(total), fixed(other), *[fixed(r) for r in reached]],
        [(shape, F32, shape, lambda i, me: (0, 0, 0))],
        after=got,
        blocks=me,
    )


def seq_bits():
    size = lax.axis_size("seq")
    bits = []
    bit = 1
    while bit < size:
        bits.append(bit)
        bit *= 2
    return bits


class Weight:
    def __init__(self, me, lefts, near, far, bits, size):
        self.me, self.lefts, self.near, self.far = me, lefts, near, far
        self.bits, self.size, self.level = bits, size, 0

    def begin(self, *earlier):
        self.send = product(
            self.me, self.lefts, self.near, self.far, self.bits, self.size, after=earlier
        )
        return self.send

    def go(self, *earlier):
        send = after(self.send, *earlier) if earlier else self.send
        self.got = swap(send, "seq", self.bits[self.level])
        self.level += 1

    def step(self, *earlier):
        if self.level == 1:
            self.send, self.keep = product(
                self.me, self.lefts, self.near, self.far, self.bits, self.size, self.got, after=earlier
            )
        else:
            self.send, self.keep = halve(self.keep, self.got, self.size, after=earlier)
        return self.send

    def last(self):
        return self.level == len(self.bits)


def on_device(
    tokens,
    in_proj,
    out_proj,
    gate_up,
    down,
    norm1_gain,
    mixer_gain,
    norm2_gain,
    lower_bound,
    cotangent,
):
    width = in_proj.shape[1]
    chans = in_proj.shape[2]
    x = tokens[0]
    g0 = cotangent[0]
    rows = x.shape[0]
    bits = seq_bits()
    y_first = bits
    z_first = bits[1:] + bits[:1]
    block = width // lax.axis_size("seq")
    me = lax.axis_index("seq").reshape(1).astype(jnp.int32)

    offset = lax.axis_index("wt") * chans
    lower_use = lax.dynamic_slice_in_dim(lower_bound, offset, chans)[None]
    mixer_use = lax.dynamic_slice_in_dim(mixer_gain, offset, chans)[None]
    gain_one, gain_two = norm1_gain[None], norm2_gain[None]

    n0 = row_call(first_norm_kernel, "first_norm", [x], [gain_one], [(x.shape, BF)])
    hop = swap(n0, "wt", 2)
    n1 = swap(n0, "wt", 1)
    g1 = swap(g0, "wt", 1)
    grad_hop = swap(after(g0, n0), "wt", 2)
    pi_n, pf_n, pg_n, loc_n, cum_n, tot = project(n0, n1, in_proj, lower_use)
    gh_n = hidden_grad(g0, g1, down, after=(tot,))
    n2 = after(hop, gh_n)
    n3 = swap(n2, "wt", 1)
    pi_f, pf_f, pg_f, loc_f, cum_f, tot = project(n2, n3, in_proj, lower_use, (tot,))
    g2 = after(grad_hop, tot)
    g3 = swap(g2, "wt", 1)
    enter = chain(me, tot, False, lambda: (g2,))
    state_f, bf0, bf1, qf0, qf1 = mix(loc_f, cum_f, pg_f, enter, 2, mixer_use, out_proj)
    q2, q3 = swap(qf0, "wt", 2), swap(qf1, "wt", 3)
    state_n, bn0, bn1, q0, qn1 = mix(
        loc_n, cum_n, pg_n, enter, 0, mixer_use, out_proj, after=(bf0,)
    )
    across = plus(bf0, swap(bf1, "wt", 1), after=(bn0,))
    hop = swap(across, "wt", 2)
    q1 = swap(qn1, "wt", 1)
    core = swap(bn1, "wt", 1)
    gh_f = hidden_grad(g2, g3, down, after=(across,))
    branch, middle, t0, scale_two = row_call(
        middle_kernel,
        "middle",
        [x, bn0, core, hop, q0, q1, q2, q3],
        [gain_two],
        [(x.shape, F32), (x.shape, F32), (x.shape, BF), ((rows, 128), F32)],
        after=(gh_f,),
    )

    hop = swap(t0, "wt", 2)
    t1 = swap(t0, "wt", 1)
    hid_n, gg_n, gu_n = feed(t0, t1, gate_up, gh_n)
    kn0, kn1 = feed_back(gg_n, gu_n, gate_up)
    core = swap(kn1, "wt", 1)
    t2 = after(hop, kn0)
    t3 = swap(t2, "wt", 1)
    hid_f, gg_f, gu_f = feed(t2, t3, gate_up, gh_f)

    twos = (t0, t1, t2, t3)
    gate = Weight(me, twos, gg_n, gg_f, y_first, block)
    up = Weight(me, twos, gu_n, gu_f, y_first, block)
    lower = Weight(me, (g0, g1, g2, g3), hid_n, hid_f, z_first, block)
    kf0, kf1 = feed_back(gg_f, gu_f, gate_up)
    gate.begin(kf0)
    gate.go()
    across = plus(kf0, swap(kf1, "wt", 1), after=(gate.send,))
    hop = swap(across, "wt", 2)
    lower.begin(across)
    lower.go()
    up.begin(lower.send, across)
    ff0, ff1 = feed_out(hid_f, down, after=(up.send,))
    grad_middle, norm2_term, b0 = turn(
        g0, kn0, core, hop, middle, branch, scale_two, gain_two, after=(ff0,)
    )

    hop = swap(b0, "wt", 2)
    b1 = swap(b0, "wt", 1)
    mixed_n, gpg_n, bloc_n, bcum_n, btot, mixer_n = back_local(
        b0, b1, out_proj, pg_n, pf_n, state_n, mixer_use, lower_use
    )
    ffn_across = plus(ff0, swap(ff1, "wt", 1), after=(btot,))
    fn0, fn1 = feed_out(hid_n, down, after=(ffn_across,))
    ffn_core = swap(fn1, "wt", 1)
    b2 = after(hop, fn0)
    b3 = swap(b2, "wt", 1)
    gate.step(b2)
    ffn_hop = swap(after(ffn_across, b2), "wt", 2)
    mixed_f, gpg_f, bloc_f, bcum_f, btot, mixer_f = back_local(
        b2, b3, out_proj, pg_f, pf_f, state_f, mixer_use, lower_use, (btot,), after=(gate.send,)
    )
    leave = chain(me, btot, True, None, lambda pair: (lower.step(pair),))
    gate.go(leave)
    up.go(leave)
    lower.go(leave)
    gpi_f, gpf_f, df0, df1, bound_f = back_mix(
        bloc_f, bcum_f, state_f, pi_f, pf_f, gpg_f, leave, enter, 2, lower_use, in_proj
    )
    across = plus(df0, swap(df1, "wt", 1))
    hop = swap(across, "wt", 2)
    gpi_n, gpf_n, dn0, dn1, bound_n = back_mix(
        bloc_n, bcum_n, state_n, pi_n, pf_n, gpg_n, leave, enter, 0, lower_use, in_proj, after=(across,)
    )
    core = swap(dn1, "wt", 1)

    def flat(values):
        return values.reshape(2 * rows, chans)

    normals = (n0, n1, n2, n3)
    ins = [
        Weight(me, normals, flat(near), flat(far), y_first, block)
        for near, far in ((gpi_n, gpi_f), (gpf_n, gpf_f), (gpg_n, gpg_f))
    ]
    out = Weight(me, (b0, b1, b2, b3), flat(mixed_n), flat(mixed_f), y_first, block)
    token = gate.step(dn0)
    gate.go()
    for one in (out, ins[0]):
        token = one.begin(token)
        one.go()
    token = up.step(token)
    up.go()
    for one in ins[1:]:
        token = one.begin(token)
        one.go()
    token = out.step(token)
    out.go()
    result = row_call(
        result_kernel, "result", [middle, fn0, ffn_core, ffn_hop], [], [(x.shape, BF)], after=(token,)
    )
    grad_inputs, norm1_term = row_call(
        last_kernel,
        "last",
        [x, dn0, core, hop, grad_middle],
        [gain_one],
        [(x.shape, F32)],
        sums=1,
        after=(result,),
    )

    wt = lax.axis_index("wt")
    span = width // lax.axis_size("wt")
    norm_terms = jnp.concatenate([norm1_term, norm2_term])

    def part(j):
        return lax.dynamic_slice_in_dim(norm_terms, (wt ^ j) * span, span, 1)

    norms = part(0)
    for j in (1, 2, 3):
        norms = norms + swap(part(j), "wt", j)
    mixer_term = (mixer_n + mixer_f)[0]
    bound_term = jnp.sum(bound_n, axis=(0, 1)) + jnp.sum(bound_f, axis=(0, 1))
    gains = jnp.stack([norms[0], mixer_term, norms[1], bound_term])

    token = grad_inputs
    order = [lower, ins[0], up, out, *ins[1:]]
    while not all(one.last() for one in (gate, *order)):
        for one in (gate, *order):
            if not one.last():
                token = one.step(token)
                one.go()
    gate_up_grad = finish([(gate.keep, gate.got), (up.keep, up.got)])
    down_grad = finish([(lower.keep, lower.got)], True)
    out_grad = finish([(out.keep, out.got)], True)
    gains = after(gains, gate_up_grad)
    for bit in bits:
        gains = gains + swap(gains, "seq", bit)
    in_grad = finish([(one.keep, one.got) for one in ins])

    return (
        result[None],
        grad_inputs[None],
        in_grad,
        out_grad,
        gate_up_grad,
        down_grad,
        gains[0],
        gains[1],
        gains[2],
        gains[3],
    )


def solution(mesh):
    placed = (
        P("wt", "seq", None),
        P(None, None, "wt"),
        P("wt", None),
        P(None, None, "wt"),
        P("wt", None),
        P(),
        P(),
        P(),
        P(),
        P("wt", "seq", None),
    )
    return jax.shard_map(
        on_device,
        mesh=mesh,
        in_specs=placed,
        out_specs=(
            P("wt", "seq", None),
            P("wt", "seq", None),
            P(None, "seq", "wt"),
            P("wt", "seq"),
            P(None, "seq", "wt"),
            P("wt", "seq"),
            P("wt"),
            P("wt"),
            P("wt"),
            P("wt"),
        ),
        check_vma=False,
    )
```

time: 1310 us -> 584 us (0.45)
  waiting for transfers between devices: 729 us -> 155 us
  Pallas kernels: 0 us -> 317 us
  local copies, waits for them, and re-layouts: 211 us -> 24.4 us
  matrix products: 172 us -> 0 us
  other arithmetic: 88.3 us -> 2.22 us
  blocking collectives: 54.5 us -> 0 us
  starting transfers between devices: 32.1 us -> 72.3 us
  between operations: 15.3 us -> 1.64 us
    reduce_scatter x8 -> x0, waiting for transfers between devices: 426 us -> none  [the longest x1 79.2 us: on_device(): lax.psum_scatter(gate_term.astype(jnp.bfloat16), 'seq', scatter_dimension...]
    pallas_call x0 -> x64, Pallas kernels: none -> 317 us  [the longest x36 223 us: call(): pl.pallas_call(body, grid=grid, in_specs=in_specs, out_specs=out_specs, s...]
    all_to_all x6 -> x0, waiting for transfers between devices: 215 us -> none  [the longest x1 44.5 us: on_device(): lax.all_to_all(drive_turned, 'seq', split_axis=1, concat_axis=2, tiled=True)]
    dot_general x20 -> x0, matrix products: 172 us -> none  [the longest x2 22.3 us: right_product(): lax.dot_general(left, right, (((1,), (1,)), ((), ())), preferred_element_...]
    ppermute x0 -> x62, waiting for transfers between devices: none -> 155 us  [the longest x56 155 us: swap(): return lax.ppermute(values, axis, [(i, i ^ bit) for i in range(size)])]
    all_gather x4 -> x0, waiting for transfers between devices: 87.7 us -> none  [the longest x1 36.5 us: on_device(): lax.all_gather(normed[None], 'wt', axis=0, tiled=True)]
    ppermute x0 -> x62, starting transfers between devices: none -> 72.3 us  [the longest x56 58.8 us: swap(): return lax.ppermute(values, axis, [(i, i ^ bit) for i in range(size)])]
    psum x3 -> x0, blocking collectives: 54.5 us -> none  [the longest x1 42.8 us: on_device(): lax.psum(jnp.stack([norm1_term, mixer_full, norm2_term, bound_full]), ('s...]
  transfers between devices with their start and end apart: 18 -> 62, of which waited for: 16 -> 24; matrix products, arithmetic and copies ran while one was open for 22% -> 1% of each run, Pallas kernels for 0% -> 47%
where the time goes in v2:
time: 584 us; the launch traced here: 573 us
  Pallas kernels  317 us (54%)
  waiting for transfers between devices  155 us (27%)
  starting transfers between devices  72.3 us (12%)
  local copies, waits for them, and re-layouts  24.4 us (4%)
    pallas_call x36, Pallas kernels, call(): pl.pallas_call(body, grid=grid, in_specs=in_specs, out_specs=out_specs, s...  223 us
    ppermute x56, waiting for transfers between devices, swap(): return lax.ppermute(values, axis, [(i, i ^ bit) for i in range(size)])  155 us
    pallas_call x18, Pallas kernels, call(): got = pl.pallas_call(body, grid_spec=spec, **settings)(blocks, *operands)  94.8 us
    ppermute x56, starting transfers between devices, swap(): return lax.ppermute(values, axis, [(i, i ^ bit) for i in range(size)])  58.8 us
    unnamed x111, local copies, waits for them, and re-layouts  21.2 us
    ppermute x6, starting transfers between devices, shift(): return lax.ppermute(values, axis, pairs)  13.5 us
  transfers between devices with their start and end apart: 62, of which 24 were waited for; matrix products, arithmetic and copies ran while one was open for 1% of the time, Pallas kernels for 47%

profile of v2, /device:TPU:0, one launch (start us, length us, event | category | flops | bytes accessed | tf_op | source)
XLA Modules:
  0.0 572.7 jit_solution(13356678968267748912)
XLA Ops:
  0.7 3.8 first_norm.1.refs_0_.refs_1_
  10.2 11.0 %project.2 = (f32[2,256,512]{2,1,0:T(8,128)}, f32[2,256,512]{2,1,0:T(8,128)}, f32[2,256,512]{2,1,0:T(8,128)}, f32[2,256,512]{2,1,0:T(8,128)}, f32[2,256,512]{2,1,0:T(8,128)}, /*index=5*/f32[2,2,512]{2,1,0:T(2,128)}) custom-call(bf16[256,2048]{1,0:T(8,128)(2,1)} %first_norm.1.refs_0_.refs_1_, bf16[256,2048]{1,0:T(8,128)(2,1)} %copy-done.1, ...), custom_call_target="tpu_custom_call" | custom-call | tf_op jit(solution)/shard_map/project/pallas_call | solution.py:70
  21.2 8.5 %hidden_grad.2.refs_1_.refs_3_ = f32[512,1408]{1,0:T(8,128)} custom-call(bf16[256,2048]{1,0:T(8,128)(2,1)} %bitcast.22, bf16[256,2048]{1,0:T(8,128)(2,1)} %collective-permute-done.2.refs_1_.refs_2_, bf16[1408,2048]{1,0:T(8,128)(2,1)} %refs_1_.3, f32[2,2,512]{2,1,0:T(2,128)} %get-tuple-element.108.refs_3_.refs_4_), custom_call_target="tpu_custom_call" | custom-call | tf_op jit(solution)/shard_map/hidden_grad/pallas_call | solution.py:70
  36.4 11.5 %project.3 = (f32[2,256,512]{2,1,0:T(8,128)}, f32[2,256,512]{2,1,0:T(8,128)}, f32[2,256,512]{2,1,0:T(8,128)}, f32[2,256,512]{2,1,0:T(8,128)}, f32[2,256,512]{2,1,0:T(8,128)}, /*index=5*/f32[2,4,512]{2,1,0:T(4,128)}) custom-call(bf16[256,2048]{1,0:T(8,128)(2,1)} %hold.10.refs_0_.refs_3_, bf16[256,2048]{1,0:T(8,128)(2,1)} %copy-done.2, ...), custom_call_target="tpu_custom_call" | custom-call | tf_op jit(solution)/shard_map/project/pallas_call | solution.py:70
  49.8 9.5 %collective-permute-done.5.refs_0_ = bf16[256,2048]{1,0:T(8,128)(2,1)S(1)} collective-permute-done((bf16[256,2048]{1,0:T(8,128)(2,1)}, bf16[256,2048]{1,0:T(8,128)(2,1)S(1)}, u32[]{:S(2)}, u32[]{:S(2)}) %collective-permute-start.5) | collective-permute-done | bytes 1048608 | tf_op jit(solution)/shard_map/ppermute | solution.py:18
  65.9 4.5 collective-permute-start.7
  75.8 5.7 mix.2
  82.1 5.6 mix.3
  95.0 8.5 %hidden_grad.3.refs_9_.refs_3_ = f32[512,1408]{1,0:T(8,128)} custom-call(bf16[256,2048]{1,0:T(8,128)(2,1)} %hold.12.refs_3_.refs_0_, bf16[256,2048]{1,0:T(8,128)(2,1)} %copy-done.13, bf16[1408,2048]{1,0:T(8,128)(2,1)} %refs_1_.3, bf16[256,2048]{1,0:T(8,128)(2,1)} %plus.4.refs_3_), custom_call_target="tpu_custom_call" | custom-call | tf_op jit(solution)/shard_map/hidden_grad/pallas_call | solution.py:70
  103.5 17.1 %collective-permute-done.13.refs_6_ = f32[256,128]{1,0:T(8,128)S(1)} collective-permute-done((f32[256,128]{1,0:T(8,128)S(1)}, f32[256,128]{1,0:T(8,128)S(1)}, u32[]{:S(2)}, u32[]{:S(2)}) %collective-permute-start.13) | collective-permute-done | bytes 131104 | tf_op jit(solution)/shard_map/ppermute | solution.py:18
  123.4 5.4 middle.1
  132.8 12.7 %feed.2 = (bf16[512,1408]{1,0:T(8,128)(2,1)}, bf16[512,1408]{1,0:T(8,128)(2,1)}, bf16[512,1408]{1,0:T(8,128)(2,1)}) custom-call(bf16[256,2048]{1,0:T(8,128)(2,1)} %get-tuple-element.122.refs_0_.refs_1_, bf16[256,2048]{1,0:T(8,128)(2,1)} %copy-done.9, bf16[2,2048,1408]{2,1,0:T(8,128)(2,1)} %refs_2_.17, f32[512,1408]{1,0:T(8,128)} %hidden_grad.2.refs_1_.refs_3_), custom_call_target="tpu_custom_call" | custom-call | tf_op jit(solution)/shard_map/feed/pallas_call | solution.py:70
  145.5 10.9 %feed_back.2 = (bf16[256,2048]{1,0:T(8,128)(2,1)}, bf16[256,2048]{1,0:T(8,128)(2,1)}) custom-call(bf16[512,1408]{1,0:T(8,128)(2,1)} %get-tuple-element.124.refs_0_.refs_5_, bf16[512,1408]{1,0:T(8,128)(2,1)} %get-tuple-element.125.refs_1_.refs_5_, bf16[2,2048,1408]{2,1,0:T(8,128)(2,1)} %refs_2_.17), custom_call_target="tpu_custom_call" | custom-call | tf_op jit(solution)/shard_map/feed_back/pallas_call | solution.py:70
  161.2 12.7 %feed.3 = (bf16[512,1408]{1,0:T(8,128)(2,1)}, bf16[512,1408]{1,0:T(8,128)(2,1)}, bf16[512,1408]{1,0:T(8,128)(2,1)}) custom-call(bf16[256,2048]{1,0:T(8,128)(2,1)} %hold.13.refs_0_.refs_3_, bf16[256,2048]{1,0:T(8,128)(2,1)} %copy-done.10, bf16[2,2048,1408]{2,1,0:T(8,128)(2,1)} %refs_2_.17, f32[512,1408]{1,0:T(8,128)} %hidden_grad.3.refs_9_.refs_3_), custom_call_target="tpu_custom_call" | custom-call | tf_op jit(solution)/shard_map/feed/pallas_call | solution.py:70
  173.9 11.0 %feed_back.3 = (bf16[256,2048]{1,0:T(8,128)(2,1)}, bf16[256,2048]{1,0:T(8,128)(2,1)}) custom-call(bf16[512,1408]{1,0:T(8,128)(2,1)} %get-tuple-element.129.refs_0_.refs_6_, bf16[512,1408]{1,0:T(8,128)(2,1)} %get-tuple-element.128.refs_1_.refs_6_, bf16[2,2048,1408]{2,1,0:T(8,128)(2,1)} %refs_2_.17), custom_call_target="tpu_custom_call" | custom-call | tf_op jit(solution)/shard_map/feed_back/pallas_call | solution.py:70
  185.5 7.4 %product.7.refs_2_ = bf16[1024,1408]{1,0:T(8,128)(2,1)} custom-call(s32[1]{0:T(128)} %bitcast.3.refs_0_, bf16[256,2048]{1,0:T(8,128)(2,1)} %get-tuple-element.122.refs_0_.refs_1_, bf16[256,2048]{1,0:T(8,128)(2,1)} %copy-done.9, bf16[256,2048]{1,0:T(8,128)(2,1)} %hold.13.refs_0_.refs_3_, bf16[256,2048]{1,0:T(8,128)(2,1)} %copy-done.10, ...), custom_call_target="tpu_custom_call" | custom-call | tf_op jit(solution)/shard_map/product/pallas_call | solution.py:81
  200.6 7.5 %product.8.refs_7_ = bf16[1024,1408]{1,0:T(8,128)(2,1)} custom-call(s32[1]{0:T(128)} %bitcast.3.refs_0_, bf16[256,2048]{1,0:T(8,128)(2,1)} %bitcast.23, bf16[256,2048]{1,0:T(8,128)(2,1)} %collective-permute-done.2.refs_1_.refs_2_, bf16[256,2048]{1,0:T(8,128)(2,1)} %hold.12.refs_3_.refs_0_, bf16[256,2048]{1,0:T(8,128)(2,1)} %copy-done.13, ...), custom_call_target="tpu_custom_call" | custom-call | tf_op jit(solution)/shard_map/product/pallas_call | solution.py:81
  208.1 7.5 %product.9.refs_2_.refs_0_ = bf16[1024,1408]{1,0:T(8,128)(2,1)} custom-call(s32[1]{0:T(128)} %bitcast.3.refs_0_, bf16[256,2048]{1,0:T(8,128)(2,1)} %get-tuple-element.122.refs_0_.refs_1_, bf16[256,2048]{1,0:T(8,128)(2,1)} %copy-done.9, bf16[256,2048]{1,0:T(8,128)(2,1)} %hold.13.refs_0_.refs_3_, bf16[256,2048]{1,0:T(8,128)(2,1)} %copy-done.10, ...), custom_call_target="tpu_custom_call" | custom-call | tf_op jit(solution)/shard_map/product/pallas_call | solution.py:81
  215.5 7.2 %feed_out.2 = (bf16[256,2048]{1,0:T(8,128)(2,1)}, bf16[256,2048]{1,0:T(8,128)(2,1)}) custom-call(bf16[512,1408]{1,0:T(8,128)(2,1)} %get-tuple-element.127.refs_6_.refs_0_, bf16[1408,2048]{1,0:T(8,128)(2,1)} %refs_1_.3, bf16[1024,1408]{1,0:T(8,128)(2,1)} %product.9.refs_2_.refs_0_), custom_call_target="tpu_custom_call" | custom-call | tf_op jit(solution)/shard_map/feed_out/pallas_call | solution.py:70
  224.1 6.5 %turn.1 = (f32[256,2048]{1,0:T(8,128)}, f32[1,2048]{1,0:T(1,128)}, bf16[272,2048]{1,0:T(8,128)(2,1)}) custom-call(bf16[256,2048]{1,0:T(8,128)(2,1)} %bitcast.24, bf16[256,2048]{1,0:T(8,128)(2,1)} %get-tuple-element.126.refs_1_, bf16[256,2048]{1,0:T(8,128)(2,1)} %copy-done.21, bf16[256,2048]{1,0:T(8,128)(2,1)} %copy-done.22, ...), custom_call_target="tpu_custom_call" | custom-call | tf_op jit(solution)/shard_map/turn/pallas_call | solution.py:70
  234.7 9.2 %back_local.2 = (bf16[2,256,512]{2,1,0:T(8,128)(2,1)}, bf16[2,256,512]{2,1,0:T(8,128)(2,1)}, f32[2,256,512]{2,1,0:T(8,128)}, f32[2,256,512]{2,1,0:T(8,128)}, f32[2,2,512]{2,1,0:T(2,128)}, /*index=5*/f32[1,512]{1,0:T(1,128)}) custom-call(bf16[272,2048]{1,0:T(8,128)(2,1)} %get-tuple-element.137.refs_0_.refs_1_, bf16[272,2048]{1,0:T(8,128)(2,1)} %copy-done.11, ...), custom_call_target="tpu_custom_call" | custom-call | tf_op jit(solution)/shard_map/back_local/pallas_call | solution.py:70
  248.5 7.2 %feed_out.3 = (bf16[256,2048]{1,0:T(8,128)(2,1)}, bf16[256,2048]{1,0:T(8,128)(2,1)}) custom-call(bf16[512,1408]{1,0:T(8,128)(2,1)} %get-tuple-element.123.refs_5_.refs_0_, bf16[1408,2048]{1,0:T(8,128)(2,1)} %refs_1_.3, bf16[256,2048]{1,0:T(8,128)(2,1)} %plus.6.refs_2_.refs_0_), custom_call_target="tpu_custom_call" | custom-call | tf_op jit(solution)/shard_map/feed_out/pallas_call | solution.py:70
  258.9 4.9 collective-permute-done.28.refs_7_
  263.8 8.5 %product_add.7 = (bf16[512,1408]{1,0:T(8,128)(2,1)}, bf16[512,1408]{1,0:T(8,128)(2,1)}) custom-call(s32[1]{0:T(128)} %bitcast.3.refs_0_, bf16[256,2048]{1,0:T(8,128)(2,1)} %get-tuple-element.122.refs_0_.refs_1_, bf16[256,2048]{1,0:T(8,128)(2,1)} %copy-done.9, bf16[256,2048]{1,0:T(8,128)(2,1)} %hold.13.refs_0_.refs_3_, bf16[256,2048]{1,0:T(8,128)(2,1)} %copy-done.10, ...), custom_call_target="tpu_custom_call" | custom-call | tf_op jit(solution)/shard_map/product_add/pallas_call | solution.py:81
  273.2 9.2 %back_local.3 = (bf16[2,256,512]{2,1,0:T(8,128)(2,1)}, bf16[2,256,512]{2,1,0:T(8,128)(2,1)}, f32[2,256,512]{2,1,0:T(8,128)}, f32[2,256,512]{2,1,0:T(8,128)}, f32[2,4,512]{2,1,0:T(4,128)}, /*index=5*/f32[1,512]{1,0:T(1,128)}) custom-call(bf16[272,2048]{1,0:T(8,128)(2,1)} %hold.14.refs_1_.refs_8_.refs_0_.refs_3_, bf16[272,2048]{1,0:T(8,128)(2,1)} %copy-done.12, ...), custom_call_target="tpu_custom_call" | custom-call | tf_op jit(solution)/shard_map/back_local/pallas_call | solution.py:70
  292.3 8.6 %product_add.8 = (bf16[512,1408]{1,0:T(8,128)(2,1)}, bf16[512,1408]{1,0:T(8,128)(2,1)}) custom-call(s32[1]{0:T(128)} %bitcast.3.refs_0_, bf16[256,2048]{1,0:T(8,128)(2,1)} %bitcast.25, bf16[256,2048]{1,0:T(8,128)(2,1)} %collective-permute-done.2.refs_1_.refs_2_, bf16[256,2048]{1,0:T(8,128)(2,1)} %hold.12.refs_3_.refs_0_, bf16[256,2048]{1,0:T(8,128)(2,1)} %copy-done.13, ...), custom_call_target="tpu_custom_call" | custom-call | tf_op jit(solution)/shard_map/product_add/pallas_call | solution.py:81
  304.4 10.3 %back_mix.2 = (bf16[2,256,512]{2,1,0:T(8,128)(2,1)}, bf16[2,256,512]{2,1,0:T(8,128)(2,1)}, bf16[256,2048]{1,0:T(8,128)(2,1)}, bf16[256,2048]{1,0:T(8,128)(2,1)}, f32[2,1,512]{2,1,0:T(1,128)}) custom-call(f32[2,256,512]{2,1,0:T(8,128)} %get-tuple-element.155.refs_0_, f32[2,256,512]{2,1,0:T(8,128)} %get-tuple-element.156.refs_1_, ...), custom_call_target="tpu_custom_call" | custom-call | tf_op jit(solution)/shard_map/back_mix/pallas_call | solution.py:70
  321.5 10.3 %back_mix.3 = (bf16[2,256,512]{2,1,0:T(8,128)(2,1)}, bf16[2,256,512]{2,1,0:T(8,128)(2,1)}, bf16[256,2048]{1,0:T(8,128)(2,1)}, bf16[256,2048]{1,0:T(8,128)(2,1)}, f32[2,1,512]{2,1,0:T(1,128)}) custom-call(f32[2,256,512]{2,1,0:T(8,128)} %get-tuple-element.151.refs_0_, f32[2,256,512]{2,1,0:T(8,128)} %get-tuple-element.152.refs_1_, ...), custom_call_target="tpu_custom_call" | custom-call | tf_op jit(solution)/shard_map/back_mix/pallas_call | solution.py:70
  331.9 17.5 %collective-permute-done.34.refs_1_ = bf16[512,1408]{1,0:T(8,128)(2,1)} collective-permute-done((bf16[512,1408]{1,0:T(8,128)(2,1)}, bf16[512,1408]{1,0:T(8,128)(2,1)}, u32[]{:S(2)}, u32[]{:S(2)}) %collective-permute-start.34) | collective-permute-done | bytes 1441824 | tf_op jit(solution)/shard_map/ppermute | solution.py:18
  349.4 4.1 collective-permute-start.41
  357.5 4.9 product.10.refs_7_
  367.1 5.0 product.11.refs_8_
  372.1 8.6 %product_add.9 = (bf16[512,1408]{1,0:T(8,128)(2,1)}, bf16[512,1408]{1,0:T(8,128)(2,1)}) custom-call(s32[1]{0:T(128)} %bitcast.3.refs_0_, bf16[256,2048]{1,0:T(8,128)(2,1)} %get-tuple-element.122.refs_0_.refs_1_, bf16[256,2048]{1,0:T(8,128)(2,1)} %copy-done.9, bf16[256,2048]{1,0:T(8,128)(2,1)} %hold.13.refs_0_.refs_3_, bf16[256,2048]{1,0:T(8,128)(2,1)} %copy-done.10, ...), custom_call_target="tpu_custom_call" | custom-call | tf_op jit(solution)/shard_map/product_add/pallas_call | solution.py:81
  384.2 5.0 product.12.refs_7_
  389.7 5.0 product.13.refs_8_
  396.2 5.4 product_add.10
  401.6 4.3 result.1.refs_6_
  405.9 5.4 last.1
  411.3 5.2 collective-permute-done.41.refs_1_
  426.2 34.5 %collective-permute-done.46.refs_1_ = bf16[512,1408]{1,0:T(8,128)(2,1)S(1)} collective-permute-done((bf16[512,1408]{1,0:T(8,128)(2,1)}, bf16[512,1408]{1,0:T(8,128)(2,1)S(1)}, u32[]{:S(2)}, u32[]{:S(2)}) %collective-permute-start.46) | collective-permute-done | bytes 1441824 | tf_op jit(solution)/shard_map/ppermute | solution.py:18
  464.4 5.4 product_add.11
  482.5 5.3 product_add.12
  488.0 5.4 product_add.13
  496.0 13.2 %collective-permute-done.54.refs_3_ = bf16[256,1408]{1,0:T(8,128)(2,1)S(1)} collective-permute-done((bf16[256,1408]{1,0:T(8,128)(2,1)}, bf16[256,1408]{1,0:T(8,128)(2,1)S(1)}, u32[]{:S(2)}, u32[]{:S(2)}) %collective-permute-start.54) | collective-permute-done | bytes 720928 | tf_op jit(solution)/shard_map/ppermute | solution.py:18
  510.1 4.2 finish.6.refs_1_
  518.9 4.2 collective-permute-start.60
  528.1 10.3 %collective-permute-done.50.refs_1_ = bf16[512,512]{1,0:T(8,128)(2,1)} collective-permute-done((bf16[512,512]{1,0:T(8,128)(2,1)}, bf16[512,512]{1,0:T(8,128)(2,1)}, u32[]{:S(2)}, u32[]{:S(2)}) %collective-permute-start.50) | collective-permute-done | bytes 524320 | tf_op jit(solution)/shard_map/ppermute | solution.py:18
  549.4 17.8 %collective-permute-done.61 = f32[4,512]{1,0:T(4,128)S(1)} collective-permute-done((f32[4,512]{1,0:T(4,128)S(1)}, f32[4,512]{1,0:T(4,128)S(1)}, u32[]{:S(2)}, u32[]{:S(2)}) %collective-permute-start.61) | collective-permute-done | bytes 8224 | tf_op jit(solution)/shard_map/ppermute | solution.py:18
  (265 shorter events, 158.2 us)
Async XLA Ops:
  4.9 16.3 %collective-permute-start.2 = (bf16[256,2048]{1,0:T(8,128)(2,1)S(1)}, bf16[256,2048]{1,0:T(8,128)(2,1)}, u32[]{:S(2)}, u32[]{:S(2)}) collective-permute-start(bf16[256,2048]{1,0:T(8,128)(2,1)S(1)} %bitcast.26), channel_id=1, source_target_pairs={{0,1},{1,0},{2,3},{3,2},{4,5},{5,4},{6,7},{7,6},{8,9},{9,8},{10,11... | collective-permute-start | bytes 3145736 | tf_op jit(solution)/shard_map/ppermute | solution.py:18
  4.9 26.5 %collective-permute-start.1 = (bf16[256,2048]{1,0:T(8,128)(2,1)}, bf16[256,2048]{1,0:T(8,128)(2,1)S(1)}, u32[]{:S(2)}, u32[]{:S(2)}) collective-permute-start(bf16[256,2048]{1,0:T(8,128)(2,1)} %first_norm.1.refs_0_.refs_1_), channel_id=1, source_target_pairs={{0,2},{1,3},{2,0},{3,1},{4,6},{5,7},{6,4},{7,5},{8,10},{9,11},{10,... | collective-permute-start | bytes 3145736 | tf_op jit(solution)/shard_map/ppermute | solution.py:18
  33.5 25.8 %collective-permute-start.5 = (bf16[256,2048]{1,0:T(8,128)(2,1)}, bf16[256,2048]{1,0:T(8,128)(2,1)S(1)}, u32[]{:S(2)}, u32[]{:S(2)}) collective-permute-start(bf16[256,2048]{1,0:T(8,128)(2,1)} %hold.11), channel_id=1, source_target_pairs={{0,2},{1,3},{2,0},{3,1},{4,6},{5,7},{6,4},{7,5},{8,10},{9,11},{10,... | collective-permute-start | bytes 3145736 | tf_op jit(solution)/shard_map/ppermute | solution.py:18
  47.9 12.3 %collective-permute-start.4 = (f32[2,4,512]{2,1,0:T(4,128)}, f32[2,4,512]{2,1,0:T(4,128)S(1)}, u32[]{:S(2)}, u32[]{:S(2)}) collective-permute-start(f32[2,4,512]{2,1,0:T(4,128)} %get-tuple-element.109.refs_1_), channel_id=1, source_target_pairs={{0,4},{4,0},{8,12},{12,8},{16,20},{20,16},{24,28},{28,24},{1,5},{5... | collective-permute-start | bytes 49160 | tf_op jit(solution)/shard_map/ppermute | solution.py:18
  62.2 11.0 %collective-permute-start.6 = (f32[2,4,512]{2,1,0:T(4,128)}, f32[2,4,512]{2,1,0:T(4,128)S(1)}, u32[]{:S(2)}, u32[]{:S(2)}) collective-permute-start(f32[2,4,512]{2,1,0:T(4,128)} %pair.2), channel_id=1, source_target_pairs={{0,8},{4,12},{8,16},{12,20},{16,24},{20,28},{1,9},{5,13},{9,17},{1... | collective-permute-start | bytes 49160 | tf_op jit(solution)/shard_map/ppermute | solution.py:24
  81.6 12.1 %collective-permute-start.15 = (bf16[256,2048]{1,0:T(8,128)(2,1)S(1)}, bf16[256,2048]{1,0:T(8,128)(2,1)S(1)}, u32[]{:S(2)}, u32[]{:S(2)}) collective-permute-start(bf16[256,2048]{1,0:T(8,128)(2,1)S(1)} %copy-done.6), channel_id=1, source_target_pairs={{0,1},{1,0},{2,3},{3,2},{4,5},{5,4},{6,7},{7,6},{8,9},{9,8},{10,11... | collective-permute-start | bytes 3145736 | tf_op jit(solution)/shard_map/ppermute | solution.py:18
  87.7 34.7 %collective-permute-start.9 = (bf16[256,2048]{1,0:T(8,128)(2,1)}, bf16[256,2048]{1,0:T(8,128)(2,1)S(1)}, u32[]{:S(2)}, u32[]{:S(2)}) collective-permute-start(bf16[256,2048]{1,0:T(8,128)(2,1)} %get-tuple-element.115), channel_id=1, source_target_pairs={{0,1},{1,0},{2,3},{3,2},{4,5},{5,4},{6,7},{7,6},{8,9},{9,8},{10,11... | collective-permute-start | bytes 3145736 | tf_op jit(solution)/shard_map/ppermute | solution.py:18
  91.6 30.9 %collective-permute-start.11 = (bf16[256,2048]{1,0:T(8,128)(2,1)}, bf16[256,2048]{1,0:T(8,128)(2,1)}, u32[]{:S(2)}, u32[]{:S(2)}) collective-permute-start(bf16[256,2048]{1,0:T(8,128)(2,1)} %plus.4.refs_3_), channel_id=1, source_target_pairs={{0,2},{1,3},{2,0},{3,1},{4,6},{5,7},{6,4},{7,5},{8,10},{9,11},{10,... | collective-permute-start | bytes 3145736 | tf_op jit(solution)/shard_map/ppermute | solution.py:18
  93.1 10.4 %collective-permute-start.12 = (f32[256,128]{1,0:T(8,128)S(1)}, f32[256,128]{1,0:T(8,128)S(1)}, u32[]{:S(2)}, u32[]{:S(2)}) collective-permute-start(f32[256,128]{1,0:T(8,128)S(1)} %copy-done.54), channel_id=1, source_target_pairs={{0,1},{1,0},{2,3},{3,2},{4,5},{5,4},{6,7},{7,6},{8,9},{9,8},{10,11... | collective-permute-start | bytes 393224 | tf_op jit(solution)/shard_map/ppermute | solution.py:18
  93.2 27.3 %collective-permute-start.13 = (f32[256,128]{1,0:T(8,128)S(1)}, f32[256,128]{1,0:T(8,128)S(1)}, u32[]{:S(2)}, u32[]{:S(2)}) collective-permute-start(f32[256,128]{1,0:T(8,128)S(1)} %copy-done.53), channel_id=1, source_target_pairs={{0,2},{1,3},{2,0},{3,1},{4,6},{5,7},{6,4},{7,5},{8,10},{9,11},{10,... | collective-permute-start | bytes 393224 | tf_op jit(solution)/shard_map/ppermute | solution.py:18
  93.8 28.7 %collective-permute-start.14 = (f32[256,128]{1,0:T(8,128)S(1)}, f32[256,128]{1,0:T(8,128)S(1)}, u32[]{:S(2)}, u32[]{:S(2)}) collective-permute-start(f32[256,128]{1,0:T(8,128)S(1)} %copy-done.52), channel_id=1, source_target_pairs={{0,3},{1,2},{2,1},{3,0},{4,7},{5,6},{6,5},{7,4},{8,11},{9,10},{10,... | collective-permute-start | bytes 393224 | tf_op jit(solution)/shard_map/ppermute | solution.py:18
  129.2 27.1 %collective-permute-start.17 = (bf16[256,2048]{1,0:T(8,128)(2,1)}, bf16[256,2048]{1,0:T(8,128)(2,1)S(1)}, u32[]{:S(2)}, u32[]{:S(2)}) collective-permute-start(bf16[256,2048]{1,0:T(8,128)(2,1)} %get-tuple-element.122.refs_0_.refs_1_), channel_id=1, source_target_pairs={{0,2},{1,3},{2,0},{3,1},{4,6},{5,7},{6,4},{7,5},{8,10},{9,11},{10,... | collective-permute-start | bytes 3145736 | tf_op jit(solution)/shard_map/ppermute | solution.py:18
  185.2 37.5 %collective-permute-start.21 = (bf16[256,2048]{1,0:T(8,128)(2,1)S(1)}, bf16[256,2048]{1,0:T(8,128)(2,1)S(1)}, u32[]{:S(2)}, u32[]{:S(2)}) collective-permute-start(bf16[256,2048]{1,0:T(8,128)(2,1)S(1)} %copy-done.51), channel_id=1, source_target_pairs={{0,1},{1,0},{2,3},{3,2},{4,5},{5,4},{6,7},{7,6},{8,9},{9,8},{10,11... | collective-permute-start | bytes 3145736 | tf_op jit(solution)/shard_map/ppermute | solution.py:18
  197.6 25.6 %collective-permute-start.22 = (bf16[256,2048]{1,0:T(8,128)(2,1)}, bf16[256,2048]{1,0:T(8,128)(2,1)S(1)}, u32[]{:S(2)}, u32[]{:S(2)}) collective-permute-start(bf16[256,2048]{1,0:T(8,128)(2,1)} %plus.5.refs_7_.refs_8_), channel_id=1, source_target_pairs={{0,2},{1,3},{2,0},{3,1},{4,6},{5,7},{6,4},{7,5},{8,10},{9,11},{10,... | collective-permute-start | bytes 3145736 | tf_op jit(solution)/shard_map/ppermute | solution.py:18
  199.0 64.7 %collective-permute-start.28 = (bf16[1024,1408]{1,0:T(8,128)(2,1)}, bf16[1024,1408]{1,0:T(8,128)(2,1)}, u32[]{:S(2)}, u32[]{:S(2)}) collective-permute-start(bf16[1024,1408]{1,0:T(8,128)(2,1)} %product.7.refs_2_), channel_id=1, source_target_pairs={{0,4},{4,0},{8,12},{12,8},{16,20},{20,16},{24,28},{28,24},{1,5},{5... | collective-permute-start | bytes 8650760 | tf_op jit(solution)/shard_map/ppermute | solution.py:18
  208.0 84.2 %collective-permute-start.33 = (bf16[1024,1408]{1,0:T(8,128)(2,1)}, bf16[1024,1408]{1,0:T(8,128)(2,1)}, u32[]{:S(2)}, u32[]{:S(2)}) collective-permute-start(bf16[1024,1408]{1,0:T(8,128)(2,1)} %product.8.refs_7_), channel_id=1, source_target_pairs={{0,8},{4,12},{8,0},{12,4},{16,24},{20,28},{24,16},{28,20},{1,9},{5... | collective-permute-start | bytes 8650760 | tf_op jit(solution)/shard_map/ppermute | solution.py:18
  230.7 27.2 %collective-permute-start.25 = (bf16[272,2048]{1,0:T(8,128)(2,1)}, bf16[272,2048]{1,0:T(8,128)(2,1)S(1)}, u32[]{:S(2)}, u32[]{:S(2)}) collective-permute-start(bf16[272,2048]{1,0:T(8,128)(2,1)} %get-tuple-element.137.refs_0_.refs_1_), channel_id=1, source_target_pairs={{0,2},{1,3},{2,0},{3,1},{4,6},{5,7},{6,4},{7,5},{8,10},{9,11},{10,... | collective-permute-start | bytes 3342344 | tf_op jit(solution)/shard_map/ppermute | solution.py:18
  232.3 11.7 %collective-permute-start.20 = (bf16[256,2048]{1,0:T(8,128)(2,1)}, bf16[256,2048]{1,0:T(8,128)(2,1)S(1)}, u32[]{:S(2)}, u32[]{:S(2)}) collective-permute-start(bf16[256,2048]{1,0:T(8,128)(2,1)} %get-tuple-element.133), channel_id=1, source_target_pairs={{0,1},{1,0},{2,3},{3,2},{4,5},{5,4},{6,7},{7,6},{8,9},{9,8},{10,11... | collective-permute-start | bytes 3145736 | tf_op jit(solution)/shard_map/ppermute | solution.py:18
  258.9 13.3 %collective-permute-start.27 = (bf16[272,2048]{1,0:T(8,128)(2,1)}, bf16[272,2048]{1,0:T(8,128)(2,1)S(1)}, u32[]{:S(2)}, u32[]{:S(2)}) collective-permute-start(bf16[272,2048]{1,0:T(8,128)(2,1)} %hold.14.refs_1_.refs_8_.refs_0_.refs_3_), channel_id=1, source_target_pairs={{0,1},{1,0},{2,3},{3,2},{4,5},{5,4},{6,7},{7,6},{8,9},{9,8},{10,11... | collective-permute-start | bytes 3342344 | tf_op jit(solution)/shard_map/ppermute | solution.py:18
  288.4 12.5 %collective-permute-start.30 = (f32[2,4,512]{2,1,0:T(4,128)}, f32[2,4,512]{2,1,0:T(4,128)S(1)}, u32[]{:S(2)}, u32[]{:S(2)}) collective-permute-start(f32[2,4,512]{2,1,0:T(4,128)} %pair.3.refs_8_), channel_id=1, source_target_pairs={{8,0},{12,4},{16,8},{20,12},{24,16},{28,20},{9,1},{13,5},{17,9},{2... | collective-permute-start | bytes 49160 | tf_op jit(solution)/shard_map/ppermute | solution.py:24
  289.7 11.2 %collective-permute-start.31 = (f32[2,4,512]{2,1,0:T(4,128)}, f32[2,4,512]{2,1,0:T(4,128)S(1)}, u32[]{:S(2)}, u32[]{:S(2)}) collective-permute-start(f32[2,4,512]{2,1,0:T(4,128)} %pair.3.refs_8_), channel_id=1, source_target_pairs={{16,0},{20,4},{24,8},{28,12},{17,1},{21,5},{25,9},{29,13},{18,2},{... | collective-permute-start | bytes 49160 | tf_op jit(solution)/shard_map/ppermute | solution.py:24
  291.0 10.0 %collective-permute-start.32 = (f32[2,4,512]{2,1,0:T(4,128)}, f32[2,4,512]{2,1,0:T(4,128)S(1)}, u32[]{:S(2)}, u32[]{:S(2)}) collective-permute-start(f32[2,4,512]{2,1,0:T(4,128)} %pair.3.refs_8_), channel_id=1, source_target_pairs={{24,0},{28,4},{25,1},{29,5},{26,2},{30,6},{27,3},{31,7}} | collective-permute-start | bytes 49160 | tf_op jit(solution)/shard_map/ppermute | solution.py:24
  302.9 62.6 %collective-permute-start.37 = (bf16[1024,1408]{1,0:T(8,128)(2,1)}, bf16[1024,1408]{1,0:T(8,128)(2,1)S(1)}, u32[]{:S(2)}, u32[]{:S(2)}) collective-permute-start(bf16[1024,1408]{1,0:T(8,128)(2,1)} %hold.17), channel_id=1, source_target_pairs={{0,4},{4,0},{8,12},{12,8},{16,20},{20,16},{24,28},{28,24},{1,5},{5... | collective-permute-start | bytes 8650760 | tf_op jit(solution)/shard_map/ppermute | solution.py:18
  314.9 34.6 %collective-permute-start.34 = (bf16[512,1408]{1,0:T(8,128)(2,1)}, bf16[512,1408]{1,0:T(8,128)(2,1)}, u32[]{:S(2)}, u32[]{:S(2)}) collective-permute-start(bf16[512,1408]{1,0:T(8,128)(2,1)} %hold.16), channel_id=1, source_target_pairs={{0,8},{4,12},{8,0},{12,4},{16,24},{20,28},{24,16},{28,20},{1,9},{5... | collective-permute-start | bytes 4325384 | tf_op jit(solution)/shard_map/ppermute | solution.py:18
  316.9 40.0 %collective-permute-start.26 = (bf16[256,2048]{1,0:T(8,128)(2,1)}, bf16[256,2048]{1,0:T(8,128)(2,1)}, u32[]{:S(2)}, u32[]{:S(2)}) collective-permute-start(bf16[256,2048]{1,0:T(8,128)(2,1)} %hold.15), channel_id=1, source_target_pairs={{0,2},{1,3},{2,0},{3,1},{4,6},{5,7},{6,4},{7,5},{8,10},{9,11},{10,... | collective-permute-start | bytes 3145736 | tf_op jit(solution)/shard_map/ppermute | solution.py:18
  317.5 63.2 %collective-permute-start.24 = (bf16[256,2048]{1,0:T(8,128)(2,1)}, bf16[256,2048]{1,0:T(8,128)(2,1)}, u32[]{:S(2)}, u32[]{:S(2)}) collective-permute-start(bf16[256,2048]{1,0:T(8,128)(2,1)} %get-tuple-element.142), channel_id=1, source_target_pairs={{0,1},{1,0},{2,3},{3,2},{4,5},{5,4},{6,7},{7,6},{8,9},{9,8},{10,11... | collective-permute-start | bytes 3145736 | tf_op jit(solution)/shard_map/ppermute | solution.py:18
  331.7 50.9 %collective-permute-start.38 = (bf16[256,2048]{1,0:T(8,128)(2,1)}, bf16[256,2048]{1,0:T(8,128)(2,1)}, u32[]{:S(2)}, u32[]{:S(2)}) collective-permute-start(bf16[256,2048]{1,0:T(8,128)(2,1)} %get-tuple-element.169), channel_id=1, source_target_pairs={{0,1},{1,0},{2,3},{3,2},{4,5},{5,4},{6,7},{7,6},{8,9},{9,8},{10,11... | collective-permute-start | bytes 3145736 | tf_op jit(solution)/shard_map/ppermute | solution.py:18
  349.4 67.0 %collective-permute-start.41 = (bf16[512,1408]{1,0:T(8,128)(2,1)}, bf16[512,1408]{1,0:T(8,128)(2,1)}, u32[]{:S(2)}, u32[]{:S(2)}) collective-permute-start(bf16[512,1408]{1,0:T(8,128)(2,1)} %hold.18), channel_id=1, source_target_pairs={{0,16},{4,20},{8,24},{12,28},{16,0},{20,4},{24,8},{28,12},{1,17},{... | collective-permute-start | bytes 4325384 | tf_op jit(solution)/shard_map/ppermute | solution.py:18
  356.9 32.2 %collective-permute-start.39 = (bf16[256,2048]{1,0:T(8,128)(2,1)S(1)}, bf16[256,2048]{1,0:T(8,128)(2,1)}, u32[]{:S(2)}, u32[]{:S(2)}) collective-permute-start(bf16[256,2048]{1,0:T(8,128)(2,1)S(1)} %copy-done.14), channel_id=1, source_target_pairs={{0,2},{1,3},{2,0},{3,1},{4,6},{5,7},{6,4},{7,5},{8,10},{9,11},{10,... | collective-permute-start | bytes 3145736 | tf_op jit(solution)/shard_map/ppermute | solution.py:18
  365.5 29.1 %collective-permute-start.36 = (bf16[1024,512]{1,0:T(8,128)(2,1)}, bf16[1024,512]{1,0:T(8,128)(2,1)}, u32[]{:S(2)}, u32[]{:S(2)}) collective-permute-start(bf16[1024,512]{1,0:T(8,128)(2,1)} %product.10.refs_7_), channel_id=1, source_target_pairs={{0,4},{4,0},{8,12},{12,8},{16,20},{20,16},{24,28},{28,24},{1,5},{5... | collective-permute-start | bytes 3145736 | tf_op jit(solution)/shard_map/ppermute | solution.py:18
  380.6 80.0 %collective-permute-start.46 = (bf16[512,1408]{1,0:T(8,128)(2,1)}, bf16[512,1408]{1,0:T(8,128)(2,1)S(1)}, u32[]{:S(2)}, u32[]{:S(2)}) collective-permute-start(bf16[512,1408]{1,0:T(8,128)(2,1)} %get-tuple-element.167.refs_7_), channel_id=1, source_target_pairs={{0,8},{4,12},{8,0},{12,4},{16,24},{20,28},{24,16},{28,20},{1,9},{5... | collective-permute-start | bytes 4325384 | tf_op jit(solution)/shard_map/ppermute | solution.py:18
  382.7 35.2 %collective-permute-start.40 = (bf16[1024,512]{1,0:T(8,128)(2,1)S(1)}, bf16[1024,512]{1,0:T(8,128)(2,1)}, u32[]{:S(2)}, u32[]{:S(2)}) collective-permute-start(bf16[1024,512]{1,0:T(8,128)(2,1)S(1)} %copy-done.15), channel_id=1, source_target_pairs={{0,4},{4,0},{8,12},{12,8},{16,20},{20,16},{24,28},{28,24},{1,5},{5... | collective-permute-start | bytes 3145736 | tf_op jit(solution)/shard_map/ppermute | solution.py:18
  389.1 91.0 %collective-permute-start.44 = (bf16[1024,512]{1,0:T(8,128)(2,1)}, bf16[1024,512]{1,0:T(8,128)(2,1)}, u32[]{:S(2)}, u32[]{:S(2)}) collective-permute-start(bf16[1024,512]{1,0:T(8,128)(2,1)} %product.12.refs_7_), channel_id=1, source_target_pairs={{0,4},{4,0},{8,12},{12,8},{16,20},{20,16},{24,28},{28,24},{1,5},{5... | collective-permute-start | bytes 3145736 | tf_op jit(solution)/shard_map/ppermute | solution.py:18
  394.6 93.2 %collective-permute-start.43 = (bf16[1024,512]{1,0:T(8,128)(2,1)}, bf16[1024,512]{1,0:T(8,128)(2,1)}, u32[]{:S(2)}, u32[]{:S(2)}) collective-permute-start(bf16[1024,512]{1,0:T(8,128)(2,1)} %product.13.refs_8_), channel_id=1, source_target_pairs={{0,4},{4,0},{8,12},{12,8},{16,20},{20,16},{24,28},{28,24},{1,5},{5... | collective-permute-start | bytes 3145736 | tf_op jit(solution)/shard_map/ppermute | solution.py:18
  416.5 60.7 %collective-permute-start.45 = (bf16[512,512]{1,0:T(8,128)(2,1)}, bf16[512,512]{1,0:T(8,128)(2,1)S(1)}, u32[]{:S(2)}, u32[]{:S(2)}) collective-permute-start(bf16[512,512]{1,0:T(8,128)(2,1)} %get-tuple-element.168.refs_4_), channel_id=1, source_target_pairs={{0,8},{4,12},{8,0},{12,4},{16,24},{20,28},{24,16},{28,20},{1,9},{5... | collective-permute-start | bytes 1572872 | tf_op jit(solution)/shard_map/ppermute | solution.py:18
  422.8 70.6 %collective-permute-start.53 = (bf16[256,1408]{1,0:T(8,128)(2,1)}, bf16[256,1408]{1,0:T(8,128)(2,1)}, u32[]{:S(2)}, u32[]{:S(2)}) collective-permute-start(bf16[256,1408]{1,0:T(8,128)(2,1)} %get-tuple-element.162.refs_7_), channel_id=1, source_target_pairs={{0,16},{4,20},{8,24},{12,28},{16,0},{20,4},{24,8},{28,12},{1,17},{... | collective-permute-start | bytes 2162696 | tf_op jit(solution)/shard_map/ppermute | solution.py:18
  460.7 12.7 %collective-permute-start.58 = (f32[2,512]{1,0:T(2,128)S(1)}, f32[2,512]{1,0:T(2,128)S(1)}, u32[]{:S(2)}, u32[]{:S(2)}) collective-permute-start(f32[2,512]{1,0:T(2,128)S(1)} %get-tuple-element.202), channel_id=1, source_target_pairs={{0,3},{1,2},{2,1},{3,0},{4,7},{5,6},{6,5},{7,4},{8,11},{9,10},{10,... | collective-permute-start | bytes 12296 | tf_op jit(solution)/shard_map/ppermute | solution.py:18
  473.4 35.9 %collective-permute-start.54 = (bf16[256,1408]{1,0:T(8,128)(2,1)}, bf16[256,1408]{1,0:T(8,128)(2,1)S(1)}, u32[]{:S(2)}, u32[]{:S(2)}) collective-permute-start(bf16[256,1408]{1,0:T(8,128)(2,1)} %get-tuple-element.178.refs_2_), channel_id=1, source_target_pairs={{0,16},{4,20},{8,24},{12,28},{16,0},{20,4},{24,8},{28,12},{1,17},{... | collective-permute-start | bytes 2162696 | tf_op jit(solution)/shard_map/ppermute | solution.py:18
  477.2 66.2 %collective-permute-start.55 = (bf16[256,1408]{1,0:T(8,128)(2,1)S(1)}, bf16[256,1408]{1,0:T(8,128)(2,1)S(1)}, u32[]{:S(2)}, u32[]{:S(2)}) collective-permute-start(bf16[256,1408]{1,0:T(8,128)(2,1)S(1)} %copy-done.23), channel_id=1, source_target_pairs={{0,4},{4,0},{8,12},{12,8},{16,20},{20,16},{24,28},{28,24},{1,5},{5... | collective-permute-start | bytes 2162696 | tf_op jit(solution)/shard_map/ppermute | solution.py:18
  480.1 38.7 %collective-permute-start.42 = (bf16[512,512]{1,0:T(8,128)(2,1)}, bf16[512,512]{1,0:T(8,128)(2,1)S(1)}, u32[]{:S(2)}, u32[]{:S(2)}) collective-permute-start(bf16[512,512]{1,0:T(8,128)(2,1)} %get-tuple-element.175.refs_2_), channel_id=1, source_target_pairs={{0,8},{4,12},{8,0},{12,4},{16,24},{20,28},{24,16},{28,20},{1,9},{5... | collective-permute-start | bytes 1572872 | tf_op jit(solution)/shard_map/ppermute | solution.py:18
  487.9 37.3 %collective-permute-start.48 = (bf16[512,512]{1,0:T(8,128)(2,1)}, bf16[512,512]{1,0:T(8,128)(2,1)S(1)}, u32[]{:S(2)}, u32[]{:S(2)}) collective-permute-start(bf16[512,512]{1,0:T(8,128)(2,1)} %get-tuple-element.180.refs_8_), channel_id=1, source_target_pairs={{0,8},{4,12},{8,0},{12,4},{16,24},{20,28},{24,16},{28,20},{1,9},{5... | collective-permute-start | bytes 1572872 | tf_op jit(solution)/shard_map/ppermute | solution.py:18
  493.4 45.0 %collective-permute-start.50 = (bf16[512,512]{1,0:T(8,128)(2,1)}, bf16[512,512]{1,0:T(8,128)(2,1)}, u32[]{:S(2)}, u32[]{:S(2)}) collective-permute-start(bf16[512,512]{1,0:T(8,128)(2,1)} %get-tuple-element.181.refs_2_), channel_id=1, source_target_pairs={{0,8},{4,12},{8,0},{12,4},{16,24},{20,28},{24,16},{28,20},{1,9},{5... | collective-permute-start | bytes 1572872 | tf_op jit(solution)/shard_map/ppermute | solution.py:18
  518.2 28.6 %collective-permute-start.52 = (bf16[256,512]{1,0:T(8,128)(2,1)S(1)}, bf16[256,512]{1,0:T(8,128)(2,1)S(1)}, u32[]{:S(2)}, u32[]{:S(2)}) collective-permute-start(bf16[256,512]{1,0:T(8,128)(2,1)S(1)} %copy-done.33), channel_id=1, source_target_pairs={{0,16},{4,20},{8,24},{12,28},{16,0},{20,4},{24,8},{28,12},{1,17},{... | collective-permute-start | bytes 786440 | tf_op jit(solution)/shard_map/ppermute | solution.py:18
  518.9 22.3 %collective-permute-start.60 = (f32[4,512]{1,0:T(4,128)S(1)}, f32[4,512]{1,0:T(4,128)S(1)}, u32[]{:S(2)}, u32[]{:S(2)}) collective-permute-start(f32[4,512]{1,0:T(4,128)S(1)} %add.58), channel_id=1, source_target_pairs={{0,8},{4,12},{8,0},{12,4},{16,24},{20,28},{24,16},{28,20},{1,9},{5... | collective-permute-start | bytes 24584 | tf_op jit(solution)/shard_map/ppermute | solution.py:18
  525.2 42.7 %collective-permute-start.47 = (bf16[256,512]{1,0:T(8,128)(2,1)}, bf16[256,512]{1,0:T(8,128)(2,1)S(1)}, u32[]{:S(2)}, u32[]{:S(2)}) collective-permute-start(bf16[256,512]{1,0:T(8,128)(2,1)} %get-tuple-element.183.refs_2_), channel_id=1, source_target_pairs={{0,16},{4,20},{8,24},{12,28},{16,0},{20,4},{24,8},{28,12},{1,17},{... | collective-permute-start | bytes 786440 | tf_op jit(solution)/shard_map/ppermute | solution.py:18
  540.5 27.4 %collective-permute-start.51 = (bf16[256,512]{1,0:T(8,128)(2,1)}, bf16[256,512]{1,0:T(8,128)(2,1)S(1)}, u32[]{:S(2)}, u32[]{:S(2)}) collective-permute-start(bf16[256,512]{1,0:T(8,128)(2,1)} %get-tuple-element.189), channel_id=1, source_target_pairs={{0,16},{4,20},{8,24},{12,28},{16,0},{20,4},{24,8},{28,12},{1,17},{... | collective-permute-start | bytes 786440 | tf_op jit(solution)/shard_map/ppermute | solution.py:18
  541.2 26.7 %collective-permute-start.49 = (bf16[256,512]{1,0:T(8,128)(2,1)}, bf16[256,512]{1,0:T(8,128)(2,1)S(1)}, u32[]{:S(2)}, u32[]{:S(2)}) collective-permute-start(bf16[256,512]{1,0:T(8,128)(2,1)} %get-tuple-element.186.refs_2_), channel_id=1, source_target_pairs={{0,16},{4,20},{8,24},{12,28},{16,0},{20,4},{24,8},{28,12},{1,17},{... | collective-permute-start | bytes 786440 | tf_op jit(solution)/shard_map/ppermute | solution.py:18
  543.4 23.8 %collective-permute-start.61 = (f32[4,512]{1,0:T(4,128)S(1)}, f32[4,512]{1,0:T(4,128)S(1)}, u32[]{:S(2)}, u32[]{:S(2)}) collective-permute-start(f32[4,512]{1,0:T(4,128)S(1)} %add.59), channel_id=1, source_target_pairs={{0,16},{4,20},{8,24},{12,28},{16,0},{20,4},{24,8},{28,12},{1,17},{... | collective-permute-start | bytes 24584 | tf_op jit(solution)/shard_map/ppermute | solution.py:18
  (69 other events, 229.5 us)

commit v3 on v2

--- a/solution.py
+++ b/solution.py
@@ -117,6 +117,12 @@
 
 def wide(column):
     return jnp.broadcast_to(column, (column.shape[0], 128))
+
+
+def in_two(values):
+    which = lax.broadcasted_iota(jnp.int32, values.shape, 0)
+    high = values.astype(BF).astype(F32)
+    return jnp.where(which == 0, high, jnp.where(which == 1, values - high, 0.0)).astype(BF)
 
 
 def upright(row):
@@ -205,7 +211,7 @@
     )
 
 
-def mix_kernel(loc_ref, cum_ref, pg_ref, carry_ref, gain_ref, w_ref, state_ref, b0, b1, q0, q1, mix_ref, sq_ref):
+def mix_kernel(loc_ref, cum_ref, pg_ref, carry_ref, gain_ref, w_ref, state_ref, b0, b1, mix_ref, sq_ref):
     rows = loc_ref.shape[1]
     steps = rows // CHUNKS
     gain = gain_ref[...]
@@ -221,22 +227,26 @@
     out = dot(mix_ref[...], w_ref[...]).astype(BF)
     first = pl.program_id(0) == 0
 
+    def put(ref):
+        ref[:rows] = out
+        ref[rows:] = jnp.zeros((EXTRA, out.shape[1]), BF)
+        ref[rows:, :rows] = in_two(sq_ref[...].T[:EXTRA])
+
     @pl.when(first)
     def _():
-        b0[...] = out
-        q0[...] = sq_ref[...]
+        put(b0)
 
     @pl.when(jnp.logical_not(first))
     def _():
-        b1[...] = out
-        q1[...] = sq_ref[...]
+        put(b1)
 
 
 def mix(loc, cum, pg, carry, shift, gain, out_proj, after=()):
     _, rows, chans = loc.shape
     width = out_proj.shape[1]
     piece = ((1, rows, chans), lambda g: (g, 0, 0))
-    whole = ((rows, width), BF, (rows, width), lambda g: (0, 0))
+    shape = (rows + EXTRA, width)
+    whole = (shape, BF, shape, lambda g: (0, 0))
     return call(
         mix_kernel,
         "mix",
@@ -253,8 +263,6 @@
             (loc.shape, F32, *piece),
             whole,
             whole,
-            ((rows, 128), F32, (rows, 128), lambda g: (0, 0)),
-            ((rows, 128), F32, (rows, 128), lambda g: (0, 0)),
         ],
         flops=4 * rows * chans * width,
         after=after,
@@ -269,7 +277,7 @@
 def hidden_grad(g0, g1, down, after=()):
     rows, width = g0.shape
     units = down.shape[0]
-    tile = min(256, units)
+    tile = min(512, units)
     return call(
         hidden_grad_kernel,
         "hidden_grad",
@@ -281,8 +289,9 @@
     )
 
 
-def feed_kernel(x0, x1, w, gh_ref, hidden, gg, gu):
-    x = stack(x0, x1)
+def feed_kernel(*refs):
+    w, gh_ref, hidden, gg, gu = refs[-5:]
+    x = stack(*refs[:-5])
     gate = dot(x, w[0])
     up = dot(x, w[1])
     gh = gh_ref[...]
@@ -293,18 +302,17 @@
     gu[...] = (gh * act).astype(BF)
 
 
-def feed(x0, x1, gate_up, gh, after=()):
-    rows, width = x0.shape
+def feed(pieces, gate_up, gh, after=()):
+    rows, width = gh.shape[0] // 2, gate_up.shape[1]
     units = gate_up.shape[2]
-    tile = min(256, units)
+    tile = min(512, units)
     col = ((2 * rows, tile), lambda n: (0, n))
     return call(
         feed_kernel,
         "feed",
         (pl.cdiv(units, tile),),
         [
-            fixed(x0),
-            fixed(x1),
+            *[fixed(x) for x in pieces],
             (gate_up, (2, width, tile), lambda n: (0, 0, n)),
             (gh, *col),
         ],
@@ -449,9 +457,9 @@
 
 def back_mix_kernel(
     loc_ref, cum_ref, state_ref, pi_ref, pf_ref, gpg_ref, carry_ref, prior_ref, lb_ref, w,
-    gpi_ref, gpf_ref, b0, b1, term_ref,
+    both_ref, b0, b1, term_ref,
 ):
-    rows = loc_ref.shape[1]
+    _, rows, chans = loc_ref.shape
     steps = rows // CHUNKS
     lb = lb_ref[...]
     rest = 1.0 - lb
@@ -470,12 +478,15 @@
         sig_in = sigmoid(pi)
         total = adj * (prev - pi * sig_in)
         left = 1.0 - sig
-        gpi_ref[0, at, :] = (adj * (rest * left) * (sig_in * (1.0 + pi * (1.0 - sig_in)))).astype(BF)
-        gpf_ref[0, at, :] = (total * rest * sig * left).astype(BF)
+        slope = sig_in * (1.0 + pi * (1.0 - sig_in))
+        both_ref[0, at, :chans] = (adj * (rest * left) * slope).astype(BF)
+        both_ref[0, at, chans:] = (total * rest * sig * left).astype(BF)
         term = term + jnp.sum(total * left, axis=0, keepdims=True)
     term_ref[0] = term
     out = (
-        dot_last(gpi_ref[0], w[0]) + dot_last(gpf_ref[0], w[1]) + dot_last(gpg_ref[0], w[2])
+        dot_last(both_ref[0, :, :chans], w[0])
+        + dot_last(both_ref[0, :, chans:], w[1])
+        + dot_last(gpg_ref[0], w[2])
     ).astype(BF)
     first = pl.program_id(0) == 0
 
@@ -502,8 +513,7 @@
         [(v, *piece) for v in (loc, cum, state, pi, pf, gpg)]
         + [(carry, *moved), (prior, *moved), fixed(lower), fixed(in_proj)],
         [
-            (state.shape, BF, *piece),
-            (state.shape, BF, *piece),
+            ((2, rows, 2 * chans), BF, (1, rows, 2 * chans), lambda g: (g, 0, 0)),
             whole,
             whole,
             ((2, 1, chans), F32, *per),
@@ -513,13 +523,20 @@
     )
 
 
-def product_kernel(me, x0, x1, x2, x3, near, far, out):
-    out[...] = (dot_first(stack(x0, x1), near[...]) + dot_first(stack(x2, x3), far[...])).astype(BF)
-
-
-def product_add_kernel(half, me, x0, x1, x2, x3, near, far, got, send, keep):
-    total = dot_first(stack(x0, x1), near[...]) + dot_first(stack(x2, x3), far[...])
-    total = (total + got[...].astype(F32)).astype(BF)
+def total_product(near_count, refs):
+    lefts, (near, far) = refs[:-2], refs[-2:]
+    return dot_first(stack(*lefts[:near_count]), near[...]) + dot_first(
+        stack(*lefts[near_count:]), far[...]
+    )
+
+
+def product_kernel(near_count, me, *refs):
+    refs[-1][...] = total_product(near_count, refs[:-1]).astype(BF)
+
+
+def product_add_kernel(near_count, half, me, *refs):
+    got, send, keep = refs[-3:]
+    total = (total_product(near_count, refs[:-3]) + got[...].astype(F32)).astype(BF)
     early = pl.program_id(0) < half
 
     @pl.when(early)
@@ -536,8 +553,9 @@
     count = 1 << (levels - 1)
     base = 0 if got is None else count
     top = 2 * count - 1 - base
-    rows = near.shape[0] // 2
     units = near.shape[1]
+    near_count = len(lefts[0])
+    lefts = [*lefts[0], *lefts[1]]
 
     def place(j, me):
         turned = top - j
@@ -547,31 +565,34 @@
         return (0, block)
 
     if size % 128:
-        def ordered(x):
+        def ordered(x, rows):
             parts = [
                 lax.dynamic_slice_in_dim(x[:rows], place(j, me)[1] * size, size, 1)
                 for j in range(count)
             ]
-            return jnp.concatenate(parts, axis=1)
-
-        lefts = [ordered(x) for x in lefts]
+            return jnp.concatenate(parts, axis=1), rows
+
+        lefts = [ordered(*x) for x in lefts]
         count, size = count * size // 128, 128
         position = lambda j, me: (0, j)
     else:
         position = place
-    inputs = [(x, (rows, size), position) for x in lefts]
+    inputs = [(x, (rows, size), position) for x, rows in lefts]
     inputs += [fixed(near), fixed(far)]
-    flops = 8 * rows * units * size * count
+    flops = 0
     if got is None:
         out = ((count * size, units), BF, (size, units), lambda j, me: (j, 0))
-        return call(product_kernel, "product", (count,), inputs, [out], flops, after, blocks=me)
+        return call(
+            functools.partial(product_kernel, near_count),
+            "product", (count,), inputs, [out], flops, after, blocks=me,
+        )
     half = count // 2
     inputs.append((got, (size, units), lambda j, me: (j, 0)))
     shape = (half * size, units)
     send = (shape, BF, (size, units), lambda j, me: (jnp.minimum(j, half - 1), 0))
     keep = (shape, BF, (size, units), lambda j, me: (jnp.maximum(j - half, 0), 0))
     return call(
-        functools.partial(product_add_kernel, half),
+        functools.partial(product_add_kernel, near_count, half),
         "product_add",
         (count,),
         inputs,
@@ -614,34 +635,42 @@
     )
 
 
-def finish_kernel(turned, *refs):
+def finish_kernel(turned, one, two, *refs):
     out = refs[-1]
-    for k in range(len(refs) // 2):
-        total = refs[2 * k][...].astype(F32) + refs[2 * k + 1][...].astype(F32)
-        if turned:
-            out[...] = total.T
-        else:
-            out[k] = total
-
-
-def finish(pairs, turned=False, after=()):
-    rows, units = pairs[0][0].shape
-    flat = [v for one in pairs for v in one]
+    total = one[...].astype(F32) + two[...].astype(F32)
+    if turned:
+        out[...] = total.T
+    else:
+        parts, _, units = out.shape
+        for part in range(parts):
+            out[part] = total[:, part * units : (part + 1) * units]
+
+
+def finish(one, two, turned=False, slot=0, parts=1, slots=1, into=None, after=()):
+    rows, units = one.shape
     if turned:
         tile = 128 if rows % 128 == 0 else rows
-        out = ((units, rows), F32, (units, tile), lambda n: (0, n))
+        shape = (units, rows)
+        out = pl.BlockSpec((units, tile), lambda n: (0, n))
     else:
         tile = 64 if rows % 64 == 0 else rows
-        count = len(pairs)
-        out = ((count, rows, units), F32, (count, tile, units), lambda n: (0, n, 0))
-    return call(
-        functools.partial(finish_kernel, turned),
-        "finish",
-        (rows // tile,),
-        [(v, (tile, units), lambda n: (n, 0)) for v in flat],
-        [out],
-        after=after,
-    )
+        shape = (slots, rows, units // parts)
+        out = pl.BlockSpec((parts, tile, units // parts), lambda n: (slot // parts, n, 0))
+    block = pl.BlockSpec((tile, units), lambda n: (n, 0))
+    held = [] if into is None else [into]
+    waits = [*held, *after]
+    count = len(waits)
+    return pl.pallas_call(
+        lambda one, two, *refs: finish_kernel(turned, one, two, *refs[count:]),
+        grid=(rows // tile,),
+        in_specs=[block, block] + [ANYWHERE] * count,
+        out_specs=out,
+        out_shape=sds(shape),
+        input_output_aliases={2: 0} if held else {},
+        compiler_params=pltpu.CompilerParams(vmem_limit_bytes=VMEM_LIMIT),
+        cost_estimate=pl.CostEstimate(flops=0, bytes_accessed=0, transcendentals=0),
+        name="finish",
+    )(one, two, *waits)
 
 
 def row_call(kernel, name, arrays, gains, outputs, sums=0, after=(), most=64, more=()):
@@ -683,15 +712,64 @@
     return row_call(plus_kernel, "plus", [one, two], [], [(one.shape, BF)], after=after)
 
 
-def middle_kernel(x, own, core, hop, q0, q1, q2, q3, gain, branch_ref, middle_ref, out, scale_ref):
-    width = x.shape[1]
+def join_kernel(one, two, top, bottom):
+    half = bottom.shape[0]
+    rows = 2 * half
+    for out, at in ((top, 0), (bottom, half)):
+        part = slice(at, at + half)
+        out[:half] = (one[part].astype(F32) + two[part].astype(F32)).astype(BF)
+    extra = one[rows:].astype(F32) + two[rows:].astype(F32)
+    top[half:] = in_two(jnp.broadcast_to(extra[0:1] + extra[1:2], extra.shape))
+
+
+def join(one, two, after=()):
+    rows, width = one.shape[0] - EXTRA, one.shape[1]
+    shapes = [(rows // 2 + EXTRA, width), (rows // 2, width)]
+    return call(
+        join_kernel, "join", (1,), [fixed(one), fixed(two)],
+        [(s, BF, s, lambda i: (0, 0)) for s in shapes], after=after,
+    )
+
+
+def middle_kernel(half, x, own, core, hop, own_more, core_more, hop_more, gain, *refs):
+    branch_ref, middle_ref, scale_ref, full, out = refs[-5:]
+    rows, width = x.shape
+    more = own_more[...].astype(F32) + core_more[...].astype(F32) + hop_more[...].astype(F32)
+    squares = (more[0:1] + more[1:2])[:, half * rows : (half + 1) * rows]
+    scale = lax.rsqrt(upright(squares) / width + EPS)
     branch = own[...].astype(F32) + core[...].astype(F32) + hop[...].astype(F32)
-    scale = lax.rsqrt((q0[...] + q1[...] + q2[...] + q3[...]) / width + EPS)
     middle = x[...].astype(F32) + branch * scale[:, :1]
     branch_ref[...] = branch
     scale_ref[...] = scale
     middle_ref[...] = middle
-    out[...] = (middle * rms_scale(middle) * gain[...]).astype(BF)
+    low = (middle * rms_scale(middle) * gain[...]).astype(BF)
+    full[...] = low
+    out[...] = low
+
+
+def middle_half(half, x, own, core, hop, top, gain, begun=(), after=()):
+    total, width = x.shape
+    rows = total // 2
+    part = pl.BlockSpec((rows, width), lambda i: (half, 0))
+    alone = pl.BlockSpec((rows, width), lambda i: (0, 0))
+    more = pl.BlockSpec((EXTRA, width), lambda i: (total // EXTRA, 0))
+    top_more = pl.BlockSpec((EXTRA, width), lambda i: (rows // EXTRA, 0))
+    waits = [*begun, *after]
+    return pl.pallas_call(
+        functools.partial(middle_kernel, half),
+        grid=(1,),
+        in_specs=[part, part, part, alone, more, more, top_more, pl.BlockSpec((1, width), lambda i: (0, 0))]
+        + [ANYWHERE] * len(waits),
+        out_specs=[part, part, pl.BlockSpec((rows, 128), lambda i: (half, 0)), part, alone],
+        out_shape=[
+            sds((total, width)), sds((total, width)), sds((total, 128)), sds((total, width), BF),
+            sds((rows, width), BF),
+        ],
+        input_output_aliases={8 + n: n for n in range(len(begun))},
+        compiler_params=pltpu.CompilerParams(vmem_limit_bytes=VMEM_LIMIT),
+        cost_estimate=pl.CostEstimate(flops=0, bytes_accessed=0, transcendentals=0),
+        name="middle",
+    )(x, own, core, hop, own, core, top, gain, *waits)
 
 
 def turn_kernel(up, own, core, hop, middle_ref, branch, scale_ref, gain, grad_ref, term, out):
@@ -838,6 +916,28 @@
         return self.level == len(self.bits)
 
 
+def gain_terms(norm1_term, norm2_term, mixer_term, bound_n, bound_f):
+    wt = lax.axis_index("wt")
+    span = norm1_term.shape[1] // lax.axis_size("wt")
+    norm_terms = jnp.concatenate([norm1_term, norm2_term])
+
+    def part(j):
+        return lax.dynamic_slice_in_dim(norm_terms, (wt ^ j) * span, span, 1)
+
+    norms = part(0)
+    for j in (1, 2, 3):
+        norms = norms + swap(part(j), "wt", j)
+    bound_term = jnp.sum(bound_n, axis=(0, 1)) + jnp.sum(bound_f, axis=(0, 1))
+    return jnp.stack([norms[0], mixer_term[0], norms[1], bound_term])
+
+
+GATE_AT, LOWER_AT, UP_AT, LOWER_BITS = "before", "beside", "pair", "m"
+ORDER = (
+    ("-p", "-n", "gs", "bb", "us", "-l", "ob", "ls", "ab", "us", "-r", "gf")
+    + ("bs", "os", "as", "lf", "bs", "uf", "as", "os", "bf", "af", "-t", "of")
+)
+
+
 def on_device(
     tokens,
     in_proj,
@@ -857,7 +957,7 @@
     rows = x.shape[0]
     bits = seq_bits()
     y_first = bits
-    z_first = bits[1:] + bits[:1]
+    mixed_order = {"m": bits[1:2] + bits[:1] + bits[2:], "z": bits[1:] + bits[:1], "y": bits}[LOWER_BITS]
     block = width // lax.axis_size("seq")
     me = lax.axis_index("seq").reshape(1).astype(jnp.int32)
 
@@ -879,38 +979,34 @@
     g2 = after(grad_hop, tot)
     g3 = swap(g2, "wt", 1)
     enter = chain(me, tot, False, lambda: (g2,))
-    state_f, bf0, bf1, qf0, qf1 = mix(loc_f, cum_f, pg_f, enter, 2, mixer_use, out_proj)
-    q2, q3 = swap(qf0, "wt", 2), swap(qf1, "wt", 3)
-    state_n, bn0, bn1, q0, qn1 = mix(
-        loc_n, cum_n, pg_n, enter, 0, mixer_use, out_proj, after=(bf0,)
-    )
-    across = plus(bf0, swap(bf1, "wt", 1), after=(bn0,))
-    hop = swap(across, "wt", 2)
-    q1 = swap(qn1, "wt", 1)
+    state_f, bf0, bf1 = mix(loc_f, cum_f, pg_f, enter, 2, mixer_use, out_proj)
+    state_n, bn0, bn1 = mix(loc_n, cum_n, pg_n, enter, 0, mixer_use, out_proj, after=(bf0,))
+    across = join(bf0, swap(bf1, "wt", 1), after=(bn0,))
+    hops = [swap(part, "wt", 2) for part in across]
     core = swap(bn1, "wt", 1)
-    gh_f = hidden_grad(g2, g3, down, after=(across,))
-    branch, middle, t0, scale_two = row_call(
-        middle_kernel,
-        "middle",
-        [x, bn0, core, hop, q0, q1, q2, q3],
-        [gain_two],
-        [(x.shape, F32), (x.shape, F32), (x.shape, BF), ((rows, 128), F32)],
-        after=(gh_f,),
-    )
-
-    hop = swap(t0, "wt", 2)
-    t1 = swap(t0, "wt", 1)
-    hid_n, gg_n, gu_n = feed(t0, t1, gate_up, gh_n)
+    gh_f = hidden_grad(g2, g3, down, after=(across[1],))
+    *begun, half0 = middle_half(0, x, bn0, core, hops[0], hops[0], gain_two, after=(gh_f,))
+    branch, middle, scale_two, t0, half1 = middle_half(
+        1, x, bn0, core, hops[1], hops[0], gain_two, begun
+    )
+
+    hops = [swap(half, "wt", 2) for half in (half0, half1)]
+    t2 = [after(hops[0], t0)]
+    t1 = [after(swap(half, "wt", 1), t2[0]) for half in (half0, half1)]
+    hid_n, gg_n, gu_n = feed((t0, *t1), gate_up, gh_n)
     kn0, kn1 = feed_back(gg_n, gu_n, gate_up)
     core = swap(kn1, "wt", 1)
-    t2 = after(hop, kn0)
-    t3 = swap(t2, "wt", 1)
-    hid_f, gg_f, gu_f = feed(t2, t3, gate_up, gh_f)
-
-    twos = (t0, t1, t2, t3)
+    t2.append(after(hops[1], kn0))
+    t3 = [swap(half, "wt", 1) for half in t2]
+    hid_f, gg_f, gu_f = feed((*t2, *t3), gate_up, gh_f)
+
+    def pieces(*arrays):
+        return [(v, min(rows, v.shape[0])) for v in arrays]
+
+    twos = (pieces(t0, *t1), pieces(*t2, *t3))
     gate = Weight(me, twos, gg_n, gg_f, y_first, block)
     up = Weight(me, twos, gu_n, gu_f, y_first, block)
-    lower = Weight(me, (g0, g1, g2, g3), hid_n, hid_f, z_first, block)
+    lower = Weight(me, (pieces(g0, g1), pieces(g2, g3)), hid_n, hid_f, mixed_order, block)
     kf0, kf1 = feed_back(gg_f, gu_f, gate_up)
     gate.begin(kf0)
     gate.go()
@@ -934,87 +1030,108 @@
     ffn_core = swap(fn1, "wt", 1)
     b2 = after(hop, fn0)
     b3 = swap(b2, "wt", 1)
-    gate.step(b2)
-    ffn_hop = swap(after(ffn_across, b2), "wt", 2)
+    early = (gate.step(b2),) if GATE_AT == "before" else ()
     mixed_f, gpg_f, bloc_f, bcum_f, btot, mixer_f = back_local(
-        b2, b3, out_proj, pg_f, pf_f, state_f, mixer_use, lower_use, (btot,), after=(gate.send,)
-    )
-    leave = chain(me, btot, True, None, lambda pair: (lower.step(pair),))
-    gate.go(leave)
-    up.go(leave)
-    lower.go(leave)
-    gpi_f, gpf_f, df0, df1, bound_f = back_mix(
+        b2, b3, out_proj, pg_f, pf_f, state_f, mixer_use, lower_use, (btot,), after=early
+    )
+
+    def beside(pair):
+        if UP_AT == "pair":
+            up.go(pair)
+        for one, place in ((gate, GATE_AT), (lower, LOWER_AT)):
+            if place == "beside":
+                pair = one.step(pair)
+        return (pair,)
+
+    leave = chain(me, btot, True, None, beside)
+    if UP_AT == "leave":
+        up.go(leave)
+    if GATE_AT == "after":
+        gate.step(leave)
+        gate.go()
+    else:
+        gate.go(leave)
+    if LOWER_AT == "beside":
+        if LOWER_BITS == "z":
+            lower.go(leave)
+        else:
+            lower.go()
+    both_f, df0, df1, bound_f = back_mix(
         bloc_f, bcum_f, state_f, pi_f, pf_f, gpg_f, leave, enter, 2, lower_use, in_proj
     )
-    across = plus(df0, swap(df1, "wt", 1))
-    hop = swap(across, "wt", 2)
-    gpi_n, gpf_n, dn0, dn1, bound_n = back_mix(
-        bloc_n, bcum_n, state_n, pi_n, pf_n, gpg_n, leave, enter, 0, lower_use, in_proj, after=(across,)
-    )
-    core = swap(dn1, "wt", 1)
 
     def flat(values):
-        return values.reshape(2 * rows, chans)
-
-    normals = (n0, n1, n2, n3)
-    ins = [
-        Weight(me, normals, flat(near), flat(far), y_first, block)
-        for near, far in ((gpi_n, gpi_f), (gpf_n, gpf_f), (gpg_n, gpg_f))
-    ]
-    out = Weight(me, (b0, b1, b2, b3), flat(mixed_n), flat(mixed_f), y_first, block)
-    token = gate.step(dn0)
-    gate.go()
-    for one in (out, ins[0]):
-        token = one.begin(token)
-        one.go()
-    token = up.step(token)
-    up.go()
-    for one in ins[1:]:
-        token = one.begin(token)
-        one.go()
-    token = out.step(token)
-    out.go()
-    result = row_call(
-        result_kernel, "result", [middle, fn0, ffn_core, ffn_hop], [], [(x.shape, BF)], after=(token,)
-    )
-    grad_inputs, norm1_term = row_call(
-        last_kernel,
-        "last",
-        [x, dn0, core, hop, grad_middle],
-        [gain_one],
-        [(x.shape, F32)],
-        sums=1,
-        after=(result,),
-    )
-
-    wt = lax.axis_index("wt")
-    span = width // lax.axis_size("wt")
-    norm_terms = jnp.concatenate([norm1_term, norm2_term])
-
-    def part(j):
-        return lax.dynamic_slice_in_dim(norm_terms, (wt ^ j) * span, span, 1)
-
-    norms = part(0)
-    for j in (1, 2, 3):
-        norms = norms + swap(part(j), "wt", j)
-    mixer_term = (mixer_n + mixer_f)[0]
-    bound_term = jnp.sum(bound_n, axis=(0, 1)) + jnp.sum(bound_f, axis=(0, 1))
-    gains = jnp.stack([norms[0], mixer_term, norms[1], bound_term])
-
-    token = grad_inputs
-    order = [lower, ins[0], up, out, *ins[1:]]
-    while not all(one.last() for one in (gate, *order)):
-        for one in (gate, *order):
-            if not one.last():
+        return values.reshape(2 * rows, values.shape[2])
+
+    normals = (pieces(n0, n1), pieces(n2, n3))
+    last_in = Weight(me, normals, flat(gpg_n), flat(gpg_f), y_first, block)
+    out = Weight(me, (pieces(b0, b1), pieces(b2, b3)), flat(mixed_n), flat(mixed_f), y_first, block)
+    both_n, dn0, dn1, bound_n = None, None, None, None
+    token = df0
+    weights = {"g": gate, "u": up, "l": lower, "a": last_in, "o": out}
+    rounds = list(bits)
+    gate_up_grad = in_grad = None
+    for kind, act in ORDER:
+        if kind in weights:
+            one = weights[kind]
+            if act == "b":
+                token = one.begin(token)
+                one.go()
+            elif act == "s":
                 token = one.step(token)
                 one.go()
-    gate_up_grad = finish([(gate.keep, gate.got), (up.keep, up.got)])
-    down_grad = finish([(lower.keep, lower.got)], True)
-    out_grad = finish([(out.keep, out.got)], True)
-    gains = after(gains, gate_up_grad)
-    for bit in bits:
-        gains = gains + swap(gains, "seq", bit)
-    in_grad = finish([(one.keep, one.got) for one in ins])
+                while one.level > 2 and not one.last():
+                    token = one.step(token)
+                    one.go()
+            elif kind in "gu":
+                slot = "gu".index(kind)
+                token = gate_up_grad = finish(
+                    one.keep, one.got, slot=slot, slots=2, into=gate_up_grad, after=(token,)
+                )
+            elif kind == "b":
+                token = in_grad = finish(
+                    one.keep, one.got, parts=2, slots=3, into=in_grad, after=(token,)
+                )
+            elif kind == "a":
+                token = in_grad = finish(
+                    one.keep, one.got, slot=2, slots=3, into=in_grad, after=(token,)
+                )
+            elif kind == "l":
+                token = down_grad = finish(one.keep, one.got, True, after=(token,))
+            else:
+                token = out_grad = finish(one.keep, one.got, True, after=(token,))
+        elif act == "p":
+            token = plus(df0, swap(df1, "wt", 1), after=(token,))
+            hop = swap(token, "wt", 2)
+        elif act == "n":
+            both_n, dn0, dn1, bound_n = back_mix(
+                bloc_n, bcum_n, state_n, pi_n, pf_n, gpg_n, leave, enter, 0, lower_use, in_proj,
+                after=(token,),
+            )
+            token = dn0
+            core = swap(dn1, "wt", 1)
+            weights["b"] = Weight(me, normals, flat(both_n), flat(both_f), y_first, block)
+        elif act == "l":
+            grad_inputs, norm1_term = row_call(
+                last_kernel,
+                "last",
+                [x, dn0, core, hop, grad_middle],
+                [gain_one],
+                [(x.shape, F32)],
+                sums=1,
+                after=(token,),
+            )
+            token = grad_inputs
+            ffn_hop = swap(after(ffn_across, token), "wt", 2)
+            gains = gain_terms(norm1_term, norm2_term, mixer_n + mixer_f, bound_n, bound_f)
+        elif act == "r":
+            token = result = row_call(
+                result_kernel, "result", [middle, fn0, ffn_core, ffn_hop], [], [(x.shape, BF)],
+                after=(token,),
+            )
+        elif act == "t":
+            for bit in rounds:
+                gains = gains + after(swap(gains, "seq", bit), token)
 
     return (
         result[None],

time: 584 us -> 562 us (0.962)
  waiting for transfers between devices: 155 us -> 137 us
  local copies, waits for them, and re-layouts: 24.4 us -> 36.7 us
  starting transfers between devices: 72.3 us -> 64.9 us
    pallas_call x0 -> x8, Pallas kernels: none -> 25.6 us  [the longest x6 18.2 us: finish(): pl.pallas_call(lambda one, two, *refs: finish_kernel(turned, one, two, *r...]
    pallas_call x36 -> x30, Pallas kernels: 223 us -> 199 us  [call(): pl.pallas_call(body, grid=grid, in_specs=in_specs, out_specs=out_specs, s...]
    ppermute x56 -> x54, waiting for transfers between devices: 155 us -> 137 us  [swap(): return lax.ppermute(values, axis, [(i, i ^ bit) for i in range(size)])]
    unnamed x111 -> x120, local copies, waits for them, and re-layouts: 21.2 us -> 33.4 us
    ppermute x56 -> x54, starting transfers between devices: 58.8 us -> 51.4 us  [swap(): return lax.ppermute(values, axis, [(i, i ^ bit) for i in range(size)])]
    pallas_call x18 -> x16, Pallas kernels: 94.8 us -> 88.5 us  [call(): got = pl.pallas_call(body, grid_spec=spec, **settings)(blocks, *operands)]
  transfers between devices with their start and end apart: 62 -> 60, of which waited for: 24 -> 30; matrix products, arithmetic and copies ran while one was open for 1% -> 1% of each run, Pallas kernels for 47% -> 50%
where the time goes in v3:
time: 562 us; the launch traced here: 555 us
  Pallas kernels  313 us (56%)
  waiting for transfers between devices  137 us (24%)
  starting transfers between devices  64.9 us (12%)
  local copies, waits for them, and re-layouts  36.7 us (7%)
    pallas_call x30, Pallas kernels, call(): pl.pallas_call(body, grid=grid, in_specs=in_specs, out_specs=out_specs, s...  199 us
    ppermute x54, waiting for transfers between devices, swap(): return lax.ppermute(values, axis, [(i, i ^ bit) for i in range(size)])  137 us
    pallas_call x16, Pallas kernels, call(): got = pl.pallas_call(body, grid_spec=spec, **settings)(blocks, *operands)  88.5 us
    ppermute x54, starting transfers between devices, swap(): return lax.ppermute(values, axis, [(i, i ^ bit) for i in range(size)])  51.4 us
    unnamed x120, local copies, waits for them, and re-layouts  33.4 us
    pallas_call x6, Pallas kernels, finish(): pl.pallas_call(lambda one, two, *refs: finish_kernel(turned, one, two, *r...  18.2 us
    ppermute x6, starting transfers between devices, shift(): return lax.ppermute(values, axis, pairs)  13.5 us
  transfers between devices with their start and end apart: 60, of which 30 were waited for; matrix products, arithmetic and copies ran while one was open for 1% of the time, Pallas kernels for 50%

profile of v3, /device:TPU:0, one launch (start us, length us, event | category | flops | bytes accessed | tf_op | source)
XLA Modules:
  0.0 554.8 jit_solution(2867730384778978122)
XLA Ops:
  10.2 11.0 %project.2 = (f32[2,256,512]{2,1,0:T(8,128)}, f32[2,256,512]{2,1,0:T(8,128)}, f32[2,256,512]{2,1,0:T(8,128)}, f32[2,256,512]{2,1,0:T(8,128)}, f32[2,256,512]{2,1,0:T(8,128)}, /*index=5*/f32[2,2,512]{2,1,0:T(2,128)}) custom-call(bf16[256,2048]{1,0:T(8,128)(2,1)} %first_norm.1.refs_0_.refs_1_, bf16[256,2048]{1,0:T(8,128)(2,1)} %copy-done.6, ...), custom_call_target="tpu_custom_call" | custom-call | tf_op jit(solution)/shard_map/project/pallas_call | solution.py:70
  21.2 7.4 %hidden_grad.2.refs_1_.refs_4_ = f32[512,1408]{1,0:T(8,128)} custom-call(bf16[256,2048]{1,0:T(8,128)(2,1)} %bitcast.20, bf16[256,2048]{1,0:T(8,128)(2,1)} %collective-permute-done.2.refs_1_.refs_2_, bf16[1408,2048]{1,0:T(8,128)(2,1)} %refs_1_.3, f32[2,2,512]{2,1,0:T(2,128)} %get-tuple-element.106.refs_3_.refs_4_), custom_call_target="tpu_custom_call" | custom-call | tf_op jit(solution)/shard_map/hidden_grad/pallas_call | solution.py:70
  36.4 11.6 %project.3 = (f32[2,256,512]{2,1,0:T(8,128)}, f32[2,256,512]{2,1,0:T(8,128)}, f32[2,256,512]{2,1,0:T(8,128)}, f32[2,256,512]{2,1,0:T(8,128)}, f32[2,256,512]{2,1,0:T(8,128)}, /*index=5*/f32[2,4,512]{2,1,0:T(4,128)}) custom-call(bf16[256,2048]{1,0:T(8,128)(2,1)} %hold.14.refs_0_.refs_3_, bf16[256,2048]{1,0:T(8,128)(2,1)} %copy-done.9, ...), custom_call_target="tpu_custom_call" | custom-call | tf_op jit(solution)/shard_map/project/pallas_call | solution.py:70
  49.8 9.4 %collective-permute-done.5.refs_0_ = bf16[256,2048]{1,0:T(8,128)(2,1)S(1)} collective-permute-done((bf16[256,2048]{1,0:T(8,128)(2,1)}, bf16[256,2048]{1,0:T(8,128)(2,1)S(1)}, u32[]{:S(2)}, u32[]{:S(2)}) %collective-permute-start.5) | collective-permute-done | bytes 1048608 | tf_op jit(solution)/shard_map/ppermute | solution.py:18
  65.9 4.5 collective-permute-start.7
  75.8 5.6 %mix.2 = (f32[2,256,512]{2,1,0:T(8,128)}, bf16[272,2048]{1,0:T(8,128)(2,1)}, bf16[272,2048]{1,0:T(8,128)(2,1)}) custom-call(f32[2,256,512]{2,1,0:T(8,128)} %get-tuple-element.108.refs_0_, f32[2,256,512]{2,1,0:T(8,128)} %get-tuple-element.109.refs_1_, f32[2,256,512]{2,1,0:T(8,128)} %get-tuple-element.110.refs_2_.refs_3_, f32[4,1,512]{2,1,0:T(1,128)} %enter.2.refs_3_.refs_7_, ...), custom_call_target="tpu_custom_call" | custom-call | tf_op jit(solution)/shard_map/mix/pallas_call | solution.py:70
  81.5 5.7 %mix.3 = (f32[2,256,512]{2,1,0:T(8,128)}, bf16[272,2048]{1,0:T(8,128)(2,1)}, bf16[272,2048]{1,0:T(8,128)(2,1)}) custom-call(f32[2,256,512]{2,1,0:T(8,128)} %get-tuple-element.103.refs_0_, f32[2,256,512]{2,1,0:T(8,128)} %get-tuple-element.104.refs_1_, f32[2,256,512]{2,1,0:T(8,128)} %get-tuple-element.105.refs_2_.refs_3_, f32[4,1,512]{2,1,0:T(1,128)} %enter.2.refs_3_.refs_7_, ...), custom_call_target="tpu_custom_call" | custom-call | tf_op jit(solution)/shard_map/mix/pallas_call | solution.py:70
  93.7 7.5 %hidden_grad.3.refs_0_.refs_5_ = f32[512,1408]{1,0:T(8,128)} custom-call(bf16[256,2048]{1,0:T(8,128)(2,1)} %hold.16.refs_3_.refs_0_, bf16[256,2048]{1,0:T(8,128)(2,1)} %copy-done.18, bf16[1408,2048]{1,0:T(8,128)(2,1)} %refs_1_.3, bf16[128,2048]{1,0:T(8,128)(2,1)} %get-tuple-element.115.refs_3_), custom_call_target="tpu_custom_call" | custom-call | tf_op jit(solution)/shard_map/hidden_grad/pallas_call | solution.py:70
  101.2 5.8 %collective-permute-done.12.hop.hop_more = bf16[144,2048]{1,0:T(8,128)(2,1)S(1)} collective-permute-done((bf16[144,2048]{1,0:T(8,128)(2,1)}, bf16[144,2048]{1,0:T(8,128)(2,1)S(1)}, u32[]{:S(2)}, u32[]{:S(2)}) %collective-permute-start.12) | collective-permute-done | bytes 589856 | tf_op jit(solution)/shard_map/ppermute | solution.py:18
  113.0 5.4 collective-permute-done.11.hop
  124.0 5.4 collective-permute-done.15.refs_0_
  131.9 12.1 %feed.2 = (bf16[512,1408]{1,0:T(8,128)(2,1)}, bf16[512,1408]{1,0:T(8,128)(2,1)}, bf16[512,1408]{1,0:T(8,128)(2,1)}) custom-call(bf16[256,2048]{1,0:T(8,128)(2,1)} %get-tuple-element.122.refs_1_.refs_0_, bf16[128,2048]{1,0:T(8,128)(2,1)} %hold.18.refs_1_.refs_2_, bf16[128,2048]{1,0:T(8,128)(2,1)} %hold.19.refs_2_.refs_3_, bf16[2,2048,1408]{2,1,0:T(8,128)(2,1)} %refs_2_.13, ...), custom_call_target="tpu_custom_call" | custom-call | tf_op jit(solution)/shard_map/feed/pallas_call | solution.py:70
  144.0 10.8 %feed_back.2 = (bf16[256,2048]{1,0:T(8,128)(2,1)}, bf16[256,2048]{1,0:T(8,128)(2,1)}) custom-call(bf16[512,1408]{1,0:T(8,128)(2,1)} %get-tuple-element.126.refs_0_.refs_8_, bf16[512,1408]{1,0:T(8,128)(2,1)} %get-tuple-element.127.refs_1_.refs_8_, bf16[2,2048,1408]{2,1,0:T(8,128)(2,1)} %refs_2_.13), custom_call_target="tpu_custom_call" | custom-call | tf_op jit(solution)/shard_map/feed_back/pallas_call | solution.py:70
  159.3 12.0 %feed.3 = (bf16[512,1408]{1,0:T(8,128)(2,1)}, bf16[512,1408]{1,0:T(8,128)(2,1)}, bf16[512,1408]{1,0:T(8,128)(2,1)}) custom-call(bf16[128,2048]{1,0:T(8,128)(2,1)} %hold.17.refs_1_.refs_0_.refs_4_, bf16[128,2048]{1,0:T(8,128)(2,1)} %hold.20.refs_1_.refs_5_, bf16[128,2048]{1,0:T(8,128)(2,1)} %copy-done.15, bf16[128,2048]{1,0:T(8,128)(2,1)} %copy-done.14, ...), custom_call_target="tpu_custom_call" | custom-call | tf_op jit(solution)/shard_map/feed/pallas_call | solution.py:70
  171.4 11.0 %feed_back.3 = (bf16[256,2048]{1,0:T(8,128)(2,1)}, bf16[256,2048]{1,0:T(8,128)(2,1)}) custom-call(bf16[512,1408]{1,0:T(8,128)(2,1)} %get-tuple-element.131.refs_0_.refs_9_, bf16[512,1408]{1,0:T(8,128)(2,1)} %get-tuple-element.130.refs_1_.refs_9_, bf16[2,2048,1408]{2,1,0:T(8,128)(2,1)} %refs_2_.13), custom_call_target="tpu_custom_call" | custom-call | tf_op jit(solution)/shard_map/feed_back/pallas_call | solution.py:70
  182.9 7.7 %product.6.refs_2_ = bf16[1024,1408]{1,0:T(8,128)(2,1)} custom-call(s32[1]{0:T(128)} %bitcast.3.refs_0_, bf16[256,2048]{1,0:T(8,128)(2,1)} %get-tuple-element.122.refs_1_.refs_0_, bf16[128,2048]{1,0:T(8,128)(2,1)} %hold.18.refs_1_.refs_2_, bf16[128,2048]{1,0:T(8,128)(2,1)} %hold.19.refs_2_.refs_3_, bf16[128,2048]{1,0:T(8,128)(2,1)} %hold.17.refs_1_.refs_0_.refs_4_, ...), custom_call_target="tpu_custom_call" | custom-call | tf_op jit(solution)/shard_map/product/pallas_call | solution.py:81
  198.2 7.5 %product.7.refs_10_ = bf16[1024,1408]{1,0:T(8,128)(2,1)} custom-call(s32[1]{0:T(128)} %bitcast.3.refs_0_, bf16[256,2048]{1,0:T(8,128)(2,1)} %bitcast.21, bf16[256,2048]{1,0:T(8,128)(2,1)} %collective-permute-done.2.refs_1_.refs_2_, bf16[256,2048]{1,0:T(8,128)(2,1)} %hold.16.refs_3_.refs_0_, bf16[256,2048]{1,0:T(8,128)(2,1)} %copy-done.18, ...), custom_call_target="tpu_custom_call" | custom-call | tf_op jit(solution)/shard_map/product/pallas_call | solution.py:81
  205.7 7.5 %product.8.refs_2_.refs_0_ = bf16[1024,1408]{1,0:T(8,128)(2,1)} custom-call(s32[1]{0:T(128)} %bitcast.3.refs_0_, bf16[256,2048]{1,0:T(8,128)(2,1)} %get-tuple-element.122.refs_1_.refs_0_, bf16[128,2048]{1,0:T(8,128)(2,1)} %hold.18.refs_1_.refs_2_, bf16[128,2048]{1,0:T(8,128)(2,1)} %hold.19.refs_2_.refs_3_, bf16[128,2048]{1,0:T(8,128)(2,1)} %hold.17.refs_1_.refs_0_.refs_4_, ...), custom_call_target="tpu_custom_call" | custom-call | tf_op jit(solution)/shard_map/product/pallas_call | solution.py:81
  213.2 7.2 %feed_out.2 = (bf16[256,2048]{1,0:T(8,128)(2,1)}, bf16[256,2048]{1,0:T(8,128)(2,1)}) custom-call(bf16[512,1408]{1,0:T(8,128)(2,1)} %get-tuple-element.129.refs_6_.refs_0_, bf16[1408,2048]{1,0:T(8,128)(2,1)} %refs_1_.3, bf16[1024,1408]{1,0:T(8,128)(2,1)} %product.8.refs_2_.refs_0_), custom_call_target="tpu_custom_call" | custom-call | tf_op jit(solution)/shard_map/feed_out/pallas_call | solution.py:70
  221.8 6.4 %turn.1 = (f32[256,2048]{1,0:T(8,128)}, f32[1,2048]{1,0:T(1,128)}, bf16[272,2048]{1,0:T(8,128)(2,1)}) custom-call(bf16[256,2048]{1,0:T(8,128)(2,1)} %bitcast.22, bf16[256,2048]{1,0:T(8,128)(2,1)} %get-tuple-element.128.refs_1_, bf16[256,2048]{1,0:T(8,128)(2,1)} %copy-done.30, bf16[256,2048]{1,0:T(8,128)(2,1)} %copy-done.31, ...), custom_call_target="tpu_custom_call" | custom-call | tf_op jit(solution)/shard_map/turn/pallas_call | solution.py:70
  232.3 9.2 %back_local.2 = (bf16[2,256,512]{2,1,0:T(8,128)(2,1)}, bf16[2,256,512]{2,1,0:T(8,128)(2,1)}, f32[2,256,512]{2,1,0:T(8,128)}, f32[2,256,512]{2,1,0:T(8,128)}, f32[2,2,512]{2,1,0:T(2,128)}, /*index=5*/f32[1,512]{1,0:T(1,128)}) custom-call(bf16[272,2048]{1,0:T(8,128)(2,1)} %get-tuple-element.139.refs_0_.refs_1_, bf16[272,2048]{1,0:T(8,128)(2,1)} %copy-done.16, ...), custom_call_target="tpu_custom_call" | custom-call | tf_op jit(solution)/shard_map/back_local/pallas_call | solution.py:70
  246.0 7.1 %feed_out.3 = (bf16[256,2048]{1,0:T(8,128)(2,1)}, bf16[256,2048]{1,0:T(8,128)(2,1)}) custom-call(bf16[512,1408]{1,0:T(8,128)(2,1)} %get-tuple-element.125.refs_5_.refs_0_, bf16[1408,2048]{1,0:T(8,128)(2,1)} %refs_1_.3, bf16[256,2048]{1,0:T(8,128)(2,1)} %plus.4.refs_2_.refs_0_), custom_call_target="tpu_custom_call" | custom-call | tf_op jit(solution)/shard_map/feed_out/pallas_call | solution.py:70
  256.4 4.8 collective-permute-done.28.refs_10_
  261.3 8.6 %product_add.6 = (bf16[512,1408]{1,0:T(8,128)(2,1)}, bf16[512,1408]{1,0:T(8,128)(2,1)}) custom-call(s32[1]{0:T(128)} %bitcast.3.refs_0_, bf16[256,2048]{1,0:T(8,128)(2,1)} %get-tuple-element.122.refs_1_.refs_0_, bf16[128,2048]{1,0:T(8,128)(2,1)} %hold.18.refs_1_.refs_2_, bf16[128,2048]{1,0:T(8,128)(2,1)} %hold.19.refs_2_.refs_3_, ...), custom_call_target="tpu_custom_call" | custom-call | tf_op jit(solution)/shard_map/product_add/pallas_call | solution.py:81
  270.9 9.2 %back_local.3 = (bf16[2,256,512]{2,1,0:T(8,128)(2,1)}, bf16[2,256,512]{2,1,0:T(8,128)(2,1)}, f32[2,256,512]{2,1,0:T(8,128)}, f32[2,256,512]{2,1,0:T(8,128)}, f32[2,4,512]{2,1,0:T(4,128)}, /*index=5*/f32[1,512]{1,0:T(1,128)}) custom-call(bf16[272,2048]{1,0:T(8,128)(2,1)} %hold.21.refs_11_.refs_0_.refs_3_, bf16[272,2048]{1,0:T(8,128)(2,1)} %copy-done.17, ...), custom_call_target="tpu_custom_call" | custom-call | tf_op jit(solution)/shard_map/back_local/pallas_call | solution.py:70
  295.2 8.9 %product_add.7 = (bf16[512,1408]{1,0:T(8,128)(2,1)}, bf16[512,1408]{1,0:T(8,128)(2,1)}) custom-call(s32[1]{0:T(128)} %bitcast.3.refs_0_, bf16[256,2048]{1,0:T(8,128)(2,1)} %bitcast.23, bf16[256,2048]{1,0:T(8,128)(2,1)} %collective-permute-done.2.refs_1_.refs_2_, bf16[256,2048]{1,0:T(8,128)(2,1)} %hold.16.refs_3_.refs_0_, bf16[256,2048]{1,0:T(8,128)(2,1)} %copy-done.18, ...), custom_call_target="tpu_custom_call" | custom-call | tf_op jit(solution)/shard_map/product_add/pallas_call | solution.py:81
  306.1 10.3 %back_mix.2 = (bf16[2,256,1024]{2,1,0:T(8,128)(2,1)}, bf16[256,2048]{1,0:T(8,128)(2,1)}, bf16[256,2048]{1,0:T(8,128)(2,1)}, f32[2,1,512]{2,1,0:T(1,128)}) custom-call(f32[2,256,512]{2,1,0:T(8,128)} %get-tuple-element.154.refs_0_, f32[2,256,512]{2,1,0:T(8,128)} %get-tuple-element.155.refs_1_, f32[2,256,512]{2,1,0:T(8,128)} %get-tuple-element.150.refs_5_.refs_2_, ...), custom_call_target="tpu_custom_call" | custom-call | tf_op jit(solution)/shard_map/back_mix/pallas_call | solution.py:70
  324.0 10.3 %back_mix.3 = (bf16[2,256,1024]{2,1,0:T(8,128)(2,1)}, bf16[256,2048]{1,0:T(8,128)(2,1)}, bf16[256,2048]{1,0:T(8,128)(2,1)}, f32[2,1,512]{2,1,0:T(1,128)}) custom-call(f32[2,256,512]{2,1,0:T(8,128)} %get-tuple-element.145.refs_0_, f32[2,256,512]{2,1,0:T(8,128)} %get-tuple-element.146.refs_1_, f32[2,256,512]{2,1,0:T(8,128)} %get-tuple-element.141.refs_5_.refs_2_, ...), custom_call_target="tpu_custom_call" | custom-call | tf_op jit(solution)/shard_map/back_mix/pallas_call | solution.py:70
  342.5 6.3 %product.9.refs_11_ = bf16[1024,1024]{1,0:T(8,128)(2,1)} custom-call(s32[1]{0:T(128)} %bitcast.3.refs_0_, bf16[256,2048]{1,0:T(8,128)(2,1)} %first_norm.1.refs_0_.refs_1_, bf16[256,2048]{1,0:T(8,128)(2,1)} %copy-done.6, bf16[256,2048]{1,0:T(8,128)(2,1)} %hold.14.refs_0_.refs_3_, bf16[256,2048]{1,0:T(8,128)(2,1)} %copy-done.9, bf16[512,1024]{1,0:T(8,128)(2,1)} %bitcast.38, ...), custom_call_target="tpu_custom_call" | custom-call | tf_op jit(solution)/shard_map/product/pallas_call | solution.py:81
  353.2 8.6 %product_add.8 = (bf16[512,1408]{1,0:T(8,128)(2,1)}, bf16[512,1408]{1,0:T(8,128)(2,1)}) custom-call(s32[1]{0:T(128)} %bitcast.3.refs_0_, bf16[256,2048]{1,0:T(8,128)(2,1)} %get-tuple-element.122.refs_1_.refs_0_, bf16[128,2048]{1,0:T(8,128)(2,1)} %hold.18.refs_1_.refs_2_, bf16[128,2048]{1,0:T(8,128)(2,1)} %hold.19.refs_2_.refs_3_, ...), custom_call_target="tpu_custom_call" | custom-call | tf_op jit(solution)/shard_map/product_add/pallas_call | solution.py:81
  362.0 5.5 last.1
  368.0 14.6 %collective-permute-done.41.refs_1_ = bf16[512,1408]{1,0:T(8,128)(2,1)} collective-permute-done((bf16[512,1408]{1,0:T(8,128)(2,1)}, bf16[512,1408]{1,0:T(8,128)(2,1)}, u32[]{:S(2)}, u32[]{:S(2)}) %collective-permute-start.41) | collective-permute-done | bytes 1441824 | tf_op jit(solution)/shard_map/ppermute | solution.py:18
  384.6 4.9 product.10.refs_2_
  392.9 5.0 product.11.refs_2_
  399.5 6.6 %collective-permute-done.40.refs_1_ = bf16[512,1408]{1,0:T(8,128)(2,1)S(1)} collective-permute-done((bf16[512,1408]{1,0:T(8,128)(2,1)}, bf16[512,1408]{1,0:T(8,128)(2,1)S(1)}, u32[]{:S(2)}, u32[]{:S(2)}) %collective-permute-start.40) | collective-permute-done | bytes 1441824 | tf_op jit(solution)/shard_map/ppermute | solution.py:18
  410.4 4.3 result.1.refs_0_
  418.3 9.3 %collective-permute-done.44.refs_7_ = bf16[1024,1024]{1,0:T(8,128)(2,1)} collective-permute-done((bf16[1024,1024]{1,0:T(8,128)(2,1)}, bf16[1024,1024]{1,0:T(8,128)(2,1)}, u32[]{:S(2)}, u32[]{:S(2)}) %collective-permute-start.44) | collective-permute-done | bytes 2097184 | tf_op jit(solution)/shard_map/ppermute | solution.py:18
  427.5 7.0 %product_add.9 = (bf16[512,1024]{1,0:T(8,128)(2,1)}, bf16[512,1024]{1,0:T(8,128)(2,1)}) custom-call(s32[1]{0:T(128)} %bitcast.3.refs_0_, bf16[256,2048]{1,0:T(8,128)(2,1)} %first_norm.1.refs_0_.refs_1_, bf16[256,2048]{1,0:T(8,128)(2,1)} %copy-done.6, bf16[256,2048]{1,0:T(8,128)(2,1)} %hold.14.refs_0_.refs_3_, bf16[256,2048]{1,0:T(8,128)(2,1)} %copy-done.9, ...), custom_call_target="tpu_custom_call" | custom-call | tf_op jit(solution)/shard_map/product_add/pallas_call | solution.py:81
  434.6 4.2 collective-permute-start.49
  438.8 11.2 %collective-permute-done.43.refs_7_ = bf16[1024,512]{1,0:T(8,128)(2,1)} collective-permute-done((bf16[1024,512]{1,0:T(8,128)(2,1)S(1)}, bf16[1024,512]{1,0:T(8,128)(2,1)}, u32[]{:S(2)}, u32[]{:S(2)}) %collective-permute-start.43) | collective-permute-done | bytes 1048608 | tf_op jit(solution)/shard_map/ppermute | solution.py:18
  450.0 5.5 product_add.10
  455.5 14.0 %collective-permute-done.42.refs_7_ = bf16[1024,512]{1,0:T(8,128)(2,1)S(1)} collective-permute-done((bf16[1024,512]{1,0:T(8,128)(2,1)}, bf16[1024,512]{1,0:T(8,128)(2,1)S(1)}, u32[]{:S(2)}, u32[]{:S(2)}) %collective-permute-start.42) | collective-permute-done | bytes 1048608 | tf_op jit(solution)/shard_map/ppermute | solution.py:18
  470.6 5.4 product_add.11
  483.6 4.6 collective-permute-start.52
  492.2 5.5 collective-permute-done.47.two
  501.3 8.9 %collective-permute-done.46.refs_1_ = bf16[512,512]{1,0:T(8,128)(2,1)S(1)} collective-permute-done((bf16[512,512]{1,0:T(8,128)(2,1)}, bf16[512,512]{1,0:T(8,128)(2,1)S(1)}, u32[]{:S(2)}, u32[]{:S(2)}) %collective-permute-start.46) | collective-permute-done | bytes 524320 | tf_op jit(solution)/shard_map/ppermute | solution.py:18
  513.2 4.0 collective-permute-start.50
  532.6 5.3 collective-permute-done.50.two
  (274 shorter events, 182.7 us)
Async XLA Ops:
  4.9 16.3 %collective-permute-start.2 = (bf16[256,2048]{1,0:T(8,128)(2,1)S(1)}, bf16[256,2048]{1,0:T(8,128)(2,1)}, u32[]{:S(2)}, u32[]{:S(2)}) collective-permute-start(bf16[256,2048]{1,0:T(8,128)(2,1)S(1)} %bitcast.24), channel_id=1, source_target_pairs={{0,1},{1,0},{2,3},{3,2},{4,5},{5,4},{6,7},{7,6},{8,9},{9,8},{10,11... | collective-permute-start | bytes 3145736 | tf_op jit(solution)/shard_map/ppermute | solution.py:18
  4.9 26.5 %collective-permute-start.1 = (bf16[256,2048]{1,0:T(8,128)(2,1)}, bf16[256,2048]{1,0:T(8,128)(2,1)S(1)}, u32[]{:S(2)}, u32[]{:S(2)}) collective-permute-start(bf16[256,2048]{1,0:T(8,128)(2,1)} %first_norm.1.refs_0_.refs_1_), channel_id=1, source_target_pairs={{0,2},{1,3},{2,0},{3,1},{4,6},{5,7},{6,4},{7,5},{8,10},{9,11},{10,... | collective-permute-start | bytes 3145736 | tf_op jit(solution)/shard_map/ppermute | solution.py:18
  33.4 25.8 %collective-permute-start.5 = (bf16[256,2048]{1,0:T(8,128)(2,1)}, bf16[256,2048]{1,0:T(8,128)(2,1)S(1)}, u32[]{:S(2)}, u32[]{:S(2)}) collective-permute-start(bf16[256,2048]{1,0:T(8,128)(2,1)} %hold.15), channel_id=1, source_target_pairs={{0,2},{1,3},{2,0},{3,1},{4,6},{5,7},{6,4},{7,5},{8,10},{9,11},{10,... | collective-permute-start | bytes 3145736 | tf_op jit(solution)/shard_map/ppermute | solution.py:18
  47.9 12.3 %collective-permute-start.4 = (f32[2,4,512]{2,1,0:T(4,128)}, f32[2,4,512]{2,1,0:T(4,128)S(1)}, u32[]{:S(2)}, u32[]{:S(2)}) collective-permute-start(f32[2,4,512]{2,1,0:T(4,128)} %get-tuple-element.107.refs_1_), channel_id=1, source_target_pairs={{0,4},{4,0},{8,12},{12,8},{16,20},{20,16},{24,28},{28,24},{1,5},{5... | collective-permute-start | bytes 49160 | tf_op jit(solution)/shard_map/ppermute | solution.py:18
  62.2 11.0 %collective-permute-start.6 = (f32[2,4,512]{2,1,0:T(4,128)}, f32[2,4,512]{2,1,0:T(4,128)S(1)}, u32[]{:S(2)}, u32[]{:S(2)}) collective-permute-start(f32[2,4,512]{2,1,0:T(4,128)} %pair.2), channel_id=1, source_target_pairs={{0,8},{4,12},{8,16},{12,20},{16,24},{20,28},{1,9},{5,13},{9,17},{1... | collective-permute-start | bytes 49160 | tf_op jit(solution)/shard_map/ppermute | solution.py:24
  65.9 7.3 %collective-permute-start.7 = (f32[2,4,512]{2,1,0:T(4,128)}, f32[2,4,512]{2,1,0:T(4,128)S(1)}, u32[]{:S(2)}, u32[]{:S(2)}) collective-permute-start(f32[2,4,512]{2,1,0:T(4,128)} %pair.2), channel_id=1, source_target_pairs={{0,16},{4,20},{8,24},{12,28},{1,17},{5,21},{9,25},{13,29},{2,18},{... | collective-permute-start | bytes 49160 | tf_op jit(solution)/shard_map/ppermute | solution.py:24
  87.2 14.0 %collective-permute-start.9 = (bf16[272,2048]{1,0:T(8,128)(2,1)}, bf16[272,2048]{1,0:T(8,128)(2,1)S(1)}, u32[]{:S(2)}, u32[]{:S(2)}) collective-permute-start(bf16[272,2048]{1,0:T(8,128)(2,1)} %get-tuple-element.113), channel_id=1, source_target_pairs={{0,1},{1,0},{2,3},{3,2},{4,5},{5,4},{6,7},{7,6},{8,9},{9,8},{10,11... | collective-permute-start | bytes 3342344 | tf_op jit(solution)/shard_map/ppermute | solution.py:18
  90.6 16.3 %collective-permute-start.12 = (bf16[144,2048]{1,0:T(8,128)(2,1)}, bf16[144,2048]{1,0:T(8,128)(2,1)S(1)}, u32[]{:S(2)}, u32[]{:S(2)}) collective-permute-start(bf16[144,2048]{1,0:T(8,128)(2,1)} %get-tuple-element.116), channel_id=1, source_target_pairs={{0,2},{1,3},{2,0},{3,1},{4,6},{5,7},{6,4},{7,5},{8,10},{9,11},{10,... | collective-permute-start | bytes 1769480 | tf_op jit(solution)/shard_map/ppermute | solution.py:18
  92.1 26.2 %collective-permute-start.11 = (bf16[128,2048]{1,0:T(8,128)(2,1)}, bf16[128,2048]{1,0:T(8,128)(2,1)}, u32[]{:S(2)}, u32[]{:S(2)}) collective-permute-start(bf16[128,2048]{1,0:T(8,128)(2,1)} %get-tuple-element.115.refs_3_), channel_id=1, source_target_pairs={{0,2},{1,3},{2,0},{3,1},{4,6},{5,7},{6,4},{7,5},{8,10},{9,11},{10,... | collective-permute-start | bytes 1572872 | tf_op jit(solution)/shard_map/ppermute | solution.py:18
  111.5 18.0 %collective-permute-start.15 = (bf16[128,2048]{1,0:T(8,128)(2,1)}, bf16[128,2048]{1,0:T(8,128)(2,1)S(1)}, u32[]{:S(2)}, u32[]{:S(2)}) collective-permute-start(bf16[128,2048]{1,0:T(8,128)(2,1)} %get-tuple-element.123), channel_id=1, source_target_pairs={{0,2},{1,3},{2,0},{3,1},{4,6},{5,7},{6,4},{7,5},{8,10},{9,11},{10,... | collective-permute-start | bytes 1572872 | tf_op jit(solution)/shard_map/ppermute | solution.py:18
  122.0 8.2 %collective-permute-start.16 = (bf16[128,2048]{1,0:T(8,128)(2,1)}, bf16[128,2048]{1,0:T(8,128)(2,1)S(1)}, u32[]{:S(2)}, u32[]{:S(2)}) collective-permute-start(bf16[128,2048]{1,0:T(8,128)(2,1)} %get-tuple-element.124), channel_id=1, source_target_pairs={{0,1},{1,0},{2,3},{3,2},{4,5},{5,4},{6,7},{7,6},{8,9},{9,8},{10,11... | collective-permute-start | bytes 1572872 | tf_op jit(solution)/shard_map/ppermute | solution.py:18
  122.0 9.0 %collective-permute-start.14 = (bf16[128,2048]{1,0:T(8,128)(2,1)S(1)}, bf16[128,2048]{1,0:T(8,128)(2,1)S(1)}, u32[]{:S(2)}, u32[]{:S(2)}) collective-permute-start(bf16[128,2048]{1,0:T(8,128)(2,1)S(1)} %copy-done.58), channel_id=1, source_target_pairs={{0,1},{1,0},{2,3},{3,2},{4,5},{5,4},{6,7},{7,6},{8,9},{9,8},{10,11... | collective-permute-start | bytes 1572872 | tf_op jit(solution)/shard_map/ppermute | solution.py:18
  122.5 32.3 %collective-permute-start.17 = (bf16[128,2048]{1,0:T(8,128)(2,1)}, bf16[128,2048]{1,0:T(8,128)(2,1)S(1)}, u32[]{:S(2)}, u32[]{:S(2)}) collective-permute-start(bf16[128,2048]{1,0:T(8,128)(2,1)} %get-tuple-element.124), channel_id=1, source_target_pairs={{0,2},{1,3},{2,0},{3,1},{4,6},{5,7},{6,4},{7,5},{8,10},{9,11},{10,... | collective-permute-start | bytes 1572872 | tf_op jit(solution)/shard_map/ppermute | solution.py:18
  182.4 8.2 %collective-permute-start.20 = (bf16[256,2048]{1,0:T(8,128)(2,1)}, bf16[256,2048]{1,0:T(8,128)(2,1)S(1)}, u32[]{:S(2)}, u32[]{:S(2)}) collective-permute-start(bf16[256,2048]{1,0:T(8,128)(2,1)} %get-tuple-element.133), channel_id=1, source_target_pairs={{0,1},{1,0},{2,3},{3,2},{4,5},{5,4},{6,7},{7,6},{8,9},{9,8},{10,11... | collective-permute-start | bytes 3145736 | tf_op jit(solution)/shard_map/ppermute | solution.py:18
  182.5 37.9 %collective-permute-start.22 = (bf16[256,2048]{1,0:T(8,128)(2,1)S(1)}, bf16[256,2048]{1,0:T(8,128)(2,1)S(1)}, u32[]{:S(2)}, u32[]{:S(2)}) collective-permute-start(bf16[256,2048]{1,0:T(8,128)(2,1)S(1)} %copy-done.57), channel_id=1, source_target_pairs={{0,1},{1,0},{2,3},{3,2},{4,5},{5,4},{6,7},{7,6},{8,9},{9,8},{10,11... | collective-permute-start | bytes 3145736 | tf_op jit(solution)/shard_map/ppermute | solution.py:18
  195.2 25.4 %collective-permute-start.23 = (bf16[256,2048]{1,0:T(8,128)(2,1)}, bf16[256,2048]{1,0:T(8,128)(2,1)S(1)}, u32[]{:S(2)}, u32[]{:S(2)}) collective-permute-start(bf16[256,2048]{1,0:T(8,128)(2,1)} %plus.3.refs_7_.refs_11_), channel_id=1, source_target_pairs={{0,2},{1,3},{2,0},{3,1},{4,6},{5,7},{6,4},{7,5},{8,10},{9,11},{10,... | collective-permute-start | bytes 3145736 | tf_op jit(solution)/shard_map/ppermute | solution.py:18
  196.7 64.6 %collective-permute-start.28 = (bf16[1024,1408]{1,0:T(8,128)(2,1)}, bf16[1024,1408]{1,0:T(8,128)(2,1)}, u32[]{:S(2)}, u32[]{:S(2)}) collective-permute-start(bf16[1024,1408]{1,0:T(8,128)(2,1)} %product.6.refs_2_), channel_id=1, source_target_pairs={{0,4},{4,0},{8,12},{12,8},{16,20},{20,16},{24,28},{28,24},{1,5},{5... | collective-permute-start | bytes 8650760 | tf_op jit(solution)/shard_map/ppermute | solution.py:18
  228.2 27.2 %collective-permute-start.26 = (bf16[272,2048]{1,0:T(8,128)(2,1)}, bf16[272,2048]{1,0:T(8,128)(2,1)S(1)}, u32[]{:S(2)}, u32[]{:S(2)}) collective-permute-start(bf16[272,2048]{1,0:T(8,128)(2,1)} %get-tuple-element.139.refs_0_.refs_1_), channel_id=1, source_target_pairs={{0,2},{1,3},{2,0},{3,1},{4,6},{5,7},{6,4},{7,5},{8,10},{9,11},{10,... | collective-permute-start | bytes 3342344 | tf_op jit(solution)/shard_map/ppermute | solution.py:18
  229.6 11.8 %collective-permute-start.21 = (bf16[256,2048]{1,0:T(8,128)(2,1)}, bf16[256,2048]{1,0:T(8,128)(2,1)S(1)}, u32[]{:S(2)}, u32[]{:S(2)}) collective-permute-start(bf16[256,2048]{1,0:T(8,128)(2,1)} %get-tuple-element.135), channel_id=1, source_target_pairs={{0,1},{1,0},{2,3},{3,2},{4,5},{5,4},{6,7},{7,6},{8,9},{9,8},{10,11... | collective-permute-start | bytes 3145736 | tf_op jit(solution)/shard_map/ppermute | solution.py:18
  229.8 65.4 %collective-permute-start.33 = (bf16[1024,1408]{1,0:T(8,128)(2,1)}, bf16[1024,1408]{1,0:T(8,128)(2,1)}, u32[]{:S(2)}, u32[]{:S(2)}) collective-permute-start(bf16[1024,1408]{1,0:T(8,128)(2,1)} %product.7.refs_10_), channel_id=1, source_target_pairs={{0,8},{4,12},{8,0},{12,4},{16,24},{20,28},{24,16},{28,20},{1,9},{5... | collective-permute-start | bytes 8650760 | tf_op jit(solution)/shard_map/ppermute | solution.py:18
  256.4 13.4 %collective-permute-start.27 = (bf16[272,2048]{1,0:T(8,128)(2,1)}, bf16[272,2048]{1,0:T(8,128)(2,1)S(1)}, u32[]{:S(2)}, u32[]{:S(2)}) collective-permute-start(bf16[272,2048]{1,0:T(8,128)(2,1)} %hold.21.refs_11_.refs_0_.refs_3_), channel_id=1, source_target_pairs={{0,1},{1,0},{2,3},{3,2},{4,5},{5,4},{6,7},{7,6},{8,9},{9,8},{10,11... | collective-permute-start | bytes 3342344 | tf_op jit(solution)/shard_map/ppermute | solution.py:18
  286.0 65.6 %collective-permute-start.37 = (bf16[1024,1408]{1,0:T(8,128)(2,1)}, bf16[1024,1408]{1,0:T(8,128)(2,1)S(1)}, u32[]{:S(2)}, u32[]{:S(2)}) collective-permute-start(bf16[1024,1408]{1,0:T(8,128)(2,1)} %hold.22), channel_id=1, source_target_pairs={{0,4},{4,0},{8,12},{12,8},{16,20},{20,16},{24,28},{28,24},{1,5},{5... | collective-permute-start | bytes 8650760 | tf_op jit(solution)/shard_map/ppermute | solution.py:18
  287.5 16.6 %collective-permute-start.30 = (f32[2,4,512]{2,1,0:T(4,128)S(1)}, f32[2,4,512]{2,1,0:T(4,128)S(1)}, u32[]{:S(2)}, u32[]{:S(2)}) collective-permute-start(f32[2,4,512]{2,1,0:T(4,128)S(1)} %copy-done.38), channel_id=1, source_target_pairs={{8,0},{12,4},{16,8},{20,12},{24,16},{28,20},{9,1},{13,5},{17,9},{2... | collective-permute-start | bytes 49160 | tf_op jit(solution)/shard_map/ppermute | solution.py:24
  288.8 15.3 %collective-permute-start.31 = (f32[2,4,512]{2,1,0:T(4,128)S(1)}, f32[2,4,512]{2,1,0:T(4,128)S(1)}, u32[]{:S(2)}, u32[]{:S(2)}) collective-permute-start(f32[2,4,512]{2,1,0:T(4,128)S(1)} %copy-done.38), channel_id=1, source_target_pairs={{16,0},{20,4},{24,8},{28,12},{17,1},{21,5},{25,9},{29,13},{18,2},{... | collective-permute-start | bytes 49160 | tf_op jit(solution)/shard_map/ppermute | solution.py:24
  290.1 14.0 %collective-permute-start.32 = (f32[2,4,512]{2,1,0:T(4,128)S(1)}, f32[2,4,512]{2,1,0:T(4,128)S(1)}, u32[]{:S(2)}, u32[]{:S(2)}) collective-permute-start(f32[2,4,512]{2,1,0:T(4,128)S(1)} %copy-done.38), channel_id=1, source_target_pairs={{24,0},{28,4},{25,1},{29,5},{26,2},{30,6},{27,3},{31,7}} | collective-permute-start | bytes 49160 | tf_op jit(solution)/shard_map/ppermute | solution.py:24
  306.1 33.2 %collective-permute-start.38 = (bf16[512,1408]{1,0:T(8,128)(2,1)}, bf16[512,1408]{1,0:T(8,128)(2,1)}, u32[]{:S(2)}, u32[]{:S(2)}) collective-permute-start(bf16[512,1408]{1,0:T(8,128)(2,1)} %hold.23), channel_id=1, source_target_pairs={{0,8},{4,12},{8,0},{12,4},{16,24},{20,28},{24,16},{28,20},{1,9},{5... | collective-permute-start | bytes 4325384 | tf_op jit(solution)/shard_map/ppermute | solution.py:18
  334.3 27.5 %collective-permute-start.35 = (bf16[256,2048]{1,0:T(8,128)(2,1)}, bf16[256,2048]{1,0:T(8,128)(2,1)}, u32[]{:S(2)}, u32[]{:S(2)}) collective-permute-start(bf16[256,2048]{1,0:T(8,128)(2,1)} %get-tuple-element.161), channel_id=1, source_target_pairs={{0,1},{1,0},{2,3},{3,2},{4,5},{5,4},{6,7},{7,6},{8,9},{9,8},{10,11... | collective-permute-start | bytes 3145736 | tf_op jit(solution)/shard_map/ppermute | solution.py:18
  334.5 48.1 %collective-permute-start.41 = (bf16[512,1408]{1,0:T(8,128)(2,1)}, bf16[512,1408]{1,0:T(8,128)(2,1)}, u32[]{:S(2)}, u32[]{:S(2)}) collective-permute-start(bf16[512,1408]{1,0:T(8,128)(2,1)} %get-tuple-element.153.refs_6_), channel_id=1, source_target_pairs={{0,4},{4,0},{8,12},{12,8},{16,20},{20,16},{24,28},{28,24},{1,5},{5... | collective-permute-start | bytes 4325384 | tf_op jit(solution)/shard_map/ppermute | solution.py:18
  336.2 25.7 %collective-permute-start.36 = (bf16[256,2048]{1,0:T(8,128)(2,1)S(1)}, bf16[256,2048]{1,0:T(8,128)(2,1)}, u32[]{:S(2)}, u32[]{:S(2)}) collective-permute-start(bf16[256,2048]{1,0:T(8,128)(2,1)S(1)} %copy-done.21), channel_id=1, source_target_pairs={{0,2},{1,3},{2,0},{3,1},{4,6},{5,7},{6,4},{7,5},{8,10},{9,11},{10,... | collective-permute-start | bytes 3145736 | tf_op jit(solution)/shard_map/ppermute | solution.py:18
  348.8 78.8 %collective-permute-start.44 = (bf16[1024,1024]{1,0:T(8,128)(2,1)}, bf16[1024,1024]{1,0:T(8,128)(2,1)}, u32[]{:S(2)}, u32[]{:S(2)}) collective-permute-start(bf16[1024,1024]{1,0:T(8,128)(2,1)} %product.9.refs_11_), channel_id=1, source_target_pairs={{0,4},{4,0},{8,12},{12,8},{16,20},{20,16},{24,28},{28,24},{1,5},{5... | collective-permute-start | bytes 6291464 | tf_op jit(solution)/shard_map/ppermute | solution.py:18
  361.8 44.3 %collective-permute-start.40 = (bf16[512,1408]{1,0:T(8,128)(2,1)}, bf16[512,1408]{1,0:T(8,128)(2,1)S(1)}, u32[]{:S(2)}, u32[]{:S(2)}) collective-permute-start(bf16[512,1408]{1,0:T(8,128)(2,1)} %get-tuple-element.167.refs_6_), channel_id=1, source_target_pairs={{0,8},{4,12},{8,0},{12,4},{16,24},{20,28},{24,16},{28,20},{1,9},{5... | collective-permute-start | bytes 4325384 | tf_op jit(solution)/shard_map/ppermute | solution.py:18
  361.9 36.0 %collective-permute-start.25 = (bf16[256,2048]{1,0:T(8,128)(2,1)}, bf16[256,2048]{1,0:T(8,128)(2,1)S(1)}, u32[]{:S(2)}, u32[]{:S(2)}) collective-permute-start(bf16[256,2048]{1,0:T(8,128)(2,1)} %get-tuple-element.144), channel_id=1, source_target_pairs={{0,1},{1,0},{2,3},{3,2},{4,5},{5,4},{6,7},{7,6},{8,9},{9,8},{10,11... | collective-permute-start | bytes 3145736 | tf_op jit(solution)/shard_map/ppermute | solution.py:18
  367.4 43.0 %collective-permute-start.39 = (bf16[256,2048]{1,0:T(8,128)(2,1)}, bf16[256,2048]{1,0:T(8,128)(2,1)}, u32[]{:S(2)}, u32[]{:S(2)}) collective-permute-start(bf16[256,2048]{1,0:T(8,128)(2,1)} %hold.24), channel_id=1, source_target_pairs={{0,2},{1,3},{2,0},{3,1},{4,6},{5,7},{6,4},{7,5},{8,10},{9,11},{10,... | collective-permute-start | bytes 3145736 | tf_op jit(solution)/shard_map/ppermute | solution.py:18
  382.6 32.1 %collective-permute-start.45 = (bf16[256,1408]{1,0:T(8,128)(2,1)}, bf16[256,1408]{1,0:T(8,128)(2,1)}, u32[]{:S(2)}, u32[]{:S(2)}) collective-permute-start(bf16[256,1408]{1,0:T(8,128)(2,1)} %get-tuple-element.166.refs_7_), channel_id=1, source_target_pairs={{0,16},{4,20},{8,24},{12,28},{16,0},{20,4},{24,8},{28,12},{1,17},{... | collective-permute-start | bytes 2162696 | tf_op jit(solution)/shard_map/ppermute | solution.py:18
  397.9 52.1 %collective-permute-start.43 = (bf16[1024,512]{1,0:T(8,128)(2,1)S(1)}, bf16[1024,512]{1,0:T(8,128)(2,1)}, u32[]{:S(2)}, u32[]{:S(2)}) collective-permute-start(bf16[1024,512]{1,0:T(8,128)(2,1)S(1)} %copy-done.20), channel_id=1, source_target_pairs={{0,4},{4,0},{8,12},{12,8},{16,20},{20,16},{24,28},{28,24},{1,5},{5... | collective-permute-start | bytes 3145736 | tf_op jit(solution)/shard_map/ppermute | solution.py:18
  406.1 63.5 %collective-permute-start.42 = (bf16[1024,512]{1,0:T(8,128)(2,1)}, bf16[1024,512]{1,0:T(8,128)(2,1)S(1)}, u32[]{:S(2)}, u32[]{:S(2)}) collective-permute-start(bf16[1024,512]{1,0:T(8,128)(2,1)} %product.11.refs_2_), channel_id=1, source_target_pairs={{0,4},{4,0},{8,12},{12,8},{16,20},{20,16},{24,28},{28,24},{1,5},{5... | collective-permute-start | bytes 3145736 | tf_op jit(solution)/shard_map/ppermute | solution.py:18
  434.6 42.4 %collective-permute-start.48 = (bf16[512,1024]{1,0:T(8,128)(2,1)}, bf16[512,1024]{1,0:T(8,128)(2,1)S(1)}, u32[]{:S(2)}, u32[]{:S(2)}) collective-permute-start(bf16[512,1024]{1,0:T(8,128)(2,1)} %get-tuple-element.176.refs_8_), channel_id=1, source_target_pairs={{0,8},{4,12},{8,0},{12,4},{16,24},{20,28},{24,16},{28,20},{1,9},{5... | collective-permute-start | bytes 3145736 | tf_op jit(solution)/shard_map/ppermute | solution.py:18
  434.6 41.7 %collective-permute-start.49 = (bf16[256,1408]{1,0:T(8,128)(2,1)}, bf16[256,1408]{1,0:T(8,128)(2,1)}, u32[]{:S(2)}, u32[]{:S(2)}) collective-permute-start(bf16[256,1408]{1,0:T(8,128)(2,1)} %get-tuple-element.173.refs_7_), channel_id=1, source_target_pairs={{0,16},{4,20},{8,24},{12,28},{16,0},{20,4},{24,8},{28,12},{1,17},{... | collective-permute-start | bytes 2162696 | tf_op jit(solution)/shard_map/ppermute | solution.py:18
  438.7 59.0 %collective-permute-start.47 = (bf16[256,1408]{1,0:T(8,128)(2,1)}, bf16[256,1408]{1,0:T(8,128)(2,1)}, u32[]{:S(2)}, u32[]{:S(2)}) collective-permute-start(bf16[256,1408]{1,0:T(8,128)(2,1)} %get-tuple-element.174.refs_4_), channel_id=1, source_target_pairs={{0,16},{4,20},{8,24},{12,28},{16,0},{20,4},{24,8},{28,12},{1,17},{... | collective-permute-start | bytes 2162696 | tf_op jit(solution)/shard_map/ppermute | solution.py:18
  476.0 34.2 %collective-permute-start.46 = (bf16[512,512]{1,0:T(8,128)(2,1)}, bf16[512,512]{1,0:T(8,128)(2,1)S(1)}, u32[]{:S(2)}, u32[]{:S(2)}) collective-permute-start(bf16[512,512]{1,0:T(8,128)(2,1)} %get-tuple-element.179.refs_0_), channel_id=1, source_target_pairs={{0,8},{4,12},{8,0},{12,4},{16,24},{20,28},{24,16},{28,20},{1,9},{5... | collective-permute-start | bytes 1572872 | tf_op jit(solution)/shard_map/ppermute | solution.py:18
  476.1 7.5 %collective-permute-start.54 = (f32[2,512]{1,0:T(2,128)S(1)}, f32[2,512]{1,0:T(2,128)S(1)}, u32[]{:S(2)}, u32[]{:S(2)}) collective-permute-start(f32[2,512]{1,0:T(2,128)S(1)} %get-tuple-element.196), channel_id=1, source_target_pairs={{0,1},{1,0},{2,3},{3,2},{4,5},{5,4},{6,7},{7,6},{8,9},{9,8},{10,11... | collective-permute-start | bytes 12296 | tf_op jit(solution)/shard_map/ppermute | solution.py:18
  476.2 12.0 %collective-permute-start.55 = (f32[2,512]{1,0:T(2,128)S(1)}, f32[2,512]{1,0:T(2,128)S(1)}, u32[]{:S(2)}, u32[]{:S(2)}) collective-permute-start(f32[2,512]{1,0:T(2,128)S(1)} %get-tuple-element.197), channel_id=1, source_target_pairs={{0,2},{1,3},{2,0},{3,1},{4,6},{5,7},{6,4},{7,5},{8,10},{9,11},{10,... | collective-permute-start | bytes 12296 | tf_op jit(solution)/shard_map/ppermute | solution.py:18
  476.9 15.2 %collective-permute-start.56 = (f32[2,512]{1,0:T(2,128)S(1)}, f32[2,512]{1,0:T(2,128)S(1)}, u32[]{:S(2)}, u32[]{:S(2)}) collective-permute-start(f32[2,512]{1,0:T(2,128)S(1)} %get-tuple-element.198), channel_id=1, source_target_pairs={{0,3},{1,2},{2,1},{3,0},{4,7},{5,6},{6,5},{7,4},{8,11},{9,10},{10,... | collective-permute-start | bytes 12296 | tf_op jit(solution)/shard_map/ppermute | solution.py:18
  483.6 37.9 %collective-permute-start.52 = (bf16[512,512]{1,0:T(8,128)(2,1)S(1)}, bf16[512,512]{1,0:T(8,128)(2,1)S(1)}, u32[]{:S(2)}, u32[]{:S(2)}) collective-permute-start(bf16[512,512]{1,0:T(8,128)(2,1)S(1)} %copy-done.35), channel_id=1, source_target_pairs={{0,8},{4,12},{8,0},{12,4},{16,24},{20,28},{24,16},{28,20},{1,9},{5... | collective-permute-start | bytes 1572872 | tf_op jit(solution)/shard_map/ppermute | solution.py:18
  488.2 37.5 %collective-permute-start.51 = (bf16[256,1024]{1,0:T(8,128)(2,1)}, bf16[256,1024]{1,0:T(8,128)(2,1)S(1)}, u32[]{:S(2)}, u32[]{:S(2)}) collective-permute-start(bf16[256,1024]{1,0:T(8,128)(2,1)} %get-tuple-element.183.refs_1_), channel_id=1, source_target_pairs={{0,16},{4,20},{8,24},{12,28},{16,0},{20,4},{24,8},{28,12},{1,17},{... | collective-permute-start | bytes 1572872 | tf_op jit(solution)/shard_map/ppermute | solution.py:18
  513.2 24.7 %collective-permute-start.50 = (bf16[256,512]{1,0:T(8,128)(2,1)}, bf16[256,512]{1,0:T(8,128)(2,1)S(1)}, u32[]{:S(2)}, u32[]{:S(2)}) collective-permute-start(bf16[256,512]{1,0:T(8,128)(2,1)} %get-tuple-element.185.refs_2_), channel_id=1, source_target_pairs={{0,16},{4,20},{8,24},{12,28},{16,0},{20,4},{24,8},{28,12},{1,17},{... | collective-permute-start | bytes 786440 | tf_op jit(solution)/shard_map/ppermute | solution.py:18
  517.2 24.5 %collective-permute-start.57 = (f32[4,512]{1,0:T(4,128)S(1)}, f32[4,512]{1,0:T(4,128)S(1)}, u32[]{:S(2)}, u32[]{:S(2)}) collective-permute-start(f32[4,512]{1,0:T(4,128)S(1)} %pad_maximum_fusion), channel_id=1, source_target_pairs={{0,4},{4,0},{8,12},{12,8},{16,20},{20,16},{24,28},{28,24},{1,5},{5... | collective-permute-start | bytes 24584 | tf_op jit(solution)/shard_map/ppermute | solution.py:18
  524.5 23.7 %collective-permute-start.53 = (bf16[256,512]{1,0:T(8,128)(2,1)}, bf16[256,512]{1,0:T(8,128)(2,1)S(1)}, u32[]{:S(2)}, u32[]{:S(2)}) collective-permute-start(bf16[256,512]{1,0:T(8,128)(2,1)} %get-tuple-element.188.refs_0_), channel_id=1, source_target_pairs={{0,16},{4,20},{8,24},{12,28},{16,0},{20,4},{24,8},{28,12},{1,17},{... | collective-permute-start | bytes 786440 | tf_op jit(solution)/shard_map/ppermute | solution.py:18
  (71 other events, 186.8 us)

commit v4 on v3

--- a/solution.py
+++ b/solution.py
@@ -41,7 +41,7 @@
 
 ANYWHERE = pl.BlockSpec(memory_space=pl.ANY)
 EXTRA = 16
-VMEM_LIMIT = 60 * 1024 * 1024
+VMEM_LIMIT = 63 * 1024 * 1024
 
 
 def sds(shape, dtype=F32):
@@ -312,7 +312,7 @@
         "feed",
         (pl.cdiv(units, tile),),
         [
-            *[fixed(x) for x in pieces],
+            *[(x, (min(x.shape[0], rows) // 128 * 128, width), lambda n: (0, 0)) for x in pieces],
             (gate_up, (2, width, tile), lambda n: (0, 0, n)),
             (gh, *col),
         ],
@@ -763,7 +763,7 @@
         out_specs=[part, part, pl.BlockSpec((rows, 128), lambda i: (half, 0)), part, alone],
         out_shape=[
             sds((total, width)), sds((total, width)), sds((total, 128)), sds((total, width), BF),
-            sds((rows, width), BF),
+            sds((rows + (16 if half == 0 else 0), width), BF),
         ],
         input_output_aliases={8 + n: n for n in range(len(begun))},
         compiler_params=pltpu.CompilerParams(vmem_limit_bytes=VMEM_LIMIT),
@@ -933,8 +933,8 @@
 
 GATE_AT, LOWER_AT, UP_AT, LOWER_BITS = "before", "beside", "pair", "m"
 ORDER = (
-    ("-p", "-n", "gs", "bb", "us", "-l", "ob", "ls", "ab", "us", "-r", "gf")
-    + ("bs", "os", "as", "lf", "bs", "uf", "as", "os", "bf", "af", "-t", "of")
+    ("-p", "-n", "gs", "bb", "us", "-l", "ob", "ls", "ab", "us", "-r", "gf", "bs")
+    + ("os", "as", "lf", "bs", "uf", "as", "os", "bf", "-1", "af", "-2", "-3", "of")
 )
 
 
@@ -976,10 +976,10 @@
     n2 = after(hop, gh_n)
     n3 = swap(n2, "wt", 1)
     pi_f, pf_f, pg_f, loc_f, cum_f, tot = project(n2, n3, in_proj, lower_use, (tot,))
-    g2 = after(grad_hop, tot)
+    enter = chain(me, tot, False)
+    state_f, bf0, bf1 = mix(loc_f, cum_f, pg_f, enter, 2, mixer_use, out_proj)
+    g2 = after(grad_hop, bf0)
     g3 = swap(g2, "wt", 1)
-    enter = chain(me, tot, False, lambda: (g2,))
-    state_f, bf0, bf1 = mix(loc_f, cum_f, pg_f, enter, 2, mixer_use, out_proj)
     state_n, bn0, bn1 = mix(loc_n, cum_n, pg_n, enter, 0, mixer_use, out_proj, after=(bf0,))
     across = join(bf0, swap(bf1, "wt", 1), after=(bn0,))
     hops = [swap(part, "wt", 2) for part in across]
@@ -991,17 +991,16 @@
     )
 
     hops = [swap(half, "wt", 2) for half in (half0, half1)]
-    t2 = [after(hops[0], t0)]
-    t1 = [after(swap(half, "wt", 1), t2[0]) for half in (half0, half1)]
+    t1 = [swap(half, "wt", 1) for half in (half0, half1)]
     hid_n, gg_n, gu_n = feed((t0, *t1), gate_up, gh_n)
     kn0, kn1 = feed_back(gg_n, gu_n, gate_up)
     core = swap(kn1, "wt", 1)
-    t2.append(after(hops[1], kn0))
+    t2 = [after(hop, kn0) for hop in hops]
     t3 = [swap(half, "wt", 1) for half in t2]
     hid_f, gg_f, gu_f = feed((*t2, *t3), gate_up, gh_f)
 
     def pieces(*arrays):
-        return [(v, min(rows, v.shape[0])) for v in arrays]
+        return [(v, min(rows, v.shape[0]) // 128 * 128) for v in arrays]
 
     twos = (pieces(t0, *t1), pieces(*t2, *t3))
     gate = Weight(me, twos, gg_n, gg_f, y_first, block)
@@ -1086,15 +1085,18 @@
             elif kind in "gu":
                 slot = "gu".index(kind)
                 token = gate_up_grad = finish(
-                    one.keep, one.got, slot=slot, slots=2, into=gate_up_grad, after=(token,)
+                    one.keep, one.got, slot=slot, slots=2, into=gate_up_grad,
+                    after=() if token is gate_up_grad else (token,),
                 )
             elif kind == "b":
                 token = in_grad = finish(
-                    one.keep, one.got, parts=2, slots=3, into=in_grad, after=(token,)
+                    one.keep, one.got, parts=2, slots=3, into=in_grad,
+                    after=() if token is in_grad else (token,),
                 )
             elif kind == "a":
                 token = in_grad = finish(
-                    one.keep, one.got, slot=2, slots=3, into=in_grad, after=(token,)
+                    one.keep, one.got, slot=2, slots=3, into=in_grad,
+                    after=() if token is in_grad else (token,),
                 )
             elif kind == "l":
                 token = down_grad = finish(one.keep, one.got, True, after=(token,))
@@ -1129,9 +1131,9 @@
                 result_kernel, "result", [middle, fn0, ffn_core, ffn_hop], [], [(x.shape, BF)],
                 after=(token,),
             )
-        elif act == "t":
-            for bit in rounds:
-                gains = gains + after(swap(gains, "seq", bit), token)
+        elif act in "123":
+            for _ in range(len(rounds) if act == "3" else 1):
+                gains = gains + after(swap(gains, "seq", rounds.pop(0)), token)
 
     return (
         result[None],

time: 562 us -> 537 us (0.956)
  local copies, waits for them, and re-layouts: 36.7 us -> 13 us
    unnamed x120 -> x55, local copies, waits for them, and re-layouts: 33.4 us -> 9.69 us
  transfers between devices with their start and end apart: 60 -> 60, of which waited for: 30 -> 30; matrix products, arithmetic and copies ran while one was open for 1% -> 1% of each run, Pallas kernels for 50% -> 54%
where the time goes in v4:
time: 537 us; the launch traced here: 530 us
  Pallas kernels  311 us (58%)
  waiting for transfers between devices  132 us (25%)
  starting transfers between devices  70.1 us (13%)
  local copies, waits for them, and re-layouts  13 us (2%)
    pallas_call x30, Pallas kernels, call(): pl.pallas_call(body, grid=grid, in_specs=in_specs, out_specs=out_specs, s...  198 us
    ppermute x54, waiting for transfers between devices, swap(): return lax.ppermute(values, axis, [(i, i ^ bit) for i in range(size)])  132 us
    pallas_call x16, Pallas kernels, call(): got = pl.pallas_call(body, grid_spec=spec, **settings)(blocks, *operands)  88.2 us
    ppermute x54, starting transfers between devices, swap(): return lax.ppermute(values, axis, [(i, i ^ bit) for i in range(size)])  56.6 us
    pallas_call x6, Pallas kernels, finish(): pl.pallas_call(lambda one, two, *refs: finish_kernel(turned, one, two, *r...  18.2 us
    ppermute x6, starting transfers between devices, shift(): return lax.ppermute(values, axis, pairs)  13.5 us
  transfers between devices with their start and end apart: 60, of which 30 were waited for; matrix products, arithmetic and copies ran while one was open for 1% of the time, Pallas kernels for 54%

profile of v4, /device:TPU:0, one launch (start us, length us, event | category | flops | bytes accessed | tf_op | source)
XLA Modules:
  0.0 530.0 jit_solution(17316884273452381491)
XLA Ops:
  9.1 11.0 %project.2 = (f32[2,256,512]{2,1,0:T(8,128)}, f32[2,256,512]{2,1,0:T(8,128)}, f32[2,256,512]{2,1,0:T(8,128)}, f32[2,256,512]{2,1,0:T(8,128)}, f32[2,256,512]{2,1,0:T(8,128)}, /*index=5*/f32[2,2,512]{2,1,0:T(2,128)}) custom-call(bf16[256,2048]{1,0:T(8,128)(2,1)} %first_norm.1.refs_0_.refs_1_, bf16[256,2048]{1,0:T(8,128)(2,1)} %collective-permute-done.refs_1_.refs_2_, ...), custom_call_target="tpu_custom_call" | custom-call | tf_op jit(solution)/shard_map/project/pallas_call | solution.py:70
  20.1 7.4 %hidden_grad.2.refs_1_.refs_4_ = f32[512,1408]{1,0:T(8,128)} custom-call(bf16[256,2048]{1,0:T(8,128)(2,1)} %bitcast.21, bf16[256,2048]{1,0:T(8,128)(2,1)} %collective-permute-done.2.refs_1_.refs_2_, bf16[1408,2048]{1,0:T(8,128)(2,1)} %refs_1_.3, f32[2,2,512]{2,1,0:T(2,128)} %get-tuple-element.106.refs_3_.refs_4_), custom_call_target="tpu_custom_call" | custom-call | tf_op jit(solution)/shard_map/hidden_grad/pallas_call | solution.py:70
  34.4 11.6 %project.3 = (f32[2,256,512]{2,1,0:T(8,128)}, f32[2,256,512]{2,1,0:T(8,128)}, f32[2,256,512]{2,1,0:T(8,128)}, f32[2,256,512]{2,1,0:T(8,128)}, f32[2,256,512]{2,1,0:T(8,128)}, /*index=5*/f32[2,4,512]{2,1,0:T(4,128)}) custom-call(bf16[256,2048]{1,0:T(8,128)(2,1)} %hold.12.refs_0_.refs_3_, bf16[256,2048]{1,0:T(8,128)(2,1)} %collective-permute-done.3.refs_1_.refs_4_, ...), custom_call_target="tpu_custom_call" | custom-call | tf_op jit(solution)/shard_map/project/pallas_call | solution.py:70
  55.7 4.5 collective-permute-start.6
  65.6 5.6 %mix.2 = (f32[2,256,512]{2,1,0:T(8,128)}, bf16[272,2048]{1,0:T(8,128)(2,1)}, bf16[272,2048]{1,0:T(8,128)(2,1)}) custom-call(f32[2,256,512]{2,1,0:T(8,128)} %get-tuple-element.108.refs_0_, f32[2,256,512]{2,1,0:T(8,128)} %get-tuple-element.109.refs_1_, f32[2,256,512]{2,1,0:T(8,128)} %get-tuple-element.110.refs_2_.refs_3_, f32[4,1,512]{2,1,0:T(1,128)} %enter.2.refs_3_.refs_7_, ...), custom_call_target="tpu_custom_call" | custom-call | tf_op jit(solution)/shard_map/mix/pallas_call | solution.py:70
  71.3 5.6 %mix.3 = (f32[2,256,512]{2,1,0:T(8,128)}, bf16[272,2048]{1,0:T(8,128)(2,1)}, bf16[272,2048]{1,0:T(8,128)(2,1)}) custom-call(f32[2,256,512]{2,1,0:T(8,128)} %get-tuple-element.103.refs_0_, f32[2,256,512]{2,1,0:T(8,128)} %get-tuple-element.104.refs_1_, f32[2,256,512]{2,1,0:T(8,128)} %get-tuple-element.105.refs_2_.refs_3_, f32[4,1,512]{2,1,0:T(1,128)} %enter.2.refs_3_.refs_7_, ...), custom_call_target="tpu_custom_call" | custom-call | tf_op jit(solution)/shard_map/mix/pallas_call | solution.py:70
  82.4 7.5 %hidden_grad.3.refs_0_.refs_5_ = f32[512,1408]{1,0:T(8,128)} custom-call(bf16[256,2048]{1,0:T(8,128)(2,1)} %hold.14.refs_0_.refs_3_, bf16[256,2048]{1,0:T(8,128)(2,1)} %collective-permute-done.13.refs_1_.refs_4_, bf16[1408,2048]{1,0:T(8,128)(2,1)} %refs_1_.3, bf16[128,2048]{1,0:T(8,128)(2,1)} %get-tuple-element.115.refs_3_), custom_call_target="tpu_custom_call" | custom-call | tf_op jit(solution)/shard_map/hidden_grad/pallas_call | solution.py:70
  89.9 6.8 %collective-permute-done.11.hop.hop_more = bf16[144,2048]{1,0:T(8,128)(2,1)S(1)} collective-permute-done((bf16[144,2048]{1,0:T(8,128)(2,1)}, bf16[144,2048]{1,0:T(8,128)(2,1)S(1)}, u32[]{:S(2)}, u32[]{:S(2)}) %collective-permute-start.11) | collective-permute-done | bytes 589856 | tf_op jit(solution)/shard_map/ppermute | solution.py:18
  102.7 5.4 %collective-permute-done.10.hop = bf16[128,2048]{1,0:T(8,128)(2,1)} collective-permute-done((bf16[128,2048]{1,0:T(8,128)(2,1)}, bf16[128,2048]{1,0:T(8,128)(2,1)}, u32[]{:S(2)}, u32[]{:S(2)}) %collective-permute-start.10) | collective-permute-done | bytes 524320 | tf_op jit(solution)/shard_map/ppermute | solution.py:18
  113.9 12.0 %feed.2 = (bf16[512,1408]{1,0:T(8,128)(2,1)}, bf16[512,1408]{1,0:T(8,128)(2,1)}, bf16[512,1408]{1,0:T(8,128)(2,1)}) custom-call(bf16[256,2048]{1,0:T(8,128)(2,1)} %get-tuple-element.122.refs_0_.refs_1_, bf16[144,2048]{1,0:T(8,128)(2,1)} %collective-permute-done.14.refs_1_.refs_2_, bf16[128,2048]{1,0:T(8,128)(2,1)} %collective-permute-done.15.refs_2_.refs_3_, ...), custom_call_target="tpu_custom_call" | custom-call | tf_op jit(solution)/shard_map/feed/pallas_call | solution.py:70
  125.9 10.9 %feed_back.2 = (bf16[256,2048]{1,0:T(8,128)(2,1)}, bf16[256,2048]{1,0:T(8,128)(2,1)}) custom-call(bf16[512,1408]{1,0:T(8,128)(2,1)} %get-tuple-element.126.refs_0_.refs_8_, bf16[512,1408]{1,0:T(8,128)(2,1)} %get-tuple-element.127.refs_1_.refs_8_, bf16[2,2048,1408]{2,1,0:T(8,128)(2,1)} %refs_2_.13), custom_call_target="tpu_custom_call" | custom-call | tf_op jit(solution)/shard_map/feed_back/pallas_call | solution.py:70
  141.6 12.0 %feed.3 = (bf16[512,1408]{1,0:T(8,128)(2,1)}, bf16[512,1408]{1,0:T(8,128)(2,1)}, bf16[512,1408]{1,0:T(8,128)(2,1)}) custom-call(bf16[144,2048]{1,0:T(8,128)(2,1)} %hold.15.refs_0_.refs_4_, bf16[128,2048]{1,0:T(8,128)(2,1)} %hold.16.refs_1_.refs_5_, bf16[144,2048]{1,0:T(8,128)(2,1)} %copy-done.2, bf16[128,2048]{1,0:T(8,128)(2,1)} %collective-permute-done.19.refs_3_.refs_7_, ...), custom_call_target="tpu_custom_call" | custom-call | tf_op jit(solution)/shard_map/feed/pallas_call | solution.py:70
  153.6 10.9 %feed_back.3 = (bf16[256,2048]{1,0:T(8,128)(2,1)}, bf16[256,2048]{1,0:T(8,128)(2,1)}) custom-call(bf16[512,1408]{1,0:T(8,128)(2,1)} %get-tuple-element.131.refs_0_.refs_9_, bf16[512,1408]{1,0:T(8,128)(2,1)} %get-tuple-element.130.refs_1_.refs_9_, bf16[2,2048,1408]{2,1,0:T(8,128)(2,1)} %refs_2_.13), custom_call_target="tpu_custom_call" | custom-call | tf_op jit(solution)/shard_map/feed_back/pallas_call | solution.py:70
  165.0 7.7 %product.6.refs_2_ = bf16[1024,1408]{1,0:T(8,128)(2,1)} custom-call(s32[1]{0:T(128)} %bitcast.3.refs_0_, bf16[256,2048]{1,0:T(8,128)(2,1)} %get-tuple-element.122.refs_0_.refs_1_, bf16[144,2048]{1,0:T(8,128)(2,1)} %collective-permute-done.14.refs_1_.refs_2_, bf16[128,2048]{1,0:T(8,128)(2,1)} %collective-permute-done.15.refs_2_.refs_3_, ...), custom_call_target="tpu_custom_call" | custom-call | tf_op jit(solution)/shard_map/product/pallas_call | solution.py:81
  179.4 7.4 %product.7.refs_10_ = bf16[1024,1408]{1,0:T(8,128)(2,1)} custom-call(s32[1]{0:T(128)} %bitcast.3.refs_0_, bf16[256,2048]{1,0:T(8,128)(2,1)} %bitcast.22, bf16[256,2048]{1,0:T(8,128)(2,1)} %collective-permute-done.2.refs_1_.refs_2_, bf16[256,2048]{1,0:T(8,128)(2,1)} %hold.14.refs_0_.refs_3_, bf16[256,2048]{1,0:T(8,128)(2,1)} %collective-permute-done.13.refs_1_.refs_4_, ...), custom_call_target="tpu_custom_call" | custom-call | tf_op jit(solution)/shard_map/product/pallas_call | solution.py:81
  186.8 7.5 %product.8.refs_2_.refs_0_ = bf16[1024,1408]{1,0:T(8,128)(2,1)} custom-call(s32[1]{0:T(128)} %bitcast.3.refs_0_, bf16[256,2048]{1,0:T(8,128)(2,1)} %get-tuple-element.122.refs_0_.refs_1_, bf16[144,2048]{1,0:T(8,128)(2,1)} %collective-permute-done.14.refs_1_.refs_2_, bf16[128,2048]{1,0:T(8,128)(2,1)} %collective-permute-done.15.refs_2_.refs_3_, ...), custom_call_target="tpu_custom_call" | custom-call | tf_op jit(solution)/shard_map/product/pallas_call | solution.py:81
  194.3 7.2 %feed_out.2 = (bf16[256,2048]{1,0:T(8,128)(2,1)}, bf16[256,2048]{1,0:T(8,128)(2,1)}) custom-call(bf16[512,1408]{1,0:T(8,128)(2,1)} %get-tuple-element.129.refs_6_.refs_0_, bf16[1408,2048]{1,0:T(8,128)(2,1)} %refs_1_.3, bf16[1024,1408]{1,0:T(8,128)(2,1)} %product.8.refs_2_.refs_0_), custom_call_target="tpu_custom_call" | custom-call | tf_op jit(solution)/shard_map/feed_out/pallas_call | solution.py:70
  201.9 6.3 %turn.1 = (f32[256,2048]{1,0:T(8,128)}, f32[1,2048]{1,0:T(1,128)}, bf16[272,2048]{1,0:T(8,128)(2,1)}) custom-call(bf16[256,2048]{1,0:T(8,128)(2,1)} %bitcast.23, bf16[256,2048]{1,0:T(8,128)(2,1)} %get-tuple-element.128.refs_1_, bf16[256,2048]{1,0:T(8,128)(2,1)} %collective-permute-done.22.refs_2_, bf16[256,2048]{1,0:T(8,128)(2,1)} %collective-permute-done.23.refs_3_, ...), custom_call_target="tpu_custom_call" | custom-call | tf_op jit(solution)/shard_map/turn/pallas_call | solution.py:70
  211.4 9.2 %back_local.2 = (bf16[2,256,512]{2,1,0:T(8,128)(2,1)}, bf16[2,256,512]{2,1,0:T(8,128)(2,1)}, f32[2,256,512]{2,1,0:T(8,128)}, f32[2,256,512]{2,1,0:T(8,128)}, f32[2,2,512]{2,1,0:T(2,128)}, /*index=5*/f32[1,512]{1,0:T(1,128)}) custom-call(bf16[272,2048]{1,0:T(8,128)(2,1)} %get-tuple-element.139.refs_0_.refs_1_, ...), custom_call_target="tpu_custom_call" | custom-call | tf_op jit(solution)/shard_map/back_local/pallas_call | solution.py:70
  224.2 7.1 %feed_out.3 = (bf16[256,2048]{1,0:T(8,128)(2,1)}, bf16[256,2048]{1,0:T(8,128)(2,1)}) custom-call(bf16[512,1408]{1,0:T(8,128)(2,1)} %get-tuple-element.125.refs_5_.refs_0_, bf16[1408,2048]{1,0:T(8,128)(2,1)} %refs_1_.3, bf16[256,2048]{1,0:T(8,128)(2,1)} %plus.4.refs_2_.refs_0_), custom_call_target="tpu_custom_call" | custom-call | tf_op jit(solution)/shard_map/feed_out/pallas_call | solution.py:70
  231.3 4.3 collective-permute-done.26.refs_0_
  235.6 6.8 %collective-permute-done.28.refs_10_ = bf16[1024,1408]{1,0:T(8,128)(2,1)} collective-permute-done((bf16[1024,1408]{1,0:T(8,128)(2,1)}, bf16[1024,1408]{1,0:T(8,128)(2,1)}, u32[]{:S(2)}, u32[]{:S(2)}) %collective-permute-start.28) | collective-permute-done | bytes 2883616 | tf_op jit(solution)/shard_map/ppermute | solution.py:18
  242.4 8.6 %product_add.6 = (bf16[512,1408]{1,0:T(8,128)(2,1)}, bf16[512,1408]{1,0:T(8,128)(2,1)}) custom-call(s32[1]{0:T(128)} %bitcast.3.refs_0_, bf16[256,2048]{1,0:T(8,128)(2,1)} %get-tuple-element.122.refs_0_.refs_1_, bf16[144,2048]{1,0:T(8,128)(2,1)} %collective-permute-done.14.refs_1_.refs_2_, bf16[128,2048]{1,0:T(8,128)(2,1)} %collective-permute-done.15.refs_2_.refs_3_, ...), custom_call_target="tpu_custom_call" | custom-call | tf_op jit(solution)/shard_map/product_add/pallas_call | solution.py:81
  251.0 9.2 %back_local.3 = (bf16[2,256,512]{2,1,0:T(8,128)(2,1)}, bf16[2,256,512]{2,1,0:T(8,128)(2,1)}, f32[2,256,512]{2,1,0:T(8,128)}, f32[2,256,512]{2,1,0:T(8,128)}, f32[2,4,512]{2,1,0:T(4,128)}, /*index=5*/f32[1,512]{1,0:T(1,128)}) custom-call(bf16[272,2048]{1,0:T(8,128)(2,1)} %hold.17.refs_11_.refs_0_.refs_3_, ...), custom_call_target="tpu_custom_call" | custom-call | tf_op jit(solution)/shard_map/back_local/pallas_call | solution.py:70
  271.5 3.9 collective-permute-done.33.refs_7_
  275.4 8.9 %product_add.7 = (bf16[512,1408]{1,0:T(8,128)(2,1)}, bf16[512,1408]{1,0:T(8,128)(2,1)}) custom-call(s32[1]{0:T(128)} %bitcast.3.refs_0_, bf16[256,2048]{1,0:T(8,128)(2,1)} %bitcast.24, bf16[256,2048]{1,0:T(8,128)(2,1)} %collective-permute-done.2.refs_1_.refs_2_, bf16[256,2048]{1,0:T(8,128)(2,1)} %hold.14.refs_0_.refs_3_, ...), custom_call_target="tpu_custom_call" | custom-call | tf_op jit(solution)/shard_map/product_add/pallas_call | solution.py:81
  286.4 10.3 %back_mix.2 = (bf16[2,256,1024]{2,1,0:T(8,128)(2,1)}, bf16[256,2048]{1,0:T(8,128)(2,1)}, bf16[256,2048]{1,0:T(8,128)(2,1)}, f32[2,1,512]{2,1,0:T(1,128)}) custom-call(f32[2,256,512]{2,1,0:T(8,128)} %get-tuple-element.154.refs_0_, f32[2,256,512]{2,1,0:T(8,128)} %get-tuple-element.155.refs_1_, f32[2,256,512]{2,1,0:T(8,128)} %get-tuple-element.150.refs_5_.refs_2_, ...), custom_call_target="tpu_custom_call" | custom-call | tf_op jit(solution)/shard_map/back_mix/pallas_call | solution.py:70
  303.3 10.3 %back_mix.3 = (bf16[2,256,1024]{2,1,0:T(8,128)(2,1)}, bf16[256,2048]{1,0:T(8,128)(2,1)}, bf16[256,2048]{1,0:T(8,128)(2,1)}, f32[2,1,512]{2,1,0:T(1,128)}) custom-call(f32[2,256,512]{2,1,0:T(8,128)} %get-tuple-element.145.refs_0_, f32[2,256,512]{2,1,0:T(8,128)} %get-tuple-element.146.refs_1_, f32[2,256,512]{2,1,0:T(8,128)} %get-tuple-element.141.refs_5_.refs_2_, ...), custom_call_target="tpu_custom_call" | custom-call | tf_op jit(solution)/shard_map/back_mix/pallas_call | solution.py:70
  322.7 6.2 %product.9.refs_11_ = bf16[1024,1024]{1,0:T(8,128)(2,1)} custom-call(s32[1]{0:T(128)} %bitcast.3.refs_0_, bf16[256,2048]{1,0:T(8,128)(2,1)} %first_norm.1.refs_0_.refs_1_, bf16[256,2048]{1,0:T(8,128)(2,1)} %collective-permute-done.refs_1_.refs_2_, bf16[256,2048]{1,0:T(8,128)(2,1)} %hold.12.refs_0_.refs_3_, ...), custom_call_target="tpu_custom_call" | custom-call | tf_op jit(solution)/shard_map/product/pallas_call | solution.py:81
  331.8 8.6 %product_add.8 = (bf16[512,1408]{1,0:T(8,128)(2,1)}, bf16[512,1408]{1,0:T(8,128)(2,1)}) custom-call(s32[1]{0:T(128)} %bitcast.3.refs_0_, bf16[256,2048]{1,0:T(8,128)(2,1)} %get-tuple-element.122.refs_0_.refs_1_, bf16[144,2048]{1,0:T(8,128)(2,1)} %collective-permute-done.14.refs_1_.refs_2_, bf16[128,2048]{1,0:T(8,128)(2,1)} %collective-permute-done.15.refs_2_.refs_3_, ...), custom_call_target="tpu_custom_call" | custom-call | tf_op jit(solution)/shard_map/product_add/pallas_call | solution.py:81
  341.0 5.4 %last.1 = (f32[256,2048]{1,0:T(8,128)}, f32[1,2048]{1,0:T(1,128)}) custom-call(bf16[256,2048]{1,0:T(8,128)(2,1)} %bitcast.29, bf16[256,2048]{1,0:T(8,128)(2,1)} %get-tuple-element.160.refs_2_.refs_1_, bf16[256,2048]{1,0:T(8,128)(2,1)} %collective-permute-done.35.refs_2_, bf16[256,2048]{1,0:T(8,128)(2,1)} %collective-permute-done.36.refs_3_, ...), custom_call_target="tpu_custom_call" | custom-call | tf_op jit(solution)/shard_map/last/pallas_call | solution.py:70
  347.0 15.7 %collective-permute-done.41.refs_1_ = bf16[512,1408]{1,0:T(8,128)(2,1)} collective-permute-done((bf16[512,1408]{1,0:T(8,128)(2,1)}, bf16[512,1408]{1,0:T(8,128)(2,1)}, u32[]{:S(2)}, u32[]{:S(2)}) %collective-permute-start.41) | collective-permute-done | bytes 1441824 | tf_op jit(solution)/shard_map/ppermute | solution.py:18
  364.7 4.9 product.10.refs_2_
  372.9 5.0 product.11.refs_2_
  386.5 4.3 result.1.refs_0_
  395.4 12.3 %collective-permute-done.44.refs_7_ = bf16[1024,1024]{1,0:T(8,128)(2,1)} collective-permute-done((bf16[1024,1024]{1,0:T(8,128)(2,1)}, bf16[1024,1024]{1,0:T(8,128)(2,1)}, u32[]{:S(2)}, u32[]{:S(2)}) %collective-permute-start.44) | collective-permute-done | bytes 2097184 | tf_op jit(solution)/shard_map/ppermute | solution.py:18
  407.7 7.0 %product_add.9 = (bf16[512,1024]{1,0:T(8,128)(2,1)}, bf16[512,1024]{1,0:T(8,128)(2,1)}) custom-call(s32[1]{0:T(128)} %bitcast.3.refs_0_, bf16[256,2048]{1,0:T(8,128)(2,1)} %first_norm.1.refs_0_.refs_1_, bf16[256,2048]{1,0:T(8,128)(2,1)} %collective-permute-done.refs_1_.refs_2_, bf16[256,2048]{1,0:T(8,128)(2,1)} %hold.12.refs_0_.refs_3_, ...), custom_call_target="tpu_custom_call" | custom-call | tf_op jit(solution)/shard_map/product_add/pallas_call | solution.py:81
  414.7 4.2 collective-permute-start.49
  418.9 11.2 %collective-permute-done.43.refs_7_ = bf16[1024,512]{1,0:T(8,128)(2,1)} collective-permute-done((bf16[1024,512]{1,0:T(8,128)(2,1)}, bf16[1024,512]{1,0:T(8,128)(2,1)}, u32[]{:S(2)}, u32[]{:S(2)}) %collective-permute-start.43) | collective-permute-done | bytes 1048608 | tf_op jit(solution)/shard_map/ppermute | solution.py:18
  430.1 5.5 %product_add.10 = (bf16[512,512]{1,0:T(8,128)(2,1)}, bf16[512,512]{1,0:T(8,128)(2,1)}) custom-call(s32[1]{0:T(128)} %bitcast.3.refs_0_, bf16[272,2048]{1,0:T(8,128)(2,1)} %get-tuple-element.139.refs_0_.refs_1_, bf16[272,2048]{1,0:T(8,128)(2,1)} %collective-permute-done.24.refs_1_.refs_2_, bf16[272,2048]{1,0:T(8,128)(2,1)} %hold.17.refs_11_.refs_0_.refs_3_, ...), custom_call_target="tpu_custom_call" | custom-call | tf_op jit(solution)/shard_map/product_add/pallas_call | solution.py:81
  435.6 14.2 %collective-permute-done.42.refs_7_ = bf16[1024,512]{1,0:T(8,128)(2,1)} collective-permute-done((bf16[1024,512]{1,0:T(8,128)(2,1)}, bf16[1024,512]{1,0:T(8,128)(2,1)}, u32[]{:S(2)}, u32[]{:S(2)}) %collective-permute-start.42) | collective-permute-done | bytes 1048608 | tf_op jit(solution)/shard_map/ppermute | solution.py:18
  449.9 5.4 %product_add.11 = (bf16[512,512]{1,0:T(8,128)(2,1)}, bf16[512,512]{1,0:T(8,128)(2,1)}) custom-call(s32[1]{0:T(128)} %bitcast.3.refs_0_, bf16[256,2048]{1,0:T(8,128)(2,1)} %first_norm.1.refs_0_.refs_1_, bf16[256,2048]{1,0:T(8,128)(2,1)} %collective-permute-done.refs_1_.refs_2_, bf16[256,2048]{1,0:T(8,128)(2,1)} %hold.12.refs_0_.refs_3_, ...), custom_call_target="tpu_custom_call" | custom-call | tf_op jit(solution)/shard_map/product_add/pallas_call | solution.py:81
  463.5 4.4 collective-permute-start.52
  467.9 3.9 collective-permute-start.51
  471.9 6.2 %collective-permute-done.47.two = bf16[256,1408]{1,0:T(8,128)(2,1)} collective-permute-done((bf16[256,1408]{1,0:T(8,128)(2,1)S(1)}, bf16[256,1408]{1,0:T(8,128)(2,1)}, u32[]{:S(2)}, u32[]{:S(2)}) %collective-permute-start.47) | collective-permute-done | bytes 720928 | tf_op jit(solution)/shard_map/ppermute | solution.py:18
  481.6 8.8 %collective-permute-done.46.refs_1_ = bf16[512,512]{1,0:T(8,128)(2,1)} collective-permute-done((bf16[512,512]{1,0:T(8,128)(2,1)}, bf16[512,512]{1,0:T(8,128)(2,1)}, u32[]{:S(2)}, u32[]{:S(2)}) %collective-permute-start.46) | collective-permute-done | bytes 524320 | tf_op jit(solution)/shard_map/ppermute | solution.py:18
  496.9 4.8 collective-permute-done.52.refs_1_
  509.0 7.1 %collective-permute-start.58 = (f32[4,512]{1,0:T(4,128)S(1)}, f32[4,512]{1,0:T(4,128)S(1)}, u32[]{:S(2)}, u32[]{:S(2)}) collective-permute-start(f32[4,512]{1,0:T(4,128)S(1)} %fusion.4), channel_id=1, source_target_pairs={{0,8},{4,12},{8,0},{12,4},{16,24},{20,28},{24,16},{28,20},{1,9},{5... | collective-permute-start | bytes 24584 | tf_op jit(solution)/shard_map/ppermute | solution.py:18
  (207 shorter events, 157.8 us)
Async XLA Ops:
  4.8 15.3 %collective-permute-start.2 = (bf16[256,2048]{1,0:T(8,128)(2,1)}, bf16[256,2048]{1,0:T(8,128)(2,1)}, u32[]{:S(2)}, u32[]{:S(2)}) collective-permute-start(bf16[256,2048]{1,0:T(8,128)(2,1)} %bitcast.20), channel_id=1, source_target_pairs={{0,1},{1,0},{2,3},{3,2},{4,5},{5,4},{6,7},{7,6},{8,9},{9,8},{10,11... | collective-permute-start | bytes 3145736 | tf_op jit(solution)/shard_map/ppermute | solution.py:18
  4.8 26.6 %collective-permute-start.1 = (bf16[256,2048]{1,0:T(8,128)(2,1)}, bf16[256,2048]{1,0:T(8,128)(2,1)}, u32[]{:S(2)}, u32[]{:S(2)}) collective-permute-start(bf16[256,2048]{1,0:T(8,128)(2,1)} %first_norm.1.refs_0_.refs_1_), channel_id=1, source_target_pairs={{0,2},{1,3},{2,0},{3,1},{4,6},{5,7},{6,4},{7,5},{8,10},{9,11},{10,... | collective-permute-start | bytes 3145736 | tf_op jit(solution)/shard_map/ppermute | solution.py:18
  32.4 45.0 %collective-permute-start.12 = (bf16[256,2048]{1,0:T(8,128)(2,1)}, bf16[256,2048]{1,0:T(8,128)(2,1)}, u32[]{:S(2)}, u32[]{:S(2)}) collective-permute-start(bf16[256,2048]{1,0:T(8,128)(2,1)} %hold.13), channel_id=1, source_target_pairs={{0,2},{1,3},{2,0},{3,1},{4,6},{5,7},{6,4},{7,5},{8,10},{9,11},{10,... | collective-permute-start | bytes 3145736 | tf_op jit(solution)/shard_map/ppermute | solution.py:18
  51.9 11.0 %collective-permute-start.5 = (f32[2,4,512]{2,1,0:T(4,128)}, f32[2,4,512]{2,1,0:T(4,128)S(1)}, u32[]{:S(2)}, u32[]{:S(2)}) collective-permute-start(f32[2,4,512]{2,1,0:T(4,128)} %pair.2), channel_id=1, source_target_pairs={{0,8},{4,12},{8,16},{12,20},{16,24},{20,28},{1,9},{5,13},{9,17},{1... | collective-permute-start | bytes 49160 | tf_op jit(solution)/shard_map/ppermute | solution.py:24
  55.7 7.3 %collective-permute-start.6 = (f32[2,4,512]{2,1,0:T(4,128)}, f32[2,4,512]{2,1,0:T(4,128)S(1)}, u32[]{:S(2)}, u32[]{:S(2)}) collective-permute-start(f32[2,4,512]{2,1,0:T(4,128)} %pair.2), channel_id=1, source_target_pairs={{0,16},{4,20},{8,24},{12,28},{1,17},{5,21},{9,25},{13,29},{2,18},{... | collective-permute-start | bytes 49160 | tf_op jit(solution)/shard_map/ppermute | solution.py:24
  71.2 6.3 %collective-permute-start.9 = (bf16[272,2048]{1,0:T(8,128)(2,1)}, bf16[272,2048]{1,0:T(8,128)(2,1)}, u32[]{:S(2)}, u32[]{:S(2)}) collective-permute-start(bf16[272,2048]{1,0:T(8,128)(2,1)} %get-tuple-element.114), channel_id=1, source_target_pairs={{0,1},{1,0},{2,3},{3,2},{4,5},{5,4},{6,7},{7,6},{8,9},{9,8},{10,11... | collective-permute-start | bytes 3342344 | tf_op jit(solution)/shard_map/ppermute | solution.py:18
  76.9 13.0 %collective-permute-start.8 = (bf16[272,2048]{1,0:T(8,128)(2,1)}, bf16[272,2048]{1,0:T(8,128)(2,1)}, u32[]{:S(2)}, u32[]{:S(2)}) collective-permute-start(bf16[272,2048]{1,0:T(8,128)(2,1)} %get-tuple-element.113), channel_id=1, source_target_pairs={{0,1},{1,0},{2,3},{3,2},{4,5},{5,4},{6,7},{7,6},{8,9},{9,8},{10,11... | collective-permute-start | bytes 3342344 | tf_op jit(solution)/shard_map/ppermute | solution.py:18
  80.3 16.3 %collective-permute-start.11 = (bf16[144,2048]{1,0:T(8,128)(2,1)}, bf16[144,2048]{1,0:T(8,128)(2,1)S(1)}, u32[]{:S(2)}, u32[]{:S(2)}) collective-permute-start(bf16[144,2048]{1,0:T(8,128)(2,1)} %get-tuple-element.116), channel_id=1, source_target_pairs={{0,2},{1,3},{2,0},{3,1},{4,6},{5,7},{6,4},{7,5},{8,10},{9,11},{10,... | collective-permute-start | bytes 1769480 | tf_op jit(solution)/shard_map/ppermute | solution.py:18
  81.8 26.2 %collective-permute-start.10 = (bf16[128,2048]{1,0:T(8,128)(2,1)}, bf16[128,2048]{1,0:T(8,128)(2,1)}, u32[]{:S(2)}, u32[]{:S(2)}) collective-permute-start(bf16[128,2048]{1,0:T(8,128)(2,1)} %get-tuple-element.115.refs_3_), channel_id=1, source_target_pairs={{0,2},{1,3},{2,0},{3,1},{4,6},{5,7},{6,4},{7,5},{8,10},{9,11},{10,... | collective-permute-start | bytes 1572872 | tf_op jit(solution)/shard_map/ppermute | solution.py:18
  101.2 12.8 %collective-permute-start.14 = (bf16[144,2048]{1,0:T(8,128)(2,1)}, bf16[144,2048]{1,0:T(8,128)(2,1)}, u32[]{:S(2)}, u32[]{:S(2)}) collective-permute-start(bf16[144,2048]{1,0:T(8,128)(2,1)} %get-tuple-element.123), channel_id=1, source_target_pairs={{0,1},{1,0},{2,3},{3,2},{4,5},{5,4},{6,7},{7,6},{8,9},{9,8},{10,11... | collective-permute-start | bytes 1769480 | tf_op jit(solution)/shard_map/ppermute | solution.py:18
  101.2 35.7 %collective-permute-start.16 = (bf16[144,2048]{1,0:T(8,128)(2,1)}, bf16[144,2048]{1,0:T(8,128)(2,1)S(1)}, u32[]{:S(2)}, u32[]{:S(2)}) collective-permute-start(bf16[144,2048]{1,0:T(8,128)(2,1)} %get-tuple-element.123), channel_id=1, source_target_pairs={{0,2},{1,3},{2,0},{3,1},{4,6},{5,7},{6,4},{7,5},{8,10},{9,11},{10,... | collective-permute-start | bytes 1769480 | tf_op jit(solution)/shard_map/ppermute | solution.py:18
  111.7 26.2 %collective-permute-start.17 = (bf16[128,2048]{1,0:T(8,128)(2,1)}, bf16[128,2048]{1,0:T(8,128)(2,1)}, u32[]{:S(2)}, u32[]{:S(2)}) collective-permute-start(bf16[128,2048]{1,0:T(8,128)(2,1)} %get-tuple-element.124), channel_id=1, source_target_pairs={{0,2},{1,3},{2,0},{3,1},{4,6},{5,7},{6,4},{7,5},{8,10},{9,11},{10,... | collective-permute-start | bytes 1572872 | tf_op jit(solution)/shard_map/ppermute | solution.py:18
  164.5 8.2 %collective-permute-start.20 = (bf16[256,2048]{1,0:T(8,128)(2,1)}, bf16[256,2048]{1,0:T(8,128)(2,1)}, u32[]{:S(2)}, u32[]{:S(2)}) collective-permute-start(bf16[256,2048]{1,0:T(8,128)(2,1)} %get-tuple-element.133), channel_id=1, source_target_pairs={{0,1},{1,0},{2,3},{3,2},{4,5},{5,4},{6,7},{7,6},{8,9},{9,8},{10,11... | collective-permute-start | bytes 3145736 | tf_op jit(solution)/shard_map/ppermute | solution.py:18
  164.6 36.9 %collective-permute-start.22 = (bf16[256,2048]{1,0:T(8,128)(2,1)}, bf16[256,2048]{1,0:T(8,128)(2,1)}, u32[]{:S(2)}, u32[]{:S(2)}) collective-permute-start(bf16[256,2048]{1,0:T(8,128)(2,1)} %get-tuple-element.136), channel_id=1, source_target_pairs={{0,1},{1,0},{2,3},{3,2},{4,5},{5,4},{6,7},{7,6},{8,9},{9,8},{10,11... | collective-permute-start | bytes 3145736 | tf_op jit(solution)/shard_map/ppermute | solution.py:18
  176.4 25.5 %collective-permute-start.23 = (bf16[256,2048]{1,0:T(8,128)(2,1)}, bf16[256,2048]{1,0:T(8,128)(2,1)}, u32[]{:S(2)}, u32[]{:S(2)}) collective-permute-start(bf16[256,2048]{1,0:T(8,128)(2,1)} %plus.3.refs_7_.refs_11_), channel_id=1, source_target_pairs={{0,2},{1,3},{2,0},{3,1},{4,6},{5,7},{6,4},{7,5},{8,10},{9,11},{10,... | collective-permute-start | bytes 3145736 | tf_op jit(solution)/shard_map/ppermute | solution.py:18
  177.8 64.6 %collective-permute-start.28 = (bf16[1024,1408]{1,0:T(8,128)(2,1)}, bf16[1024,1408]{1,0:T(8,128)(2,1)}, u32[]{:S(2)}, u32[]{:S(2)}) collective-permute-start(bf16[1024,1408]{1,0:T(8,128)(2,1)} %product.6.refs_2_), channel_id=1, source_target_pairs={{0,4},{4,0},{8,12},{12,8},{16,20},{20,16},{24,28},{28,24},{1,5},{5... | collective-permute-start | bytes 8650760 | tf_op jit(solution)/shard_map/ppermute | solution.py:18
  208.3 27.3 %collective-permute-start.26 = (bf16[272,2048]{1,0:T(8,128)(2,1)}, bf16[272,2048]{1,0:T(8,128)(2,1)}, u32[]{:S(2)}, u32[]{:S(2)}) collective-permute-start(bf16[272,2048]{1,0:T(8,128)(2,1)} %get-tuple-element.139.refs_0_.refs_1_), channel_id=1, source_target_pairs={{0,2},{1,3},{2,0},{3,1},{4,6},{5,7},{6,4},{7,5},{8,10},{9,11},{10,... | collective-permute-start | bytes 3342344 | tf_op jit(solution)/shard_map/ppermute | solution.py:18
  209.8 10.7 %collective-permute-start.21 = (bf16[256,2048]{1,0:T(8,128)(2,1)}, bf16[256,2048]{1,0:T(8,128)(2,1)}, u32[]{:S(2)}, u32[]{:S(2)}) collective-permute-start(bf16[256,2048]{1,0:T(8,128)(2,1)} %get-tuple-element.135), channel_id=1, source_target_pairs={{0,1},{1,0},{2,3},{3,2},{4,5},{5,4},{6,7},{7,6},{8,9},{9,8},{10,11... | collective-permute-start | bytes 3145736 | tf_op jit(solution)/shard_map/ppermute | solution.py:18
  210.0 65.4 %collective-permute-start.33 = (bf16[1024,1408]{1,0:T(8,128)(2,1)}, bf16[1024,1408]{1,0:T(8,128)(2,1)}, u32[]{:S(2)}, u32[]{:S(2)}) collective-permute-start(bf16[1024,1408]{1,0:T(8,128)(2,1)} %product.7.refs_10_), channel_id=1, source_target_pairs={{0,8},{4,12},{8,0},{12,4},{16,24},{20,28},{24,16},{28,20},{1,9},{5... | collective-permute-start | bytes 8650760 | tf_op jit(solution)/shard_map/ppermute | solution.py:18
  235.6 15.4 %collective-permute-start.27 = (bf16[272,2048]{1,0:T(8,128)(2,1)}, bf16[272,2048]{1,0:T(8,128)(2,1)}, u32[]{:S(2)}, u32[]{:S(2)}) collective-permute-start(bf16[272,2048]{1,0:T(8,128)(2,1)} %hold.17.refs_11_.refs_0_.refs_3_), channel_id=1, source_target_pairs={{0,1},{1,0},{2,3},{3,2},{4,5},{5,4},{6,7},{7,6},{8,9},{9,8},{10,11... | collective-permute-start | bytes 3342344 | tf_op jit(solution)/shard_map/ppermute | solution.py:18
  266.1 65.7 %collective-permute-start.37 = (bf16[1024,1408]{1,0:T(8,128)(2,1)}, bf16[1024,1408]{1,0:T(8,128)(2,1)}, u32[]{:S(2)}, u32[]{:S(2)}) collective-permute-start(bf16[1024,1408]{1,0:T(8,128)(2,1)} %hold.18), channel_id=1, source_target_pairs={{0,4},{4,0},{8,12},{12,8},{16,20},{20,16},{24,28},{28,24},{1,5},{5... | collective-permute-start | bytes 8650760 | tf_op jit(solution)/shard_map/ppermute | solution.py:18
  267.6 16.7 %collective-permute-start.30 = (f32[2,4,512]{2,1,0:T(4,128)S(1)}, f32[2,4,512]{2,1,0:T(4,128)S(1)}, u32[]{:S(2)}, u32[]{:S(2)}) collective-permute-start(f32[2,4,512]{2,1,0:T(4,128)S(1)} %copy-done.8), channel_id=1, source_target_pairs={{8,0},{12,4},{16,8},{20,12},{24,16},{28,20},{9,1},{13,5},{17,9},{2... | collective-permute-start | bytes 49160 | tf_op jit(solution)/shard_map/ppermute | solution.py:24
  268.9 15.4 %collective-permute-start.31 = (f32[2,4,512]{2,1,0:T(4,128)S(1)}, f32[2,4,512]{2,1,0:T(4,128)S(1)}, u32[]{:S(2)}, u32[]{:S(2)}) collective-permute-start(f32[2,4,512]{2,1,0:T(4,128)S(1)} %copy-done.8), channel_id=1, source_target_pairs={{16,0},{20,4},{24,8},{28,12},{17,1},{21,5},{25,9},{29,13},{18,2},{... | collective-permute-start | bytes 49160 | tf_op jit(solution)/shard_map/ppermute | solution.py:24
  270.2 14.1 %collective-permute-start.32 = (f32[2,4,512]{2,1,0:T(4,128)S(1)}, f32[2,4,512]{2,1,0:T(4,128)S(1)}, u32[]{:S(2)}, u32[]{:S(2)}) collective-permute-start(f32[2,4,512]{2,1,0:T(4,128)S(1)} %copy-done.8), channel_id=1, source_target_pairs={{24,0},{28,4},{25,1},{29,5},{26,2},{30,6},{27,3},{31,7}} | collective-permute-start | bytes 49160 | tf_op jit(solution)/shard_map/ppermute | solution.py:24
  286.4 33.2 %collective-permute-start.38 = (bf16[512,1408]{1,0:T(8,128)(2,1)}, bf16[512,1408]{1,0:T(8,128)(2,1)}, u32[]{:S(2)}, u32[]{:S(2)}) collective-permute-start(bf16[512,1408]{1,0:T(8,128)(2,1)} %hold.19), channel_id=1, source_target_pairs={{0,8},{4,12},{8,0},{12,4},{16,24},{20,28},{24,16},{28,20},{1,9},{5... | collective-permute-start | bytes 4325384 | tf_op jit(solution)/shard_map/ppermute | solution.py:18
  313.6 26.9 %collective-permute-start.35 = (bf16[256,2048]{1,0:T(8,128)(2,1)}, bf16[256,2048]{1,0:T(8,128)(2,1)}, u32[]{:S(2)}, u32[]{:S(2)}) collective-permute-start(bf16[256,2048]{1,0:T(8,128)(2,1)} %get-tuple-element.161), channel_id=1, source_target_pairs={{0,1},{1,0},{2,3},{3,2},{4,5},{5,4},{6,7},{7,6},{8,9},{9,8},{10,11... | collective-permute-start | bytes 3145736 | tf_op jit(solution)/shard_map/ppermute | solution.py:18
  313.8 48.9 %collective-permute-start.41 = (bf16[512,1408]{1,0:T(8,128)(2,1)}, bf16[512,1408]{1,0:T(8,128)(2,1)}, u32[]{:S(2)}, u32[]{:S(2)}) collective-permute-start(bf16[512,1408]{1,0:T(8,128)(2,1)} %get-tuple-element.153.refs_6_), channel_id=1, source_target_pairs={{0,4},{4,0},{8,12},{12,8},{16,20},{20,16},{24,28},{28,24},{1,5},{5... | collective-permute-start | bytes 4325384 | tf_op jit(solution)/shard_map/ppermute | solution.py:18
  315.5 25.4 %collective-permute-start.36 = (bf16[256,2048]{1,0:T(8,128)(2,1)}, bf16[256,2048]{1,0:T(8,128)(2,1)}, u32[]{:S(2)}, u32[]{:S(2)}) collective-permute-start(bf16[256,2048]{1,0:T(8,128)(2,1)} %plus.5.refs_10_), channel_id=1, source_target_pairs={{0,2},{1,3},{2,0},{3,1},{4,6},{5,7},{6,4},{7,5},{8,10},{9,11},{10,... | collective-permute-start | bytes 3145736 | tf_op jit(solution)/shard_map/ppermute | solution.py:18
  329.0 78.7 %collective-permute-start.44 = (bf16[1024,1024]{1,0:T(8,128)(2,1)}, bf16[1024,1024]{1,0:T(8,128)(2,1)}, u32[]{:S(2)}, u32[]{:S(2)}) collective-permute-start(bf16[1024,1024]{1,0:T(8,128)(2,1)} %product.9.refs_11_), channel_id=1, source_target_pairs={{0,4},{4,0},{8,12},{12,8},{16,20},{20,16},{24,28},{28,24},{1,5},{5... | collective-permute-start | bytes 6291464 | tf_op jit(solution)/shard_map/ppermute | solution.py:18
  340.4 42.9 %collective-permute-start.40 = (bf16[512,1408]{1,0:T(8,128)(2,1)}, bf16[512,1408]{1,0:T(8,128)(2,1)}, u32[]{:S(2)}, u32[]{:S(2)}) collective-permute-start(bf16[512,1408]{1,0:T(8,128)(2,1)} %get-tuple-element.167.refs_6_), channel_id=1, source_target_pairs={{0,8},{4,12},{8,0},{12,4},{16,24},{20,28},{24,16},{28,20},{1,9},{5... | collective-permute-start | bytes 4325384 | tf_op jit(solution)/shard_map/ppermute | solution.py:18
  340.5 37.4 %collective-permute-start.25 = (bf16[256,2048]{1,0:T(8,128)(2,1)}, bf16[256,2048]{1,0:T(8,128)(2,1)}, u32[]{:S(2)}, u32[]{:S(2)}) collective-permute-start(bf16[256,2048]{1,0:T(8,128)(2,1)} %get-tuple-element.144), channel_id=1, source_target_pairs={{0,1},{1,0},{2,3},{3,2},{4,5},{5,4},{6,7},{7,6},{8,9},{9,8},{10,11... | collective-permute-start | bytes 3145736 | tf_op jit(solution)/shard_map/ppermute | solution.py:18
  346.4 40.1 %collective-permute-start.39 = (bf16[256,2048]{1,0:T(8,128)(2,1)}, bf16[256,2048]{1,0:T(8,128)(2,1)}, u32[]{:S(2)}, u32[]{:S(2)}) collective-permute-start(bf16[256,2048]{1,0:T(8,128)(2,1)} %hold.20), channel_id=1, source_target_pairs={{0,2},{1,3},{2,0},{3,1},{4,6},{5,7},{6,4},{7,5},{8,10},{9,11},{10,... | collective-permute-start | bytes 3145736 | tf_op jit(solution)/shard_map/ppermute | solution.py:18
  362.7 29.1 %collective-permute-start.45 = (bf16[256,1408]{1,0:T(8,128)(2,1)S(1)}, bf16[256,1408]{1,0:T(8,128)(2,1)}, u32[]{:S(2)}, u32[]{:S(2)}) collective-permute-start(bf16[256,1408]{1,0:T(8,128)(2,1)S(1)} %copy-done.5), channel_id=1, source_target_pairs={{0,16},{4,20},{8,24},{12,28},{16,0},{20,4},{24,8},{28,12},{1,17},{... | collective-permute-start | bytes 2162696 | tf_op jit(solution)/shard_map/ppermute | solution.py:18
  377.9 52.2 %collective-permute-start.43 = (bf16[1024,512]{1,0:T(8,128)(2,1)}, bf16[1024,512]{1,0:T(8,128)(2,1)}, u32[]{:S(2)}, u32[]{:S(2)}) collective-permute-start(bf16[1024,512]{1,0:T(8,128)(2,1)} %product.10.refs_2_), channel_id=1, source_target_pairs={{0,4},{4,0},{8,12},{12,8},{16,20},{20,16},{24,28},{28,24},{1,5},{5... | collective-permute-start | bytes 3145736 | tf_op jit(solution)/shard_map/ppermute | solution.py:18
  383.3 66.5 %collective-permute-start.42 = (bf16[1024,512]{1,0:T(8,128)(2,1)}, bf16[1024,512]{1,0:T(8,128)(2,1)}, u32[]{:S(2)}, u32[]{:S(2)}) collective-permute-start(bf16[1024,512]{1,0:T(8,128)(2,1)} %product.11.refs_2_), channel_id=1, source_target_pairs={{0,4},{4,0},{8,12},{12,8},{16,20},{20,16},{24,28},{28,24},{1,5},{5... | collective-permute-start | bytes 3145736 | tf_op jit(solution)/shard_map/ppermute | solution.py:18
  414.7 43.4 %collective-permute-start.48 = (bf16[512,1024]{1,0:T(8,128)(2,1)}, bf16[512,1024]{1,0:T(8,128)(2,1)}, u32[]{:S(2)}, u32[]{:S(2)}) collective-permute-start(bf16[512,1024]{1,0:T(8,128)(2,1)} %get-tuple-element.176.refs_8_), channel_id=1, source_target_pairs={{0,8},{4,12},{8,0},{12,4},{16,24},{20,28},{24,16},{28,20},{1,9},{5... | collective-permute-start | bytes 3145736 | tf_op jit(solution)/shard_map/ppermute | solution.py:18
  414.7 40.8 %collective-permute-start.49 = (bf16[256,1408]{1,0:T(8,128)(2,1)}, bf16[256,1408]{1,0:T(8,128)(2,1)}, u32[]{:S(2)}, u32[]{:S(2)}) collective-permute-start(bf16[256,1408]{1,0:T(8,128)(2,1)} %get-tuple-element.173.refs_7_), channel_id=1, source_target_pairs={{0,16},{4,20},{8,24},{12,28},{16,0},{20,4},{24,8},{28,12},{1,17},{... | collective-permute-start | bytes 2162696 | tf_op jit(solution)/shard_map/ppermute | solution.py:18
  418.9 59.2 %collective-permute-start.47 = (bf16[256,1408]{1,0:T(8,128)(2,1)S(1)}, bf16[256,1408]{1,0:T(8,128)(2,1)}, u32[]{:S(2)}, u32[]{:S(2)}) collective-permute-start(bf16[256,1408]{1,0:T(8,128)(2,1)S(1)} %copy-done.4), channel_id=1, source_target_pairs={{0,16},{4,20},{8,24},{12,28},{16,0},{20,4},{24,8},{28,12},{1,17},{... | collective-permute-start | bytes 2162696 | tf_op jit(solution)/shard_map/ppermute | solution.py:18
  455.2 35.2 %collective-permute-start.46 = (bf16[512,512]{1,0:T(8,128)(2,1)}, bf16[512,512]{1,0:T(8,128)(2,1)}, u32[]{:S(2)}, u32[]{:S(2)}) collective-permute-start(bf16[512,512]{1,0:T(8,128)(2,1)} %get-tuple-element.179.refs_0_), channel_id=1, source_target_pairs={{0,8},{4,12},{8,0},{12,4},{16,24},{20,28},{24,16},{28,20},{1,9},{5... | collective-permute-start | bytes 1572872 | tf_op jit(solution)/shard_map/ppermute | solution.py:18
  455.4 8.1 %collective-permute-start.54 = (f32[2,512]{1,0:T(2,128)S(1)}, f32[2,512]{1,0:T(2,128)S(1)}, u32[]{:S(2)}, u32[]{:S(2)}) collective-permute-start(f32[2,512]{1,0:T(2,128)S(1)} %get-tuple-element.196), channel_id=1, source_target_pairs={{0,1},{1,0},{2,3},{3,2},{4,5},{5,4},{6,7},{7,6},{8,9},{9,8},{10,11... | collective-permute-start | bytes 12296 | tf_op jit(solution)/shard_map/ppermute | solution.py:18
  455.5 12.4 %collective-permute-start.55 = (f32[2,512]{1,0:T(2,128)S(1)}, f32[2,512]{1,0:T(2,128)S(1)}, u32[]{:S(2)}, u32[]{:S(2)}) collective-permute-start(f32[2,512]{1,0:T(2,128)S(1)} %get-tuple-element.197), channel_id=1, source_target_pairs={{0,2},{1,3},{2,0},{3,1},{4,6},{5,7},{6,4},{7,5},{8,10},{9,11},{10,... | collective-permute-start | bytes 12296 | tf_op jit(solution)/shard_map/ppermute | solution.py:18
  458.1 13.7 %collective-permute-start.56 = (f32[2,512]{1,0:T(2,128)S(1)}, f32[2,512]{1,0:T(2,128)S(1)}, u32[]{:S(2)}, u32[]{:S(2)}) collective-permute-start(f32[2,512]{1,0:T(2,128)S(1)} %get-tuple-element.198), channel_id=1, source_target_pairs={{0,3},{1,2},{2,1},{3,0},{4,7},{5,6},{6,5},{7,4},{8,11},{9,10},{10,... | collective-permute-start | bytes 12296 | tf_op jit(solution)/shard_map/ppermute | solution.py:18
  463.5 38.3 %collective-permute-start.52 = (bf16[512,512]{1,0:T(8,128)(2,1)}, bf16[512,512]{1,0:T(8,128)(2,1)}, u32[]{:S(2)}, u32[]{:S(2)}) collective-permute-start(bf16[512,512]{1,0:T(8,128)(2,1)} %get-tuple-element.177.refs_8_), channel_id=1, source_target_pairs={{0,8},{4,12},{8,0},{12,4},{16,24},{20,28},{24,16},{28,20},{1,9},{5... | collective-permute-start | bytes 1572872 | tf_op jit(solution)/shard_map/ppermute | solution.py:18
  467.9 36.3 %collective-permute-start.51 = (bf16[256,1024]{1,0:T(8,128)(2,1)}, bf16[256,1024]{1,0:T(8,128)(2,1)}, u32[]{:S(2)}, u32[]{:S(2)}) collective-permute-start(bf16[256,1024]{1,0:T(8,128)(2,1)} %get-tuple-element.183.refs_1_), channel_id=1, source_target_pairs={{0,16},{4,20},{8,24},{12,28},{16,0},{20,4},{24,8},{28,12},{1,17},{... | collective-permute-start | bytes 1572872 | tf_op jit(solution)/shard_map/ppermute | solution.py:18
  492.5 25.5 %collective-permute-start.50 = (bf16[256,512]{1,0:T(8,128)(2,1)}, bf16[256,512]{1,0:T(8,128)(2,1)S(1)}, u32[]{:S(2)}, u32[]{:S(2)}) collective-permute-start(bf16[256,512]{1,0:T(8,128)(2,1)} %get-tuple-element.185.refs_2_), channel_id=1, source_target_pairs={{0,16},{4,20},{8,24},{12,28},{16,0},{20,4},{24,8},{28,12},{1,17},{... | collective-permute-start | bytes 786440 | tf_op jit(solution)/shard_map/ppermute | solution.py:18
  495.4 12.3 %collective-permute-start.57 = (f32[4,512]{1,0:T(4,128)S(1)}, f32[4,512]{1,0:T(4,128)S(1)}, u32[]{:S(2)}, u32[]{:S(2)}) collective-permute-start(f32[4,512]{1,0:T(4,128)S(1)} %pad_maximum_fusion), channel_id=1, source_target_pairs={{0,4},{4,0},{8,12},{12,8},{16,20},{20,16},{24,28},{28,24},{1,5},{5... | collective-permute-start | bytes 24584 | tf_op jit(solution)/shard_map/ppermute | solution.py:18
  503.9 20.9 %collective-permute-start.53 = (bf16[256,512]{1,0:T(8,128)(2,1)}, bf16[256,512]{1,0:T(8,128)(2,1)S(1)}, u32[]{:S(2)}, u32[]{:S(2)}) collective-permute-start(bf16[256,512]{1,0:T(8,128)(2,1)} %get-tuple-element.188.refs_0_), channel_id=1, source_target_pairs={{0,16},{4,20},{8,24},{12,28},{16,0},{20,4},{24,8},{28,12},{1,17},{... | collective-permute-start | bytes 786440 | tf_op jit(solution)/shard_map/ppermute | solution.py:18
  509.0 12.9 %collective-permute-start.58 = (f32[4,512]{1,0:T(4,128)S(1)}, f32[4,512]{1,0:T(4,128)S(1)}, u32[]{:S(2)}, u32[]{:S(2)}) collective-permute-start(f32[4,512]{1,0:T(4,128)S(1)} %fusion.4), channel_id=1, source_target_pairs={{0,8},{4,12},{8,0},{12,4},{16,24},{20,28},{24,16},{28,20},{1,9},{5... | collective-permute-start | bytes 24584 | tf_op jit(solution)/shard_map/ppermute | solution.py:18
  (39 other events, 143.3 us)

commit v5 on v4

--- a/solution.py
+++ b/solution.py
@@ -548,7 +548,7 @@
         keep[...] = total
 
 
-def product(me, lefts, near, far, bits, size, got=None, after=()):
+def product(me, lefts, near, far, bits, size, got=None, after=(), more=0):
     levels = len(bits)
     count = 1 << (levels - 1)
     base = 0 if got is None else count
@@ -581,7 +581,7 @@
     inputs += [fixed(near), fixed(far)]
     flops = 0
     if got is None:
-        out = ((count * size, units), BF, (size, units), lambda j, me: (j, 0))
+        out = ((count * size + more, units), BF, (size, units), lambda j, me: (j, 0))
         return call(
             functools.partial(product_kernel, near_count),
             "product", (count,), inputs, [out], flops, after, blocks=me,
@@ -892,9 +892,9 @@
         self.me, self.lefts, self.near, self.far = me, lefts, near, far
         self.bits, self.size, self.level = bits, size, 0
 
-    def begin(self, *earlier):
+    def begin(self, *earlier, more=0):
         self.send = product(
-            self.me, self.lefts, self.near, self.far, self.bits, self.size, after=earlier
+            self.me, self.lefts, self.near, self.far, self.bits, self.size, after=earlier, more=more
         )
         return self.send
 
@@ -931,10 +931,10 @@
     return jnp.stack([norms[0], mixer_term[0], norms[1], bound_term])
 
 
-GATE_AT, LOWER_AT, UP_AT, LOWER_BITS = "before", "beside", "pair", "m"
+GATE_AT, LOWER_AT, UP_AT, LOWER_BITS = "beside", "beside", "pair", "m"
 ORDER = (
-    ("-p", "-n", "gs", "bb", "us", "-l", "ob", "ls", "ab", "us", "-r", "gf", "bs")
-    + ("os", "as", "lf", "bs", "uf", "as", "os", "bf", "-1", "af", "-2", "-3", "of")
+    ("-p", "-n", "gs", "bb", "us", "-l", "ob", "ls", "ab", "-r", "us", "gf", "bs")
+    + ("os", "as", "bs", "lf", "uf", "as", "os", "-1", "bf", "af", "-2", "-3", "of")
 )
 
 
@@ -1007,13 +1007,13 @@
     up = Weight(me, twos, gu_n, gu_f, y_first, block)
     lower = Weight(me, (pieces(g0, g1), pieces(g2, g3)), hid_n, hid_f, mixed_order, block)
     kf0, kf1 = feed_back(gg_f, gu_f, gate_up)
-    gate.begin(kf0)
+    gate.begin(kf0, more=128)
     gate.go()
     across = plus(kf0, swap(kf1, "wt", 1), after=(gate.send,))
     hop = swap(across, "wt", 2)
-    lower.begin(across)
+    lower.begin(across, more=128)
     lower.go()
-    up.begin(lower.send, across)
+    up.begin(lower.send, across, more=0)
     ff0, ff1 = feed_out(hid_f, down, after=(up.send,))
     grad_middle, norm2_term, b0 = turn(
         g0, kn0, core, hop, middle, branch, scale_two, gain_two, after=(ff0,)

time: 537 us -> 528 us (0.983)
  transfers between devices with their start and end apart: 60 -> 60, of which waited for: 30 -> 30; matrix products, arithmetic and copies ran while one was open for 1% -> 1% of each run, Pallas kernels for 54% -> 55%
where the time goes in v5:
time: 528 us; the launch traced here: 521 us
  Pallas kernels  312 us (59%)
  waiting for transfers between devices  127 us (24%)
  starting transfers between devices  65.3 us (12%)
  local copies, waits for them, and re-layouts  13.8 us (3%)
    pallas_call x30, Pallas kernels, call(): pl.pallas_call(body, grid=grid, in_specs=in_specs, out_specs=out_specs, s...  198 us
    ppermute x54, waiting for transfers between devices, swap(): return lax.ppermute(values, axis, [(i, i ^ bit) for i in range(size)])  127 us
    pallas_call x16, Pallas kernels, call(): got = pl.pallas_call(body, grid_spec=spec, **settings)(blocks, *operands)  88.4 us
    ppermute x54, starting transfers between devices, swap(): return lax.ppermute(values, axis, [(i, i ^ bit) for i in range(size)])  51.7 us
    pallas_call x6, Pallas kernels, finish(): pl.pallas_call(lambda one, two, *refs: finish_kernel(turned, one, two, *r...  18.2 us
    ppermute x6, starting transfers between devices, shift(): return lax.ppermute(values, axis, pairs)  13.5 us
  transfers between devices with their start and end apart: 60, of which 30 were waited for; matrix products, arithmetic and copies ran while one was open for 1% of the time, Pallas kernels for 55%

profile of v5, /device:TPU:0, one launch (start us, length us, event | category | flops | bytes accessed | tf_op | source)
XLA Modules:
  0.0 521.4 jit_solution(6755159777124612665)
XLA Ops:
  9.1 11.0 %project.2 = (f32[2,256,512]{2,1,0:T(8,128)}, f32[2,256,512]{2,1,0:T(8,128)}, f32[2,256,512]{2,1,0:T(8,128)}, f32[2,256,512]{2,1,0:T(8,128)}, f32[2,256,512]{2,1,0:T(8,128)}, /*index=5*/f32[2,2,512]{2,1,0:T(2,128)}) custom-call(bf16[256,2048]{1,0:T(8,128)(2,1)} %first_norm.1.refs_0_.refs_1_, bf16[256,2048]{1,0:T(8,128)(2,1)} %collective-permute-done.refs_1_.refs_2_, ...), custom_call_target="tpu_custom_call" | custom-call | tf_op jit(solution)/shard_map/project/pallas_call | solution.py:70
  20.1 7.4 %hidden_grad.2.refs_1_.refs_4_ = f32[512,1408]{1,0:T(8,128)} custom-call(bf16[256,2048]{1,0:T(8,128)(2,1)} %bitcast.21, bf16[256,2048]{1,0:T(8,128)(2,1)} %collective-permute-done.2.refs_1_.refs_2_, bf16[1408,2048]{1,0:T(8,128)(2,1)} %refs_1_.3, f32[2,2,512]{2,1,0:T(2,128)} %get-tuple-element.106.refs_3_.refs_4_), custom_call_target="tpu_custom_call" | custom-call | tf_op jit(solution)/shard_map/hidden_grad/pallas_call | solution.py:70
  27.6 3.8 collective-permute-done.1.refs_0_
  34.4 11.5 %project.3 = (f32[2,256,512]{2,1,0:T(8,128)}, f32[2,256,512]{2,1,0:T(8,128)}, f32[2,256,512]{2,1,0:T(8,128)}, f32[2,256,512]{2,1,0:T(8,128)}, f32[2,256,512]{2,1,0:T(8,128)}, /*index=5*/f32[2,4,512]{2,1,0:T(4,128)}) custom-call(bf16[256,2048]{1,0:T(8,128)(2,1)} %hold.12.refs_0_.refs_3_, bf16[256,2048]{1,0:T(8,128)(2,1)} %collective-permute-done.3.refs_1_.refs_4_, ...), custom_call_target="tpu_custom_call" | custom-call | tf_op jit(solution)/shard_map/project/pallas_call | solution.py:70
  51.9 3.7 collective-permute-start.5
  55.6 4.5 collective-permute-start.6
  65.6 5.6 %mix.2 = (f32[2,256,512]{2,1,0:T(8,128)}, bf16[272,2048]{1,0:T(8,128)(2,1)}, bf16[272,2048]{1,0:T(8,128)(2,1)}) custom-call(f32[2,256,512]{2,1,0:T(8,128)} %get-tuple-element.108.refs_0_, f32[2,256,512]{2,1,0:T(8,128)} %get-tuple-element.109.refs_1_, f32[2,256,512]{2,1,0:T(8,128)} %get-tuple-element.110.refs_2_.refs_3_, f32[4,1,512]{2,1,0:T(1,128)} %enter.2.refs_3_.refs_7_, ...), custom_call_target="tpu_custom_call" | custom-call | tf_op jit(solution)/shard_map/mix/pallas_call | solution.py:70
  71.3 5.6 %mix.3 = (f32[2,256,512]{2,1,0:T(8,128)}, bf16[272,2048]{1,0:T(8,128)(2,1)}, bf16[272,2048]{1,0:T(8,128)(2,1)}) custom-call(f32[2,256,512]{2,1,0:T(8,128)} %get-tuple-element.103.refs_0_, f32[2,256,512]{2,1,0:T(8,128)} %get-tuple-element.104.refs_1_, f32[2,256,512]{2,1,0:T(8,128)} %get-tuple-element.105.refs_2_.refs_3_, f32[4,1,512]{2,1,0:T(1,128)} %enter.2.refs_3_.refs_7_, ...), custom_call_target="tpu_custom_call" | custom-call | tf_op jit(solution)/shard_map/mix/pallas_call | solution.py:70
  82.3 7.5 %hidden_grad.3.refs_0_.refs_5_ = f32[512,1408]{1,0:T(8,128)} custom-call(bf16[256,2048]{1,0:T(8,128)(2,1)} %hold.14.refs_0_.refs_3_, bf16[256,2048]{1,0:T(8,128)(2,1)} %collective-permute-done.13.refs_1_.refs_4_, bf16[1408,2048]{1,0:T(8,128)(2,1)} %refs_1_.3, bf16[128,2048]{1,0:T(8,128)(2,1)} %get-tuple-element.115.refs_3_), custom_call_target="tpu_custom_call" | custom-call | tf_op jit(solution)/shard_map/hidden_grad/pallas_call | solution.py:70
  89.9 6.8 %collective-permute-done.11.hop.hop_more = bf16[144,2048]{1,0:T(8,128)(2,1)S(1)} collective-permute-done((bf16[144,2048]{1,0:T(8,128)(2,1)}, bf16[144,2048]{1,0:T(8,128)(2,1)S(1)}, u32[]{:S(2)}, u32[]{:S(2)}) %collective-permute-start.11) | collective-permute-done | bytes 589856 | tf_op jit(solution)/shard_map/ppermute | solution.py:18
  102.6 5.4 %collective-permute-done.10.hop = bf16[128,2048]{1,0:T(8,128)(2,1)} collective-permute-done((bf16[128,2048]{1,0:T(8,128)(2,1)}, bf16[128,2048]{1,0:T(8,128)(2,1)}, u32[]{:S(2)}, u32[]{:S(2)}) %collective-permute-start.10) | collective-permute-done | bytes 524320 | tf_op jit(solution)/shard_map/ppermute | solution.py:18
  113.9 12.0 %feed.2 = (bf16[512,1408]{1,0:T(8,128)(2,1)}, bf16[512,1408]{1,0:T(8,128)(2,1)}, bf16[512,1408]{1,0:T(8,128)(2,1)}) custom-call(bf16[256,2048]{1,0:T(8,128)(2,1)} %get-tuple-element.122.refs_0_.refs_1_, bf16[144,2048]{1,0:T(8,128)(2,1)} %collective-permute-done.14.refs_1_.refs_2_, bf16[128,2048]{1,0:T(8,128)(2,1)} %collective-permute-done.15.refs_2_.refs_3_, ...), custom_call_target="tpu_custom_call" | custom-call | tf_op jit(solution)/shard_map/feed/pallas_call | solution.py:70
  125.9 10.9 %feed_back.2 = (bf16[256,2048]{1,0:T(8,128)(2,1)}, bf16[256,2048]{1,0:T(8,128)(2,1)}) custom-call(bf16[512,1408]{1,0:T(8,128)(2,1)} %get-tuple-element.126.refs_0_.refs_8_, bf16[512,1408]{1,0:T(8,128)(2,1)} %get-tuple-element.127.refs_1_.refs_8_, bf16[2,2048,1408]{2,1,0:T(8,128)(2,1)} %refs_2_.13), custom_call_target="tpu_custom_call" | custom-call | tf_op jit(solution)/shard_map/feed_back/pallas_call | solution.py:70
  141.5 12.0 %feed.3 = (bf16[512,1408]{1,0:T(8,128)(2,1)}, bf16[512,1408]{1,0:T(8,128)(2,1)}, bf16[512,1408]{1,0:T(8,128)(2,1)}) custom-call(bf16[144,2048]{1,0:T(8,128)(2,1)} %hold.15.refs_0_.refs_4_, bf16[128,2048]{1,0:T(8,128)(2,1)} %hold.16.refs_1_.refs_5_, bf16[144,2048]{1,0:T(8,128)(2,1)} %copy-done.2, bf16[128,2048]{1,0:T(8,128)(2,1)} %collective-permute-done.19.refs_3_.refs_7_, ...), custom_call_target="tpu_custom_call" | custom-call | tf_op jit(solution)/shard_map/feed/pallas_call | solution.py:70
  153.6 10.9 %feed_back.3 = (bf16[256,2048]{1,0:T(8,128)(2,1)}, bf16[256,2048]{1,0:T(8,128)(2,1)}) custom-call(bf16[512,1408]{1,0:T(8,128)(2,1)} %get-tuple-element.131.refs_0_.refs_9_, bf16[512,1408]{1,0:T(8,128)(2,1)} %get-tuple-element.130.refs_1_.refs_9_, bf16[2,2048,1408]{2,1,0:T(8,128)(2,1)} %refs_2_.13), custom_call_target="tpu_custom_call" | custom-call | tf_op jit(solution)/shard_map/feed_back/pallas_call | solution.py:70
  165.0 7.8 %product.6.refs_2_ = bf16[1152,1408]{1,0:T(8,128)(2,1)} custom-call(s32[1]{0:T(128)} %bitcast.3.refs_0_, bf16[256,2048]{1,0:T(8,128)(2,1)} %get-tuple-element.122.refs_0_.refs_1_, bf16[144,2048]{1,0:T(8,128)(2,1)} %collective-permute-done.14.refs_1_.refs_2_, bf16[128,2048]{1,0:T(8,128)(2,1)} %collective-permute-done.15.refs_2_.refs_3_, ...), custom_call_target="tpu_custom_call" | custom-call | tf_op jit(solution)/shard_map/product/pallas_call | solution.py:81
  179.4 7.5 %product.7.refs_10_ = bf16[1152,1408]{1,0:T(8,128)(2,1)} custom-call(s32[1]{0:T(128)} %bitcast.3.refs_0_, bf16[256,2048]{1,0:T(8,128)(2,1)} %bitcast.22, bf16[256,2048]{1,0:T(8,128)(2,1)} %collective-permute-done.2.refs_1_.refs_2_, bf16[256,2048]{1,0:T(8,128)(2,1)} %hold.14.refs_0_.refs_3_, bf16[256,2048]{1,0:T(8,128)(2,1)} %collective-permute-done.13.refs_1_.refs_4_, ...), custom_call_target="tpu_custom_call" | custom-call | tf_op jit(solution)/shard_map/product/pallas_call | solution.py:81
  186.9 7.5 %product.8.refs_2_.refs_0_ = bf16[1024,1408]{1,0:T(8,128)(2,1)} custom-call(s32[1]{0:T(128)} %bitcast.3.refs_0_, bf16[256,2048]{1,0:T(8,128)(2,1)} %get-tuple-element.122.refs_0_.refs_1_, bf16[144,2048]{1,0:T(8,128)(2,1)} %collective-permute-done.14.refs_1_.refs_2_, bf16[128,2048]{1,0:T(8,128)(2,1)} %collective-permute-done.15.refs_2_.refs_3_, ...), custom_call_target="tpu_custom_call" | custom-call | tf_op jit(solution)/shard_map/product/pallas_call | solution.py:81
  194.4 7.1 %feed_out.2 = (bf16[256,2048]{1,0:T(8,128)(2,1)}, bf16[256,2048]{1,0:T(8,128)(2,1)}) custom-call(bf16[512,1408]{1,0:T(8,128)(2,1)} %get-tuple-element.129.refs_6_.refs_0_, bf16[1408,2048]{1,0:T(8,128)(2,1)} %refs_1_.3, bf16[1024,1408]{1,0:T(8,128)(2,1)} %product.8.refs_2_.refs_0_), custom_call_target="tpu_custom_call" | custom-call | tf_op jit(solution)/shard_map/feed_out/pallas_call | solution.py:70
  201.9 6.3 %turn.1 = (f32[256,2048]{1,0:T(8,128)}, f32[1,2048]{1,0:T(1,128)}, bf16[272,2048]{1,0:T(8,128)(2,1)}) custom-call(bf16[256,2048]{1,0:T(8,128)(2,1)} %bitcast.23, bf16[256,2048]{1,0:T(8,128)(2,1)} %get-tuple-element.128.refs_1_, bf16[256,2048]{1,0:T(8,128)(2,1)} %collective-permute-done.22.refs_2_, bf16[256,2048]{1,0:T(8,128)(2,1)} %collective-permute-done.23.refs_3_, ...), custom_call_target="tpu_custom_call" | custom-call | tf_op jit(solution)/shard_map/turn/pallas_call | solution.py:70
  211.4 9.2 %back_local.2 = (bf16[2,256,512]{2,1,0:T(8,128)(2,1)}, bf16[2,256,512]{2,1,0:T(8,128)(2,1)}, f32[2,256,512]{2,1,0:T(8,128)}, f32[2,256,512]{2,1,0:T(8,128)}, f32[2,2,512]{2,1,0:T(2,128)}, /*index=5*/f32[1,512]{1,0:T(1,128)}) custom-call(bf16[272,2048]{1,0:T(8,128)(2,1)} %get-tuple-element.139.refs_0_.refs_1_, ...), custom_call_target="tpu_custom_call" | custom-call | tf_op jit(solution)/shard_map/back_local/pallas_call | solution.py:70
  224.3 7.1 %feed_out.3 = (bf16[256,2048]{1,0:T(8,128)(2,1)}, bf16[256,2048]{1,0:T(8,128)(2,1)}) custom-call(bf16[512,1408]{1,0:T(8,128)(2,1)} %get-tuple-element.125.refs_5_.refs_0_, bf16[1408,2048]{1,0:T(8,128)(2,1)} %refs_1_.3, bf16[256,2048]{1,0:T(8,128)(2,1)} %plus.4.refs_2_.refs_0_), custom_call_target="tpu_custom_call" | custom-call | tf_op jit(solution)/shard_map/feed_out/pallas_call | solution.py:70
  231.4 4.2 collective-permute-done.26.refs_0_
  238.7 9.2 %back_local.3 = (bf16[2,256,512]{2,1,0:T(8,128)(2,1)}, bf16[2,256,512]{2,1,0:T(8,128)(2,1)}, f32[2,256,512]{2,1,0:T(8,128)}, f32[2,256,512]{2,1,0:T(8,128)}, f32[2,4,512]{2,1,0:T(4,128)}, /*index=5*/f32[1,512]{1,0:T(1,128)}) custom-call(bf16[272,2048]{1,0:T(8,128)(2,1)} %hold.17.refs_0_.refs_3_, bf16[272,2048]{1,0:T(8,128)(2,1)} %collective-permute-done.27.refs_1_.refs_4_, ...), custom_call_target="tpu_custom_call" | custom-call | tf_op jit(solution)/shard_map/back_local/pallas_call | solution.py:70
  259.3 9.0 %product_add.6 = (bf16[512,1408]{1,0:T(8,128)(2,1)}, bf16[512,1408]{1,0:T(8,128)(2,1)}) custom-call(s32[1]{0:T(128)} %bitcast.3.refs_0_, bf16[256,2048]{1,0:T(8,128)(2,1)} %get-tuple-element.122.refs_0_.refs_1_, bf16[144,2048]{1,0:T(8,128)(2,1)} %collective-permute-done.14.refs_1_.refs_2_, bf16[128,2048]{1,0:T(8,128)(2,1)} %collective-permute-done.15.refs_2_.refs_3_, ...), custom_call_target="tpu_custom_call" | custom-call | tf_op jit(solution)/shard_map/product_add/pallas_call | solution.py:81
  268.3 8.5 %product_add.7 = (bf16[512,1408]{1,0:T(8,128)(2,1)}, bf16[512,1408]{1,0:T(8,128)(2,1)}) custom-call(s32[1]{0:T(128)} %bitcast.3.refs_0_, bf16[256,2048]{1,0:T(8,128)(2,1)} %bitcast.24, bf16[256,2048]{1,0:T(8,128)(2,1)} %collective-permute-done.2.refs_1_.refs_2_, bf16[256,2048]{1,0:T(8,128)(2,1)} %hold.14.refs_0_.refs_3_, ...), custom_call_target="tpu_custom_call" | custom-call | tf_op jit(solution)/shard_map/product_add/pallas_call | solution.py:81
  280.9 10.3 %back_mix.2 = (bf16[2,256,1024]{2,1,0:T(8,128)(2,1)}, bf16[256,2048]{1,0:T(8,128)(2,1)}, bf16[256,2048]{1,0:T(8,128)(2,1)}, f32[2,1,512]{2,1,0:T(1,128)}) custom-call(f32[2,256,512]{2,1,0:T(8,128)} %get-tuple-element.154.refs_0_, f32[2,256,512]{2,1,0:T(8,128)} %get-tuple-element.155.refs_1_, f32[2,256,512]{2,1,0:T(8,128)} %get-tuple-element.150.refs_5_.refs_2_, ...), custom_call_target="tpu_custom_call" | custom-call | tf_op jit(solution)/shard_map/back_mix/pallas_call | solution.py:70
  297.8 10.2 %back_mix.3 = (bf16[2,256,1024]{2,1,0:T(8,128)(2,1)}, bf16[256,2048]{1,0:T(8,128)(2,1)}, bf16[256,2048]{1,0:T(8,128)(2,1)}, f32[2,1,512]{2,1,0:T(1,128)}) custom-call(f32[2,256,512]{2,1,0:T(8,128)} %get-tuple-element.145.refs_0_, f32[2,256,512]{2,1,0:T(8,128)} %get-tuple-element.146.refs_1_, f32[2,256,512]{2,1,0:T(8,128)} %get-tuple-element.141.refs_5_.refs_2_, ...), custom_call_target="tpu_custom_call" | custom-call | tf_op jit(solution)/shard_map/back_mix/pallas_call | solution.py:70
  315.0 6.3 %product.9.refs_11_ = bf16[1024,1024]{1,0:T(8,128)(2,1)} custom-call(s32[1]{0:T(128)} %bitcast.3.refs_0_, bf16[256,2048]{1,0:T(8,128)(2,1)} %first_norm.1.refs_0_.refs_1_, bf16[256,2048]{1,0:T(8,128)(2,1)} %collective-permute-done.refs_1_.refs_2_, bf16[256,2048]{1,0:T(8,128)(2,1)} %hold.12.refs_0_.refs_3_, ...), custom_call_target="tpu_custom_call" | custom-call | tf_op jit(solution)/shard_map/product/pallas_call | solution.py:81
  322.2 8.6 %product_add.8 = (bf16[512,1408]{1,0:T(8,128)(2,1)}, bf16[512,1408]{1,0:T(8,128)(2,1)}) custom-call(s32[1]{0:T(128)} %bitcast.3.refs_0_, bf16[256,2048]{1,0:T(8,128)(2,1)} %get-tuple-element.122.refs_0_.refs_1_, bf16[144,2048]{1,0:T(8,128)(2,1)} %collective-permute-done.14.refs_1_.refs_2_, bf16[128,2048]{1,0:T(8,128)(2,1)} %collective-permute-done.15.refs_2_.refs_3_, ...), custom_call_target="tpu_custom_call" | custom-call | tf_op jit(solution)/shard_map/product_add/pallas_call | solution.py:81
  334.0 5.4 %last.1 = (f32[256,2048]{1,0:T(8,128)}, f32[1,2048]{1,0:T(1,128)}) custom-call(bf16[256,2048]{1,0:T(8,128)(2,1)} %bitcast.29, bf16[256,2048]{1,0:T(8,128)(2,1)} %get-tuple-element.160.refs_2_.refs_1_, bf16[256,2048]{1,0:T(8,128)(2,1)} %collective-permute-done.35.refs_2_, bf16[256,2048]{1,0:T(8,128)(2,1)} %collective-permute-done.36.refs_3_, ...), custom_call_target="tpu_custom_call" | custom-call | tf_op jit(solution)/shard_map/last/pallas_call | solution.py:70
  341.0 9.5 %collective-permute-done.40.refs_1_ = bf16[512,1408]{1,0:T(8,128)(2,1)} collective-permute-done((bf16[512,1408]{1,0:T(8,128)(2,1)}, bf16[512,1408]{1,0:T(8,128)(2,1)}, u32[]{:S(2)}, u32[]{:S(2)}) %collective-permute-start.40) | collective-permute-done | bytes 1441824 | tf_op jit(solution)/shard_map/ppermute | solution.py:18
  350.5 3.8 collective-permute-start.44
  354.3 4.9 product.10.refs_2_
  362.6 5.0 product.11.refs_4_
  369.6 4.3 result.1.refs_2_
  373.9 4.0 collective-permute-done.45.refs_1_
  387.6 7.8 %collective-permute-done.43.refs_7_ = bf16[1024,1024]{1,0:T(8,128)(2,1)} collective-permute-done((bf16[1024,1024]{1,0:T(8,128)(2,1)}, bf16[1024,1024]{1,0:T(8,128)(2,1)}, u32[]{:S(2)}, u32[]{:S(2)}) %collective-permute-start.43) | collective-permute-done | bytes 2097184 | tf_op jit(solution)/shard_map/ppermute | solution.py:18
  395.5 7.2 %product_add.9 = (bf16[512,1024]{1,0:T(8,128)(2,1)}, bf16[512,1024]{1,0:T(8,128)(2,1)}) custom-call(s32[1]{0:T(128)} %bitcast.3.refs_0_, bf16[256,2048]{1,0:T(8,128)(2,1)} %first_norm.1.refs_0_.refs_1_, bf16[256,2048]{1,0:T(8,128)(2,1)} %collective-permute-done.refs_1_.refs_2_, bf16[256,2048]{1,0:T(8,128)(2,1)} %hold.12.refs_0_.refs_3_, ...), custom_call_target="tpu_custom_call" | custom-call | tf_op jit(solution)/shard_map/product_add/pallas_call | solution.py:81
  407.2 10.7 %collective-permute-done.42.refs_7_ = bf16[1024,512]{1,0:T(8,128)(2,1)} collective-permute-done((bf16[1024,512]{1,0:T(8,128)(2,1)}, bf16[1024,512]{1,0:T(8,128)(2,1)}, u32[]{:S(2)}, u32[]{:S(2)}) %collective-permute-start.42) | collective-permute-done | bytes 1048608 | tf_op jit(solution)/shard_map/ppermute | solution.py:18
  417.9 5.4 %product_add.10 = (bf16[512,512]{1,0:T(8,128)(2,1)}, bf16[512,512]{1,0:T(8,128)(2,1)}) custom-call(s32[1]{0:T(128)} %bitcast.3.refs_0_, bf16[272,2048]{1,0:T(8,128)(2,1)} %get-tuple-element.139.refs_0_.refs_1_, bf16[272,2048]{1,0:T(8,128)(2,1)} %collective-permute-done.24.refs_1_.refs_2_, bf16[272,2048]{1,0:T(8,128)(2,1)} %hold.17.refs_0_.refs_3_, ...), custom_call_target="tpu_custom_call" | custom-call | tf_op jit(solution)/shard_map/product_add/pallas_call | solution.py:81
  423.3 15.5 %collective-permute-done.41.refs_7_ = bf16[1024,512]{1,0:T(8,128)(2,1)} collective-permute-done((bf16[1024,512]{1,0:T(8,128)(2,1)}, bf16[1024,512]{1,0:T(8,128)(2,1)}, u32[]{:S(2)}, u32[]{:S(2)}) %collective-permute-start.41) | collective-permute-done | bytes 1048608 | tf_op jit(solution)/shard_map/ppermute | solution.py:18
  438.8 5.4 %product_add.11 = (bf16[512,512]{1,0:T(8,128)(2,1)}, bf16[512,512]{1,0:T(8,128)(2,1)}) custom-call(s32[1]{0:T(128)} %bitcast.3.refs_0_, bf16[256,2048]{1,0:T(8,128)(2,1)} %first_norm.1.refs_0_.refs_1_, bf16[256,2048]{1,0:T(8,128)(2,1)} %collective-permute-done.refs_1_.refs_2_, bf16[256,2048]{1,0:T(8,128)(2,1)} %hold.12.refs_0_.refs_3_, ...), custom_call_target="tpu_custom_call" | custom-call | tf_op jit(solution)/shard_map/product_add/pallas_call | solution.py:81
  457.1 3.8 collective-permute-start.51
  463.4 7.2 %collective-permute-done.47.two = bf16[256,1408]{1,0:T(8,128)(2,1)} collective-permute-done((bf16[256,1408]{1,0:T(8,128)(2,1)S(1)}, bf16[256,1408]{1,0:T(8,128)(2,1)}, u32[]{:S(2)}, u32[]{:S(2)}) %collective-permute-start.47) | collective-permute-done | bytes 720928 | tf_op jit(solution)/shard_map/ppermute | solution.py:18
  474.2 8.8 %collective-permute-done.46.refs_1_ = bf16[512,512]{1,0:T(8,128)(2,1)} collective-permute-done((bf16[512,512]{1,0:T(8,128)(2,1)}, bf16[512,512]{1,0:T(8,128)(2,1)}, u32[]{:S(2)}, u32[]{:S(2)}) %collective-permute-start.46) | collective-permute-done | bytes 524320 | tf_op jit(solution)/shard_map/ppermute | solution.py:18
  487.1 5.3 %collective-permute-done.52.refs_1_ = bf16[512,512]{1,0:T(8,128)(2,1)} collective-permute-done((bf16[512,512]{1,0:T(8,128)(2,1)}, bf16[512,512]{1,0:T(8,128)(2,1)}, u32[]{:S(2)}, u32[]{:S(2)}) %collective-permute-start.52) | collective-permute-done | bytes 524320 | tf_op jit(solution)/shard_map/ppermute | solution.py:18
  501.6 7.8 %collective-permute-done.50.two = bf16[256,512]{1,0:T(8,128)(2,1)S(1)} collective-permute-done((bf16[256,512]{1,0:T(8,128)(2,1)}, bf16[256,512]{1,0:T(8,128)(2,1)S(1)}, u32[]{:S(2)}, u32[]{:S(2)}) %collective-permute-start.50) | collective-permute-done | bytes 262176 | tf_op jit(solution)/shard_map/ppermute | solution.py:18
  (207 shorter events, 160.7 us)
Async XLA Ops:
  4.3 4.8 collective-permute-start
  4.8 15.3 %collective-permute-start.2 = (bf16[256,2048]{1,0:T(8,128)(2,1)}, bf16[256,2048]{1,0:T(8,128)(2,1)}, u32[]{:S(2)}, u32[]{:S(2)}) collective-permute-start(bf16[256,2048]{1,0:T(8,128)(2,1)} %bitcast.20), channel_id=1, source_target_pairs={{0,1},{1,0},{2,3},{3,2},{4,5},{5,4},{6,7},{7,6},{8,9},{9,8},{10,11... | collective-permute-start | bytes 3145736 | tf_op jit(solution)/shard_map/ppermute | solution.py:18
  4.8 26.6 %collective-permute-start.1 = (bf16[256,2048]{1,0:T(8,128)(2,1)}, bf16[256,2048]{1,0:T(8,128)(2,1)}, u32[]{:S(2)}, u32[]{:S(2)}) collective-permute-start(bf16[256,2048]{1,0:T(8,128)(2,1)} %first_norm.1.refs_0_.refs_1_), channel_id=1, source_target_pairs={{0,2},{1,3},{2,0},{3,1},{4,6},{5,7},{6,4},{7,5},{8,10},{9,11},{10,... | collective-permute-start | bytes 3145736 | tf_op jit(solution)/shard_map/ppermute | solution.py:18
  32.4 45.0 %collective-permute-start.12 = (bf16[256,2048]{1,0:T(8,128)(2,1)}, bf16[256,2048]{1,0:T(8,128)(2,1)}, u32[]{:S(2)}, u32[]{:S(2)}) collective-permute-start(bf16[256,2048]{1,0:T(8,128)(2,1)} %hold.13), channel_id=1, source_target_pairs={{0,2},{1,3},{2,0},{3,1},{4,6},{5,7},{6,4},{7,5},{8,10},{9,11},{10,... | collective-permute-start | bytes 3145736 | tf_op jit(solution)/shard_map/ppermute | solution.py:18
  51.9 11.0 %collective-permute-start.5 = (f32[2,4,512]{2,1,0:T(4,128)}, f32[2,4,512]{2,1,0:T(4,128)S(1)}, u32[]{:S(2)}, u32[]{:S(2)}) collective-permute-start(f32[2,4,512]{2,1,0:T(4,128)} %pair.2), channel_id=1, source_target_pairs={{0,8},{4,12},{8,16},{12,20},{16,24},{20,28},{1,9},{5,13},{9,17},{1... | collective-permute-start | bytes 49160 | tf_op jit(solution)/shard_map/ppermute | solution.py:24
  55.6 7.3 %collective-permute-start.6 = (f32[2,4,512]{2,1,0:T(4,128)}, f32[2,4,512]{2,1,0:T(4,128)S(1)}, u32[]{:S(2)}, u32[]{:S(2)}) collective-permute-start(f32[2,4,512]{2,1,0:T(4,128)} %pair.2), channel_id=1, source_target_pairs={{0,16},{4,20},{8,24},{12,28},{1,17},{5,21},{9,25},{13,29},{2,18},{... | collective-permute-start | bytes 49160 | tf_op jit(solution)/shard_map/ppermute | solution.py:24
  71.2 6.3 %collective-permute-start.9 = (bf16[272,2048]{1,0:T(8,128)(2,1)}, bf16[272,2048]{1,0:T(8,128)(2,1)}, u32[]{:S(2)}, u32[]{:S(2)}) collective-permute-start(bf16[272,2048]{1,0:T(8,128)(2,1)} %get-tuple-element.114), channel_id=1, source_target_pairs={{0,1},{1,0},{2,3},{3,2},{4,5},{5,4},{6,7},{7,6},{8,9},{9,8},{10,11... | collective-permute-start | bytes 3342344 | tf_op jit(solution)/shard_map/ppermute | solution.py:18
  76.9 13.0 %collective-permute-start.8 = (bf16[272,2048]{1,0:T(8,128)(2,1)}, bf16[272,2048]{1,0:T(8,128)(2,1)}, u32[]{:S(2)}, u32[]{:S(2)}) collective-permute-start(bf16[272,2048]{1,0:T(8,128)(2,1)} %get-tuple-element.113), channel_id=1, source_target_pairs={{0,1},{1,0},{2,3},{3,2},{4,5},{5,4},{6,7},{7,6},{8,9},{9,8},{10,11... | collective-permute-start | bytes 3342344 | tf_op jit(solution)/shard_map/ppermute | solution.py:18
  77.4 4.9 collective-permute-start.13
  80.3 16.3 %collective-permute-start.11 = (bf16[144,2048]{1,0:T(8,128)(2,1)}, bf16[144,2048]{1,0:T(8,128)(2,1)S(1)}, u32[]{:S(2)}, u32[]{:S(2)}) collective-permute-start(bf16[144,2048]{1,0:T(8,128)(2,1)} %get-tuple-element.116), channel_id=1, source_target_pairs={{0,2},{1,3},{2,0},{3,1},{4,6},{5,7},{6,4},{7,5},{8,10},{9,11},{10,... | collective-permute-start | bytes 1769480 | tf_op jit(solution)/shard_map/ppermute | solution.py:18
  81.8 26.2 %collective-permute-start.10 = (bf16[128,2048]{1,0:T(8,128)(2,1)}, bf16[128,2048]{1,0:T(8,128)(2,1)}, u32[]{:S(2)}, u32[]{:S(2)}) collective-permute-start(bf16[128,2048]{1,0:T(8,128)(2,1)} %get-tuple-element.115.refs_3_), channel_id=1, source_target_pairs={{0,2},{1,3},{2,0},{3,1},{4,6},{5,7},{6,4},{7,5},{8,10},{9,11},{10,... | collective-permute-start | bytes 1572872 | tf_op jit(solution)/shard_map/ppermute | solution.py:18
  101.1 12.8 %collective-permute-start.14 = (bf16[144,2048]{1,0:T(8,128)(2,1)}, bf16[144,2048]{1,0:T(8,128)(2,1)}, u32[]{:S(2)}, u32[]{:S(2)}) collective-permute-start(bf16[144,2048]{1,0:T(8,128)(2,1)} %get-tuple-element.123), channel_id=1, source_target_pairs={{0,1},{1,0},{2,3},{3,2},{4,5},{5,4},{6,7},{7,6},{8,9},{9,8},{10,11... | collective-permute-start | bytes 1769480 | tf_op jit(solution)/shard_map/ppermute | solution.py:18
  101.1 35.7 %collective-permute-start.16 = (bf16[144,2048]{1,0:T(8,128)(2,1)}, bf16[144,2048]{1,0:T(8,128)(2,1)S(1)}, u32[]{:S(2)}, u32[]{:S(2)}) collective-permute-start(bf16[144,2048]{1,0:T(8,128)(2,1)} %get-tuple-element.123), channel_id=1, source_target_pairs={{0,2},{1,3},{2,0},{3,1},{4,6},{5,7},{6,4},{7,5},{8,10},{9,11},{10,... | collective-permute-start | bytes 1769480 | tf_op jit(solution)/shard_map/ppermute | solution.py:18
  111.6 26.1 %collective-permute-start.17 = (bf16[128,2048]{1,0:T(8,128)(2,1)}, bf16[128,2048]{1,0:T(8,128)(2,1)}, u32[]{:S(2)}, u32[]{:S(2)}) collective-permute-start(bf16[128,2048]{1,0:T(8,128)(2,1)} %get-tuple-element.124), channel_id=1, source_target_pairs={{0,2},{1,3},{2,0},{3,1},{4,6},{5,7},{6,4},{7,5},{8,10},{9,11},{10,... | collective-permute-start | bytes 1572872 | tf_op jit(solution)/shard_map/ppermute | solution.py:18
  164.5 8.3 %collective-permute-start.20 = (bf16[256,2048]{1,0:T(8,128)(2,1)}, bf16[256,2048]{1,0:T(8,128)(2,1)}, u32[]{:S(2)}, u32[]{:S(2)}) collective-permute-start(bf16[256,2048]{1,0:T(8,128)(2,1)} %get-tuple-element.133), channel_id=1, source_target_pairs={{0,1},{1,0},{2,3},{3,2},{4,5},{5,4},{6,7},{7,6},{8,9},{9,8},{10,11... | collective-permute-start | bytes 3145736 | tf_op jit(solution)/shard_map/ppermute | solution.py:18
  164.6 37.0 %collective-permute-start.22 = (bf16[256,2048]{1,0:T(8,128)(2,1)}, bf16[256,2048]{1,0:T(8,128)(2,1)}, u32[]{:S(2)}, u32[]{:S(2)}) collective-permute-start(bf16[256,2048]{1,0:T(8,128)(2,1)} %get-tuple-element.136), channel_id=1, source_target_pairs={{0,1},{1,0},{2,3},{3,2},{4,5},{5,4},{6,7},{7,6},{8,9},{9,8},{10,11... | collective-permute-start | bytes 3145736 | tf_op jit(solution)/shard_map/ppermute | solution.py:18
  176.4 25.5 %collective-permute-start.23 = (bf16[256,2048]{1,0:T(8,128)(2,1)}, bf16[256,2048]{1,0:T(8,128)(2,1)}, u32[]{:S(2)}, u32[]{:S(2)}) collective-permute-start(bf16[256,2048]{1,0:T(8,128)(2,1)} %plus.3.refs_7_.refs_11_), channel_id=1, source_target_pairs={{0,2},{1,3},{2,0},{3,1},{4,6},{5,7},{6,4},{7,5},{8,10},{9,11},{10,... | collective-permute-start | bytes 3145736 | tf_op jit(solution)/shard_map/ppermute | solution.py:18
  177.9 80.1 %collective-permute-start.33 = (bf16[1152,1408]{1,0:T(8,128)(2,1)}, bf16[1152,1408]{1,0:T(8,128)(2,1)}, u32[]{:S(2)}, u32[]{:S(2)}) collective-permute-start(bf16[1152,1408]{1,0:T(8,128)(2,1)} %product.6.refs_2_), channel_id=1, source_target_pairs={{0,4},{4,0},{8,12},{12,8},{16,20},{20,16},{24,28},{28,24},{1,5},{5... | collective-permute-start | bytes 9732104 | tf_op jit(solution)/shard_map/ppermute | solution.py:18
  186.9 81.4 %collective-permute-start.32 = (bf16[1152,1408]{1,0:T(8,128)(2,1)}, bf16[1152,1408]{1,0:T(8,128)(2,1)}, u32[]{:S(2)}, u32[]{:S(2)}) collective-permute-start(bf16[1152,1408]{1,0:T(8,128)(2,1)} %product.7.refs_10_), channel_id=1, source_target_pairs={{0,8},{4,12},{8,0},{12,4},{16,24},{20,28},{24,16},{28,20},{1,9},{5... | collective-permute-start | bytes 9732104 | tf_op jit(solution)/shard_map/ppermute | solution.py:18
  208.3 27.3 %collective-permute-start.26 = (bf16[272,2048]{1,0:T(8,128)(2,1)}, bf16[272,2048]{1,0:T(8,128)(2,1)}, u32[]{:S(2)}, u32[]{:S(2)}) collective-permute-start(bf16[272,2048]{1,0:T(8,128)(2,1)} %get-tuple-element.139.refs_0_.refs_1_), channel_id=1, source_target_pairs={{0,2},{1,3},{2,0},{3,1},{4,6},{5,7},{6,4},{7,5},{8,10},{9,11},{10,... | collective-permute-start | bytes 3342344 | tf_op jit(solution)/shard_map/ppermute | solution.py:18
  209.9 10.7 %collective-permute-start.21 = (bf16[256,2048]{1,0:T(8,128)(2,1)}, bf16[256,2048]{1,0:T(8,128)(2,1)}, u32[]{:S(2)}, u32[]{:S(2)}) collective-permute-start(bf16[256,2048]{1,0:T(8,128)(2,1)} %get-tuple-element.135), channel_id=1, source_target_pairs={{0,1},{1,0},{2,3},{3,2},{4,5},{5,4},{6,7},{7,6},{8,9},{9,8},{10,11... | collective-permute-start | bytes 3145736 | tf_op jit(solution)/shard_map/ppermute | solution.py:18
  247.9 4.0 collective-permute-start.28
  253.9 68.4 %collective-permute-start.37 = (bf16[1024,1408]{1,0:T(8,128)(2,1)}, bf16[1024,1408]{1,0:T(8,128)(2,1)}, u32[]{:S(2)}, u32[]{:S(2)}) collective-permute-start(bf16[1024,1408]{1,0:T(8,128)(2,1)} %hold.18), channel_id=1, source_target_pairs={{0,4},{4,0},{8,12},{12,8},{16,20},{20,16},{24,28},{28,24},{1,5},{5... | collective-permute-start | bytes 8650760 | tf_op jit(solution)/shard_map/ppermute | solution.py:18
  255.4 21.4 %collective-permute-start.29 = (f32[2,4,512]{2,1,0:T(4,128)S(1)}, f32[2,4,512]{2,1,0:T(4,128)S(1)}, u32[]{:S(2)}, u32[]{:S(2)}) collective-permute-start(f32[2,4,512]{2,1,0:T(4,128)S(1)} %copy-done.8), channel_id=1, source_target_pairs={{8,0},{12,4},{16,8},{20,12},{24,16},{28,20},{9,1},{13,5},{17,9},{2... | collective-permute-start | bytes 49160 | tf_op jit(solution)/shard_map/ppermute | solution.py:24
  256.7 20.1 %collective-permute-start.30 = (f32[2,4,512]{2,1,0:T(4,128)S(1)}, f32[2,4,512]{2,1,0:T(4,128)S(1)}, u32[]{:S(2)}, u32[]{:S(2)}) collective-permute-start(f32[2,4,512]{2,1,0:T(4,128)S(1)} %copy-done.8), channel_id=1, source_target_pairs={{16,0},{20,4},{24,8},{28,12},{17,1},{21,5},{25,9},{29,13},{18,2},{... | collective-permute-start | bytes 49160 | tf_op jit(solution)/shard_map/ppermute | solution.py:24
  258.0 18.8 %collective-permute-start.31 = (f32[2,4,512]{2,1,0:T(4,128)S(1)}, f32[2,4,512]{2,1,0:T(4,128)S(1)}, u32[]{:S(2)}, u32[]{:S(2)}) collective-permute-start(f32[2,4,512]{2,1,0:T(4,128)S(1)} %copy-done.8), channel_id=1, source_target_pairs={{24,0},{28,4},{25,1},{29,5},{26,2},{30,6},{27,3},{31,7}} | collective-permute-start | bytes 49160 | tf_op jit(solution)/shard_map/ppermute | solution.py:24
  278.8 32.9 %collective-permute-start.38 = (bf16[512,1408]{1,0:T(8,128)(2,1)}, bf16[512,1408]{1,0:T(8,128)(2,1)}, u32[]{:S(2)}, u32[]{:S(2)}) collective-permute-start(bf16[512,1408]{1,0:T(8,128)(2,1)} %hold.19), channel_id=1, source_target_pairs={{0,8},{4,12},{8,0},{12,4},{16,24},{20,28},{24,16},{28,20},{1,9},{5... | collective-permute-start | bytes 4325384 | tf_op jit(solution)/shard_map/ppermute | solution.py:18
  308.1 24.5 %collective-permute-start.35 = (bf16[256,2048]{1,0:T(8,128)(2,1)}, bf16[256,2048]{1,0:T(8,128)(2,1)}, u32[]{:S(2)}, u32[]{:S(2)}) collective-permute-start(bf16[256,2048]{1,0:T(8,128)(2,1)} %get-tuple-element.161), channel_id=1, source_target_pairs={{0,1},{1,0},{2,3},{3,2},{4,5},{5,4},{6,7},{7,6},{8,9},{9,8},{10,11... | collective-permute-start | bytes 3145736 | tf_op jit(solution)/shard_map/ppermute | solution.py:18
  308.3 25.7 %collective-permute-start.36 = (bf16[256,2048]{1,0:T(8,128)(2,1)}, bf16[256,2048]{1,0:T(8,128)(2,1)}, u32[]{:S(2)}, u32[]{:S(2)}) collective-permute-start(bf16[256,2048]{1,0:T(8,128)(2,1)} %plus.5.refs_10_), channel_id=1, source_target_pairs={{0,2},{1,3},{2,0},{3,1},{4,6},{5,7},{6,4},{7,5},{8,10},{9,11},{10,... | collective-permute-start | bytes 3145736 | tf_op jit(solution)/shard_map/ppermute | solution.py:18
  309.8 40.7 %collective-permute-start.40 = (bf16[512,1408]{1,0:T(8,128)(2,1)}, bf16[512,1408]{1,0:T(8,128)(2,1)}, u32[]{:S(2)}, u32[]{:S(2)}) collective-permute-start(bf16[512,1408]{1,0:T(8,128)(2,1)} %get-tuple-element.153.refs_6_), channel_id=1, source_target_pairs={{0,4},{4,0},{8,12},{12,8},{16,20},{20,16},{24,28},{28,24},{1,5},{5... | collective-permute-start | bytes 4325384 | tf_op jit(solution)/shard_map/ppermute | solution.py:18
  321.2 74.2 %collective-permute-start.43 = (bf16[1024,1024]{1,0:T(8,128)(2,1)}, bf16[1024,1024]{1,0:T(8,128)(2,1)}, u32[]{:S(2)}, u32[]{:S(2)}) collective-permute-start(bf16[1024,1024]{1,0:T(8,128)(2,1)} %product.9.refs_11_), channel_id=1, source_target_pairs={{0,4},{4,0},{8,12},{12,8},{16,20},{20,16},{24,28},{28,24},{1,5},{5... | collective-permute-start | bytes 6291464 | tf_op jit(solution)/shard_map/ppermute | solution.py:18
  330.8 47.1 %collective-permute-start.45 = (bf16[512,1408]{1,0:T(8,128)(2,1)}, bf16[512,1408]{1,0:T(8,128)(2,1)}, u32[]{:S(2)}, u32[]{:S(2)}) collective-permute-start(bf16[512,1408]{1,0:T(8,128)(2,1)} %get-tuple-element.167.refs_6_), channel_id=1, source_target_pairs={{0,8},{4,12},{8,0},{12,4},{16,24},{20,28},{24,16},{28,20},{1,9},{5... | collective-permute-start | bytes 4325384 | tf_op jit(solution)/shard_map/ppermute | solution.py:18
  332.6 34.9 %collective-permute-start.25 = (bf16[256,2048]{1,0:T(8,128)(2,1)}, bf16[256,2048]{1,0:T(8,128)(2,1)}, u32[]{:S(2)}, u32[]{:S(2)}) collective-permute-start(bf16[256,2048]{1,0:T(8,128)(2,1)} %get-tuple-element.144), channel_id=1, source_target_pairs={{0,1},{1,0},{2,3},{3,2},{4,5},{5,4},{6,7},{7,6},{8,9},{9,8},{10,11... | collective-permute-start | bytes 3145736 | tf_op jit(solution)/shard_map/ppermute | solution.py:18
  339.5 28.7 %collective-permute-start.39 = (bf16[256,2048]{1,0:T(8,128)(2,1)}, bf16[256,2048]{1,0:T(8,128)(2,1)}, u32[]{:S(2)}, u32[]{:S(2)}) collective-permute-start(bf16[256,2048]{1,0:T(8,128)(2,1)} %hold.20), channel_id=1, source_target_pairs={{0,2},{1,3},{2,0},{3,1},{4,6},{5,7},{6,4},{7,5},{8,10},{9,11},{10,... | collective-permute-start | bytes 3145736 | tf_op jit(solution)/shard_map/ppermute | solution.py:18
  350.5 32.6 %collective-permute-start.44 = (bf16[256,1408]{1,0:T(8,128)(2,1)}, bf16[256,1408]{1,0:T(8,128)(2,1)S(1)}, u32[]{:S(2)}, u32[]{:S(2)}) collective-permute-start(bf16[256,1408]{1,0:T(8,128)(2,1)} %get-tuple-element.166.refs_7_), channel_id=1, source_target_pairs={{0,16},{4,20},{8,24},{12,28},{16,0},{20,4},{24,8},{28,12},{1,17},{... | collective-permute-start | bytes 2162696 | tf_op jit(solution)/shard_map/ppermute | solution.py:18
  367.5 50.4 %collective-permute-start.42 = (bf16[1024,512]{1,0:T(8,128)(2,1)}, bf16[1024,512]{1,0:T(8,128)(2,1)}, u32[]{:S(2)}, u32[]{:S(2)}) collective-permute-start(bf16[1024,512]{1,0:T(8,128)(2,1)} %product.10.refs_2_), channel_id=1, source_target_pairs={{0,4},{4,0},{8,12},{12,8},{16,20},{20,16},{24,28},{28,24},{1,5},{5... | collective-permute-start | bytes 3145736 | tf_op jit(solution)/shard_map/ppermute | solution.py:18
  368.1 70.6 %collective-permute-start.41 = (bf16[1024,512]{1,0:T(8,128)(2,1)}, bf16[1024,512]{1,0:T(8,128)(2,1)}, u32[]{:S(2)}, u32[]{:S(2)}) collective-permute-start(bf16[1024,512]{1,0:T(8,128)(2,1)} %product.11.refs_4_), channel_id=1, source_target_pairs={{0,4},{4,0},{8,12},{12,8},{16,20},{20,16},{24,28},{28,24},{1,5},{5... | collective-permute-start | bytes 3145736 | tf_op jit(solution)/shard_map/ppermute | solution.py:18
  402.7 51.6 %collective-permute-start.49 = (bf16[512,1024]{1,0:T(8,128)(2,1)}, bf16[512,1024]{1,0:T(8,128)(2,1)}, u32[]{:S(2)}, u32[]{:S(2)}) collective-permute-start(bf16[512,1024]{1,0:T(8,128)(2,1)} %get-tuple-element.176.refs_8_), channel_id=1, source_target_pairs={{0,8},{4,12},{8,0},{12,4},{16,24},{20,28},{24,16},{28,20},{1,9},{5... | collective-permute-start | bytes 3145736 | tf_op jit(solution)/shard_map/ppermute | solution.py:18
  404.3 56.6 %collective-permute-start.48 = (bf16[256,1408]{1,0:T(8,128)(2,1)}, bf16[256,1408]{1,0:T(8,128)(2,1)}, u32[]{:S(2)}, u32[]{:S(2)}) collective-permute-start(bf16[256,1408]{1,0:T(8,128)(2,1)} %get-tuple-element.172.refs_7_), channel_id=1, source_target_pairs={{0,16},{4,20},{8,24},{12,28},{16,0},{20,4},{24,8},{28,12},{1,17},{... | collective-permute-start | bytes 2162696 | tf_op jit(solution)/shard_map/ppermute | solution.py:18
  406.8 63.8 %collective-permute-start.47 = (bf16[256,1408]{1,0:T(8,128)(2,1)S(1)}, bf16[256,1408]{1,0:T(8,128)(2,1)}, u32[]{:S(2)}, u32[]{:S(2)}) collective-permute-start(bf16[256,1408]{1,0:T(8,128)(2,1)S(1)} %copy-done.4), channel_id=1, source_target_pairs={{0,16},{4,20},{8,24},{12,28},{16,0},{20,4},{24,8},{28,12},{1,17},{... | collective-permute-start | bytes 2162696 | tf_op jit(solution)/shard_map/ppermute | solution.py:18
  444.2 38.9 %collective-permute-start.46 = (bf16[512,512]{1,0:T(8,128)(2,1)}, bf16[512,512]{1,0:T(8,128)(2,1)}, u32[]{:S(2)}, u32[]{:S(2)}) collective-permute-start(bf16[512,512]{1,0:T(8,128)(2,1)} %get-tuple-element.179.refs_2_), channel_id=1, source_target_pairs={{0,8},{4,12},{8,0},{12,4},{16,24},{20,28},{24,16},{28,20},{1,9},{5... | collective-permute-start | bytes 1572872 | tf_op jit(solution)/shard_map/ppermute | solution.py:18
  453.8 38.6 %collective-permute-start.52 = (bf16[512,512]{1,0:T(8,128)(2,1)}, bf16[512,512]{1,0:T(8,128)(2,1)}, u32[]{:S(2)}, u32[]{:S(2)}) collective-permute-start(bf16[512,512]{1,0:T(8,128)(2,1)} %get-tuple-element.177.refs_8_), channel_id=1, source_target_pairs={{0,8},{4,12},{8,0},{12,4},{16,24},{20,28},{24,16},{28,20},{1,9},{5... | collective-permute-start | bytes 1572872 | tf_op jit(solution)/shard_map/ppermute | solution.py:18
  457.1 41.1 %collective-permute-start.51 = (bf16[256,1024]{1,0:T(8,128)(2,1)}, bf16[256,1024]{1,0:T(8,128)(2,1)}, u32[]{:S(2)}, u32[]{:S(2)}) collective-permute-start(bf16[256,1024]{1,0:T(8,128)(2,1)} %get-tuple-element.183.refs_0_), channel_id=1, source_target_pairs={{0,16},{4,20},{8,24},{12,28},{16,0},{20,4},{24,8},{28,12},{1,17},{... | collective-permute-start | bytes 1572872 | tf_op jit(solution)/shard_map/ppermute | solution.py:18
  485.2 24.2 %collective-permute-start.50 = (bf16[256,512]{1,0:T(8,128)(2,1)}, bf16[256,512]{1,0:T(8,128)(2,1)S(1)}, u32[]{:S(2)}, u32[]{:S(2)}) collective-permute-start(bf16[256,512]{1,0:T(8,128)(2,1)} %get-tuple-element.185.refs_2_), channel_id=1, source_target_pairs={{0,16},{4,20},{8,24},{12,28},{16,0},{20,4},{24,8},{28,12},{1,17},{... | collective-permute-start | bytes 786440 | tf_op jit(solution)/shard_map/ppermute | solution.py:18
  485.2 9.3 %collective-permute-start.57 = (f32[4,512]{1,0:T(4,128)S(1)}, f32[4,512]{1,0:T(4,128)S(1)}, u32[]{:S(2)}, u32[]{:S(2)}) collective-permute-start(f32[4,512]{1,0:T(4,128)S(1)} %pad_maximum_fusion), channel_id=1, source_target_pairs={{0,4},{4,0},{8,12},{12,8},{16,20},{20,16},{24,28},{28,24},{1,5},{5... | collective-permute-start | bytes 24584 | tf_op jit(solution)/shard_map/ppermute | solution.py:18
  494.5 20.2 %collective-permute-start.53 = (bf16[256,512]{1,0:T(8,128)(2,1)}, bf16[256,512]{1,0:T(8,128)(2,1)S(1)}, u32[]{:S(2)}, u32[]{:S(2)}) collective-permute-start(bf16[256,512]{1,0:T(8,128)(2,1)} %get-tuple-element.188.refs_0_.refs_1_), channel_id=1, source_target_pairs={{0,16},{4,20},{8,24},{12,28},{16,0},{20,4},{24,8},{28,12},{1,17},{... | collective-permute-start | bytes 786440 | tf_op jit(solution)/shard_map/ppermute | solution.py:18
  495.8 17.4 %collective-permute-start.58 = (f32[4,512]{1,0:T(4,128)S(1)}, f32[4,512]{1,0:T(4,128)S(1)}, u32[]{:S(2)}, u32[]{:S(2)}) collective-permute-start(f32[4,512]{1,0:T(4,128)S(1)} %fusion.4), channel_id=1, source_target_pairs={{0,8},{4,12},{8,0},{12,4},{16,24},{20,28},{24,16},{28,20},{1,9},{5... | collective-permute-start | bytes 24584 | tf_op jit(solution)/shard_map/ppermute | solution.py:18
  514.6 4.7 collective-permute-start.59
  (39 other events, 134.4 us)

commit v6 on v5

--- a/solution.py
+++ b/solution.py
@@ -934,7 +934,7 @@
 GATE_AT, LOWER_AT, UP_AT, LOWER_BITS = "beside", "beside", "pair", "m"
 ORDER = (
     ("-p", "-n", "gs", "bb", "us", "-l", "ob", "ls", "ab", "-r", "us", "gf", "bs")
-    + ("os", "as", "bs", "lf", "uf", "as", "os", "-1", "bf", "af", "-2", "-3", "of")
+    + ("lf", "as", "os", "bs", "uf", "as", "os", "-1", "bf", "af", "-2", "-3", "of")
 )
 
 

time: 528 us -> 519 us (0.983)
  waiting for transfers between devices: 127 us -> 97 us
  starting transfers between devices: 65.3 us -> 85 us
    ppermute x54, waiting for transfers between devices: 127 us -> 96.9 us  [swap(): return lax.ppermute(values, axis, [(i, i ^ bit) for i in range(size)])]
    ppermute x54, starting transfers between devices: 51.7 us -> 71.5 us  [swap(): return lax.ppermute(values, axis, [(i, i ^ bit) for i in range(size)])]
  transfers between devices with their start and end apart: 60 -> 60, of which waited for: 30 -> 26; matrix products, arithmetic and copies ran while one was open for 1% -> 1% of each run, Pallas kernels for 55% -> 56%
where the time goes in v6:
time: 519 us; the launch traced here: 512 us
  Pallas kernels  312 us (60%)
  waiting for transfers between devices  97 us (19%)
  starting transfers between devices  85 us (16%)
  local copies, waits for them, and re-layouts  13.9 us (3%)
    pallas_call x30, Pallas kernels, call(): pl.pallas_call(body, grid=grid, in_specs=in_specs, out_specs=out_specs, s...  198 us
    ppermute x54, waiting for transfers between devices, swap(): return lax.ppermute(values, axis, [(i, i ^ bit) for i in range(size)])  96.9 us
    pallas_call x16, Pallas kernels, call(): got = pl.pallas_call(body, grid_spec=spec, **settings)(blocks, *operands)  88.6 us
    ppermute x54, starting transfers between devices, swap(): return lax.ppermute(values, axis, [(i, i ^ bit) for i in range(size)])  71.5 us
    pallas_call x6, Pallas kernels, finish(): pl.pallas_call(lambda one, two, *refs: finish_kernel(turned, one, two, *r...  18.2 us
    ppermute x6, starting transfers between devices, shift(): return lax.ppermute(values, axis, pairs)  13.5 us
    unnamed x55, local copies, waits for them, and re-layouts  10.6 us
  transfers between devices with their start and end apart: 60, of which 26 were waited for; matrix products, arithmetic and copies ran while one was open for 1% of the time, Pallas kernels for 56%

profile of v6, /device:TPU:0, one launch (start us, length us, event | category | flops | bytes accessed | tf_op | source)
XLA Modules:
  0.0 511.6 jit_solution(13949297962568177301)
XLA Ops:
  9.1 11.1 %project.2 = (f32[2,256,512]{2,1,0:T(8,128)}, f32[2,256,512]{2,1,0:T(8,128)}, f32[2,256,512]{2,1,0:T(8,128)}, f32[2,256,512]{2,1,0:T(8,128)}, f32[2,256,512]{2,1,0:T(8,128)}, /*index=5*/f32[2,2,512]{2,1,0:T(2,128)}) custom-call(bf16[256,2048]{1,0:T(8,128)(2,1)} %first_norm.1.refs_0_.refs_1_, bf16[256,2048]{1,0:T(8,128)(2,1)} %collective-permute-done.refs_1_.refs_2_, ...), custom_call_target="tpu_custom_call" | custom-call | tf_op jit(solution)/shard_map/project/pallas_call | solution.py:70
  20.1 7.4 %hidden_grad.2.refs_1_.refs_4_ = f32[512,1408]{1,0:T(8,128)} custom-call(bf16[256,2048]{1,0:T(8,128)(2,1)} %bitcast.21, bf16[256,2048]{1,0:T(8,128)(2,1)} %collective-permute-done.2.refs_1_.refs_2_, bf16[1408,2048]{1,0:T(8,128)(2,1)} %refs_1_.3, f32[2,2,512]{2,1,0:T(2,128)} %get-tuple-element.106.refs_3_.refs_4_), custom_call_target="tpu_custom_call" | custom-call | tf_op jit(solution)/shard_map/hidden_grad/pallas_call | solution.py:70
  27.6 3.8 collective-permute-done.1.refs_0_
  34.4 11.5 %project.3 = (f32[2,256,512]{2,1,0:T(8,128)}, f32[2,256,512]{2,1,0:T(8,128)}, f32[2,256,512]{2,1,0:T(8,128)}, f32[2,256,512]{2,1,0:T(8,128)}, f32[2,256,512]{2,1,0:T(8,128)}, /*index=5*/f32[2,4,512]{2,1,0:T(4,128)}) custom-call(bf16[256,2048]{1,0:T(8,128)(2,1)} %hold.12.refs_0_.refs_3_, bf16[256,2048]{1,0:T(8,128)(2,1)} %collective-permute-done.3.refs_1_.refs_4_, ...), custom_call_target="tpu_custom_call" | custom-call | tf_op jit(solution)/shard_map/project/pallas_call | solution.py:70
  51.9 3.7 collective-permute-start.5
  55.6 4.5 collective-permute-start.6
  65.6 5.6 %mix.2 = (f32[2,256,512]{2,1,0:T(8,128)}, bf16[272,2048]{1,0:T(8,128)(2,1)}, bf16[272,2048]{1,0:T(8,128)(2,1)}) custom-call(f32[2,256,512]{2,1,0:T(8,128)} %get-tuple-element.108.refs_0_, f32[2,256,512]{2,1,0:T(8,128)} %get-tuple-element.109.refs_1_, f32[2,256,512]{2,1,0:T(8,128)} %get-tuple-element.110.refs_2_.refs_3_, f32[4,1,512]{2,1,0:T(1,128)} %enter.2.refs_3_.refs_7_, ...), custom_call_target="tpu_custom_call" | custom-call | tf_op jit(solution)/shard_map/mix/pallas_call | solution.py:70
  71.3 5.6 %mix.3 = (f32[2,256,512]{2,1,0:T(8,128)}, bf16[272,2048]{1,0:T(8,128)(2,1)}, bf16[272,2048]{1,0:T(8,128)(2,1)}) custom-call(f32[2,256,512]{2,1,0:T(8,128)} %get-tuple-element.103.refs_0_, f32[2,256,512]{2,1,0:T(8,128)} %get-tuple-element.104.refs_1_, f32[2,256,512]{2,1,0:T(8,128)} %get-tuple-element.105.refs_2_.refs_3_, f32[4,1,512]{2,1,0:T(1,128)} %enter.2.refs_3_.refs_7_, ...), custom_call_target="tpu_custom_call" | custom-call | tf_op jit(solution)/shard_map/mix/pallas_call | solution.py:70
  82.3 7.5 %hidden_grad.3.refs_0_.refs_5_ = f32[512,1408]{1,0:T(8,128)} custom-call(bf16[256,2048]{1,0:T(8,128)(2,1)} %hold.14.refs_0_.refs_3_, bf16[256,2048]{1,0:T(8,128)(2,1)} %collective-permute-done.13.refs_1_.refs_4_, bf16[1408,2048]{1,0:T(8,128)(2,1)} %refs_1_.3, bf16[128,2048]{1,0:T(8,128)(2,1)} %get-tuple-element.115.refs_3_), custom_call_target="tpu_custom_call" | custom-call | tf_op jit(solution)/shard_map/hidden_grad/pallas_call | solution.py:70
  89.9 6.8 %collective-permute-done.11.hop.hop_more = bf16[144,2048]{1,0:T(8,128)(2,1)S(1)} collective-permute-done((bf16[144,2048]{1,0:T(8,128)(2,1)}, bf16[144,2048]{1,0:T(8,128)(2,1)S(1)}, u32[]{:S(2)}, u32[]{:S(2)}) %collective-permute-start.11) | collective-permute-done | bytes 589856 | tf_op jit(solution)/shard_map/ppermute | solution.py:18
  97.5 3.7 middle.2
  102.7 5.3 %collective-permute-done.10.hop = bf16[128,2048]{1,0:T(8,128)(2,1)} collective-permute-done((bf16[128,2048]{1,0:T(8,128)(2,1)}, bf16[128,2048]{1,0:T(8,128)(2,1)}, u32[]{:S(2)}, u32[]{:S(2)}) %collective-permute-start.10) | collective-permute-done | bytes 524320 | tf_op jit(solution)/shard_map/ppermute | solution.py:18
  113.9 12.0 %feed.2 = (bf16[512,1408]{1,0:T(8,128)(2,1)}, bf16[512,1408]{1,0:T(8,128)(2,1)}, bf16[512,1408]{1,0:T(8,128)(2,1)}) custom-call(bf16[256,2048]{1,0:T(8,128)(2,1)} %get-tuple-element.122.refs_0_.refs_1_, bf16[144,2048]{1,0:T(8,128)(2,1)} %collective-permute-done.14.refs_1_.refs_2_, bf16[128,2048]{1,0:T(8,128)(2,1)} %collective-permute-done.15.refs_2_.refs_3_, ...), custom_call_target="tpu_custom_call" | custom-call | tf_op jit(solution)/shard_map/feed/pallas_call | solution.py:70
  125.9 10.9 %feed_back.2 = (bf16[256,2048]{1,0:T(8,128)(2,1)}, bf16[256,2048]{1,0:T(8,128)(2,1)}) custom-call(bf16[512,1408]{1,0:T(8,128)(2,1)} %get-tuple-element.126.refs_0_.refs_8_, bf16[512,1408]{1,0:T(8,128)(2,1)} %get-tuple-element.127.refs_1_.refs_8_, bf16[2,2048,1408]{2,1,0:T(8,128)(2,1)} %refs_2_.13), custom_call_target="tpu_custom_call" | custom-call | tf_op jit(solution)/shard_map/feed_back/pallas_call | solution.py:70
  141.7 12.0 %feed.3 = (bf16[512,1408]{1,0:T(8,128)(2,1)}, bf16[512,1408]{1,0:T(8,128)(2,1)}, bf16[512,1408]{1,0:T(8,128)(2,1)}) custom-call(bf16[144,2048]{1,0:T(8,128)(2,1)} %hold.15.refs_0_.refs_4_, bf16[128,2048]{1,0:T(8,128)(2,1)} %hold.16.refs_1_.refs_5_, bf16[144,2048]{1,0:T(8,128)(2,1)} %copy-done.2, bf16[128,2048]{1,0:T(8,128)(2,1)} %collective-permute-done.19.refs_3_.refs_7_, ...), custom_call_target="tpu_custom_call" | custom-call | tf_op jit(solution)/shard_map/feed/pallas_call | solution.py:70
  153.7 10.9 %feed_back.3 = (bf16[256,2048]{1,0:T(8,128)(2,1)}, bf16[256,2048]{1,0:T(8,128)(2,1)}) custom-call(bf16[512,1408]{1,0:T(8,128)(2,1)} %get-tuple-element.131.refs_0_.refs_9_, bf16[512,1408]{1,0:T(8,128)(2,1)} %get-tuple-element.130.refs_1_.refs_9_, bf16[2,2048,1408]{2,1,0:T(8,128)(2,1)} %refs_2_.13), custom_call_target="tpu_custom_call" | custom-call | tf_op jit(solution)/shard_map/feed_back/pallas_call | solution.py:70
  165.1 7.8 %product.6.refs_2_ = bf16[1152,1408]{1,0:T(8,128)(2,1)} custom-call(s32[1]{0:T(128)} %bitcast.3.refs_0_, bf16[256,2048]{1,0:T(8,128)(2,1)} %get-tuple-element.122.refs_0_.refs_1_, bf16[144,2048]{1,0:T(8,128)(2,1)} %collective-permute-done.14.refs_1_.refs_2_, bf16[128,2048]{1,0:T(8,128)(2,1)} %collective-permute-done.15.refs_2_.refs_3_, ...), custom_call_target="tpu_custom_call" | custom-call | tf_op jit(solution)/shard_map/product/pallas_call | solution.py:81
  179.5 7.5 %product.7.refs_10_ = bf16[1152,1408]{1,0:T(8,128)(2,1)} custom-call(s32[1]{0:T(128)} %bitcast.3.refs_0_, bf16[256,2048]{1,0:T(8,128)(2,1)} %bitcast.22, bf16[256,2048]{1,0:T(8,128)(2,1)} %collective-permute-done.2.refs_1_.refs_2_, bf16[256,2048]{1,0:T(8,128)(2,1)} %hold.14.refs_0_.refs_3_, bf16[256,2048]{1,0:T(8,128)(2,1)} %collective-permute-done.13.refs_1_.refs_4_, ...), custom_call_target="tpu_custom_call" | custom-call | tf_op jit(solution)/shard_map/product/pallas_call | solution.py:81
  187.0 7.5 %product.8.refs_2_.refs_0_ = bf16[1024,1408]{1,0:T(8,128)(2,1)} custom-call(s32[1]{0:T(128)} %bitcast.3.refs_0_, bf16[256,2048]{1,0:T(8,128)(2,1)} %get-tuple-element.122.refs_0_.refs_1_, bf16[144,2048]{1,0:T(8,128)(2,1)} %collective-permute-done.14.refs_1_.refs_2_, bf16[128,2048]{1,0:T(8,128)(2,1)} %collective-permute-done.15.refs_2_.refs_3_, ...), custom_call_target="tpu_custom_call" | custom-call | tf_op jit(solution)/shard_map/product/pallas_call | solution.py:81
  194.5 7.1 %feed_out.2 = (bf16[256,2048]{1,0:T(8,128)(2,1)}, bf16[256,2048]{1,0:T(8,128)(2,1)}) custom-call(bf16[512,1408]{1,0:T(8,128)(2,1)} %get-tuple-element.129.refs_6_.refs_0_, bf16[1408,2048]{1,0:T(8,128)(2,1)} %refs_1_.3, bf16[1024,1408]{1,0:T(8,128)(2,1)} %product.8.refs_2_.refs_0_), custom_call_target="tpu_custom_call" | custom-call | tf_op jit(solution)/shard_map/feed_out/pallas_call | solution.py:70
  202.0 6.4 %turn.1 = (f32[256,2048]{1,0:T(8,128)}, f32[1,2048]{1,0:T(1,128)}, bf16[272,2048]{1,0:T(8,128)(2,1)}) custom-call(bf16[256,2048]{1,0:T(8,128)(2,1)} %bitcast.23, bf16[256,2048]{1,0:T(8,128)(2,1)} %get-tuple-element.128.refs_1_, bf16[256,2048]{1,0:T(8,128)(2,1)} %collective-permute-done.22.refs_2_, bf16[256,2048]{1,0:T(8,128)(2,1)} %collective-permute-done.23.refs_3_, ...), custom_call_target="tpu_custom_call" | custom-call | tf_op jit(solution)/shard_map/turn/pallas_call | solution.py:70
  211.6 9.2 %back_local.2 = (bf16[2,256,512]{2,1,0:T(8,128)(2,1)}, bf16[2,256,512]{2,1,0:T(8,128)(2,1)}, f32[2,256,512]{2,1,0:T(8,128)}, f32[2,256,512]{2,1,0:T(8,128)}, f32[2,2,512]{2,1,0:T(2,128)}, /*index=5*/f32[1,512]{1,0:T(1,128)}) custom-call(bf16[272,2048]{1,0:T(8,128)(2,1)} %get-tuple-element.139.refs_0_.refs_1_, ...), custom_call_target="tpu_custom_call" | custom-call | tf_op jit(solution)/shard_map/back_local/pallas_call | solution.py:70
  224.4 7.1 %feed_out.3 = (bf16[256,2048]{1,0:T(8,128)(2,1)}, bf16[256,2048]{1,0:T(8,128)(2,1)}) custom-call(bf16[512,1408]{1,0:T(8,128)(2,1)} %get-tuple-element.125.refs_5_.refs_0_, bf16[1408,2048]{1,0:T(8,128)(2,1)} %refs_1_.3, bf16[256,2048]{1,0:T(8,128)(2,1)} %plus.4.refs_2_.refs_0_), custom_call_target="tpu_custom_call" | custom-call | tf_op jit(solution)/shard_map/feed_out/pallas_call | solution.py:70
  231.6 4.2 collective-permute-done.26.refs_0_
  238.9 9.2 %back_local.3 = (bf16[2,256,512]{2,1,0:T(8,128)(2,1)}, bf16[2,256,512]{2,1,0:T(8,128)(2,1)}, f32[2,256,512]{2,1,0:T(8,128)}, f32[2,256,512]{2,1,0:T(8,128)}, f32[2,4,512]{2,1,0:T(4,128)}, /*index=5*/f32[1,512]{1,0:T(1,128)}) custom-call(bf16[272,2048]{1,0:T(8,128)(2,1)} %hold.17.refs_0_.refs_3_, bf16[272,2048]{1,0:T(8,128)(2,1)} %collective-permute-done.27.refs_1_.refs_4_, ...), custom_call_target="tpu_custom_call" | custom-call | tf_op jit(solution)/shard_map/back_local/pallas_call | solution.py:70
  259.4 9.0 %product_add.6 = (bf16[512,1408]{1,0:T(8,128)(2,1)}, bf16[512,1408]{1,0:T(8,128)(2,1)}) custom-call(s32[1]{0:T(128)} %bitcast.3.refs_0_, bf16[256,2048]{1,0:T(8,128)(2,1)} %get-tuple-element.122.refs_0_.refs_1_, bf16[144,2048]{1,0:T(8,128)(2,1)} %collective-permute-done.14.refs_1_.refs_2_, bf16[128,2048]{1,0:T(8,128)(2,1)} %collective-permute-done.15.refs_2_.refs_3_, ...), custom_call_target="tpu_custom_call" | custom-call | tf_op jit(solution)/shard_map/product_add/pallas_call | solution.py:81
  268.4 8.5 %product_add.7 = (bf16[512,1408]{1,0:T(8,128)(2,1)}, bf16[512,1408]{1,0:T(8,128)(2,1)}) custom-call(s32[1]{0:T(128)} %bitcast.3.refs_0_, bf16[256,2048]{1,0:T(8,128)(2,1)} %bitcast.24, bf16[256,2048]{1,0:T(8,128)(2,1)} %collective-permute-done.2.refs_1_.refs_2_, bf16[256,2048]{1,0:T(8,128)(2,1)} %hold.14.refs_0_.refs_3_, ...), custom_call_target="tpu_custom_call" | custom-call | tf_op jit(solution)/shard_map/product_add/pallas_call | solution.py:81
  281.0 10.3 %back_mix.2 = (bf16[2,256,1024]{2,1,0:T(8,128)(2,1)}, bf16[256,2048]{1,0:T(8,128)(2,1)}, bf16[256,2048]{1,0:T(8,128)(2,1)}, f32[2,1,512]{2,1,0:T(1,128)}) custom-call(f32[2,256,512]{2,1,0:T(8,128)} %get-tuple-element.154.refs_0_, f32[2,256,512]{2,1,0:T(8,128)} %get-tuple-element.155.refs_1_, f32[2,256,512]{2,1,0:T(8,128)} %get-tuple-element.150.refs_5_.refs_2_, ...), custom_call_target="tpu_custom_call" | custom-call | tf_op jit(solution)/shard_map/back_mix/pallas_call | solution.py:70
  298.0 10.2 %back_mix.3 = (bf16[2,256,1024]{2,1,0:T(8,128)(2,1)}, bf16[256,2048]{1,0:T(8,128)(2,1)}, bf16[256,2048]{1,0:T(8,128)(2,1)}, f32[2,1,512]{2,1,0:T(1,128)}) custom-call(f32[2,256,512]{2,1,0:T(8,128)} %get-tuple-element.145.refs_0_, f32[2,256,512]{2,1,0:T(8,128)} %get-tuple-element.146.refs_1_, f32[2,256,512]{2,1,0:T(8,128)} %get-tuple-element.141.refs_5_.refs_2_, ...), custom_call_target="tpu_custom_call" | custom-call | tf_op jit(solution)/shard_map/back_mix/pallas_call | solution.py:70
  315.1 6.3 %product.9.refs_11_ = bf16[1024,1024]{1,0:T(8,128)(2,1)} custom-call(s32[1]{0:T(128)} %bitcast.3.refs_0_, bf16[256,2048]{1,0:T(8,128)(2,1)} %first_norm.1.refs_0_.refs_1_, bf16[256,2048]{1,0:T(8,128)(2,1)} %collective-permute-done.refs_1_.refs_2_, bf16[256,2048]{1,0:T(8,128)(2,1)} %hold.12.refs_0_.refs_3_, ...), custom_call_target="tpu_custom_call" | custom-call | tf_op jit(solution)/shard_map/product/pallas_call | solution.py:81
  322.4 8.6 %product_add.8 = (bf16[512,1408]{1,0:T(8,128)(2,1)}, bf16[512,1408]{1,0:T(8,128)(2,1)}) custom-call(s32[1]{0:T(128)} %bitcast.3.refs_0_, bf16[256,2048]{1,0:T(8,128)(2,1)} %get-tuple-element.122.refs_0_.refs_1_, bf16[144,2048]{1,0:T(8,128)(2,1)} %collective-permute-done.14.refs_1_.refs_2_, bf16[128,2048]{1,0:T(8,128)(2,1)} %collective-permute-done.15.refs_2_.refs_3_, ...), custom_call_target="tpu_custom_call" | custom-call | tf_op jit(solution)/shard_map/product_add/pallas_call | solution.py:81
  334.2 5.4 %last.1 = (f32[256,2048]{1,0:T(8,128)}, f32[1,2048]{1,0:T(1,128)}) custom-call(bf16[256,2048]{1,0:T(8,128)(2,1)} %bitcast.29, bf16[256,2048]{1,0:T(8,128)(2,1)} %get-tuple-element.160.refs_2_.refs_1_, bf16[256,2048]{1,0:T(8,128)(2,1)} %collective-permute-done.35.refs_2_, bf16[256,2048]{1,0:T(8,128)(2,1)} %collective-permute-done.36.refs_3_, ...), custom_call_target="tpu_custom_call" | custom-call | tf_op jit(solution)/shard_map/last/pallas_call | solution.py:70
  341.1 9.5 %collective-permute-done.40.refs_1_ = bf16[512,1408]{1,0:T(8,128)(2,1)} collective-permute-done((bf16[512,1408]{1,0:T(8,128)(2,1)}, bf16[512,1408]{1,0:T(8,128)(2,1)}, u32[]{:S(2)}, u32[]{:S(2)}) %collective-permute-start.40) | collective-permute-done | bytes 1441824 | tf_op jit(solution)/shard_map/ppermute | solution.py:18
  350.7 3.8 collective-permute-start.44
  354.5 4.9 product.10.refs_2_
  362.7 5.0 product.11.refs_4_
  369.8 8.3 %collective-permute-done.45.refs_1_ = bf16[512,1408]{1,0:T(8,128)(2,1)} collective-permute-done((bf16[512,1408]{1,0:T(8,128)(2,1)}, bf16[512,1408]{1,0:T(8,128)(2,1)}, u32[]{:S(2)}, u32[]{:S(2)}) %collective-permute-start.45) | collective-permute-done | bytes 1441824 | tf_op jit(solution)/shard_map/ppermute | solution.py:18
  378.0 4.3 result.1.refs_2_
  385.6 13.9 %collective-permute-done.44.two = bf16[256,1408]{1,0:T(8,128)(2,1)S(1)} collective-permute-done((bf16[256,1408]{1,0:T(8,128)(2,1)}, bf16[256,1408]{1,0:T(8,128)(2,1)S(1)}, u32[]{:S(2)}, u32[]{:S(2)}) %collective-permute-start.44) | collective-permute-done | bytes 720928 | tf_op jit(solution)/shard_map/ppermute | solution.py:18
  404.0 7.2 %product_add.9 = (bf16[512,1024]{1,0:T(8,128)(2,1)}, bf16[512,1024]{1,0:T(8,128)(2,1)}) custom-call(s32[1]{0:T(128)} %bitcast.3.refs_0_, bf16[256,2048]{1,0:T(8,128)(2,1)} %first_norm.1.refs_0_.refs_1_, bf16[256,2048]{1,0:T(8,128)(2,1)} %collective-permute-done.refs_1_.refs_2_, bf16[256,2048]{1,0:T(8,128)(2,1)} %hold.12.refs_0_.refs_3_, ...), custom_call_target="tpu_custom_call" | custom-call | tf_op jit(solution)/shard_map/product_add/pallas_call | solution.py:81
  419.9 5.4 %product_add.10 = (bf16[512,512]{1,0:T(8,128)(2,1)}, bf16[512,512]{1,0:T(8,128)(2,1)}) custom-call(s32[1]{0:T(128)} %bitcast.3.refs_0_, bf16[256,2048]{1,0:T(8,128)(2,1)} %first_norm.1.refs_0_.refs_1_, bf16[256,2048]{1,0:T(8,128)(2,1)} %collective-permute-done.refs_1_.refs_2_, bf16[256,2048]{1,0:T(8,128)(2,1)} %hold.12.refs_0_.refs_3_, ...), custom_call_target="tpu_custom_call" | custom-call | tf_op jit(solution)/shard_map/product_add/pallas_call | solution.py:81
  425.3 6.0 %collective-permute-start.46 = (bf16[512,512]{1,0:T(8,128)(2,1)}, bf16[512,512]{1,0:T(8,128)(2,1)}, u32[]{:S(2)}, u32[]{:S(2)}) collective-permute-start(bf16[512,512]{1,0:T(8,128)(2,1)} %get-tuple-element.179.refs_8_), channel_id=1, source_target_pairs={{0,8},{4,12},{8,0},{12,4},{16,24},{20,28},{24,16},{28,20},{1,9},{5... | collective-permute-start | bytes 1572872 | tf_op jit(solution)/shard_map/ppermute | solution.py:18
  439.0 5.4 %product_add.11 = (bf16[512,512]{1,0:T(8,128)(2,1)}, bf16[512,512]{1,0:T(8,128)(2,1)}) custom-call(s32[1]{0:T(128)} %bitcast.3.refs_0_, bf16[272,2048]{1,0:T(8,128)(2,1)} %get-tuple-element.139.refs_0_.refs_1_, bf16[272,2048]{1,0:T(8,128)(2,1)} %collective-permute-done.24.refs_1_.refs_2_, bf16[272,2048]{1,0:T(8,128)(2,1)} %hold.17.refs_0_.refs_3_, ...), custom_call_target="tpu_custom_call" | custom-call | tf_op jit(solution)/shard_map/product_add/pallas_call | solution.py:81
  446.2 6.1 %collective-permute-done.48.refs_1_ = bf16[512,1024]{1,0:T(8,128)(2,1)} collective-permute-done((bf16[512,1024]{1,0:T(8,128)(2,1)}, bf16[512,1024]{1,0:T(8,128)(2,1)}, u32[]{:S(2)}, u32[]{:S(2)}) %collective-permute-start.48) | collective-permute-done | bytes 1048608 | tf_op jit(solution)/shard_map/ppermute | solution.py:18
  462.2 8.8 %collective-permute-done.46.refs_1_ = bf16[512,512]{1,0:T(8,128)(2,1)} collective-permute-done((bf16[512,512]{1,0:T(8,128)(2,1)}, bf16[512,512]{1,0:T(8,128)(2,1)}, u32[]{:S(2)}, u32[]{:S(2)}) %collective-permute-start.46) | collective-permute-done | bytes 524320 | tf_op jit(solution)/shard_map/ppermute | solution.py:18
  473.1 4.2 collective-permute-start.50
  477.4 5.6 %collective-permute-done.52.refs_1_ = bf16[512,512]{1,0:T(8,128)(2,1)} collective-permute-done((bf16[512,512]{1,0:T(8,128)(2,1)}, bf16[512,512]{1,0:T(8,128)(2,1)}, u32[]{:S(2)}, u32[]{:S(2)}) %collective-permute-start.52) | collective-permute-done | bytes 524320 | tf_op jit(solution)/shard_map/ppermute | solution.py:18
  485.1 7.2 %collective-permute-start.53 = (bf16[256,512]{1,0:T(8,128)(2,1)}, bf16[256,512]{1,0:T(8,128)(2,1)S(1)}, u32[]{:S(2)}, u32[]{:S(2)}) collective-permute-start(bf16[256,512]{1,0:T(8,128)(2,1)} %get-tuple-element.188.refs_0_.refs_1_), channel_id=1, source_target_pairs={{0,16},{4,20},{8,24},{12,28},{16,0},{20,4},{24,8},{28,12},{1,17},{... | collective-permute-start | bytes 786440 | tf_op jit(solution)/shard_map/ppermute | solution.py:18
  (207 shorter events, 158.0 us)
Async XLA Ops:
  4.3 4.8 collective-permute-start
  4.8 15.4 %collective-permute-start.2 = (bf16[256,2048]{1,0:T(8,128)(2,1)}, bf16[256,2048]{1,0:T(8,128)(2,1)}, u32[]{:S(2)}, u32[]{:S(2)}) collective-permute-start(bf16[256,2048]{1,0:T(8,128)(2,1)} %bitcast.20), channel_id=1, source_target_pairs={{0,1},{1,0},{2,3},{3,2},{4,5},{5,4},{6,7},{7,6},{8,9},{9,8},{10,11... | collective-permute-start | bytes 3145736 | tf_op jit(solution)/shard_map/ppermute | solution.py:18
  4.8 26.6 %collective-permute-start.1 = (bf16[256,2048]{1,0:T(8,128)(2,1)}, bf16[256,2048]{1,0:T(8,128)(2,1)}, u32[]{:S(2)}, u32[]{:S(2)}) collective-permute-start(bf16[256,2048]{1,0:T(8,128)(2,1)} %first_norm.1.refs_0_.refs_1_), channel_id=1, source_target_pairs={{0,2},{1,3},{2,0},{3,1},{4,6},{5,7},{6,4},{7,5},{8,10},{9,11},{10,... | collective-permute-start | bytes 3145736 | tf_op jit(solution)/shard_map/ppermute | solution.py:18
  32.4 45.0 %collective-permute-start.12 = (bf16[256,2048]{1,0:T(8,128)(2,1)}, bf16[256,2048]{1,0:T(8,128)(2,1)}, u32[]{:S(2)}, u32[]{:S(2)}) collective-permute-start(bf16[256,2048]{1,0:T(8,128)(2,1)} %hold.13), channel_id=1, source_target_pairs={{0,2},{1,3},{2,0},{3,1},{4,6},{5,7},{6,4},{7,5},{8,10},{9,11},{10,... | collective-permute-start | bytes 3145736 | tf_op jit(solution)/shard_map/ppermute | solution.py:18
  51.9 11.0 %collective-permute-start.5 = (f32[2,4,512]{2,1,0:T(4,128)}, f32[2,4,512]{2,1,0:T(4,128)S(1)}, u32[]{:S(2)}, u32[]{:S(2)}) collective-permute-start(f32[2,4,512]{2,1,0:T(4,128)} %pair.2), channel_id=1, source_target_pairs={{0,8},{4,12},{8,16},{12,20},{16,24},{20,28},{1,9},{5,13},{9,17},{1... | collective-permute-start | bytes 49160 | tf_op jit(solution)/shard_map/ppermute | solution.py:24
  55.6 7.3 %collective-permute-start.6 = (f32[2,4,512]{2,1,0:T(4,128)}, f32[2,4,512]{2,1,0:T(4,128)S(1)}, u32[]{:S(2)}, u32[]{:S(2)}) collective-permute-start(f32[2,4,512]{2,1,0:T(4,128)} %pair.2), channel_id=1, source_target_pairs={{0,16},{4,20},{8,24},{12,28},{1,17},{5,21},{9,25},{13,29},{2,18},{... | collective-permute-start | bytes 49160 | tf_op jit(solution)/shard_map/ppermute | solution.py:24
  71.2 6.3 %collective-permute-start.9 = (bf16[272,2048]{1,0:T(8,128)(2,1)}, bf16[272,2048]{1,0:T(8,128)(2,1)}, u32[]{:S(2)}, u32[]{:S(2)}) collective-permute-start(bf16[272,2048]{1,0:T(8,128)(2,1)} %get-tuple-element.114), channel_id=1, source_target_pairs={{0,1},{1,0},{2,3},{3,2},{4,5},{5,4},{6,7},{7,6},{8,9},{9,8},{10,11... | collective-permute-start | bytes 3342344 | tf_op jit(solution)/shard_map/ppermute | solution.py:18
  76.9 13.0 %collective-permute-start.8 = (bf16[272,2048]{1,0:T(8,128)(2,1)}, bf16[272,2048]{1,0:T(8,128)(2,1)}, u32[]{:S(2)}, u32[]{:S(2)}) collective-permute-start(bf16[272,2048]{1,0:T(8,128)(2,1)} %get-tuple-element.113), channel_id=1, source_target_pairs={{0,1},{1,0},{2,3},{3,2},{4,5},{5,4},{6,7},{7,6},{8,9},{9,8},{10,11... | collective-permute-start | bytes 3342344 | tf_op jit(solution)/shard_map/ppermute | solution.py:18
  77.4 4.9 collective-permute-start.13
  80.3 16.3 %collective-permute-start.11 = (bf16[144,2048]{1,0:T(8,128)(2,1)}, bf16[144,2048]{1,0:T(8,128)(2,1)S(1)}, u32[]{:S(2)}, u32[]{:S(2)}) collective-permute-start(bf16[144,2048]{1,0:T(8,128)(2,1)} %get-tuple-element.116), channel_id=1, source_target_pairs={{0,2},{1,3},{2,0},{3,1},{4,6},{5,7},{6,4},{7,5},{8,10},{9,11},{10,... | collective-permute-start | bytes 1769480 | tf_op jit(solution)/shard_map/ppermute | solution.py:18
  81.8 26.2 %collective-permute-start.10 = (bf16[128,2048]{1,0:T(8,128)(2,1)}, bf16[128,2048]{1,0:T(8,128)(2,1)}, u32[]{:S(2)}, u32[]{:S(2)}) collective-permute-start(bf16[128,2048]{1,0:T(8,128)(2,1)} %get-tuple-element.115.refs_3_), channel_id=1, source_target_pairs={{0,2},{1,3},{2,0},{3,1},{4,6},{5,7},{6,4},{7,5},{8,10},{9,11},{10,... | collective-permute-start | bytes 1572872 | tf_op jit(solution)/shard_map/ppermute | solution.py:18
  101.2 12.7 %collective-permute-start.14 = (bf16[144,2048]{1,0:T(8,128)(2,1)}, bf16[144,2048]{1,0:T(8,128)(2,1)}, u32[]{:S(2)}, u32[]{:S(2)}) collective-permute-start(bf16[144,2048]{1,0:T(8,128)(2,1)} %get-tuple-element.123), channel_id=1, source_target_pairs={{0,1},{1,0},{2,3},{3,2},{4,5},{5,4},{6,7},{7,6},{8,9},{9,8},{10,11... | collective-permute-start | bytes 1769480 | tf_op jit(solution)/shard_map/ppermute | solution.py:18
  101.2 35.7 %collective-permute-start.16 = (bf16[144,2048]{1,0:T(8,128)(2,1)}, bf16[144,2048]{1,0:T(8,128)(2,1)S(1)}, u32[]{:S(2)}, u32[]{:S(2)}) collective-permute-start(bf16[144,2048]{1,0:T(8,128)(2,1)} %get-tuple-element.123), channel_id=1, source_target_pairs={{0,2},{1,3},{2,0},{3,1},{4,6},{5,7},{6,4},{7,5},{8,10},{9,11},{10,... | collective-permute-start | bytes 1769480 | tf_op jit(solution)/shard_map/ppermute | solution.py:18
  111.6 26.2 %collective-permute-start.17 = (bf16[128,2048]{1,0:T(8,128)(2,1)}, bf16[128,2048]{1,0:T(8,128)(2,1)}, u32[]{:S(2)}, u32[]{:S(2)}) collective-permute-start(bf16[128,2048]{1,0:T(8,128)(2,1)} %get-tuple-element.124), channel_id=1, source_target_pairs={{0,2},{1,3},{2,0},{3,1},{4,6},{5,7},{6,4},{7,5},{8,10},{9,11},{10,... | collective-permute-start | bytes 1572872 | tf_op jit(solution)/shard_map/ppermute | solution.py:18
  164.6 8.3 %collective-permute-start.20 = (bf16[256,2048]{1,0:T(8,128)(2,1)}, bf16[256,2048]{1,0:T(8,128)(2,1)}, u32[]{:S(2)}, u32[]{:S(2)}) collective-permute-start(bf16[256,2048]{1,0:T(8,128)(2,1)} %get-tuple-element.133), channel_id=1, source_target_pairs={{0,1},{1,0},{2,3},{3,2},{4,5},{5,4},{6,7},{7,6},{8,9},{9,8},{10,11... | collective-permute-start | bytes 3145736 | tf_op jit(solution)/shard_map/ppermute | solution.py:18
  164.7 37.0 %collective-permute-start.22 = (bf16[256,2048]{1,0:T(8,128)(2,1)}, bf16[256,2048]{1,0:T(8,128)(2,1)}, u32[]{:S(2)}, u32[]{:S(2)}) collective-permute-start(bf16[256,2048]{1,0:T(8,128)(2,1)} %get-tuple-element.136), channel_id=1, source_target_pairs={{0,1},{1,0},{2,3},{3,2},{4,5},{5,4},{6,7},{7,6},{8,9},{9,8},{10,11... | collective-permute-start | bytes 3145736 | tf_op jit(solution)/shard_map/ppermute | solution.py:18
  176.5 25.5 %collective-permute-start.23 = (bf16[256,2048]{1,0:T(8,128)(2,1)}, bf16[256,2048]{1,0:T(8,128)(2,1)}, u32[]{:S(2)}, u32[]{:S(2)}) collective-permute-start(bf16[256,2048]{1,0:T(8,128)(2,1)} %plus.3.refs_7_.refs_11_), channel_id=1, source_target_pairs={{0,2},{1,3},{2,0},{3,1},{4,6},{5,7},{6,4},{7,5},{8,10},{9,11},{10,... | collective-permute-start | bytes 3145736 | tf_op jit(solution)/shard_map/ppermute | solution.py:18
  178.0 80.2 %collective-permute-start.33 = (bf16[1152,1408]{1,0:T(8,128)(2,1)}, bf16[1152,1408]{1,0:T(8,128)(2,1)}, u32[]{:S(2)}, u32[]{:S(2)}) collective-permute-start(bf16[1152,1408]{1,0:T(8,128)(2,1)} %product.6.refs_2_), channel_id=1, source_target_pairs={{0,4},{4,0},{8,12},{12,8},{16,20},{20,16},{24,28},{28,24},{1,5},{5... | collective-permute-start | bytes 9732104 | tf_op jit(solution)/shard_map/ppermute | solution.py:18
  187.0 81.4 %collective-permute-start.32 = (bf16[1152,1408]{1,0:T(8,128)(2,1)}, bf16[1152,1408]{1,0:T(8,128)(2,1)}, u32[]{:S(2)}, u32[]{:S(2)}) collective-permute-start(bf16[1152,1408]{1,0:T(8,128)(2,1)} %product.7.refs_10_), channel_id=1, source_target_pairs={{0,8},{4,12},{8,0},{12,4},{16,24},{20,28},{24,16},{28,20},{1,9},{5... | collective-permute-start | bytes 9732104 | tf_op jit(solution)/shard_map/ppermute | solution.py:18
  208.5 27.3 %collective-permute-start.26 = (bf16[272,2048]{1,0:T(8,128)(2,1)}, bf16[272,2048]{1,0:T(8,128)(2,1)}, u32[]{:S(2)}, u32[]{:S(2)}) collective-permute-start(bf16[272,2048]{1,0:T(8,128)(2,1)} %get-tuple-element.139.refs_0_.refs_1_), channel_id=1, source_target_pairs={{0,2},{1,3},{2,0},{3,1},{4,6},{5,7},{6,4},{7,5},{8,10},{9,11},{10,... | collective-permute-start | bytes 3342344 | tf_op jit(solution)/shard_map/ppermute | solution.py:18
  210.0 10.7 %collective-permute-start.21 = (bf16[256,2048]{1,0:T(8,128)(2,1)}, bf16[256,2048]{1,0:T(8,128)(2,1)}, u32[]{:S(2)}, u32[]{:S(2)}) collective-permute-start(bf16[256,2048]{1,0:T(8,128)(2,1)} %get-tuple-element.135), channel_id=1, source_target_pairs={{0,1},{1,0},{2,3},{3,2},{4,5},{5,4},{6,7},{7,6},{8,9},{9,8},{10,11... | collective-permute-start | bytes 3145736 | tf_op jit(solution)/shard_map/ppermute | solution.py:18
  254.0 68.4 %collective-permute-start.37 = (bf16[1024,1408]{1,0:T(8,128)(2,1)}, bf16[1024,1408]{1,0:T(8,128)(2,1)}, u32[]{:S(2)}, u32[]{:S(2)}) collective-permute-start(bf16[1024,1408]{1,0:T(8,128)(2,1)} %hold.18), channel_id=1, source_target_pairs={{0,4},{4,0},{8,12},{12,8},{16,20},{20,16},{24,28},{28,24},{1,5},{5... | collective-permute-start | bytes 8650760 | tf_op jit(solution)/shard_map/ppermute | solution.py:18
  255.5 21.4 %collective-permute-start.29 = (f32[2,4,512]{2,1,0:T(4,128)S(1)}, f32[2,4,512]{2,1,0:T(4,128)S(1)}, u32[]{:S(2)}, u32[]{:S(2)}) collective-permute-start(f32[2,4,512]{2,1,0:T(4,128)S(1)} %copy-done.8), channel_id=1, source_target_pairs={{8,0},{12,4},{16,8},{20,12},{24,16},{28,20},{9,1},{13,5},{17,9},{2... | collective-permute-start | bytes 49160 | tf_op jit(solution)/shard_map/ppermute | solution.py:24
  256.8 20.1 %collective-permute-start.30 = (f32[2,4,512]{2,1,0:T(4,128)S(1)}, f32[2,4,512]{2,1,0:T(4,128)S(1)}, u32[]{:S(2)}, u32[]{:S(2)}) collective-permute-start(f32[2,4,512]{2,1,0:T(4,128)S(1)} %copy-done.8), channel_id=1, source_target_pairs={{16,0},{20,4},{24,8},{28,12},{17,1},{21,5},{25,9},{29,13},{18,2},{... | collective-permute-start | bytes 49160 | tf_op jit(solution)/shard_map/ppermute | solution.py:24
  258.1 18.8 %collective-permute-start.31 = (f32[2,4,512]{2,1,0:T(4,128)S(1)}, f32[2,4,512]{2,1,0:T(4,128)S(1)}, u32[]{:S(2)}, u32[]{:S(2)}) collective-permute-start(f32[2,4,512]{2,1,0:T(4,128)S(1)} %copy-done.8), channel_id=1, source_target_pairs={{24,0},{28,4},{25,1},{29,5},{26,2},{30,6},{27,3},{31,7}} | collective-permute-start | bytes 49160 | tf_op jit(solution)/shard_map/ppermute | solution.py:24
  279.0 32.9 %collective-permute-start.38 = (bf16[512,1408]{1,0:T(8,128)(2,1)}, bf16[512,1408]{1,0:T(8,128)(2,1)}, u32[]{:S(2)}, u32[]{:S(2)}) collective-permute-start(bf16[512,1408]{1,0:T(8,128)(2,1)} %hold.19), channel_id=1, source_target_pairs={{0,8},{4,12},{8,0},{12,4},{16,24},{20,28},{24,16},{28,20},{1,9},{5... | collective-permute-start | bytes 4325384 | tf_op jit(solution)/shard_map/ppermute | solution.py:18
  308.2 24.5 %collective-permute-start.35 = (bf16[256,2048]{1,0:T(8,128)(2,1)}, bf16[256,2048]{1,0:T(8,128)(2,1)}, u32[]{:S(2)}, u32[]{:S(2)}) collective-permute-start(bf16[256,2048]{1,0:T(8,128)(2,1)} %get-tuple-element.161), channel_id=1, source_target_pairs={{0,1},{1,0},{2,3},{3,2},{4,5},{5,4},{6,7},{7,6},{8,9},{9,8},{10,11... | collective-permute-start | bytes 3145736 | tf_op jit(solution)/shard_map/ppermute | solution.py:18
  308.4 25.7 %collective-permute-start.36 = (bf16[256,2048]{1,0:T(8,128)(2,1)}, bf16[256,2048]{1,0:T(8,128)(2,1)}, u32[]{:S(2)}, u32[]{:S(2)}) collective-permute-start(bf16[256,2048]{1,0:T(8,128)(2,1)} %plus.5.refs_10_), channel_id=1, source_target_pairs={{0,2},{1,3},{2,0},{3,1},{4,6},{5,7},{6,4},{7,5},{8,10},{9,11},{10,... | collective-permute-start | bytes 3145736 | tf_op jit(solution)/shard_map/ppermute | solution.py:18
  309.9 40.7 %collective-permute-start.40 = (bf16[512,1408]{1,0:T(8,128)(2,1)}, bf16[512,1408]{1,0:T(8,128)(2,1)}, u32[]{:S(2)}, u32[]{:S(2)}) collective-permute-start(bf16[512,1408]{1,0:T(8,128)(2,1)} %get-tuple-element.153.refs_6_), channel_id=1, source_target_pairs={{0,4},{4,0},{8,12},{12,8},{16,20},{20,16},{24,28},{28,24},{1,5},{5... | collective-permute-start | bytes 4325384 | tf_op jit(solution)/shard_map/ppermute | solution.py:18
  321.4 82.6 %collective-permute-start.43 = (bf16[1024,1024]{1,0:T(8,128)(2,1)}, bf16[1024,1024]{1,0:T(8,128)(2,1)}, u32[]{:S(2)}, u32[]{:S(2)}) collective-permute-start(bf16[1024,1024]{1,0:T(8,128)(2,1)} %product.9.refs_11_), channel_id=1, source_target_pairs={{0,4},{4,0},{8,12},{12,8},{16,20},{20,16},{24,28},{28,24},{1,5},{5... | collective-permute-start | bytes 6291464 | tf_op jit(solution)/shard_map/ppermute | solution.py:18
  331.0 47.1 %collective-permute-start.45 = (bf16[512,1408]{1,0:T(8,128)(2,1)}, bf16[512,1408]{1,0:T(8,128)(2,1)}, u32[]{:S(2)}, u32[]{:S(2)}) collective-permute-start(bf16[512,1408]{1,0:T(8,128)(2,1)} %get-tuple-element.167.refs_6_), channel_id=1, source_target_pairs={{0,8},{4,12},{8,0},{12,4},{16,24},{20,28},{24,16},{28,20},{1,9},{5... | collective-permute-start | bytes 4325384 | tf_op jit(solution)/shard_map/ppermute | solution.py:18
  332.8 34.9 %collective-permute-start.25 = (bf16[256,2048]{1,0:T(8,128)(2,1)}, bf16[256,2048]{1,0:T(8,128)(2,1)}, u32[]{:S(2)}, u32[]{:S(2)}) collective-permute-start(bf16[256,2048]{1,0:T(8,128)(2,1)} %get-tuple-element.144), channel_id=1, source_target_pairs={{0,1},{1,0},{2,3},{3,2},{4,5},{5,4},{6,7},{7,6},{8,9},{9,8},{10,11... | collective-permute-start | bytes 3145736 | tf_op jit(solution)/shard_map/ppermute | solution.py:18
  339.6 28.6 %collective-permute-start.39 = (bf16[256,2048]{1,0:T(8,128)(2,1)}, bf16[256,2048]{1,0:T(8,128)(2,1)}, u32[]{:S(2)}, u32[]{:S(2)}) collective-permute-start(bf16[256,2048]{1,0:T(8,128)(2,1)} %hold.20), channel_id=1, source_target_pairs={{0,2},{1,3},{2,0},{3,1},{4,6},{5,7},{6,4},{7,5},{8,10},{9,11},{10,... | collective-permute-start | bytes 3145736 | tf_op jit(solution)/shard_map/ppermute | solution.py:18
  350.7 48.8 %collective-permute-start.44 = (bf16[256,1408]{1,0:T(8,128)(2,1)}, bf16[256,1408]{1,0:T(8,128)(2,1)S(1)}, u32[]{:S(2)}, u32[]{:S(2)}) collective-permute-start(bf16[256,1408]{1,0:T(8,128)(2,1)} %get-tuple-element.166.refs_7_), channel_id=1, source_target_pairs={{0,16},{4,20},{8,24},{12,28},{16,0},{20,4},{24,8},{28,12},{1,17},{... | collective-permute-start | bytes 2162696 | tf_op jit(solution)/shard_map/ppermute | solution.py:18
  367.7 52.3 %collective-permute-start.41 = (bf16[1024,512]{1,0:T(8,128)(2,1)}, bf16[1024,512]{1,0:T(8,128)(2,1)}, u32[]{:S(2)}, u32[]{:S(2)}) collective-permute-start(bf16[1024,512]{1,0:T(8,128)(2,1)} %product.11.refs_4_), channel_id=1, source_target_pairs={{0,4},{4,0},{8,12},{12,8},{16,20},{20,16},{24,28},{28,24},{1,5},{5... | collective-permute-start | bytes 3145736 | tf_op jit(solution)/shard_map/ppermute | solution.py:18
  368.2 70.7 %collective-permute-start.49 = (bf16[1024,512]{1,0:T(8,128)(2,1)}, bf16[1024,512]{1,0:T(8,128)(2,1)}, u32[]{:S(2)}, u32[]{:S(2)}) collective-permute-start(bf16[1024,512]{1,0:T(8,128)(2,1)} %product.10.refs_2_), channel_id=1, source_target_pairs={{0,4},{4,0},{8,12},{12,8},{16,20},{20,16},{24,28},{28,24},{1,5},{5... | collective-permute-start | bytes 3145736 | tf_op jit(solution)/shard_map/ppermute | solution.py:18
  378.0 39.4 %collective-permute-start.42 = (bf16[256,1408]{1,0:T(8,128)(2,1)}, bf16[256,1408]{1,0:T(8,128)(2,1)}, u32[]{:S(2)}, u32[]{:S(2)}) collective-permute-start(bf16[256,1408]{1,0:T(8,128)(2,1)} %get-tuple-element.172.refs_7_), channel_id=1, source_target_pairs={{0,16},{4,20},{8,24},{12,28},{16,0},{20,4},{24,8},{28,12},{1,17},{... | collective-permute-start | bytes 2162696 | tf_op jit(solution)/shard_map/ppermute | solution.py:18
  411.2 41.1 %collective-permute-start.48 = (bf16[512,1024]{1,0:T(8,128)(2,1)}, bf16[512,1024]{1,0:T(8,128)(2,1)}, u32[]{:S(2)}, u32[]{:S(2)}) collective-permute-start(bf16[512,1024]{1,0:T(8,128)(2,1)} %get-tuple-element.177.refs_0_), channel_id=1, source_target_pairs={{0,8},{4,12},{8,0},{12,4},{16,24},{20,28},{24,16},{28,20},{1,9},{5... | collective-permute-start | bytes 3145736 | tf_op jit(solution)/shard_map/ppermute | solution.py:18
  414.1 44.5 %collective-permute-start.47 = (bf16[256,1408]{1,0:T(8,128)(2,1)S(1)}, bf16[256,1408]{1,0:T(8,128)(2,1)}, u32[]{:S(2)}, u32[]{:S(2)}) collective-permute-start(bf16[256,1408]{1,0:T(8,128)(2,1)S(1)} %copy-done.4), channel_id=1, source_target_pairs={{0,16},{4,20},{8,24},{12,28},{16,0},{20,4},{24,8},{28,12},{1,17},{... | collective-permute-start | bytes 2162696 | tf_op jit(solution)/shard_map/ppermute | solution.py:18
  425.3 45.6 %collective-permute-start.46 = (bf16[512,512]{1,0:T(8,128)(2,1)}, bf16[512,512]{1,0:T(8,128)(2,1)}, u32[]{:S(2)}, u32[]{:S(2)}) collective-permute-start(bf16[512,512]{1,0:T(8,128)(2,1)} %get-tuple-element.179.refs_8_), channel_id=1, source_target_pairs={{0,8},{4,12},{8,0},{12,4},{16,24},{20,28},{24,16},{28,20},{1,9},{5... | collective-permute-start | bytes 1572872 | tf_op jit(solution)/shard_map/ppermute | solution.py:18
  432.7 11.7 %collective-permute-start.55 = (f32[2,512]{1,0:T(2,128)S(1)}, f32[2,512]{1,0:T(2,128)S(1)}, u32[]{:S(2)}, u32[]{:S(2)}) collective-permute-start(f32[2,512]{1,0:T(2,128)S(1)} %get-tuple-element.197), channel_id=1, source_target_pairs={{0,2},{1,3},{2,0},{3,1},{4,6},{5,7},{6,4},{7,5},{8,10},{9,11},{10,... | collective-permute-start | bytes 12296 | tf_op jit(solution)/shard_map/ppermute | solution.py:18
  438.9 7.2 %collective-permute-start.56 = (f32[2,512]{1,0:T(2,128)S(1)}, f32[2,512]{1,0:T(2,128)S(1)}, u32[]{:S(2)}, u32[]{:S(2)}) collective-permute-start(f32[2,512]{1,0:T(2,128)S(1)} %get-tuple-element.198), channel_id=1, source_target_pairs={{0,3},{1,2},{2,1},{3,0},{4,7},{5,6},{6,5},{7,4},{8,11},{9,10},{10,... | collective-permute-start | bytes 12296 | tf_op jit(solution)/shard_map/ppermute | solution.py:18
  444.4 38.6 %collective-permute-start.52 = (bf16[512,512]{1,0:T(8,128)(2,1)}, bf16[512,512]{1,0:T(8,128)(2,1)}, u32[]{:S(2)}, u32[]{:S(2)}) collective-permute-start(bf16[512,512]{1,0:T(8,128)(2,1)} %get-tuple-element.182.refs_2_), channel_id=1, source_target_pairs={{0,8},{4,12},{8,0},{12,4},{16,24},{20,28},{24,16},{28,20},{1,9},{5... | collective-permute-start | bytes 1572872 | tf_op jit(solution)/shard_map/ppermute | solution.py:18
  455.1 41.0 %collective-permute-start.51 = (bf16[256,1024]{1,0:T(8,128)(2,1)}, bf16[256,1024]{1,0:T(8,128)(2,1)}, u32[]{:S(2)}, u32[]{:S(2)}) collective-permute-start(bf16[256,1024]{1,0:T(8,128)(2,1)} %get-tuple-element.183.refs_1_), channel_id=1, source_target_pairs={{0,16},{4,20},{8,24},{12,28},{16,0},{20,4},{24,8},{28,12},{1,17},{... | collective-permute-start | bytes 1572872 | tf_op jit(solution)/shard_map/ppermute | solution.py:18
  473.1 26.6 %collective-permute-start.50 = (bf16[256,512]{1,0:T(8,128)(2,1)}, bf16[256,512]{1,0:T(8,128)(2,1)S(1)}, u32[]{:S(2)}, u32[]{:S(2)}) collective-permute-start(bf16[256,512]{1,0:T(8,128)(2,1)} %get-tuple-element.185.refs_2_), channel_id=1, source_target_pairs={{0,16},{4,20},{8,24},{12,28},{16,0},{20,4},{24,8},{28,12},{1,17},{... | collective-permute-start | bytes 786440 | tf_op jit(solution)/shard_map/ppermute | solution.py:18
  477.3 14.9 %collective-permute-start.57 = (f32[4,512]{1,0:T(4,128)S(1)}, f32[4,512]{1,0:T(4,128)S(1)}, u32[]{:S(2)}, u32[]{:S(2)}) collective-permute-start(f32[4,512]{1,0:T(4,128)S(1)} %pad_maximum_fusion), channel_id=1, source_target_pairs={{0,4},{4,0},{8,12},{12,8},{16,20},{20,16},{24,28},{28,24},{1,5},{5... | collective-permute-start | bytes 24584 | tf_op jit(solution)/shard_map/ppermute | solution.py:18
  485.1 19.9 %collective-permute-start.53 = (bf16[256,512]{1,0:T(8,128)(2,1)}, bf16[256,512]{1,0:T(8,128)(2,1)S(1)}, u32[]{:S(2)}, u32[]{:S(2)}) collective-permute-start(bf16[256,512]{1,0:T(8,128)(2,1)} %get-tuple-element.188.refs_0_.refs_1_), channel_id=1, source_target_pairs={{0,16},{4,20},{8,24},{12,28},{16,0},{20,4},{24,8},{28,12},{1,17},{... | collective-permute-start | bytes 786440 | tf_op jit(solution)/shard_map/ppermute | solution.py:18
  493.6 10.0 %collective-permute-start.58 = (f32[4,512]{1,0:T(4,128)S(1)}, f32[4,512]{1,0:T(4,128)S(1)}, u32[]{:S(2)}, u32[]{:S(2)}) collective-permute-start(f32[4,512]{1,0:T(4,128)S(1)} %fusion.4), channel_id=1, source_target_pairs={{0,8},{4,12},{8,0},{12,4},{16,24},{20,28},{24,16},{28,20},{1,9},{5... | collective-permute-start | bytes 24584 | tf_op jit(solution)/shard_map/ppermute | solution.py:18
  (39 other events, 164.1 us)

commit v7 on v6

--- a/solution.py
+++ b/solution.py
@@ -1007,11 +1007,11 @@
     up = Weight(me, twos, gu_n, gu_f, y_first, block)
     lower = Weight(me, (pieces(g0, g1), pieces(g2, g3)), hid_n, hid_f, mixed_order, block)
     kf0, kf1 = feed_back(gg_f, gu_f, gate_up)
-    gate.begin(kf0, more=128)
+    gate.begin(kf0, more=96)
     gate.go()
     across = plus(kf0, swap(kf1, "wt", 1), after=(gate.send,))
     hop = swap(across, "wt", 2)
-    lower.begin(across, more=128)
+    lower.begin(across, more=96)
     lower.go()
     up.begin(lower.send, across, more=0)
     ff0, ff1 = feed_out(hid_f, down, after=(up.send,))

time: 519 us -> 519 us (level)
  no operation moved by 1% of the time
where the time goes in v7:
time: 519 us; the launch traced here: 512 us
  Pallas kernels  312 us (60%)
  waiting for transfers between devices  96.9 us (19%)
  starting transfers between devices  85 us (16%)
  local copies, waits for them, and re-layouts  13.9 us (3%)
    pallas_call x30, Pallas kernels, call(): pl.pallas_call(body, grid=grid, in_specs=in_specs, out_specs=out_specs, s...  198 us
    ppermute x54, waiting for transfers between devices, swap(): return lax.ppermute(values, axis, [(i, i ^ bit) for i in range(size)])  96.8 us
    pallas_call x16, Pallas kernels, call(): got = pl.pallas_call(body, grid_spec=spec, **settings)(blocks, *operands)  88.6 us
    ppermute x54, starting transfers between devices, swap(): return lax.ppermute(values, axis, [(i, i ^ bit) for i in range(size)])  71.5 us
    pallas_call x6, Pallas kernels, finish(): pl.pallas_call(lambda one, two, *refs: finish_kernel(turned, one, two, *r...  18.2 us
    ppermute x6, starting transfers between devices, shift(): return lax.ppermute(values, axis, pairs)  13.5 us
    unnamed x55, local copies, waits for them, and re-layouts  10.6 us
  transfers between devices with their start and end apart: 60, of which 26 were waited for; matrix products, arithmetic and copies ran while one was open for 1% of the time, Pallas kernels for 56%

profile of v7, /device:TPU:0, one launch (start us, length us, event | category | flops | bytes accessed | tf_op | source)
XLA Modules:
  0.0 511.6 jit_solution(8778239508061077486)
XLA Ops:
  9.1 11.1 %project.2 = (f32[2,256,512]{2,1,0:T(8,128)}, f32[2,256,512]{2,1,0:T(8,128)}, f32[2,256,512]{2,1,0:T(8,128)}, f32[2,256,512]{2,1,0:T(8,128)}, f32[2,256,512]{2,1,0:T(8,128)}, /*index=5*/f32[2,2,512]{2,1,0:T(2,128)}) custom-call(bf16[256,2048]{1,0:T(8,128)(2,1)} %first_norm.1.refs_0_.refs_1_, bf16[256,2048]{1,0:T(8,128)(2,1)} %collective-permute-done.refs_1_.refs_2_, ...), custom_call_target="tpu_custom_call" | custom-call | tf_op jit(solution)/shard_map/project/pallas_call | solution.py:70
  20.1 7.4 %hidden_grad.2.refs_1_.refs_4_ = f32[512,1408]{1,0:T(8,128)} custom-call(bf16[256,2048]{1,0:T(8,128)(2,1)} %bitcast.21, bf16[256,2048]{1,0:T(8,128)(2,1)} %collective-permute-done.2.refs_1_.refs_2_, bf16[1408,2048]{1,0:T(8,128)(2,1)} %refs_1_.3, f32[2,2,512]{2,1,0:T(2,128)} %get-tuple-element.106.refs_3_.refs_4_), custom_call_target="tpu_custom_call" | custom-call | tf_op jit(solution)/shard_map/hidden_grad/pallas_call | solution.py:70
  27.6 3.8 collective-permute-done.1.refs_0_
  34.4 11.5 %project.3 = (f32[2,256,512]{2,1,0:T(8,128)}, f32[2,256,512]{2,1,0:T(8,128)}, f32[2,256,512]{2,1,0:T(8,128)}, f32[2,256,512]{2,1,0:T(8,128)}, f32[2,256,512]{2,1,0:T(8,128)}, /*index=5*/f32[2,4,512]{2,1,0:T(4,128)}) custom-call(bf16[256,2048]{1,0:T(8,128)(2,1)} %hold.12.refs_0_.refs_3_, bf16[256,2048]{1,0:T(8,128)(2,1)} %collective-permute-done.3.refs_1_.refs_4_, ...), custom_call_target="tpu_custom_call" | custom-call | tf_op jit(solution)/shard_map/project/pallas_call | solution.py:70
  51.9 3.7 collective-permute-start.5
  55.6 4.5 collective-permute-start.6
  65.6 5.6 %mix.2 = (f32[2,256,512]{2,1,0:T(8,128)}, bf16[272,2048]{1,0:T(8,128)(2,1)}, bf16[272,2048]{1,0:T(8,128)(2,1)}) custom-call(f32[2,256,512]{2,1,0:T(8,128)} %get-tuple-element.108.refs_0_, f32[2,256,512]{2,1,0:T(8,128)} %get-tuple-element.109.refs_1_, f32[2,256,512]{2,1,0:T(8,128)} %get-tuple-element.110.refs_2_.refs_3_, f32[4,1,512]{2,1,0:T(1,128)} %enter.2.refs_3_.refs_7_, ...), custom_call_target="tpu_custom_call" | custom-call | tf_op jit(solution)/shard_map/mix/pallas_call | solution.py:70
  71.3 5.6 %mix.3 = (f32[2,256,512]{2,1,0:T(8,128)}, bf16[272,2048]{1,0:T(8,128)(2,1)}, bf16[272,2048]{1,0:T(8,128)(2,1)}) custom-call(f32[2,256,512]{2,1,0:T(8,128)} %get-tuple-element.103.refs_0_, f32[2,256,512]{2,1,0:T(8,128)} %get-tuple-element.104.refs_1_, f32[2,256,512]{2,1,0:T(8,128)} %get-tuple-element.105.refs_2_.refs_3_, f32[4,1,512]{2,1,0:T(1,128)} %enter.2.refs_3_.refs_7_, ...), custom_call_target="tpu_custom_call" | custom-call | tf_op jit(solution)/shard_map/mix/pallas_call | solution.py:70
  82.3 7.5 %hidden_grad.3.refs_0_.refs_5_ = f32[512,1408]{1,0:T(8,128)} custom-call(bf16[256,2048]{1,0:T(8,128)(2,1)} %hold.14.refs_0_.refs_3_, bf16[256,2048]{1,0:T(8,128)(2,1)} %collective-permute-done.13.refs_1_.refs_4_, bf16[1408,2048]{1,0:T(8,128)(2,1)} %refs_1_.3, bf16[128,2048]{1,0:T(8,128)(2,1)} %get-tuple-element.115.refs_3_), custom_call_target="tpu_custom_call" | custom-call | tf_op jit(solution)/shard_map/hidden_grad/pallas_call | solution.py:70
  89.9 6.8 %collective-permute-done.11.hop.hop_more = bf16[144,2048]{1,0:T(8,128)(2,1)S(1)} collective-permute-done((bf16[144,2048]{1,0:T(8,128)(2,1)}, bf16[144,2048]{1,0:T(8,128)(2,1)S(1)}, u32[]{:S(2)}, u32[]{:S(2)}) %collective-permute-start.11) | collective-permute-done | bytes 589856 | tf_op jit(solution)/shard_map/ppermute | solution.py:18
  97.5 3.7 middle.2
  102.7 5.3 %collective-permute-done.10.hop = bf16[128,2048]{1,0:T(8,128)(2,1)} collective-permute-done((bf16[128,2048]{1,0:T(8,128)(2,1)}, bf16[128,2048]{1,0:T(8,128)(2,1)}, u32[]{:S(2)}, u32[]{:S(2)}) %collective-permute-start.10) | collective-permute-done | bytes 524320 | tf_op jit(solution)/shard_map/ppermute | solution.py:18
  113.9 12.0 %feed.2 = (bf16[512,1408]{1,0:T(8,128)(2,1)}, bf16[512,1408]{1,0:T(8,128)(2,1)}, bf16[512,1408]{1,0:T(8,128)(2,1)}) custom-call(bf16[256,2048]{1,0:T(8,128)(2,1)} %get-tuple-element.122.refs_0_.refs_1_, bf16[144,2048]{1,0:T(8,128)(2,1)} %collective-permute-done.14.refs_1_.refs_2_, bf16[128,2048]{1,0:T(8,128)(2,1)} %collective-permute-done.15.refs_2_.refs_3_, ...), custom_call_target="tpu_custom_call" | custom-call | tf_op jit(solution)/shard_map/feed/pallas_call | solution.py:70
  125.9 10.9 %feed_back.2 = (bf16[256,2048]{1,0:T(8,128)(2,1)}, bf16[256,2048]{1,0:T(8,128)(2,1)}) custom-call(bf16[512,1408]{1,0:T(8,128)(2,1)} %get-tuple-element.126.refs_0_.refs_8_, bf16[512,1408]{1,0:T(8,128)(2,1)} %get-tuple-element.127.refs_1_.refs_8_, bf16[2,2048,1408]{2,1,0:T(8,128)(2,1)} %refs_2_.13), custom_call_target="tpu_custom_call" | custom-call | tf_op jit(solution)/shard_map/feed_back/pallas_call | solution.py:70
  141.7 12.0 %feed.3 = (bf16[512,1408]{1,0:T(8,128)(2,1)}, bf16[512,1408]{1,0:T(8,128)(2,1)}, bf16[512,1408]{1,0:T(8,128)(2,1)}) custom-call(bf16[144,2048]{1,0:T(8,128)(2,1)} %hold.15.refs_0_.refs_4_, bf16[128,2048]{1,0:T(8,128)(2,1)} %hold.16.refs_1_.refs_5_, bf16[144,2048]{1,0:T(8,128)(2,1)} %copy-done.2, bf16[128,2048]{1,0:T(8,128)(2,1)} %collective-permute-done.19.refs_3_.refs_7_, ...), custom_call_target="tpu_custom_call" | custom-call | tf_op jit(solution)/shard_map/feed/pallas_call | solution.py:70
  153.7 10.9 %feed_back.3 = (bf16[256,2048]{1,0:T(8,128)(2,1)}, bf16[256,2048]{1,0:T(8,128)(2,1)}) custom-call(bf16[512,1408]{1,0:T(8,128)(2,1)} %get-tuple-element.131.refs_0_.refs_9_, bf16[512,1408]{1,0:T(8,128)(2,1)} %get-tuple-element.130.refs_1_.refs_9_, bf16[2,2048,1408]{2,1,0:T(8,128)(2,1)} %refs_2_.13), custom_call_target="tpu_custom_call" | custom-call | tf_op jit(solution)/shard_map/feed_back/pallas_call | solution.py:70
  165.1 7.8 %product.6.refs_2_ = bf16[1120,1408]{1,0:T(8,128)(2,1)} custom-call(s32[1]{0:T(128)} %bitcast.3.refs_0_, bf16[256,2048]{1,0:T(8,128)(2,1)} %get-tuple-element.122.refs_0_.refs_1_, bf16[144,2048]{1,0:T(8,128)(2,1)} %collective-permute-done.14.refs_1_.refs_2_, bf16[128,2048]{1,0:T(8,128)(2,1)} %collective-permute-done.15.refs_2_.refs_3_, ...), custom_call_target="tpu_custom_call" | custom-call | tf_op jit(solution)/shard_map/product/pallas_call | solution.py:81
  179.5 7.5 %product.7.refs_10_ = bf16[1120,1408]{1,0:T(8,128)(2,1)} custom-call(s32[1]{0:T(128)} %bitcast.3.refs_0_, bf16[256,2048]{1,0:T(8,128)(2,1)} %bitcast.22, bf16[256,2048]{1,0:T(8,128)(2,1)} %collective-permute-done.2.refs_1_.refs_2_, bf16[256,2048]{1,0:T(8,128)(2,1)} %hold.14.refs_0_.refs_3_, bf16[256,2048]{1,0:T(8,128)(2,1)} %collective-permute-done.13.refs_1_.refs_4_, ...), custom_call_target="tpu_custom_call" | custom-call | tf_op jit(solution)/shard_map/product/pallas_call | solution.py:81
  187.0 7.5 %product.8.refs_2_.refs_0_ = bf16[1024,1408]{1,0:T(8,128)(2,1)} custom-call(s32[1]{0:T(128)} %bitcast.3.refs_0_, bf16[256,2048]{1,0:T(8,128)(2,1)} %get-tuple-element.122.refs_0_.refs_1_, bf16[144,2048]{1,0:T(8,128)(2,1)} %collective-permute-done.14.refs_1_.refs_2_, bf16[128,2048]{1,0:T(8,128)(2,1)} %collective-permute-done.15.refs_2_.refs_3_, ...), custom_call_target="tpu_custom_call" | custom-call | tf_op jit(solution)/shard_map/product/pallas_call | solution.py:81
  194.6 7.1 %feed_out.2 = (bf16[256,2048]{1,0:T(8,128)(2,1)}, bf16[256,2048]{1,0:T(8,128)(2,1)}) custom-call(bf16[512,1408]{1,0:T(8,128)(2,1)} %get-tuple-element.129.refs_6_.refs_0_, bf16[1408,2048]{1,0:T(8,128)(2,1)} %refs_1_.3, bf16[1024,1408]{1,0:T(8,128)(2,1)} %product.8.refs_2_.refs_0_), custom_call_target="tpu_custom_call" | custom-call | tf_op jit(solution)/shard_map/feed_out/pallas_call | solution.py:70
  202.0 6.4 %turn.1 = (f32[256,2048]{1,0:T(8,128)}, f32[1,2048]{1,0:T(1,128)}, bf16[272,2048]{1,0:T(8,128)(2,1)}) custom-call(bf16[256,2048]{1,0:T(8,128)(2,1)} %bitcast.23, bf16[256,2048]{1,0:T(8,128)(2,1)} %get-tuple-element.128.refs_1_, bf16[256,2048]{1,0:T(8,128)(2,1)} %collective-permute-done.22.refs_2_, bf16[256,2048]{1,0:T(8,128)(2,1)} %collective-permute-done.23.refs_3_, ...), custom_call_target="tpu_custom_call" | custom-call | tf_op jit(solution)/shard_map/turn/pallas_call | solution.py:70
  211.6 9.2 %back_local.2 = (bf16[2,256,512]{2,1,0:T(8,128)(2,1)}, bf16[2,256,512]{2,1,0:T(8,128)(2,1)}, f32[2,256,512]{2,1,0:T(8,128)}, f32[2,256,512]{2,1,0:T(8,128)}, f32[2,2,512]{2,1,0:T(2,128)}, /*index=5*/f32[1,512]{1,0:T(1,128)}) custom-call(bf16[272,2048]{1,0:T(8,128)(2,1)} %get-tuple-element.139.refs_0_.refs_1_, ...), custom_call_target="tpu_custom_call" | custom-call | tf_op jit(solution)/shard_map/back_local/pallas_call | solution.py:70
  224.4 7.1 %feed_out.3 = (bf16[256,2048]{1,0:T(8,128)(2,1)}, bf16[256,2048]{1,0:T(8,128)(2,1)}) custom-call(bf16[512,1408]{1,0:T(8,128)(2,1)} %get-tuple-element.125.refs_5_.refs_0_, bf16[1408,2048]{1,0:T(8,128)(2,1)} %refs_1_.3, bf16[256,2048]{1,0:T(8,128)(2,1)} %plus.4.refs_2_.refs_0_), custom_call_target="tpu_custom_call" | custom-call | tf_op jit(solution)/shard_map/feed_out/pallas_call | solution.py:70
  231.6 4.2 collective-permute-done.26.refs_0_
  238.9 9.2 %back_local.3 = (bf16[2,256,512]{2,1,0:T(8,128)(2,1)}, bf16[2,256,512]{2,1,0:T(8,128)(2,1)}, f32[2,256,512]{2,1,0:T(8,128)}, f32[2,256,512]{2,1,0:T(8,128)}, f32[2,4,512]{2,1,0:T(4,128)}, /*index=5*/f32[1,512]{1,0:T(1,128)}) custom-call(bf16[272,2048]{1,0:T(8,128)(2,1)} %hold.17.refs_0_.refs_3_, bf16[272,2048]{1,0:T(8,128)(2,1)} %collective-permute-done.27.refs_1_.refs_4_, ...), custom_call_target="tpu_custom_call" | custom-call | tf_op jit(solution)/shard_map/back_local/pallas_call | solution.py:70
  259.4 9.0 %product_add.6 = (bf16[512,1408]{1,0:T(8,128)(2,1)}, bf16[512,1408]{1,0:T(8,128)(2,1)}) custom-call(s32[1]{0:T(128)} %bitcast.3.refs_0_, bf16[256,2048]{1,0:T(8,128)(2,1)} %get-tuple-element.122.refs_0_.refs_1_, bf16[144,2048]{1,0:T(8,128)(2,1)} %collective-permute-done.14.refs_1_.refs_2_, bf16[128,2048]{1,0:T(8,128)(2,1)} %collective-permute-done.15.refs_2_.refs_3_, ...), custom_call_target="tpu_custom_call" | custom-call | tf_op jit(solution)/shard_map/product_add/pallas_call | solution.py:81
  268.4 8.5 %product_add.7 = (bf16[512,1408]{1,0:T(8,128)(2,1)}, bf16[512,1408]{1,0:T(8,128)(2,1)}) custom-call(s32[1]{0:T(128)} %bitcast.3.refs_0_, bf16[256,2048]{1,0:T(8,128)(2,1)} %bitcast.24, bf16[256,2048]{1,0:T(8,128)(2,1)} %collective-permute-done.2.refs_1_.refs_2_, bf16[256,2048]{1,0:T(8,128)(2,1)} %hold.14.refs_0_.refs_3_, ...), custom_call_target="tpu_custom_call" | custom-call | tf_op jit(solution)/shard_map/product_add/pallas_call | solution.py:81
  281.0 10.3 %back_mix.2 = (bf16[2,256,1024]{2,1,0:T(8,128)(2,1)}, bf16[256,2048]{1,0:T(8,128)(2,1)}, bf16[256,2048]{1,0:T(8,128)(2,1)}, f32[2,1,512]{2,1,0:T(1,128)}) custom-call(f32[2,256,512]{2,1,0:T(8,128)} %get-tuple-element.154.refs_0_, f32[2,256,512]{2,1,0:T(8,128)} %get-tuple-element.155.refs_1_, f32[2,256,512]{2,1,0:T(8,128)} %get-tuple-element.150.refs_5_.refs_2_, ...), custom_call_target="tpu_custom_call" | custom-call | tf_op jit(solution)/shard_map/back_mix/pallas_call | solution.py:70
  298.0 10.3 %back_mix.3 = (bf16[2,256,1024]{2,1,0:T(8,128)(2,1)}, bf16[256,2048]{1,0:T(8,128)(2,1)}, bf16[256,2048]{1,0:T(8,128)(2,1)}, f32[2,1,512]{2,1,0:T(1,128)}) custom-call(f32[2,256,512]{2,1,0:T(8,128)} %get-tuple-element.145.refs_0_, f32[2,256,512]{2,1,0:T(8,128)} %get-tuple-element.146.refs_1_, f32[2,256,512]{2,1,0:T(8,128)} %get-tuple-element.141.refs_5_.refs_2_, ...), custom_call_target="tpu_custom_call" | custom-call | tf_op jit(solution)/shard_map/back_mix/pallas_call | solution.py:70
  315.1 6.3 %product.9.refs_11_ = bf16[1024,1024]{1,0:T(8,128)(2,1)} custom-call(s32[1]{0:T(128)} %bitcast.3.refs_0_, bf16[256,2048]{1,0:T(8,128)(2,1)} %first_norm.1.refs_0_.refs_1_, bf16[256,2048]{1,0:T(8,128)(2,1)} %collective-permute-done.refs_1_.refs_2_, bf16[256,2048]{1,0:T(8,128)(2,1)} %hold.12.refs_0_.refs_3_, ...), custom_call_target="tpu_custom_call" | custom-call | tf_op jit(solution)/shard_map/product/pallas_call | solution.py:81
  322.4 8.6 %product_add.8 = (bf16[512,1408]{1,0:T(8,128)(2,1)}, bf16[512,1408]{1,0:T(8,128)(2,1)}) custom-call(s32[1]{0:T(128)} %bitcast.3.refs_0_, bf16[256,2048]{1,0:T(8,128)(2,1)} %get-tuple-element.122.refs_0_.refs_1_, bf16[144,2048]{1,0:T(8,128)(2,1)} %collective-permute-done.14.refs_1_.refs_2_, bf16[128,2048]{1,0:T(8,128)(2,1)} %collective-permute-done.15.refs_2_.refs_3_, ...), custom_call_target="tpu_custom_call" | custom-call | tf_op jit(solution)/shard_map/product_add/pallas_call | solution.py:81
  334.2 5.4 %last.1 = (f32[256,2048]{1,0:T(8,128)}, f32[1,2048]{1,0:T(1,128)}) custom-call(bf16[256,2048]{1,0:T(8,128)(2,1)} %bitcast.29, bf16[256,2048]{1,0:T(8,128)(2,1)} %get-tuple-element.160.refs_2_.refs_1_, bf16[256,2048]{1,0:T(8,128)(2,1)} %collective-permute-done.35.refs_2_, bf16[256,2048]{1,0:T(8,128)(2,1)} %collective-permute-done.36.refs_3_, ...), custom_call_target="tpu_custom_call" | custom-call | tf_op jit(solution)/shard_map/last/pallas_call | solution.py:70
  341.2 9.5 %collective-permute-done.40.refs_1_ = bf16[512,1408]{1,0:T(8,128)(2,1)} collective-permute-done((bf16[512,1408]{1,0:T(8,128)(2,1)}, bf16[512,1408]{1,0:T(8,128)(2,1)}, u32[]{:S(2)}, u32[]{:S(2)}) %collective-permute-start.40) | collective-permute-done | bytes 1441824 | tf_op jit(solution)/shard_map/ppermute | solution.py:18
  350.7 3.8 collective-permute-start.44
  354.5 4.9 product.10.refs_2_
  362.7 5.0 product.11.refs_4_
  369.8 8.3 %collective-permute-done.45.refs_1_ = bf16[512,1408]{1,0:T(8,128)(2,1)} collective-permute-done((bf16[512,1408]{1,0:T(8,128)(2,1)}, bf16[512,1408]{1,0:T(8,128)(2,1)}, u32[]{:S(2)}, u32[]{:S(2)}) %collective-permute-start.45) | collective-permute-done | bytes 1441824 | tf_op jit(solution)/shard_map/ppermute | solution.py:18
  378.1 4.3 result.1.refs_2_
  385.6 13.8 %collective-permute-done.44.two = bf16[256,1408]{1,0:T(8,128)(2,1)S(1)} collective-permute-done((bf16[256,1408]{1,0:T(8,128)(2,1)}, bf16[256,1408]{1,0:T(8,128)(2,1)S(1)}, u32[]{:S(2)}, u32[]{:S(2)}) %collective-permute-start.44) | collective-permute-done | bytes 720928 | tf_op jit(solution)/shard_map/ppermute | solution.py:18
  403.9 7.2 %product_add.9 = (bf16[512,1024]{1,0:T(8,128)(2,1)}, bf16[512,1024]{1,0:T(8,128)(2,1)}) custom-call(s32[1]{0:T(128)} %bitcast.3.refs_0_, bf16[256,2048]{1,0:T(8,128)(2,1)} %first_norm.1.refs_0_.refs_1_, bf16[256,2048]{1,0:T(8,128)(2,1)} %collective-permute-done.refs_1_.refs_2_, bf16[256,2048]{1,0:T(8,128)(2,1)} %hold.12.refs_0_.refs_3_, ...), custom_call_target="tpu_custom_call" | custom-call | tf_op jit(solution)/shard_map/product_add/pallas_call | solution.py:81
  419.9 5.4 %product_add.10 = (bf16[512,512]{1,0:T(8,128)(2,1)}, bf16[512,512]{1,0:T(8,128)(2,1)}) custom-call(s32[1]{0:T(128)} %bitcast.3.refs_0_, bf16[256,2048]{1,0:T(8,128)(2,1)} %first_norm.1.refs_0_.refs_1_, bf16[256,2048]{1,0:T(8,128)(2,1)} %collective-permute-done.refs_1_.refs_2_, bf16[256,2048]{1,0:T(8,128)(2,1)} %hold.12.refs_0_.refs_3_, ...), custom_call_target="tpu_custom_call" | custom-call | tf_op jit(solution)/shard_map/product_add/pallas_call | solution.py:81
  425.4 6.0 %collective-permute-start.46 = (bf16[512,512]{1,0:T(8,128)(2,1)}, bf16[512,512]{1,0:T(8,128)(2,1)}, u32[]{:S(2)}, u32[]{:S(2)}) collective-permute-start(bf16[512,512]{1,0:T(8,128)(2,1)} %get-tuple-element.179.refs_8_), channel_id=1, source_target_pairs={{0,8},{4,12},{8,0},{12,4},{16,24},{20,28},{24,16},{28,20},{1,9},{5... | collective-permute-start | bytes 1572872 | tf_op jit(solution)/shard_map/ppermute | solution.py:18
  439.0 5.4 %product_add.11 = (bf16[512,512]{1,0:T(8,128)(2,1)}, bf16[512,512]{1,0:T(8,128)(2,1)}) custom-call(s32[1]{0:T(128)} %bitcast.3.refs_0_, bf16[272,2048]{1,0:T(8,128)(2,1)} %get-tuple-element.139.refs_0_.refs_1_, bf16[272,2048]{1,0:T(8,128)(2,1)} %collective-permute-done.24.refs_1_.refs_2_, bf16[272,2048]{1,0:T(8,128)(2,1)} %hold.17.refs_0_.refs_3_, ...), custom_call_target="tpu_custom_call" | custom-call | tf_op jit(solution)/shard_map/product_add/pallas_call | solution.py:81
  446.2 6.1 %collective-permute-done.48.refs_1_ = bf16[512,1024]{1,0:T(8,128)(2,1)} collective-permute-done((bf16[512,1024]{1,0:T(8,128)(2,1)}, bf16[512,1024]{1,0:T(8,128)(2,1)}, u32[]{:S(2)}, u32[]{:S(2)}) %collective-permute-start.48) | collective-permute-done | bytes 1048608 | tf_op jit(solution)/shard_map/ppermute | solution.py:18
  462.2 8.8 %collective-permute-done.46.refs_1_ = bf16[512,512]{1,0:T(8,128)(2,1)} collective-permute-done((bf16[512,512]{1,0:T(8,128)(2,1)}, bf16[512,512]{1,0:T(8,128)(2,1)}, u32[]{:S(2)}, u32[]{:S(2)}) %collective-permute-start.46) | collective-permute-done | bytes 524320 | tf_op jit(solution)/shard_map/ppermute | solution.py:18
  473.1 4.2 collective-permute-start.50
  477.4 5.6 %collective-permute-done.52.refs_1_ = bf16[512,512]{1,0:T(8,128)(2,1)} collective-permute-done((bf16[512,512]{1,0:T(8,128)(2,1)}, bf16[512,512]{1,0:T(8,128)(2,1)}, u32[]{:S(2)}, u32[]{:S(2)}) %collective-permute-start.52) | collective-permute-done | bytes 524320 | tf_op jit(solution)/shard_map/ppermute | solution.py:18
  485.1 7.2 %collective-permute-start.53 = (bf16[256,512]{1,0:T(8,128)(2,1)}, bf16[256,512]{1,0:T(8,128)(2,1)S(1)}, u32[]{:S(2)}, u32[]{:S(2)}) collective-permute-start(bf16[256,512]{1,0:T(8,128)(2,1)} %get-tuple-element.188.refs_0_.refs_1_), channel_id=1, source_target_pairs={{0,16},{4,20},{8,24},{12,28},{16,0},{20,4},{24,8},{28,12},{1,17},{... | collective-permute-start | bytes 786440 | tf_op jit(solution)/shard_map/ppermute | solution.py:18
  (207 shorter events, 158.0 us)
Async XLA Ops:
  4.3 4.8 collective-permute-start
  4.8 15.4 %collective-permute-start.2 = (bf16[256,2048]{1,0:T(8,128)(2,1)}, bf16[256,2048]{1,0:T(8,128)(2,1)}, u32[]{:S(2)}, u32[]{:S(2)}) collective-permute-start(bf16[256,2048]{1,0:T(8,128)(2,1)} %bitcast.20), channel_id=1, source_target_pairs={{0,1},{1,0},{2,3},{3,2},{4,5},{5,4},{6,7},{7,6},{8,9},{9,8},{10,11... | collective-permute-start | bytes 3145736 | tf_op jit(solution)/shard_map/ppermute | solution.py:18
  4.8 26.6 %collective-permute-start.1 = (bf16[256,2048]{1,0:T(8,128)(2,1)}, bf16[256,2048]{1,0:T(8,128)(2,1)}, u32[]{:S(2)}, u32[]{:S(2)}) collective-permute-start(bf16[256,2048]{1,0:T(8,128)(2,1)} %first_norm.1.refs_0_.refs_1_), channel_id=1, source_target_pairs={{0,2},{1,3},{2,0},{3,1},{4,6},{5,7},{6,4},{7,5},{8,10},{9,11},{10,... | collective-permute-start | bytes 3145736 | tf_op jit(solution)/shard_map/ppermute | solution.py:18
  32.4 45.0 %collective-permute-start.12 = (bf16[256,2048]{1,0:T(8,128)(2,1)}, bf16[256,2048]{1,0:T(8,128)(2,1)}, u32[]{:S(2)}, u32[]{:S(2)}) collective-permute-start(bf16[256,2048]{1,0:T(8,128)(2,1)} %hold.13), channel_id=1, source_target_pairs={{0,2},{1,3},{2,0},{3,1},{4,6},{5,7},{6,4},{7,5},{8,10},{9,11},{10,... | collective-permute-start | bytes 3145736 | tf_op jit(solution)/shard_map/ppermute | solution.py:18
  51.9 11.0 %collective-permute-start.5 = (f32[2,4,512]{2,1,0:T(4,128)}, f32[2,4,512]{2,1,0:T(4,128)S(1)}, u32[]{:S(2)}, u32[]{:S(2)}) collective-permute-start(f32[2,4,512]{2,1,0:T(4,128)} %pair.2), channel_id=1, source_target_pairs={{0,8},{4,12},{8,16},{12,20},{16,24},{20,28},{1,9},{5,13},{9,17},{1... | collective-permute-start | bytes 49160 | tf_op jit(solution)/shard_map/ppermute | solution.py:24
  55.6 7.3 %collective-permute-start.6 = (f32[2,4,512]{2,1,0:T(4,128)}, f32[2,4,512]{2,1,0:T(4,128)S(1)}, u32[]{:S(2)}, u32[]{:S(2)}) collective-permute-start(f32[2,4,512]{2,1,0:T(4,128)} %pair.2), channel_id=1, source_target_pairs={{0,16},{4,20},{8,24},{12,28},{1,17},{5,21},{9,25},{13,29},{2,18},{... | collective-permute-start | bytes 49160 | tf_op jit(solution)/shard_map/ppermute | solution.py:24
  71.2 6.3 %collective-permute-start.9 = (bf16[272,2048]{1,0:T(8,128)(2,1)}, bf16[272,2048]{1,0:T(8,128)(2,1)}, u32[]{:S(2)}, u32[]{:S(2)}) collective-permute-start(bf16[272,2048]{1,0:T(8,128)(2,1)} %get-tuple-element.114), channel_id=1, source_target_pairs={{0,1},{1,0},{2,3},{3,2},{4,5},{5,4},{6,7},{7,6},{8,9},{9,8},{10,11... | collective-permute-start | bytes 3342344 | tf_op jit(solution)/shard_map/ppermute | solution.py:18
  76.9 13.0 %collective-permute-start.8 = (bf16[272,2048]{1,0:T(8,128)(2,1)}, bf16[272,2048]{1,0:T(8,128)(2,1)}, u32[]{:S(2)}, u32[]{:S(2)}) collective-permute-start(bf16[272,2048]{1,0:T(8,128)(2,1)} %get-tuple-element.113), channel_id=1, source_target_pairs={{0,1},{1,0},{2,3},{3,2},{4,5},{5,4},{6,7},{7,6},{8,9},{9,8},{10,11... | collective-permute-start | bytes 3342344 | tf_op jit(solution)/shard_map/ppermute | solution.py:18
  77.4 4.9 collective-permute-start.13
  80.3 16.3 %collective-permute-start.11 = (bf16[144,2048]{1,0:T(8,128)(2,1)}, bf16[144,2048]{1,0:T(8,128)(2,1)S(1)}, u32[]{:S(2)}, u32[]{:S(2)}) collective-permute-start(bf16[144,2048]{1,0:T(8,128)(2,1)} %get-tuple-element.116), channel_id=1, source_target_pairs={{0,2},{1,3},{2,0},{3,1},{4,6},{5,7},{6,4},{7,5},{8,10},{9,11},{10,... | collective-permute-start | bytes 1769480 | tf_op jit(solution)/shard_map/ppermute | solution.py:18
  81.8 26.2 %collective-permute-start.10 = (bf16[128,2048]{1,0:T(8,128)(2,1)}, bf16[128,2048]{1,0:T(8,128)(2,1)}, u32[]{:S(2)}, u32[]{:S(2)}) collective-permute-start(bf16[128,2048]{1,0:T(8,128)(2,1)} %get-tuple-element.115.refs_3_), channel_id=1, source_target_pairs={{0,2},{1,3},{2,0},{3,1},{4,6},{5,7},{6,4},{7,5},{8,10},{9,11},{10,... | collective-permute-start | bytes 1572872 | tf_op jit(solution)/shard_map/ppermute | solution.py:18
  101.2 12.7 %collective-permute-start.14 = (bf16[144,2048]{1,0:T(8,128)(2,1)}, bf16[144,2048]{1,0:T(8,128)(2,1)}, u32[]{:S(2)}, u32[]{:S(2)}) collective-permute-start(bf16[144,2048]{1,0:T(8,128)(2,1)} %get-tuple-element.123), channel_id=1, source_target_pairs={{0,1},{1,0},{2,3},{3,2},{4,5},{5,4},{6,7},{7,6},{8,9},{9,8},{10,11... | collective-permute-start | bytes 1769480 | tf_op jit(solution)/shard_map/ppermute | solution.py:18
  101.2 35.7 %collective-permute-start.16 = (bf16[144,2048]{1,0:T(8,128)(2,1)}, bf16[144,2048]{1,0:T(8,128)(2,1)S(1)}, u32[]{:S(2)}, u32[]{:S(2)}) collective-permute-start(bf16[144,2048]{1,0:T(8,128)(2,1)} %get-tuple-element.123), channel_id=1, source_target_pairs={{0,2},{1,3},{2,0},{3,1},{4,6},{5,7},{6,4},{7,5},{8,10},{9,11},{10,... | collective-permute-start | bytes 1769480 | tf_op jit(solution)/shard_map/ppermute | solution.py:18
  111.6 26.2 %collective-permute-start.17 = (bf16[128,2048]{1,0:T(8,128)(2,1)}, bf16[128,2048]{1,0:T(8,128)(2,1)}, u32[]{:S(2)}, u32[]{:S(2)}) collective-permute-start(bf16[128,2048]{1,0:T(8,128)(2,1)} %get-tuple-element.124), channel_id=1, source_target_pairs={{0,2},{1,3},{2,0},{3,1},{4,6},{5,7},{6,4},{7,5},{8,10},{9,11},{10,... | collective-permute-start | bytes 1572872 | tf_op jit(solution)/shard_map/ppermute | solution.py:18
  164.6 8.3 %collective-permute-start.20 = (bf16[256,2048]{1,0:T(8,128)(2,1)}, bf16[256,2048]{1,0:T(8,128)(2,1)}, u32[]{:S(2)}, u32[]{:S(2)}) collective-permute-start(bf16[256,2048]{1,0:T(8,128)(2,1)} %get-tuple-element.133), channel_id=1, source_target_pairs={{0,1},{1,0},{2,3},{3,2},{4,5},{5,4},{6,7},{7,6},{8,9},{9,8},{10,11... | collective-permute-start | bytes 3145736 | tf_op jit(solution)/shard_map/ppermute | solution.py:18
  164.7 37.0 %collective-permute-start.22 = (bf16[256,2048]{1,0:T(8,128)(2,1)}, bf16[256,2048]{1,0:T(8,128)(2,1)}, u32[]{:S(2)}, u32[]{:S(2)}) collective-permute-start(bf16[256,2048]{1,0:T(8,128)(2,1)} %get-tuple-element.136), channel_id=1, source_target_pairs={{0,1},{1,0},{2,3},{3,2},{4,5},{5,4},{6,7},{7,6},{8,9},{9,8},{10,11... | collective-permute-start | bytes 3145736 | tf_op jit(solution)/shard_map/ppermute | solution.py:18
  176.5 25.5 %collective-permute-start.23 = (bf16[256,2048]{1,0:T(8,128)(2,1)}, bf16[256,2048]{1,0:T(8,128)(2,1)}, u32[]{:S(2)}, u32[]{:S(2)}) collective-permute-start(bf16[256,2048]{1,0:T(8,128)(2,1)} %plus.3.refs_7_.refs_11_), channel_id=1, source_target_pairs={{0,2},{1,3},{2,0},{3,1},{4,6},{5,7},{6,4},{7,5},{8,10},{9,11},{10,... | collective-permute-start | bytes 3145736 | tf_op jit(solution)/shard_map/ppermute | solution.py:18
  178.0 80.1 %collective-permute-start.33 = (bf16[1120,1408]{1,0:T(8,128)(2,1)}, bf16[1120,1408]{1,0:T(8,128)(2,1)}, u32[]{:S(2)}, u32[]{:S(2)}) collective-permute-start(bf16[1120,1408]{1,0:T(8,128)(2,1)} %product.6.refs_2_), channel_id=1, source_target_pairs={{0,4},{4,0},{8,12},{12,8},{16,20},{20,16},{24,28},{28,24},{1,5},{5... | collective-permute-start | bytes 9461768 | tf_op jit(solution)/shard_map/ppermute | solution.py:18
  187.0 81.4 %collective-permute-start.32 = (bf16[1120,1408]{1,0:T(8,128)(2,1)}, bf16[1120,1408]{1,0:T(8,128)(2,1)}, u32[]{:S(2)}, u32[]{:S(2)}) collective-permute-start(bf16[1120,1408]{1,0:T(8,128)(2,1)} %product.7.refs_10_), channel_id=1, source_target_pairs={{0,8},{4,12},{8,0},{12,4},{16,24},{20,28},{24,16},{28,20},{1,9},{5... | collective-permute-start | bytes 9461768 | tf_op jit(solution)/shard_map/ppermute | solution.py:18
  208.5 27.3 %collective-permute-start.26 = (bf16[272,2048]{1,0:T(8,128)(2,1)}, bf16[272,2048]{1,0:T(8,128)(2,1)}, u32[]{:S(2)}, u32[]{:S(2)}) collective-permute-start(bf16[272,2048]{1,0:T(8,128)(2,1)} %get-tuple-element.139.refs_0_.refs_1_), channel_id=1, source_target_pairs={{0,2},{1,3},{2,0},{3,1},{4,6},{5,7},{6,4},{7,5},{8,10},{9,11},{10,... | collective-permute-start | bytes 3342344 | tf_op jit(solution)/shard_map/ppermute | solution.py:18
  210.1 10.7 %collective-permute-start.21 = (bf16[256,2048]{1,0:T(8,128)(2,1)}, bf16[256,2048]{1,0:T(8,128)(2,1)}, u32[]{:S(2)}, u32[]{:S(2)}) collective-permute-start(bf16[256,2048]{1,0:T(8,128)(2,1)} %get-tuple-element.135), channel_id=1, source_target_pairs={{0,1},{1,0},{2,3},{3,2},{4,5},{5,4},{6,7},{7,6},{8,9},{9,8},{10,11... | collective-permute-start | bytes 3145736 | tf_op jit(solution)/shard_map/ppermute | solution.py:18
  254.0 68.4 %collective-permute-start.37 = (bf16[1024,1408]{1,0:T(8,128)(2,1)}, bf16[1024,1408]{1,0:T(8,128)(2,1)}, u32[]{:S(2)}, u32[]{:S(2)}) collective-permute-start(bf16[1024,1408]{1,0:T(8,128)(2,1)} %hold.18), channel_id=1, source_target_pairs={{0,4},{4,0},{8,12},{12,8},{16,20},{20,16},{24,28},{28,24},{1,5},{5... | collective-permute-start | bytes 8650760 | tf_op jit(solution)/shard_map/ppermute | solution.py:18
  255.5 21.4 %collective-permute-start.29 = (f32[2,4,512]{2,1,0:T(4,128)S(1)}, f32[2,4,512]{2,1,0:T(4,128)S(1)}, u32[]{:S(2)}, u32[]{:S(2)}) collective-permute-start(f32[2,4,512]{2,1,0:T(4,128)S(1)} %copy-done.8), channel_id=1, source_target_pairs={{8,0},{12,4},{16,8},{20,12},{24,16},{28,20},{9,1},{13,5},{17,9},{2... | collective-permute-start | bytes 49160 | tf_op jit(solution)/shard_map/ppermute | solution.py:24
  256.8 20.1 %collective-permute-start.30 = (f32[2,4,512]{2,1,0:T(4,128)S(1)}, f32[2,4,512]{2,1,0:T(4,128)S(1)}, u32[]{:S(2)}, u32[]{:S(2)}) collective-permute-start(f32[2,4,512]{2,1,0:T(4,128)S(1)} %copy-done.8), channel_id=1, source_target_pairs={{16,0},{20,4},{24,8},{28,12},{17,1},{21,5},{25,9},{29,13},{18,2},{... | collective-permute-start | bytes 49160 | tf_op jit(solution)/shard_map/ppermute | solution.py:24
  258.1 18.8 %collective-permute-start.31 = (f32[2,4,512]{2,1,0:T(4,128)S(1)}, f32[2,4,512]{2,1,0:T(4,128)S(1)}, u32[]{:S(2)}, u32[]{:S(2)}) collective-permute-start(f32[2,4,512]{2,1,0:T(4,128)S(1)} %copy-done.8), channel_id=1, source_target_pairs={{24,0},{28,4},{25,1},{29,5},{26,2},{30,6},{27,3},{31,7}} | collective-permute-start | bytes 49160 | tf_op jit(solution)/shard_map/ppermute | solution.py:24
  279.0 32.9 %collective-permute-start.38 = (bf16[512,1408]{1,0:T(8,128)(2,1)}, bf16[512,1408]{1,0:T(8,128)(2,1)}, u32[]{:S(2)}, u32[]{:S(2)}) collective-permute-start(bf16[512,1408]{1,0:T(8,128)(2,1)} %hold.19), channel_id=1, source_target_pairs={{0,8},{4,12},{8,0},{12,4},{16,24},{20,28},{24,16},{28,20},{1,9},{5... | collective-permute-start | bytes 4325384 | tf_op jit(solution)/shard_map/ppermute | solution.py:18
  308.3 24.5 %collective-permute-start.35 = (bf16[256,2048]{1,0:T(8,128)(2,1)}, bf16[256,2048]{1,0:T(8,128)(2,1)}, u32[]{:S(2)}, u32[]{:S(2)}) collective-permute-start(bf16[256,2048]{1,0:T(8,128)(2,1)} %get-tuple-element.161), channel_id=1, source_target_pairs={{0,1},{1,0},{2,3},{3,2},{4,5},{5,4},{6,7},{7,6},{8,9},{9,8},{10,11... | collective-permute-start | bytes 3145736 | tf_op jit(solution)/shard_map/ppermute | solution.py:18
  308.5 25.8 %collective-permute-start.36 = (bf16[256,2048]{1,0:T(8,128)(2,1)}, bf16[256,2048]{1,0:T(8,128)(2,1)}, u32[]{:S(2)}, u32[]{:S(2)}) collective-permute-start(bf16[256,2048]{1,0:T(8,128)(2,1)} %plus.5.refs_10_), channel_id=1, source_target_pairs={{0,2},{1,3},{2,0},{3,1},{4,6},{5,7},{6,4},{7,5},{8,10},{9,11},{10,... | collective-permute-start | bytes 3145736 | tf_op jit(solution)/shard_map/ppermute | solution.py:18
  310.0 40.7 %collective-permute-start.40 = (bf16[512,1408]{1,0:T(8,128)(2,1)}, bf16[512,1408]{1,0:T(8,128)(2,1)}, u32[]{:S(2)}, u32[]{:S(2)}) collective-permute-start(bf16[512,1408]{1,0:T(8,128)(2,1)} %get-tuple-element.153.refs_6_), channel_id=1, source_target_pairs={{0,4},{4,0},{8,12},{12,8},{16,20},{20,16},{24,28},{28,24},{1,5},{5... | collective-permute-start | bytes 4325384 | tf_op jit(solution)/shard_map/ppermute | solution.py:18
  321.4 82.5 %collective-permute-start.43 = (bf16[1024,1024]{1,0:T(8,128)(2,1)}, bf16[1024,1024]{1,0:T(8,128)(2,1)}, u32[]{:S(2)}, u32[]{:S(2)}) collective-permute-start(bf16[1024,1024]{1,0:T(8,128)(2,1)} %product.9.refs_11_), channel_id=1, source_target_pairs={{0,4},{4,0},{8,12},{12,8},{16,20},{20,16},{24,28},{28,24},{1,5},{5... | collective-permute-start | bytes 6291464 | tf_op jit(solution)/shard_map/ppermute | solution.py:18
  331.0 47.1 %collective-permute-start.45 = (bf16[512,1408]{1,0:T(8,128)(2,1)}, bf16[512,1408]{1,0:T(8,128)(2,1)}, u32[]{:S(2)}, u32[]{:S(2)}) collective-permute-start(bf16[512,1408]{1,0:T(8,128)(2,1)} %get-tuple-element.167.refs_6_), channel_id=1, source_target_pairs={{0,8},{4,12},{8,0},{12,4},{16,24},{20,28},{24,16},{28,20},{1,9},{5... | collective-permute-start | bytes 4325384 | tf_op jit(solution)/shard_map/ppermute | solution.py:18
  332.8 34.9 %collective-permute-start.25 = (bf16[256,2048]{1,0:T(8,128)(2,1)}, bf16[256,2048]{1,0:T(8,128)(2,1)}, u32[]{:S(2)}, u32[]{:S(2)}) collective-permute-start(bf16[256,2048]{1,0:T(8,128)(2,1)} %get-tuple-element.144), channel_id=1, source_target_pairs={{0,1},{1,0},{2,3},{3,2},{4,5},{5,4},{6,7},{7,6},{8,9},{9,8},{10,11... | collective-permute-start | bytes 3145736 | tf_op jit(solution)/shard_map/ppermute | solution.py:18
  339.6 28.6 %collective-permute-start.39 = (bf16[256,2048]{1,0:T(8,128)(2,1)}, bf16[256,2048]{1,0:T(8,128)(2,1)}, u32[]{:S(2)}, u32[]{:S(2)}) collective-permute-start(bf16[256,2048]{1,0:T(8,128)(2,1)} %hold.20), channel_id=1, source_target_pairs={{0,2},{1,3},{2,0},{3,1},{4,6},{5,7},{6,4},{7,5},{8,10},{9,11},{10,... | collective-permute-start | bytes 3145736 | tf_op jit(solution)/shard_map/ppermute | solution.py:18
  350.7 48.8 %collective-permute-start.44 = (bf16[256,1408]{1,0:T(8,128)(2,1)}, bf16[256,1408]{1,0:T(8,128)(2,1)S(1)}, u32[]{:S(2)}, u32[]{:S(2)}) collective-permute-start(bf16[256,1408]{1,0:T(8,128)(2,1)} %get-tuple-element.166.refs_7_), channel_id=1, source_target_pairs={{0,16},{4,20},{8,24},{12,28},{16,0},{20,4},{24,8},{28,12},{1,17},{... | collective-permute-start | bytes 2162696 | tf_op jit(solution)/shard_map/ppermute | solution.py:18
  367.7 52.3 %collective-permute-start.41 = (bf16[1024,512]{1,0:T(8,128)(2,1)}, bf16[1024,512]{1,0:T(8,128)(2,1)}, u32[]{:S(2)}, u32[]{:S(2)}) collective-permute-start(bf16[1024,512]{1,0:T(8,128)(2,1)} %product.11.refs_4_), channel_id=1, source_target_pairs={{0,4},{4,0},{8,12},{12,8},{16,20},{20,16},{24,28},{28,24},{1,5},{5... | collective-permute-start | bytes 3145736 | tf_op jit(solution)/shard_map/ppermute | solution.py:18
  368.2 70.7 %collective-permute-start.49 = (bf16[1024,512]{1,0:T(8,128)(2,1)}, bf16[1024,512]{1,0:T(8,128)(2,1)}, u32[]{:S(2)}, u32[]{:S(2)}) collective-permute-start(bf16[1024,512]{1,0:T(8,128)(2,1)} %product.10.refs_2_), channel_id=1, source_target_pairs={{0,4},{4,0},{8,12},{12,8},{16,20},{20,16},{24,28},{28,24},{1,5},{5... | collective-permute-start | bytes 3145736 | tf_op jit(solution)/shard_map/ppermute | solution.py:18
  378.1 39.3 %collective-permute-start.42 = (bf16[256,1408]{1,0:T(8,128)(2,1)}, bf16[256,1408]{1,0:T(8,128)(2,1)}, u32[]{:S(2)}, u32[]{:S(2)}) collective-permute-start(bf16[256,1408]{1,0:T(8,128)(2,1)} %get-tuple-element.172.refs_7_), channel_id=1, source_target_pairs={{0,16},{4,20},{8,24},{12,28},{16,0},{20,4},{24,8},{28,12},{1,17},{... | collective-permute-start | bytes 2162696 | tf_op jit(solution)/shard_map/ppermute | solution.py:18
  411.2 41.1 %collective-permute-start.48 = (bf16[512,1024]{1,0:T(8,128)(2,1)}, bf16[512,1024]{1,0:T(8,128)(2,1)}, u32[]{:S(2)}, u32[]{:S(2)}) collective-permute-start(bf16[512,1024]{1,0:T(8,128)(2,1)} %get-tuple-element.177.refs_0_), channel_id=1, source_target_pairs={{0,8},{4,12},{8,0},{12,4},{16,24},{20,28},{24,16},{28,20},{1,9},{5... | collective-permute-start | bytes 3145736 | tf_op jit(solution)/shard_map/ppermute | solution.py:18
  414.1 44.5 %collective-permute-start.47 = (bf16[256,1408]{1,0:T(8,128)(2,1)S(1)}, bf16[256,1408]{1,0:T(8,128)(2,1)}, u32[]{:S(2)}, u32[]{:S(2)}) collective-permute-start(bf16[256,1408]{1,0:T(8,128)(2,1)S(1)} %copy-done.4), channel_id=1, source_target_pairs={{0,16},{4,20},{8,24},{12,28},{16,0},{20,4},{24,8},{28,12},{1,17},{... | collective-permute-start | bytes 2162696 | tf_op jit(solution)/shard_map/ppermute | solution.py:18
  425.4 45.6 %collective-permute-start.46 = (bf16[512,512]{1,0:T(8,128)(2,1)}, bf16[512,512]{1,0:T(8,128)(2,1)}, u32[]{:S(2)}, u32[]{:S(2)}) collective-permute-start(bf16[512,512]{1,0:T(8,128)(2,1)} %get-tuple-element.179.refs_8_), channel_id=1, source_target_pairs={{0,8},{4,12},{8,0},{12,4},{16,24},{20,28},{24,16},{28,20},{1,9},{5... | collective-permute-start | bytes 1572872 | tf_op jit(solution)/shard_map/ppermute | solution.py:18
  432.7 11.7 %collective-permute-start.55 = (f32[2,512]{1,0:T(2,128)S(1)}, f32[2,512]{1,0:T(2,128)S(1)}, u32[]{:S(2)}, u32[]{:S(2)}) collective-permute-start(f32[2,512]{1,0:T(2,128)S(1)} %get-tuple-element.197), channel_id=1, source_target_pairs={{0,2},{1,3},{2,0},{3,1},{4,6},{5,7},{6,4},{7,5},{8,10},{9,11},{10,... | collective-permute-start | bytes 12296 | tf_op jit(solution)/shard_map/ppermute | solution.py:18
  438.9 7.2 %collective-permute-start.56 = (f32[2,512]{1,0:T(2,128)S(1)}, f32[2,512]{1,0:T(2,128)S(1)}, u32[]{:S(2)}, u32[]{:S(2)}) collective-permute-start(f32[2,512]{1,0:T(2,128)S(1)} %get-tuple-element.198), channel_id=1, source_target_pairs={{0,3},{1,2},{2,1},{3,0},{4,7},{5,6},{6,5},{7,4},{8,11},{9,10},{10,... | collective-permute-start | bytes 12296 | tf_op jit(solution)/shard_map/ppermute | solution.py:18
  444.4 38.6 %collective-permute-start.52 = (bf16[512,512]{1,0:T(8,128)(2,1)}, bf16[512,512]{1,0:T(8,128)(2,1)}, u32[]{:S(2)}, u32[]{:S(2)}) collective-permute-start(bf16[512,512]{1,0:T(8,128)(2,1)} %get-tuple-element.182.refs_2_), channel_id=1, source_target_pairs={{0,8},{4,12},{8,0},{12,4},{16,24},{20,28},{24,16},{28,20},{1,9},{5... | collective-permute-start | bytes 1572872 | tf_op jit(solution)/shard_map/ppermute | solution.py:18
  455.1 41.1 %collective-permute-start.51 = (bf16[256,1024]{1,0:T(8,128)(2,1)}, bf16[256,1024]{1,0:T(8,128)(2,1)}, u32[]{:S(2)}, u32[]{:S(2)}) collective-permute-start(bf16[256,1024]{1,0:T(8,128)(2,1)} %get-tuple-element.183.refs_1_), channel_id=1, source_target_pairs={{0,16},{4,20},{8,24},{12,28},{16,0},{20,4},{24,8},{28,12},{1,17},{... | collective-permute-start | bytes 1572872 | tf_op jit(solution)/shard_map/ppermute | solution.py:18
  473.1 26.6 %collective-permute-start.50 = (bf16[256,512]{1,0:T(8,128)(2,1)}, bf16[256,512]{1,0:T(8,128)(2,1)S(1)}, u32[]{:S(2)}, u32[]{:S(2)}) collective-permute-start(bf16[256,512]{1,0:T(8,128)(2,1)} %get-tuple-element.185.refs_2_), channel_id=1, source_target_pairs={{0,16},{4,20},{8,24},{12,28},{16,0},{20,4},{24,8},{28,12},{1,17},{... | collective-permute-start | bytes 786440 | tf_op jit(solution)/shard_map/ppermute | solution.py:18
  477.3 14.9 %collective-permute-start.57 = (f32[4,512]{1,0:T(4,128)S(1)}, f32[4,512]{1,0:T(4,128)S(1)}, u32[]{:S(2)}, u32[]{:S(2)}) collective-permute-start(f32[4,512]{1,0:T(4,128)S(1)} %pad_maximum_fusion), channel_id=1, source_target_pairs={{0,4},{4,0},{8,12},{12,8},{16,20},{20,16},{24,28},{28,24},{1,5},{5... | collective-permute-start | bytes 24584 | tf_op jit(solution)/shard_map/ppermute | solution.py:18
  485.1 19.9 %collective-permute-start.53 = (bf16[256,512]{1,0:T(8,128)(2,1)}, bf16[256,512]{1,0:T(8,128)(2,1)S(1)}, u32[]{:S(2)}, u32[]{:S(2)}) collective-permute-start(bf16[256,512]{1,0:T(8,128)(2,1)} %get-tuple-element.188.refs_0_.refs_1_), channel_id=1, source_target_pairs={{0,16},{4,20},{8,24},{12,28},{16,0},{20,4},{24,8},{28,12},{1,17},{... | collective-permute-start | bytes 786440 | tf_op jit(solution)/shard_map/ppermute | solution.py:18
  493.6 10.0 %collective-permute-start.58 = (f32[4,512]{1,0:T(4,128)S(1)}, f32[4,512]{1,0:T(4,128)S(1)}, u32[]{:S(2)}, u32[]{:S(2)}) collective-permute-start(f32[4,512]{1,0:T(4,128)S(1)} %fusion.4), channel_id=1, source_target_pairs={{0,8},{4,12},{8,0},{12,4},{16,24},{20,28},{24,16},{28,20},{1,9},{5... | collective-permute-start | bytes 24584 | tf_op jit(solution)/shard_map/ppermute | solution.py:18
  (39 other events, 164.1 us)
